TPU v7x, 32 devices: a whole 2x2x4 slice. The times are simulated.
32 devices in a mesh: gx: 8 (over z, x), gy: 4 (over y, core).
Axes of the slice: x: 2, y: 2, z: 4, core: 2. Of those that a mesh axis runs over, the one named last changes fastest.
Arguments:
- source_term: float32 [128, 64, 128], P('gx', 'gy'), may hold values from -24 to 24
- initial_guess: float32 [128, 64, 128], P('gx', 'gy'), may hold values from -6 to 6
- face_x: float32 [128, 64, 128], P('gx', 'gy'), may hold values from 0.2 to 5
- face_y: float32 [128, 64, 128], P('gx', 'gy'), may hold values from 0.2 to 5
- face_z: float32 [128, 64, 128], P('gx', 'gy'), may hold values from 0.2 to 5
Outputs:
- pressure: float32 [128, 64, 128], P('gx', 'gy')
All inputs are finite; a program needn't handle non-finite values.
Results may differ from a plain program's by a relative error of at most 0.00002.
Values sent between devices are 32-bit elements; how exact they have to be, the bound alone decides.
No kernel may reach another device: no remote copies, remote signals or barrier semaphores. Data moves between devices by JAX's collectives and lax.ppermute only.
A program may use at most 192 MiB of HBM per device.

v0:
```python
import jax
import jax.numpy as jnp
from jax import lax
from jax.sharding import PartitionSpec as P

LEVELS = 6


OMEGA = 0.8


def with_halo(block, sides, width):
    for axis, dim in sides:
        count = lax.axis_size(axis)
        forward = [(i, i + 1) for i in range(count - 1)]
        backward = [(target, source) for source, target in forward]
        low = lax.ppermute(
            lax.slice_in_dim(block, block.shape[dim] - width, None, axis=dim), axis, forward
        )
        high = lax.ppermute(lax.slice_in_dim(block, 0, width, axis=dim), axis, backward)
        block = jnp.concatenate([low, block, high], axis=dim)
    return block


def passed_along(block, axis, distance):
    devices = range(lax.axis_size(axis))
    route = [(i - distance, i) for i in devices if i - distance in devices]
    return lax.ppermute(block, axis, route)


def stencil(padded, padded_x, padded_y, face_z):
    center = padded[1:-1, 1:-1]
    zero_plane = jnp.zeros(center.shape[:2] + (1,), center.dtype)
    above_face = jnp.concatenate((face_z[:, :, 1:], zero_plane), axis=2)
    below_z = jnp.concatenate((zero_plane, center[:, :, :-1]), axis=2)
    above_z = jnp.concatenate((center[:, :, 1:], zero_plane), axis=2)
    lower_x = padded_x[1:-1, 1:-1]
    upper_x = padded_x[2:, 1:-1]
    lower_y = padded_y[1:-1, 1:-1]
    upper_y = padded_y[1:-1, 2:]
    applied = lower_x * (center - padded[:-2, 1:-1]) + upper_x * (center - padded[2:, 1:-1])
    applied = (
        applied + lower_y * (center - padded[1:-1, :-2]) + upper_y * (center - padded[1:-1, 2:])
    )
    applied = applied + face_z * (center - below_z) + above_face * (center - above_z)
    diagonal = lower_x + upper_x + lower_y + upper_y + face_z + above_face
    return (applied, diagonal)


def jacobi_sweep(padded, source, padded_x, padded_y, face_z):
    applied, diagonal = stencil(padded, padded_x, padded_y, face_z)
    return padded[1:-1, 1:-1] + OMEGA * (source - applied) / diagonal


def pad_plane(values, width):
    return jnp.pad(values, ((width, width), (width, width), (0, 0)))


def restrict(residual):
    shape = residual.shape
    blocks = residual.reshape(shape[0] // 2, 2, shape[1] // 2, 2, shape[2] // 2, 2)
    return 4.0 * jnp.mean(blocks, axis=(1, 3, 5))


def coarsen_faces(face_x, face_y, face_z):
    shape = face_x.shape
    blocks = (shape[0] // 2, 2, shape[1] // 2, 2, shape[2] // 2, 2)
    coarse_x = jnp.mean(face_x.reshape(blocks)[:, 0], axis=(2, 4))
    coarse_y = jnp.mean(face_y.reshape(blocks)[:, :, :, 0], axis=(1, 4))
    coarse_z = jnp.mean(face_z.reshape(blocks)[..., 0], axis=(1, 3))
    return (coarse_x, coarse_y, coarse_z)


def prolong(coarse):
    return jnp.repeat(jnp.repeat(jnp.repeat(coarse, 2, axis=0), 2, axis=1), 2, axis=2)


def local_cycle(grid_level, iterate, source, face_x, face_y, face_z):
    padded_x = pad_plane(face_x, 1)
    padded_y = pad_plane(face_y, 1)
    if grid_level == LEVELS - 1:
        count = 4 * max(iterate.shape[0], iterate.shape[1])

        def one_sweep(index, values):
            return jacobi_sweep(pad_plane(values, 1), source, padded_x, padded_y, face_z)

        return lax.fori_loop(0, count, one_sweep, iterate)
    for sweep_index in range(2):
        iterate = jacobi_sweep(pad_plane(iterate, 1), source, padded_x, padded_y, face_z)
    applied, diagonal = stencil(pad_plane(iterate, 1), padded_x, padded_y, face_z)
    coarse_src = restrict(source - applied)
    coarse_x, coarse_y, coarse_z = coarsen_faces(face_x, face_y, face_z)
    correction = local_cycle(
        grid_level + 1, jnp.zeros_like(coarse_src), coarse_src, coarse_x, coarse_y, coarse_z
    )
    iterate = iterate + prolong(correction)
    for sweep_index in range(2):
        iterate = jacobi_sweep(pad_plane(iterate, 1), source, padded_x, padded_y, face_z)
    return iterate


def field_rim(iterate):
    return with_halo(iterate, (("gx", 0), ("gy", 1)), 1)


def sweep_pair_narrow(iterate, source, padded_x, padded_y, face_z, zero_start):
    for sweep_index in range(2):
        if sweep_index == 0 and zero_start:
            padded = pad_plane(iterate, 1)
        else:
            padded = field_rim(iterate)
        iterate = jacobi_sweep(padded, source, padded_x, padded_y, face_z)
    return iterate


def descend(grid_level, iterate, source, face_x, face_y, face_z, zero_start, gather_level):
    if grid_level == gather_level:
        pieces = (
            lax.all_gather(source, "gy", axis=1, tiled=True),
            lax.all_gather(face_x, "gy", axis=1, tiled=True),
            lax.all_gather(face_y, "gy", axis=1, tiled=True),
            lax.all_gather(face_z, "gy", axis=1, tiled=True),
        )
        gathered = (
            lax.all_gather(pieces[0], "gx", axis=0, tiled=True),
            lax.all_gather(pieces[1], "gx", axis=0, tiled=True),
            lax.all_gather(pieces[2], "gx", axis=0, tiled=True),
            lax.all_gather(pieces[3], "gx", axis=0, tiled=True),
        )
        correction = local_cycle(
            grid_level,
            jnp.zeros_like(gathered[0]),
            gathered[0],
            gathered[1],
            gathered[2],
            gathered[3],
        )
        start_x = lax.axis_index("gx") * source.shape[0]
        start_y = lax.axis_index("gy") * source.shape[1]
        return lax.dynamic_slice(
            correction, (start_x, start_y, jnp.zeros((), jnp.int32)), source.shape
        )
    next_x = passed_along(face_x[:1], "gx", -1)
    next_y = passed_along(face_y[:, :1], "gy", -1)
    lower_row = jnp.zeros_like(next_x)
    lower_col = jnp.zeros_like(next_y)
    padded_x = jnp.pad(
        jnp.concatenate((lower_row, face_x, next_x), axis=0), ((0, 0), (1, 1), (0, 0))
    )
    padded_y = jnp.pad(
        jnp.concatenate((lower_col, face_y, next_y), axis=1), ((1, 1), (0, 0), (0, 0))
    )

    def smoother(values, starting):
        return sweep_pair_narrow(values, source, padded_x, padded_y, face_z, starting)

    iterate = smoother(iterate, zero_start)
    applied, diagonal = stencil(field_rim(iterate), padded_x, padded_y, face_z)
    coarse_src = restrict(source - applied)
    coarse_x, coarse_y, coarse_z = coarsen_faces(face_x, face_y, face_z)
    correction = descend(
        grid_level + 1,
        jnp.zeros_like(coarse_src),
        coarse_src,
        coarse_x,
        coarse_y,
        coarse_z,
        True,
        gather_level,
    )
    iterate = iterate + prolong(correction)
    return smoother(iterate, False)


def local(source_term, initial_guess, face_x, face_y, face_z):
    gather_level = 4
    return descend(0, initial_guess, source_term, face_x, face_y, face_z, False, gather_level)


def solution(mesh):
    placed = (
        P("gx", "gy", None),
        P("gx", "gy", None),
        P("gx", "gy", None),
        P("gx", "gy", None),
        P("gx", "gy", None),
    )
    return jax.shard_map(
        local, mesh=mesh, in_specs=placed, out_specs=P("gx", "gy", None), check_vma=False
    )
```

profile of v0, /device:TPU:1, one launch (start us, length us, event | category | flops | bytes accessed | tf_op | source)
XLA Modules:
  0.0 473.8 jit_solution(10722076119014614173)
XLA Ops:
  0.8 3.9 collective-permute-start
  11.7 10.5 %reshape.185 = f32[8,2,8,2,64,2]{5,4,3,2,1,0:T(8,128)} reshape(f32[16,16,128]{2,1,0:T(8,128)} %param.9) | data formatting | bytes 262144 | tf_op jit(solution)/shard_map/reshape | solution.py:68
  26.5 9.8 %reshape.186 = f32[8,2,8,2,64,2]{5,4,3,2,1,0:T(8,128)} reshape(f32[16,16,128]{2,1,0:T(8,128)S(1)} %copy-done.1) | data formatting | bytes 262144 | tf_op jit(solution)/shard_map/reshape | solution.py:69
  40.3 9.8 %reshape.187 = f32[8,2,8,2,64,2]{5,4,3,2,1,0:T(8,128)} reshape(f32[16,16,128]{2,1,0:T(8,128)S(1)} %copy-done) | data formatting | bytes 262144 | tf_op jit(solution)/shard_map/reshape | solution.py:70
  50.1 4.1 slice_reduce_fusion
  59.9 3.0 collective-permute-start.3
  68.7 6.2 %collective-permute-start.6 = (f32[1,16,128]{2,1,0:T(8,128)S(1)}, f32[1,16,128]{2,1,0:T(8,128)S(1)}, u32[]{:S(2)}, u32[]{:S(2)}) collective-permute-start(f32[1,16,128]{2,1,0:T(8,128)S(1)} %get-tuple-element.197), channel_id=1, source_target_pairs={{0,4},{4,8},{8,12},{12,16},{16,20},{20,24},{24,28},{1,5},{5,9},{9,... | collective-permute-start | bytes 24584 | tf_op jit(solution)/shard_map/ppermute | solution.py:17
  76.1 4.2 collective-permute-done.7
  80.4 4.8 %collective-permute-start.8 = (f32[18,1,128]{2,1,0:T(1,128)S(1)}, f32[18,1,128]{2,1,0:T(1,128)S(1)}, u32[]{:S(2)}, u32[]{:S(2)}) collective-permute-start(f32[18,1,128]{2,1,0:T(1,128)S(1)} %get-tuple-element.179), channel_id=1, source_target_pairs={{0,1},{1,2},{2,3},{4,5},{5,6},{6,7},{8,9},{9,10},{10,11},{12,13},{... | collective-permute-start | bytes 27656 | tf_op jit(solution)/shard_map/ppermute | solution.py:17
  90.4 4.5 collective-permute-start.10
  96.4 3.3 collective-permute-done.11
  99.6 3.1 collective-permute-start.12
  109.4 9.8 %reshape.184 = f32[8,2,8,2,64,2]{5,4,3,2,1,0:T(8,128)} reshape(f32[16,16,128]{2,1,0:T(8,128)S(1)} %fusion.50) | data formatting | bytes 262144 | tf_op jit(solution)/shard_map/reshape | solution.py:61
  119.2 4.0 reduce_sum.187
  123.3 5.2 %collective-permute-start.16 = (f32[1,8,64]{2,1,0:T(8,128)S(1)}, f32[1,8,64]{2,1,0:T(8,128)S(1)}, u32[]{:S(2)}, u32[]{:S(2)}) collective-permute-start(f32[1,8,64]{2,1,0:T(8,128)S(1)} %get-tuple-element.227), channel_id=1, source_target_pairs={{0,4},{4,8},{8,12},{12,16},{16,20},{20,24},{24,28},{1,5},{5,9},{9,... | collective-permute-start | bytes 6152 | tf_op jit(solution)/shard_map/ppermute | solution.py:17
  129.8 3.9 collective-permute-done.17
  133.8 4.1 collective-permute-start.18
  142.9 4.5 collective-permute-start.20
  151.8 3.4 collective-permute-start.22
  161.6 3.2 collective-permute-start.26
  166.1 3.3 collective-permute-done.27
  169.4 3.8 collective-permute-start.28
  178.2 4.5 collective-permute-start.30
  187.1 3.4 collective-permute-start.32
  199.7 3.3 collective-permute-done.37
  203.0 3.1 collective-permute-start.38
  211.1 4.5 collective-permute-start.40
  220.0 3.4 collective-permute-start.42
  228.7 5.1 %all-reduce.71 = (f32[32]{0:T(128)S(1)}, f32[32]{0:T(128)S(1)}, f32[32]{0:T(128)S(1)}, f32[32]{0:T(128)S(1)}) all-reduce(f32[32]{0:T(128)S(1)} %multiply_dynamic-update-slice_fusion, f32[32]{0:T(128)S(1)} %multiply_dynamic-update-slice_fusion.1, f32[32]{0:T(128)S(1)} %multiply_dynamic-update-slice_fusion.2, ...), channel_id=5, replica_groups=mesh['gx'=8,'gy'=4] {'gy'}, use_global_device_ids=true, to_apply=%add.70 | all-reduce | flops 128 | bytes 1024
  233.9 21.4 %all_gather.29 = f32[8,4,8]{2,1,0:T(4,128)S(1)} all-gather(f32[1,4,8]{2,1,0:T(4,128)S(1)} %reshape.208), channel_id=1, replica_groups=mesh['gx'=8,'gy'=4] {'gx'}, dimensions={0}, use_global_device_ids=true | all-gather | bytes 1152 | tf_op jit(solution)/shard_map/all_gather | solution.py:127
  255.4 21.4 %all_gather.27 = f32[8,4,8]{2,1,0:T(4,128)S(1)} all-gather(f32[1,4,8]{2,1,0:T(4,128)S(1)} %reshape.207), channel_id=1, replica_groups=mesh['gx'=8,'gy'=4] {'gx'}, dimensions={0}, use_global_device_ids=true | all-gather | bytes 1152 | tf_op jit(solution)/shard_map/all_gather | solution.py:126
  277.0 21.4 %all_gather.31 = f32[8,4,8]{2,1,0:T(4,128)S(1)} all-gather(f32[1,4,8]{2,1,0:T(4,128)S(1)} %reshape.209), channel_id=1, replica_groups=mesh['gx'=8,'gy'=4] {'gx'}, dimensions={0}, use_global_device_ids=true | all-gather | bytes 1152 | tf_op jit(solution)/shard_map/all_gather | solution.py:128
  298.6 21.4 %all_gather.25 = f32[8,4,8]{2,1,0:T(4,128)S(1)} all-gather(f32[1,4,8]{2,1,0:T(4,128)S(1)} %reshape.206), channel_id=1, replica_groups=mesh['gx'=8,'gy'=4] {'gx'}, dimensions={0}, use_global_device_ids=true | all-gather | bytes 1152 | tf_op jit(solution)/shard_map/all_gather | solution.py:125
  321.3 3.9 while.13
  331.6 24.0 %collective-permute-start.46 = (f32[4,1,16]{2,1,0:T(1,128)S(1)}, f32[4,1,16]{2,1,0:T(1,128)S(1)}, u32[]{:S(2)}, u32[]{:S(2)}) collective-permute-start(f32[4,1,16]{2,1,0:T(1,128)S(1)} %get-tuple-element.266), channel_id=1, source_target_pairs={{0,1},{1,2},{2,3},{4,5},{5,6},{6,7},{8,9},{9,10},{10,11},{12,13},{... | collective-permute-start | bytes 776 | tf_op jit(solution)/shard_map/ppermute | solution.py:17
  360.6 4.5 collective-permute-start.48
  369.5 3.4 collective-permute-start.50
  385.0 3.4 collective-permute-start.54
  393.4 3.3 collective-permute-start.56
  401.1 3.4 collective-permute-start.58
  413.6 3.0 collective-permute-done.61
  416.7 3.4 collective-permute-start.62
  425.1 3.3 collective-permute-start.64
  432.8 3.4 collective-permute-start.66
  446.0 3.1 collective-permute-done.69
  449.1 3.4 collective-permute-start.70
  461.5 3.1 collective-permute-done.73
  464.6 3.4 collective-permute-start.74
  (413 shorter events, 178.1 us)
Async XLA Ops:
  0.8 59.1 %collective-permute-start = (f32[1,16,128]{2,1,0:T(8,128)S(1)}, f32[1,16,128]{2,1,0:T(8,128)S(1)}, u32[]{:S(2)}, u32[]{:S(2)}) collective-permute-start(f32[1,16,128]{2,1,0:T(8,128)S(1)} %get-tuple-element.202), channel_id=1, source_target_pairs={{0,4},{4,8},{8,12},{12,16},{16,20},{20,24},{24,28},{1,5},{5,9},{9,... | collective-permute-start | bytes 24584 | tf_op jit(solution)/shard_map/ppermute | solution.py:17
  4.7 55.2 %collective-permute-start.2 = (f32[1,16,128]{2,1,0:T(8,128)S(1)}, f32[1,16,128]{2,1,0:T(8,128)S(1)}, u32[]{:S(2)}, u32[]{:S(2)}) collective-permute-start(f32[1,16,128]{2,1,0:T(8,128)S(1)} %get-tuple-element.201), channel_id=1, source_target_pairs={{4,0},{8,4},{12,8},{16,12},{20,16},{24,20},{28,24},{5,1},{9,5},{13... | collective-permute-start | bytes 24584 | tf_op jit(solution)/shard_map/ppermute | solution.py:20
  6.9 58.3 %collective-permute-start.4 = (f32[16,1,128]{2,0,1:T(8,128)S(1)}, f32[16,1,128]{2,0,1:T(8,128)S(1)}, u32[]{:S(2)}, u32[]{:S(2)}) collective-permute-start(f32[16,1,128]{2,0,1:T(8,128)S(1)} %bitcast.40), channel_id=1, source_target_pairs={{1,0},{2,1},{3,2},{5,4},{6,5},{7,6},{9,8},{10,9},{11,10},{13,12},{... | collective-permute-start | bytes 24584 | tf_op jit(solution)/shard_map/ppermute | solution.py:28
  10.4 56.7 %collective-permute-start.1 = (f32[1,16,128]{2,1,0:T(8,128)S(1)}, f32[1,16,128]{2,1,0:T(8,128)S(1)}, u32[]{:S(2)}, u32[]{:S(2)}) collective-permute-start(f32[1,16,128]{2,1,0:T(8,128)S(1)} %slice.1075), channel_id=1, source_target_pairs={{4,0},{8,4},{12,8},{16,12},{20,16},{24,20},{28,24},{5,1},{9,5},{13... | collective-permute-start | bytes 24584 | tf_op jit(solution)/shard_map/ppermute | solution.py:28
  25.1 98.0 %collective-permute-start.14 = (f32[1,8,64]{2,1,0:T(8,128)S(1)}, f32[1,8,64]{2,1,0:T(8,128)S(1)}, u32[]{:S(2)}, u32[]{:S(2)}) collective-permute-start(f32[1,8,64]{2,1,0:T(8,128)S(1)} %slice.1351), channel_id=1, source_target_pairs={{4,0},{8,4},{12,8},{16,12},{20,16},{24,20},{28,24},{5,1},{9,5},{13... | collective-permute-start | bytes 6152 | tf_op jit(solution)/shard_map/ppermute | solution.py:28
  59.9 8.5 %collective-permute-start.3 = (f32[18,1,128]{2,1,0:T(1,128)S(1)}, f32[18,1,128]{2,1,0:T(1,128)S(1)}, u32[]{:S(2)}, u32[]{:S(2)}) collective-permute-start(f32[18,1,128]{2,1,0:T(1,128)S(1)} %get-tuple-element.181), channel_id=1, source_target_pairs={{0,1},{1,2},{2,3},{4,5},{5,6},{6,7},{8,9},{9,10},{10,11},{12,13},{... | collective-permute-start | bytes 27656 | tf_op jit(solution)/shard_map/ppermute | solution.py:17
  63.0 5.4 %collective-permute-start.5 = (f32[18,1,128]{2,1,0:T(1,128)S(1)}, f32[18,1,128]{2,1,0:T(1,128)S(1)}, u32[]{:S(2)}, u32[]{:S(2)}) collective-permute-start(f32[18,1,128]{2,1,0:T(1,128)S(1)} %get-tuple-element.182), channel_id=1, source_target_pairs={{1,0},{2,1},{3,2},{5,4},{6,5},{7,6},{9,8},{10,9},{11,10},{13,12},{... | collective-permute-start | bytes 27656 | tf_op jit(solution)/shard_map/ppermute | solution.py:20
  65.2 58.0 %collective-permute-start.15 = (f32[8,1,64]{2,1,0:T(1,128)S(1)}, f32[8,1,64]{2,1,0:T(1,128)S(1)}, u32[]{:S(2)}, u32[]{:S(2)}) collective-permute-start(f32[8,1,64]{2,1,0:T(1,128)S(1)} %slice.1353), channel_id=1, source_target_pairs={{1,0},{2,1},{3,2},{5,4},{6,5},{7,6},{9,8},{10,9},{11,10},{13,12},{... | collective-permute-start | bytes 6152 | tf_op jit(solution)/shard_map/ppermute | solution.py:28
  67.1 94.3 %collective-permute-start.24 = (f32[1,4,32]{2,1,0:T(4,128)S(1)}, f32[1,4,32]{2,1,0:T(4,128)S(1)}, u32[]{:S(2)}, u32[]{:S(2)}) collective-permute-start(f32[1,4,32]{2,1,0:T(4,128)S(1)} %slice.1365), channel_id=1, source_target_pairs={{4,0},{8,4},{12,8},{16,12},{20,16},{24,20},{28,24},{5,1},{9,5},{13... | collective-permute-start | bytes 1544 | tf_op jit(solution)/shard_map/ppermute | solution.py:28
  68.7 7.5 %collective-permute-start.6 = (f32[1,16,128]{2,1,0:T(8,128)S(1)}, f32[1,16,128]{2,1,0:T(8,128)S(1)}, u32[]{:S(2)}, u32[]{:S(2)}) collective-permute-start(f32[1,16,128]{2,1,0:T(8,128)S(1)} %get-tuple-element.197), channel_id=1, source_target_pairs={{0,4},{4,8},{8,12},{12,16},{16,20},{20,24},{24,28},{1,5},{5,9},{9,... | collective-permute-start | bytes 24584 | tf_op jit(solution)/shard_map/ppermute | solution.py:17
  74.8 5.6 %collective-permute-start.7 = (f32[1,16,128]{2,1,0:T(8,128)S(1)}, f32[1,16,128]{2,1,0:T(8,128)S(1)}, u32[]{:S(2)}, u32[]{:S(2)}) collective-permute-start(f32[1,16,128]{2,1,0:T(8,128)S(1)} %get-tuple-element.198), channel_id=1, source_target_pairs={{4,0},{8,4},{12,8},{16,12},{20,16},{24,20},{28,24},{5,1},{9,5},{13... | collective-permute-start | bytes 24584 | tf_op jit(solution)/shard_map/ppermute | solution.py:20
  80.4 6.8 %collective-permute-start.8 = (f32[18,1,128]{2,1,0:T(1,128)S(1)}, f32[18,1,128]{2,1,0:T(1,128)S(1)}, u32[]{:S(2)}, u32[]{:S(2)}) collective-permute-start(f32[18,1,128]{2,1,0:T(1,128)S(1)} %get-tuple-element.179), channel_id=1, source_target_pairs={{0,1},{1,2},{2,3},{4,5},{5,6},{6,7},{8,9},{9,10},{10,11},{12,13},{... | collective-permute-start | bytes 27656 | tf_op jit(solution)/shard_map/ppermute | solution.py:17
  85.2 5.0 %collective-permute-start.9 = (f32[18,1,128]{2,1,0:T(1,128)S(1)}, f32[18,1,128]{2,1,0:T(1,128)S(1)}, u32[]{:S(2)}, u32[]{:S(2)}) collective-permute-start(f32[18,1,128]{2,1,0:T(1,128)S(1)} %get-tuple-element.180), channel_id=1, source_target_pairs={{1,0},{2,1},{3,2},{5,4},{6,5},{7,6},{9,8},{10,9},{11,10},{13,12},{... | collective-permute-start | bytes 27656 | tf_op jit(solution)/shard_map/ppermute | solution.py:20
  90.4 5.9 %collective-permute-start.10 = (f32[1,16,128]{2,1,0:T(8,128)S(1)}, f32[1,16,128]{2,1,0:T(8,128)S(1)}, u32[]{:S(2)}, u32[]{:S(2)}) collective-permute-start(f32[1,16,128]{2,1,0:T(8,128)S(1)} %get-tuple-element.193), channel_id=1, source_target_pairs={{0,4},{4,8},{8,12},{12,16},{16,20},{20,24},{24,28},{1,5},{5,9},{9,... | collective-permute-start | bytes 24584 | tf_op jit(solution)/shard_map/ppermute | solution.py:17
  99.6 5.1 %collective-permute-start.12 = (f32[18,1,128]{2,1,0:T(1,128)S(1)}, f32[18,1,128]{2,1,0:T(1,128)S(1)}, u32[]{:S(2)}, u32[]{:S(2)}) collective-permute-start(f32[18,1,128]{2,1,0:T(1,128)S(1)} %get-tuple-element.177), channel_id=1, source_target_pairs={{0,1},{1,2},{2,3},{4,5},{5,6},{6,7},{8,9},{9,10},{10,11},{12,13},{... | collective-permute-start | bytes 27656 | tf_op jit(solution)/shard_map/ppermute | solution.py:17
  102.7 5.0 %collective-permute-start.13 = (f32[18,1,128]{2,1,0:T(1,128)S(1)}, f32[18,1,128]{2,1,0:T(1,128)S(1)}, u32[]{:S(2)}, u32[]{:S(2)}) collective-permute-start(f32[18,1,128]{2,1,0:T(1,128)S(1)} %get-tuple-element.178), channel_id=1, source_target_pairs={{1,0},{2,1},{3,2},{5,4},{6,5},{7,6},{9,8},{10,9},{11,10},{13,12},{... | collective-permute-start | bytes 27656 | tf_op jit(solution)/shard_map/ppermute | solution.py:20
  104.8 56.7 %collective-permute-start.25 = (f32[4,1,32]{2,1,0:T(1,128)S(1)}, f32[4,1,32]{2,1,0:T(1,128)S(1)}, u32[]{:S(2)}, u32[]{:S(2)}) collective-permute-start(f32[4,1,32]{2,1,0:T(1,128)S(1)} %slice.1367), channel_id=1, source_target_pairs={{1,0},{2,1},{3,2},{5,4},{6,5},{7,6},{9,8},{10,9},{11,10},{13,12},{... | collective-permute-start | bytes 1544 | tf_op jit(solution)/shard_map/ppermute | solution.py:28
  107.7 88.0 %collective-permute-start.34 = (f32[1,2,16]{2,1,0:T(2,128)S(1)}, f32[1,2,16]{2,1,0:T(2,128)S(1)}, u32[]{:S(2)}, u32[]{:S(2)}) collective-permute-start(f32[1,2,16]{2,1,0:T(2,128)S(1)} %slice.1379), channel_id=1, source_target_pairs={{4,0},{8,4},{12,8},{16,12},{20,16},{24,20},{28,24},{5,1},{9,5},{13... | collective-permute-start | bytes 392 | tf_op jit(solution)/shard_map/ppermute | solution.py:28
  123.3 6.5 %collective-permute-start.16 = (f32[1,8,64]{2,1,0:T(8,128)S(1)}, f32[1,8,64]{2,1,0:T(8,128)S(1)}, u32[]{:S(2)}, u32[]{:S(2)}) collective-permute-start(f32[1,8,64]{2,1,0:T(8,128)S(1)} %get-tuple-element.227), channel_id=1, source_target_pairs={{0,4},{4,8},{8,12},{12,16},{16,20},{20,24},{24,28},{1,5},{5,9},{9,... | collective-permute-start | bytes 6152 | tf_op jit(solution)/shard_map/ppermute | solution.py:17
  128.5 5.3 %collective-permute-start.17 = (f32[1,8,64]{2,1,0:T(8,128)S(1)}, f32[1,8,64]{2,1,0:T(8,128)S(1)}, u32[]{:S(2)}, u32[]{:S(2)}) collective-permute-start(f32[1,8,64]{2,1,0:T(8,128)S(1)} %get-tuple-element.228), channel_id=1, source_target_pairs={{4,0},{8,4},{12,8},{16,12},{20,16},{24,20},{28,24},{5,1},{9,5},{13... | collective-permute-start | bytes 6152 | tf_op jit(solution)/shard_map/ppermute | solution.py:20
  133.8 6.1 %collective-permute-start.18 = (f32[10,1,64]{2,1,0:T(1,128)S(1)}, f32[10,1,64]{2,1,0:T(1,128)S(1)}, u32[]{:S(2)}, u32[]{:S(2)}) collective-permute-start(f32[10,1,64]{2,1,0:T(1,128)S(1)} %get-tuple-element.211), channel_id=1, source_target_pairs={{0,1},{1,2},{2,3},{4,5},{5,6},{6,7},{8,9},{9,10},{10,11},{12,13},{... | collective-permute-start | bytes 7688 | tf_op jit(solution)/shard_map/ppermute | solution.py:17
  137.8 4.9 %collective-permute-start.19 = (f32[10,1,64]{2,1,0:T(1,128)S(1)}, f32[10,1,64]{2,1,0:T(1,128)S(1)}, u32[]{:S(2)}, u32[]{:S(2)}) collective-permute-start(f32[10,1,64]{2,1,0:T(1,128)S(1)} %get-tuple-element.212), channel_id=1, source_target_pairs={{1,0},{2,1},{3,2},{5,4},{6,5},{7,6},{9,8},{10,9},{11,10},{13,12},{... | collective-permute-start | bytes 7688 | tf_op jit(solution)/shard_map/ppermute | solution.py:20
  142.9 6.0 %collective-permute-start.20 = (f32[1,8,64]{2,1,0:T(8,128)S(1)}, f32[1,8,64]{2,1,0:T(8,128)S(1)}, u32[]{:S(2)}, u32[]{:S(2)}) collective-permute-start(f32[1,8,64]{2,1,0:T(8,128)S(1)} %get-tuple-element.223), channel_id=1, source_target_pairs={{0,4},{4,8},{8,12},{12,16},{16,20},{20,24},{24,28},{1,5},{5,9},{9,... | collective-permute-start | bytes 6152 | tf_op jit(solution)/shard_map/ppermute | solution.py:17
  151.8 5.4 %collective-permute-start.22 = (f32[10,1,64]{2,1,0:T(1,128)S(1)}, f32[10,1,64]{2,1,0:T(1,128)S(1)}, u32[]{:S(2)}, u32[]{:S(2)}) collective-permute-start(f32[10,1,64]{2,1,0:T(1,128)S(1)} %get-tuple-element.209), channel_id=1, source_target_pairs={{0,1},{1,2},{2,3},{4,5},{5,6},{6,7},{8,9},{9,10},{10,11},{12,13},{... | collective-permute-start | bytes 7688 | tf_op jit(solution)/shard_map/ppermute | solution.py:17
  155.2 4.9 %collective-permute-start.23 = (f32[10,1,64]{2,1,0:T(1,128)S(1)}, f32[10,1,64]{2,1,0:T(1,128)S(1)}, u32[]{:S(2)}, u32[]{:S(2)}) collective-permute-start(f32[10,1,64]{2,1,0:T(1,128)S(1)} %get-tuple-element.210), channel_id=1, source_target_pairs={{1,0},{2,1},{3,2},{5,4},{6,5},{7,6},{9,8},{10,9},{11,10},{13,12},{... | collective-permute-start | bytes 7688 | tf_op jit(solution)/shard_map/ppermute | solution.py:20
  157.2 38.5 %collective-permute-start.35 = (f32[2,1,16]{2,1,0:T(1,128)S(1)}, f32[2,1,16]{2,1,0:T(1,128)S(1)}, u32[]{:S(2)}, u32[]{:S(2)}) collective-permute-start(f32[2,1,16]{2,1,0:T(1,128)S(1)} %slice.1381), channel_id=1, source_target_pairs={{1,0},{2,1},{3,2},{5,4},{6,5},{7,6},{9,8},{10,9},{11,10},{13,12},{... | collective-permute-start | bytes 392 | tf_op jit(solution)/shard_map/ppermute | solution.py:28
  169.4 5.8 %collective-permute-start.28 = (f32[6,1,32]{2,1,0:T(1,128)S(1)}, f32[6,1,32]{2,1,0:T(1,128)S(1)}, u32[]{:S(2)}, u32[]{:S(2)}) collective-permute-start(f32[6,1,32]{2,1,0:T(1,128)S(1)} %get-tuple-element.246), channel_id=1, source_target_pairs={{0,1},{1,2},{2,3},{4,5},{5,6},{6,7},{8,9},{9,10},{10,11},{12,13},{... | collective-permute-start | bytes 2312 | tf_op jit(solution)/shard_map/ppermute | solution.py:17
  173.2 4.9 %collective-permute-start.29 = (f32[6,1,32]{2,1,0:T(1,128)S(1)}, f32[6,1,32]{2,1,0:T(1,128)S(1)}, u32[]{:S(2)}, u32[]{:S(2)}) collective-permute-start(f32[6,1,32]{2,1,0:T(1,128)S(1)} %get-tuple-element.247), channel_id=1, source_target_pairs={{1,0},{2,1},{3,2},{5,4},{6,5},{7,6},{9,8},{10,9},{11,10},{13,12},{... | collective-permute-start | bytes 2312 | tf_op jit(solution)/shard_map/ppermute | solution.py:20
  178.2 5.8 %collective-permute-start.30 = (f32[1,4,32]{2,1,0:T(4,128)S(1)}, f32[1,4,32]{2,1,0:T(4,128)S(1)}, u32[]{:S(2)}, u32[]{:S(2)}) collective-permute-start(f32[1,4,32]{2,1,0:T(4,128)S(1)} %get-tuple-element.258), channel_id=1, source_target_pairs={{0,4},{4,8},{8,12},{12,16},{16,20},{20,24},{24,28},{1,5},{5,9},{9,... | collective-permute-start | bytes 1544 | tf_op jit(solution)/shard_map/ppermute | solution.py:17
  187.1 5.4 %collective-permute-start.32 = (f32[6,1,32]{2,1,0:T(1,128)S(1)}, f32[6,1,32]{2,1,0:T(1,128)S(1)}, u32[]{:S(2)}, u32[]{:S(2)}) collective-permute-start(f32[6,1,32]{2,1,0:T(1,128)S(1)} %get-tuple-element.244), channel_id=1, source_target_pairs={{0,1},{1,2},{2,3},{4,5},{5,6},{6,7},{8,9},{9,10},{10,11},{12,13},{... | collective-permute-start | bytes 2312 | tf_op jit(solution)/shard_map/ppermute | solution.py:17
  190.5 4.9 %collective-permute-start.33 = (f32[6,1,32]{2,1,0:T(1,128)S(1)}, f32[6,1,32]{2,1,0:T(1,128)S(1)}, u32[]{:S(2)}, u32[]{:S(2)}) collective-permute-start(f32[6,1,32]{2,1,0:T(1,128)S(1)} %get-tuple-element.245), channel_id=1, source_target_pairs={{1,0},{2,1},{3,2},{5,4},{6,5},{7,6},{9,8},{10,9},{11,10},{13,12},{... | collective-permute-start | bytes 2312 | tf_op jit(solution)/shard_map/ppermute | solution.py:20
  203.0 5.1 %collective-permute-start.38 = (f32[4,1,16]{2,1,0:T(1,128)S(1)}, f32[4,1,16]{2,1,0:T(1,128)S(1)}, u32[]{:S(2)}, u32[]{:S(2)}) collective-permute-start(f32[4,1,16]{2,1,0:T(1,128)S(1)} %get-tuple-element.272), channel_id=1, source_target_pairs={{0,1},{1,2},{2,3},{4,5},{5,6},{6,7},{8,9},{9,10},{10,11},{12,13},{... | collective-permute-start | bytes 776 | tf_op jit(solution)/shard_map/ppermute | solution.py:17
  211.1 5.8 %collective-permute-start.40 = (f32[1,2,16]{2,1,0:T(2,128)S(1)}, f32[1,2,16]{2,1,0:T(2,128)S(1)}, u32[]{:S(2)}, u32[]{:S(2)}) collective-permute-start(f32[1,2,16]{2,1,0:T(2,128)S(1)} %get-tuple-element.290), channel_id=1, source_target_pairs={{0,4},{4,8},{8,12},{12,16},{16,20},{20,24},{24,28},{1,5},{5,9},{9,... | collective-permute-start | bytes 392 | tf_op jit(solution)/shard_map/ppermute | solution.py:17
  220.0 5.4 %collective-permute-start.42 = (f32[4,1,16]{2,1,0:T(1,128)S(1)}, f32[4,1,16]{2,1,0:T(1,128)S(1)}, u32[]{:S(2)}, u32[]{:S(2)}) collective-permute-start(f32[4,1,16]{2,1,0:T(1,128)S(1)} %get-tuple-element.270), channel_id=1, source_target_pairs={{0,1},{1,2},{2,3},{4,5},{5,6},{6,7},{8,9},{9,10},{10,11},{12,13},{... | collective-permute-start | bytes 776 | tf_op jit(solution)/shard_map/ppermute | solution.py:17
  331.6 26.0 %collective-permute-start.46 = (f32[4,1,16]{2,1,0:T(1,128)S(1)}, f32[4,1,16]{2,1,0:T(1,128)S(1)}, u32[]{:S(2)}, u32[]{:S(2)}) collective-permute-start(f32[4,1,16]{2,1,0:T(1,128)S(1)} %get-tuple-element.266), channel_id=1, source_target_pairs={{0,1},{1,2},{2,3},{4,5},{5,6},{6,7},{8,9},{9,10},{10,11},{12,13},{... | collective-permute-start | bytes 776 | tf_op jit(solution)/shard_map/ppermute | solution.py:17
  360.6 5.8 %collective-permute-start.48 = (f32[1,2,16]{2,1,0:T(2,128)S(1)}, f32[1,2,16]{2,1,0:T(2,128)S(1)}, u32[]{:S(2)}, u32[]{:S(2)}) collective-permute-start(f32[1,2,16]{2,1,0:T(2,128)S(1)} %get-tuple-element.280), channel_id=1, source_target_pairs={{0,4},{4,8},{8,12},{12,16},{16,20},{20,24},{24,28},{1,5},{5,9},{9,... | collective-permute-start | bytes 392 | tf_op jit(solution)/shard_map/ppermute | solution.py:17
  369.5 5.4 %collective-permute-start.50 = (f32[4,1,16]{2,1,0:T(1,128)S(1)}, f32[4,1,16]{2,1,0:T(1,128)S(1)}, u32[]{:S(2)}, u32[]{:S(2)}) collective-permute-start(f32[4,1,16]{2,1,0:T(1,128)S(1)} %get-tuple-element.264), channel_id=1, source_target_pairs={{0,1},{1,2},{2,3},{4,5},{5,6},{6,7},{8,9},{9,10},{10,11},{12,13},{... | collective-permute-start | bytes 776 | tf_op jit(solution)/shard_map/ppermute | solution.py:17
  385.0 5.4 %collective-permute-start.54 = (f32[6,1,32]{2,1,0:T(1,128)S(1)}, f32[6,1,32]{2,1,0:T(1,128)S(1)}, u32[]{:S(2)}, u32[]{:S(2)}) collective-permute-start(f32[6,1,32]{2,1,0:T(1,128)S(1)} %get-tuple-element.242), channel_id=1, source_target_pairs={{0,1},{1,2},{2,3},{4,5},{5,6},{6,7},{8,9},{9,10},{10,11},{12,13},{... | collective-permute-start | bytes 2312 | tf_op jit(solution)/shard_map/ppermute | solution.py:17
  388.4 4.9 %collective-permute-start.55 = (f32[6,1,32]{2,1,0:T(1,128)S(1)}, f32[6,1,32]{2,1,0:T(1,128)S(1)}, u32[]{:S(2)}, u32[]{:S(2)}) collective-permute-start(f32[6,1,32]{2,1,0:T(1,128)S(1)} %get-tuple-element.243), channel_id=1, source_target_pairs={{1,0},{2,1},{3,2},{5,4},{6,5},{7,6},{9,8},{10,9},{11,10},{13,12},{... | collective-permute-start | bytes 2312 | tf_op jit(solution)/shard_map/ppermute | solution.py:20
  401.1 5.4 %collective-permute-start.58 = (f32[6,1,32]{2,1,0:T(1,128)S(1)}, f32[6,1,32]{2,1,0:T(1,128)S(1)}, u32[]{:S(2)}, u32[]{:S(2)}) collective-permute-start(f32[6,1,32]{2,1,0:T(1,128)S(1)} %get-tuple-element.240), channel_id=1, source_target_pairs={{0,1},{1,2},{2,3},{4,5},{5,6},{6,7},{8,9},{9,10},{10,11},{12,13},{... | collective-permute-start | bytes 2312 | tf_op jit(solution)/shard_map/ppermute | solution.py:17
  416.7 5.4 %collective-permute-start.62 = (f32[10,1,64]{2,1,0:T(1,128)S(1)}, f32[10,1,64]{2,1,0:T(1,128)S(1)}, u32[]{:S(2)}, u32[]{:S(2)}) collective-permute-start(f32[10,1,64]{2,1,0:T(1,128)S(1)} %get-tuple-element.207), channel_id=1, source_target_pairs={{0,1},{1,2},{2,3},{4,5},{5,6},{6,7},{8,9},{9,10},{10,11},{12,13},{... | collective-permute-start | bytes 7688 | tf_op jit(solution)/shard_map/ppermute | solution.py:17
  420.1 4.9 %collective-permute-start.63 = (f32[10,1,64]{2,1,0:T(1,128)S(1)}, f32[10,1,64]{2,1,0:T(1,128)S(1)}, u32[]{:S(2)}, u32[]{:S(2)}) collective-permute-start(f32[10,1,64]{2,1,0:T(1,128)S(1)} %get-tuple-element.208), channel_id=1, source_target_pairs={{1,0},{2,1},{3,2},{5,4},{6,5},{7,6},{9,8},{10,9},{11,10},{13,12},{... | collective-permute-start | bytes 7688 | tf_op jit(solution)/shard_map/ppermute | solution.py:20
  432.8 5.4 %collective-permute-start.66 = (f32[10,1,64]{2,1,0:T(1,128)S(1)}, f32[10,1,64]{2,1,0:T(1,128)S(1)}, u32[]{:S(2)}, u32[]{:S(2)}) collective-permute-start(f32[10,1,64]{2,1,0:T(1,128)S(1)} %get-tuple-element.205), channel_id=1, source_target_pairs={{0,1},{1,2},{2,3},{4,5},{5,6},{6,7},{8,9},{9,10},{10,11},{12,13},{... | collective-permute-start | bytes 7688 | tf_op jit(solution)/shard_map/ppermute | solution.py:17
  436.2 4.9 %collective-permute-start.67 = (f32[10,1,64]{2,1,0:T(1,128)S(1)}, f32[10,1,64]{2,1,0:T(1,128)S(1)}, u32[]{:S(2)}, u32[]{:S(2)}) collective-permute-start(f32[10,1,64]{2,1,0:T(1,128)S(1)} %get-tuple-element.206), channel_id=1, source_target_pairs={{1,0},{2,1},{3,2},{5,4},{6,5},{7,6},{9,8},{10,9},{11,10},{13,12},{... | collective-permute-start | bytes 7688 | tf_op jit(solution)/shard_map/ppermute | solution.py:20
  449.1 5.4 %collective-permute-start.70 = (f32[18,1,128]{2,1,0:T(1,128)S(1)}, f32[18,1,128]{2,1,0:T(1,128)S(1)}, u32[]{:S(2)}, u32[]{:S(2)}) collective-permute-start(f32[18,1,128]{2,1,0:T(1,128)S(1)} %get-tuple-element.175), channel_id=1, source_target_pairs={{0,1},{1,2},{2,3},{4,5},{5,6},{6,7},{8,9},{9,10},{10,11},{12,13},{... | collective-permute-start | bytes 27656 | tf_op jit(solution)/shard_map/ppermute | solution.py:17
  452.5 5.0 %collective-permute-start.71 = (f32[18,1,128]{2,1,0:T(1,128)S(1)}, f32[18,1,128]{2,1,0:T(1,128)S(1)}, u32[]{:S(2)}, u32[]{:S(2)}) collective-permute-start(f32[18,1,128]{2,1,0:T(1,128)S(1)} %get-tuple-element.176), channel_id=1, source_target_pairs={{1,0},{2,1},{3,2},{5,4},{6,5},{7,6},{9,8},{10,9},{11,10},{13,12},{... | collective-permute-start | bytes 27656 | tf_op jit(solution)/shard_map/ppermute | solution.py:20
  464.6 5.4 %collective-permute-start.74 = (f32[18,1,128]{2,1,0:T(1,128)S(1)}, f32[18,1,128]{2,1,0:T(1,128)S(1)}, u32[]{:S(2)}, u32[]{:S(2)}) collective-permute-start(f32[18,1,128]{2,1,0:T(1,128)S(1)} %get-tuple-element.173), channel_id=1, source_target_pairs={{0,1},{1,2},{2,3},{4,5},{5,6},{6,7},{8,9},{9,10},{10,11},{12,13},{... | collective-permute-start | bytes 27656 | tf_op jit(solution)/shard_map/ppermute | solution.py:17
  468.0 5.0 %collective-permute-start.75 = (f32[18,1,128]{2,1,0:T(1,128)S(1)}, f32[18,1,128]{2,1,0:T(1,128)S(1)}, u32[]{:S(2)}, u32[]{:S(2)}) collective-permute-start(f32[18,1,128]{2,1,0:T(1,128)S(1)} %get-tuple-element.174), channel_id=1, source_target_pairs={{1,0},{2,1},{3,2},{5,4},{6,5},{7,6},{9,8},{10,9},{11,10},{13,12},{... | collective-permute-start | bytes 27656 | tf_op jit(solution)/shard_map/ppermute | solution.py:20
  (34 other events, 237.8 us)
where the time goes:
time: 476 us; the launch traced here: 474 us
  starting transfers between devices  210 us (44%)
  waiting for transfers between devices  94.2 us (20%)
  blocking collectives  90.7 us (19%)
  local copies, waits for them, and re-layouts  54.8 us (12%)
  other arithmetic  21.7 us (5%)
    ppermute x34, starting transfers between devices, with_halo(): lax.ppermute(lax.slice_in_dim(block, block.shape[dim] - width, None, axis...  142 us
    ppermute x34, waiting for transfers between devices, with_halo(): lax.ppermute(lax.slice_in_dim(block, 0, width, axis=dim), axis, backward)  94.1 us
    ppermute x34, starting transfers between devices, with_halo(): lax.ppermute(lax.slice_in_dim(block, 0, width, axis=dim), axis, backward)  54.6 us
    all_gather x1, blocking collectives, descend(): lax.all_gather(pieces[2], 'gx', axis=0, tiled=True)  21.4 us
    all_gather x1, blocking collectives, descend(): lax.all_gather(pieces[1], 'gx', axis=0, tiled=True)  21.4 us
    all_gather x1, blocking collectives, descend(): lax.all_gather(pieces[3], 'gx', axis=0, tiled=True)  21.4 us
    all_gather x1, blocking collectives, descend(): lax.all_gather(pieces[0], 'gx', axis=0, tiled=True)  21.4 us
    ppermute x8, starting transfers between devices, passed_along(): return lax.ppermute(block, axis, route)  13.9 us
  transfers between devices with their start and end apart: 76, of which 32 were waited for; matrix products, arithmetic and copies ran while one was open for 14% of the time, Pallas kernels for 0%

commit v1 on v0

--- a/solution.py
+++ b/solution.py
@@ -1,12 +1,508 @@
+import functools
+
 import jax
 import jax.numpy as jnp
 from jax import lax
+from jax.experimental import pallas as pl
+from jax.experimental.pallas import tpu as pltpu
 from jax.sharding import PartitionSpec as P
 
 LEVELS = 6
-
-
 OMEGA = 0.8
+LANES = 128
+RIM = 4
+PAD = 8
+F32 = jnp.float32
+
+V, F, FX, FY, ZL, ZH, W, D, U = range(9)
+
+
+def lanes_of(shape):
+    return lax.broadcasted_iota(jnp.int32, shape, len(shape) - 1)
+
+
+def rows_of(shape):
+    return lax.broadcasted_iota(jnp.int32, shape, len(shape) - 2)
+
+
+def roll_lanes(values, step):
+    return pltpu.roll(values, step % LANES, values.ndim - 1)
+
+
+def roll_rows(values, step):
+    return pltpu.roll(values, step % values.shape[-2], values.ndim - 2)
+
+
+def exact_dot(left, right):
+    return jnp.dot(left, right, precision=lax.Precision.HIGHEST, preferred_element_type=F32)
+
+
+def compact(depth, part, even_only=False):
+    source = lax.broadcasted_iota(jnp.int32, (LANES, LANES), 0)
+    target = lax.broadcasted_iota(jnp.int32, (LANES, LANES), 1)
+    half = depth // 2
+    hit = target == (source // depth * 2 + part) * half + source % depth // 2
+    if even_only:
+        hit = hit & (source % 2 == 0)
+    return jnp.where(hit, 1.0, 0.0).astype(F32)
+
+
+def expand(depth, part):
+    target = lax.broadcasted_iota(jnp.int32, (LANES, LANES), 0)
+    source = lax.broadcasted_iota(jnp.int32, (LANES, LANES), 1)
+    half = depth // 2
+    hit = target == (source // depth * 2 + part) * half + source % depth // 2
+    return jnp.where(hit, 1.0, 0.0).astype(F32)
+
+
+def merge_lanes(values, depth, even_only=False):
+    count, rows, _ = values.shape
+    half = count // 2
+    flat = values.reshape(2, half * rows, LANES)
+    out = exact_dot(flat[0], compact(depth, 0, even_only))
+    out = out + exact_dot(flat[1], compact(depth, 1, even_only))
+    return out.reshape(half, rows, LANES)
+
+
+def even_rows(ref, rows):
+    return ref[:, pl.ds(0, rows // 2, stride=2), :]
+
+
+def odd_rows(ref, rows):
+    return ref[:, pl.ds(1, rows // 2, stride=2), :]
+
+
+def pack_x(*refs):
+    fields, (low, high) = refs[:5], refs[5:]
+    for index, ref in enumerate(fields):
+        low[index] = ref[:RIM]
+        high[index] = ref[ref.shape[0] - RIM :]
+
+
+def pack_y(*refs):
+    fields, (x_low, x_high, low, high) = refs[:5], refs[5:]
+    for index, ref in enumerate(fields):
+        nx, ny = ref.shape[:2]
+        for out, start in ((low, 0), (high, ny - RIM)):
+            rows = slice(start, start + RIM)
+            out[index, :RIM] = x_low[index, :, rows]
+            out[index, RIM : RIM + nx] = ref[:, rows]
+            out[index, RIM + nx :] = x_high[index, :, rows]
+
+
+def pair_slabs(ref):
+    count = ref.shape[0]
+    values = ref[...].reshape((count // 2, 2) + ref.shape[1:])
+    return values[:, 0], values[:, 1]
+
+
+def coarse_faces(fx, fy, fz, out, tmp):
+    rows = fx.shape[1]
+    tmp[...] = pair_slabs(fx)[0]
+    out[0] = 0.25 * merge_lanes(even_rows(tmp, rows) + odd_rows(tmp, rows), LANES)
+    first, second = pair_slabs(fy)
+    tmp[...] = first + second
+    out[1] = 0.25 * merge_lanes(even_rows(tmp, rows), LANES)
+    first, second = pair_slabs(fz)
+    tmp[...] = first + second
+    out[2] = 0.25 * merge_lanes(even_rows(tmp, rows) + odd_rows(tmp, rows), LANES, True)
+
+
+def weighted(lev, src, slab, start, rows):
+    here = pl.ds(start, rows)
+    below = pl.ds(start - 1, rows)
+    above = pl.ds(start + 1, rows)
+    v = src[slab, here]
+    total = lev[F, slab, here] + lev[FX, slab, here] * src[slab - 1, here]
+    total = total + lev[FX, slab + 1, here] * src[slab + 1, here]
+    total = total + lev[FY, slab, here] * src[slab, below]
+    total = total + lev[FY, slab, above] * src[slab, above]
+    total = total + lev[ZL, slab, here] * roll_lanes(v, 1)
+    total = total + lev[ZH, slab, here] * roll_lanes(v, -1)
+    return v, total
+
+
+def swept(lev, src, slab, start, rows):
+    v, total = weighted(lev, src, slab, start, rows)
+    return (1.0 - OMEGA) * v + lev[W, slab, pl.ds(start, rows)] * total
+
+
+def set_weights(lev, slab, start, rows, depth, inside=None):
+    here = pl.ds(start, rows)
+    fz = lev[ZL, slab, here]
+    z = lanes_of(fz.shape) % depth
+    upper = jnp.where(z == depth - 1, 0.0, roll_lanes(fz, -1))
+    diagonal = lev[FX, slab, here] + lev[FX, slab + 1, here]
+    diagonal = diagonal + lev[FY, slab, here] + lev[FY, slab, pl.ds(start + 1, rows)] + fz + upper
+    valid = diagonal > 0.0
+    if inside is not None:
+        valid = valid & inside
+    lev[ZL, slab, here] = jnp.where(z == 0, 0.0, fz)
+    lev[ZH, slab, here] = upper
+    lev[D, slab, here] = diagonal
+    lev[W, slab, here] = jnp.where(valid, OMEGA / jnp.where(valid, diagonal, 1.0), 0.0)
+
+
+def run(count, body, unroll=1):
+    def step(index, carry):
+        body(index)
+        return carry
+
+    lax.fori_loop(0, count, step, 0, unroll=unroll)
+
+
+def level_down(axes, *refs):
+    fields, (x_low, x_high, y_low, y_high, lev, chunk, other, tmp) = refs[:5], refs[5:]
+    nx, ny = fields[0].shape[:2]
+    slabs, rows = nx + 2 * RIM, ny + 2 * RIM
+    me_x, me_y = lax.axis_index(axes[0]), lax.axis_index(axes[1])
+    for index, slot in enumerate((F, V, FX, FY, ZL)):
+        lev[slot, :, :PAD] = jnp.zeros((slabs, PAD, LANES), F32)
+        lev[slot, :, PAD + rows :] = jnp.zeros((slabs, PAD, LANES), F32)
+        inner = pl.ds(PAD + RIM, ny)
+        lev[slot, :RIM, inner] = x_low[index]
+        lev[slot, RIM : RIM + nx, inner] = fields[index][...]
+        lev[slot, RIM + nx :, inner] = x_high[index]
+        lev[slot, :, PAD : PAD + RIM] = y_low[index]
+        lev[slot, :, PAD + RIM + ny : PAD + rows] = y_high[index]
+    other[:, :PAD] = jnp.zeros((slabs, PAD, LANES), F32)
+    other[:, PAD + rows :] = jnp.zeros((slabs, PAD, LANES), F32)
+    row_inside = (rows_of((rows, LANES)) >= RIM) | (me_y > 0)
+    main = pl.ds(PAD, rows)
+
+    def first(index):
+        slab = index + 1
+        inside = row_inside & ((slab >= RIM) | (me_x > 0))
+        set_weights(lev, slab, PAD, rows, LANES, inside)
+        other[slab, main] = swept(lev, lev.at[V], slab, PAD, rows)
+
+    run(slabs - 2, first, 2)
+
+    def second(index):
+        slab = index + 2
+        lev[V, slab, main] = swept(lev, other, slab, PAD, rows)
+
+    run(slabs - 4, second, 2)
+
+    def rest(slab):
+        v, total = weighted(lev, lev.at[V], slab, PAD + RIM, ny)
+        return total - lev[D, slab, pl.ds(PAD + RIM, ny)] * v
+
+    def residual(index):
+        slab = RIM + 2 * index
+        tmp[index] = rest(slab) + rest(slab + 1)
+
+    run(nx // 2, residual, 2)
+    chunk[...] = 0.5 * merge_lanes(even_rows(tmp, ny) + odd_rows(tmp, ny), LANES)
+
+
+def pair_rows(values, stride):
+    return values + roll_rows(values, -stride)
+
+
+def pair_lanes(values, stride):
+    return values + roll_lanes(values, -stride)
+
+
+class Listed:
+    def __init__(self, fx, fy, fz, stride, depth):
+        self.fx, self.fy, self.fz, self.stride, self.depth = fx, fy, fz, stride, depth
+        shape = fx[0].shape
+        rows = shape[0]
+        row, lane = rows_of(shape), lanes_of(shape)
+        z = lane % depth
+        count = self.count = len(fx)
+        self.x_high = [
+            fx[s + 1] if s + 1 < count else jnp.where(lane < LANES - depth, roll_lanes(fx[0], -depth), 0.0)
+            for s in range(count)
+        ]
+        self.x_low = [fx[s] if s > 0 else jnp.where(lane >= depth, fx[0], 0.0) for s in range(count)]
+        self.y_high = [jnp.where(row < rows - stride, roll_rows(f, -stride), 0.0) for f in fy]
+        self.y_low = [jnp.where(row >= stride, f, 0.0) for f in fy]
+        self.z_high = [jnp.where(z < depth - stride, roll_lanes(f, -stride), 0.0) for f in fz]
+        self.z_low = [jnp.where(z >= stride, f, 0.0) for f in fz]
+        self.d = [
+            fx[s] + self.x_high[s] + fy[s] + self.y_high[s] + fz[s] + self.z_high[s] for s in range(count)
+        ]
+        self.w = [jnp.where(d > 0.0, OMEGA / jnp.where(d > 0.0, d, 1.0), 0.0) for d in self.d]
+
+    def weighted(self, v, f):
+        count = self.count
+        out = []
+        for s in range(count):
+            low = v[s - 1] if s > 0 else roll_lanes(v[count - 1], self.depth)
+            high = v[s + 1] if s + 1 < count else roll_lanes(v[0], -self.depth)
+            total = f[s] + self.x_low[s] * low + self.x_high[s] * high
+            total = total + self.y_low[s] * roll_rows(v[s], self.stride)
+            total = total + self.y_high[s] * roll_rows(v[s], -self.stride)
+            total = total + self.z_low[s] * roll_lanes(v[s], self.stride)
+            total = total + self.z_high[s] * roll_lanes(v[s], -self.stride)
+            out.append(total)
+        return out
+
+    def sweep(self, v, f):
+        totals = self.weighted(v, f)
+        return [(1.0 - OMEGA) * v[s] + self.w[s] * totals[s] for s in range(self.count)]
+
+    def start(self, f):
+        return [self.w[s] * f[s] for s in range(self.count)]
+
+    def residual(self, v, f):
+        totals = self.weighted(v, f)
+        return [totals[s] - self.d[s] * v[s] for s in range(self.count)]
+
+    def kept(self):
+        shape = self.fx[0].shape
+        step = 2 * self.stride
+        return (rows_of(shape) % step == 0) & (lanes_of(shape) % step == 0)
+
+    def coarser(self):
+        keep, stride = self.kept(), self.stride
+        half = range(self.count // 2)
+
+        def kept(values):
+            return jnp.where(keep, 0.25 * values, 0.0)
+
+        fx = [kept(pair_lanes(pair_rows(self.fx[2 * s], stride), stride)) for s in half]
+        fy = [kept(pair_lanes(self.fy[2 * s] + self.fy[2 * s + 1], stride)) for s in half]
+        fz = [kept(pair_rows(self.fz[2 * s] + self.fz[2 * s + 1], stride)) for s in half]
+        return Listed(fx, fy, fz, 2 * stride, self.depth)
+
+    def restrict(self, r):
+        keep, stride = self.kept(), self.stride
+        return [
+            jnp.where(keep, 0.5 * pair_lanes(pair_rows(r[2 * s] + r[2 * s + 1], stride), stride), 0.0)
+            for s in range(self.count // 2)
+        ]
+
+    def prolong(self, e):
+        out = []
+        for values in e:
+            values = values + roll_rows(values, self.stride)
+            values = values + roll_lanes(values, self.stride)
+            out += [values, values]
+        return out
+
+
+def listed_cycle(levels, sweeps, f):
+    level = levels[0]
+    v = level.start(f)
+    if len(levels) == 1:
+        return lax.fori_loop(0, sweeps - 1, lambda index, values: level.sweep(values, f), v)
+    v = level.sweep(v, f)
+    e = listed_cycle(levels[1:], sweeps, level.restrict(level.residual(v, f)))
+    v = [a + b for a, b in zip(v, level.prolong(e))]
+    return level.sweep(level.sweep(v, f), f)
+
+
+def wrap_slabs(ref, count, depth, main):
+    first, last = ref[1, main], ref[count, main]
+    lane = lanes_of(first.shape)
+    ref[0, main] = jnp.where(lane < depth, 0.0, roll_lanes(last, depth))
+    ref[count + 1, main] = jnp.where(lane >= LANES - depth, 0.0, roll_lanes(first, -depth))
+
+
+def level_up(axes, grid, sweeps, top, sources, faces, out, lev, post, tmp, up):
+    devices_x, devices_y = grid
+    me_x, me_y = lax.axis_index(axes[0]), lax.axis_index(axes[1])
+    depth = LANES // 2
+    count = lev.shape[1] - 2
+    rows = lev.shape[2] - 2 * PAD
+    main = pl.ds(PAD, rows)
+    parts = sources.shape[1]
+    low_lanes = lanes_of((PAD, LANES)) < depth
+    for slot in (V, U, FY):
+        for start in (0, PAD + rows):
+            lev[slot, :, start : start + PAD] = jnp.zeros((count + 2, PAD, LANES), F32)
+
+    def unpack(index):
+        for y in range(devices_y):
+            here = pl.ds(PAD + y * PAD, PAD)
+            near = index * devices_y + y
+            far = (index + devices_x // 2) * devices_y + y
+            for slot, ref, place in ((F, sources, ()), (FX, faces, (0,)), (FY, faces, (1,)), (ZL, faces, (2,))):
+                for part in range(parts):
+                    a, b = ref[(near,) + place + (part,)], ref[(far,) + place + (part,)]
+                    slab = 1 + index * 2 * parts + part
+                    lev[slot, slab, here] = jnp.where(low_lanes, a, roll_lanes(b, depth))
+                    lev[slot, slab + parts, here] = jnp.where(low_lanes, roll_lanes(a, depth), b)
+
+    run(devices_x // 2, unpack)
+    wrap_slabs(lev.at[FX], count, depth, main)
+
+    half = count // 2
+
+    def pairs(slot, combine):
+        def pair(index):
+            tmp[index] = combine(lev[slot, 1 + 2 * index, main], lev[slot, 2 + 2 * index, main])
+
+        run(half, pair, 2)
+
+    def slabs_of(values):
+        return [values[s] for s in range(half // 2)]
+
+    pairs(FX, lambda a, b: a)
+    fx = 0.25 * merge_lanes(even_rows(tmp, rows) + odd_rows(tmp, rows), depth)
+    pairs(FY, lambda a, b: a + b)
+    fy = 0.25 * merge_lanes(even_rows(tmp, rows), depth)
+    pairs(ZL, lambda a, b: a + b)
+    fz = 0.25 * merge_lanes(even_rows(tmp, rows) + odd_rows(tmp, rows), depth, True)
+    levels = [Listed(slabs_of(fx), slabs_of(fy), slabs_of(fz), 1, depth // 2)]
+    while len(levels) < LEVELS - 2:
+        levels.append(levels[-1].coarser())
+
+    def first(index):
+        slab = index + 1
+        set_weights(lev, slab, PAD, rows, depth)
+        lev[V, slab, main] = lev[W, slab, main] * lev[F, slab, main]
+
+    run(count, first, 2)
+    wrap_slabs(lev.at[V], count, depth, main)
+
+    def second(index):
+        slab = index + 1
+        lev[U, slab, main] = swept(lev, lev.at[V], slab, PAD, rows)
+
+    run(count, second, 2)
+    wrap_slabs(lev.at[U], count, depth, main)
+
+    def rest(slab):
+        v, total = weighted(lev, lev.at[U], slab, PAD, rows)
+        return total - lev[D, slab, main] * v
+
+    def residual(index):
+        tmp[index] = rest(1 + 2 * index) + rest(2 + 2 * index)
+
+    run(half, residual)
+    coarse = 0.5 * merge_lanes(even_rows(tmp, rows) + odd_rows(tmp, rows), depth)
+    e = listed_cycle(levels, sweeps, slabs_of(coarse))
+
+    flat = jnp.stack(e).reshape(half // 2 * rows // 2, LANES)
+    for part in range(2):
+        fine = exact_dot(flat, expand(depth, part)).reshape(half // 2, rows // 2, LANES)
+        for odd in range(2):
+            tmp[part * half // 2 : (part + 1) * half // 2, pl.ds(odd, rows // 2, stride=2), :] = fine
+
+    def correct(index):
+        for slab in (1 + 2 * index, 2 + 2 * index):
+            lev[U, slab, main] = lev[U, slab, main] + tmp[index]
+
+    run(half, correct, 2)
+    wrap_slabs(lev.at[U], count, depth, main)
+
+    near = 2 * parts
+    base = me_x % (devices_x // 2) * near
+
+    def third(index):
+        slab = (base + index - 2 + count) % count + 1
+        lev[V, slab, main] = swept(lev, lev.at[U], slab, PAD, rows)
+
+    run(near + 4, third, 2)
+    wrap_slabs(lev.at[V], count, depth, main)
+
+    def fourth(index):
+        slab = (base + index - 1 + count) % count + 1
+        lev[U, slab, main] = swept(lev, lev.at[V], slab, PAD, rows)
+
+    run(near + 2, fourth, 2)
+    wrap_slabs(lev.at[U], count, depth, main)
+
+    slabs = near + 2
+    nx, ny = out.shape[:2]
+    fine_rows = ny + 2 * RIM
+    window = ny // 2 + 2 * PAD
+    top_row = pl.multiple_of(me_y * (ny // 2), PAD)
+    e = lev[U, pl.ds(base, slabs), pl.ds(top_row, window), :]
+    side = me_x // (devices_x // 2)
+    fine = exact_dot(e.reshape(slabs * window, LANES), expand(LANES, side)).reshape(slabs, window, LANES)
+    skip = PAD - RIM // 2
+    fine = fine[:, skip : skip + fine_rows // 2]
+    for odd in range(2):
+        up[:, pl.ds(odd, fine_rows // 2, stride=2), :] = fine
+    body = pl.ds(PAD, fine_rows)
+    for slot in (0, 1):
+        for start in (0, PAD + fine_rows):
+            post[slot, :, start : start + PAD] = jnp.zeros((post.shape[1], PAD, LANES), F32)
+
+    def raise_level(index):
+        for slab in (RIM - 2 + 2 * index, RIM - 1 + 2 * index):
+            post[0, slab, body] = top[V, slab, body] + up[index]
+
+    run(slabs, raise_level, 2)
+
+    def fifth(index):
+        slab = RIM - 1 + index
+        post[1, slab, body] = swept(top, post.at[0], slab, PAD, fine_rows)
+
+    run(nx + 2, fifth, 2)
+
+    def sixth(index):
+        out[index] = swept(top, post.at[1], RIM + index, PAD + RIM, ny)
+
+    run(nx, sixth, 2)
+
+
+def call(kernel, shapes, scratch=(), **kwargs):
+    vmem = pl.BlockSpec(memory_space=pltpu.VMEM)
+
+    def launch(*args):
+        return pl.pallas_call(
+            kernel,
+            out_shape=[jax.ShapeDtypeStruct(shape, F32) for shape in shapes],
+            in_specs=[vmem] * len(args),
+            out_specs=[vmem] * len(shapes),
+            scratch_shapes=[pltpu.VMEM(shape, F32) for shape in scratch],
+            compiler_params=pltpu.CompilerParams(vmem_limit_bytes=48 * 2**20),
+            **kwargs,
+        )(*args)
+
+    return launch
+
+
+def from_sides(low, high, axis):
+    count = lax.axis_size(axis)
+    up = [(i, i + 1) for i in range(count - 1)]
+    down = [(target, source) for source, target in up]
+    return lax.ppermute(high, axis, up), lax.ppermute(low, axis, down)
+
+
+def gathered(block):
+    return lax.all_gather(block, ("gx", "gy"), axis=0, tiled=False)
+
+
+def fused_cycle(source, guess, face_x, face_y, face_z):
+    axes = ("gx", "gy")
+    devices_x, devices_y = lax.axis_size("gx"), lax.axis_size("gy")
+    nx, ny, nz = source.shape
+    fields = (source, guess, face_x, face_y, face_z)
+    x_low, x_high = call(pack_x, [(5, RIM, ny, nz)] * 2)(*fields)
+    x_low, x_high = from_sides(x_low, x_high, "gx")
+    parts = nx // 4
+    (faces,) = call(coarse_faces, [(3, parts, ny // 2, LANES)], [(nx // 2, ny, LANES)])(face_x, face_y, face_z)
+    faces = gathered(faces)
+    slabs, rows = nx + 2 * RIM, ny + 2 * RIM
+    y_low, y_high = call(pack_y, [(5, slabs, RIM, nz)] * 2)(*fields, x_low, x_high)
+    y_low, y_high = from_sides(y_low, y_high, "gy")
+    top, chunk = call(
+        functools.partial(level_down, axes),
+        [(8, slabs, rows + 2 * PAD, LANES), (parts, ny // 2, LANES)],
+        [(slabs, rows + 2 * PAD, LANES), (nx // 2, ny, LANES)],
+    )(*fields, x_low, x_high, y_low, y_high)
+    sources = gathered(chunk)
+    count = devices_x * nx // 4
+    rows_1 = devices_y * ny // 2
+    coarsest = (devices_x * nx >> LEVELS - 1, devices_y * ny >> LEVELS - 1)
+    (out,) = call(
+        functools.partial(level_up, axes, (devices_x, devices_y), 4 * max(coarsest)),
+        [(nx, ny, nz)],
+        [
+            (9, count + 2, rows_1 + 2 * PAD, LANES),
+            (2, slabs, rows + 2 * PAD, LANES),
+            (count // 2, rows_1, LANES),
+            (nx // 2 + 2, rows, LANES),
+        ],
+    )(top, sources, faces)
+    return out
 
 
 def with_halo(block, sides, width):
@@ -172,19 +668,20 @@
     return smoother(iterate, False)
 
 
+def fits(nx, ny, nz, devices_x, devices_y):
+    cells = devices_x * nx * devices_y * ny * nz // 8
+    return cells <= 2**18 and devices_x % 2 == 0 and (nx, ny, nz) == (16, 16, LANES)
+
+
 def local(source_term, initial_guess, face_x, face_y, face_z):
+    if fits(*source_term.shape, lax.axis_size("gx"), lax.axis_size("gy")):
+        return fused_cycle(source_term, initial_guess, face_x, face_y, face_z)
     gather_level = 4
     return descend(0, initial_guess, source_term, face_x, face_y, face_z, False, gather_level)
 
 
 def solution(mesh):
-    placed = (
-        P("gx", "gy", None),
-        P("gx", "gy", None),
-        P("gx", "gy", None),
-        P("gx", "gy", None),
-        P("gx", "gy", None),
-    )
+    placed = (P("gx", "gy", None),) * 5
     return jax.shard_map(
         local, mesh=mesh, in_specs=placed, out_specs=P("gx", "gy", None), check_vma=False
     )

time: 476 us -> 109 us (0.23)
  starting transfers between devices: 210 us -> 11.6 us
  waiting for transfers between devices: 94.2 us -> 11.7 us
  blocking collectives: 90.7 us -> 41.4 us
  local copies, waits for them, and re-layouts: 54.8 us -> 12.6 us
  other arithmetic: 21.7 us -> 0 us
  Pallas kernels: 0 us -> 18.1 us
  between operations: 2.33 us -> 13.5 us
    ppermute x76 -> x4, starting transfers between devices: 210 us -> 11.6 us  [from_sides(): return (lax.ppermute(high, axis, up), lax.ppermute(low, axis, down))]
    ppermute x76 -> x4, waiting for transfers between devices: 94.2 us -> 11.7 us  [from_sides(): return (lax.ppermute(high, axis, up), lax.ppermute(low, axis, down))]
    all_gather x4 -> x1, blocking collectives: 85.6 us -> 41.4 us  [gathered(): return lax.all_gather(block, ('gx', 'gy'), axis=0, tiled=False)]
    reshape x17 -> x0, local copies, waits for them, and re-layouts: 42.7 us -> none  [the longest x4 11.1 us: restrict(): residual.reshape(shape[0] // 2, 2, shape[1] // 2, 2, shape[2] // 2, 2)]
    pallas_call x0 -> x5, Pallas kernels: none -> 18.1 us  [launch(): pl.pallas_call(kernel, out_shape=[jax.ShapeDtypeStruct(shape, F32) for sh...]
    reduce_sum x21 -> x0, other arithmetic: 15.7 us -> none  [the longest x6 4.59 us: restrict(): return 4.0 * jnp.mean(blocks, axis=(1, 3, 5))]
    unnamed x20 -> x22, local copies, waits for them, and re-layouts: 0.65 us -> 12.6 us
    slice x92 -> x0, local copies, waits for them, and re-layouts: 6.48 us -> none  [the longest x37 2.55 us: stencil(): below_z = jnp.concatenate((zero_plane, center[:, :, :-1]), axis=2)]
  transfers between devices with their start and end apart: 76 -> 5, of which waited for: 32 -> 4; matrix products, arithmetic and copies ran while one was open for 14% -> 0% of each run, Pallas kernels for 0% -> 3%
where the time goes in v1:
time: 109 us
  blocking collectives  41.4 us (38%)
  Pallas kernels  18.1 us (17%)
  between operations  13.5 us (12%)
  local copies, waits for them, and re-layouts  12.6 us (12%)
  waiting for transfers between devices  11.7 us (11%)
  starting transfers between devices  11.6 us (11%)
    all_gather x1, blocking collectives, gathered(): return lax.all_gather(block, ('gx', 'gy'), axis=0, tiled=False)  41.4 us
    pallas_call x5, Pallas kernels, launch(): pl.pallas_call(kernel, out_shape=[jax.ShapeDtypeStruct(shape, F32) for sh...  18.1 us
    unnamed x22, local copies, waits for them, and re-layouts  12.6 us
    ppermute x4, waiting for transfers between devices, from_sides(): return (lax.ppermute(high, axis, up), lax.ppermute(low, axis, down))  11.7 us
    ppermute x4, starting transfers between devices, from_sides(): return (lax.ppermute(high, axis, up), lax.ppermute(low, axis, down))  11.6 us
  transfers between devices with their start and end apart: 5, of which 4 were waited for; matrix products, arithmetic and copies ran while one was open for 0% of the time, Pallas kernels for 3%

profile of v1, /device:TPU:1, one launch (start us, length us, event | category | flops | bytes accessed | tf_op | source)
XLA Modules:
  0.0 109.0 jit_solution(15167684789132871963)
XLA Ops:
  6.5 0.0 all-gather.4.cloned.1.call-start
  6.5 0.0 copy-start.2
  6.5 0.9 copy-done.2
  7.4 0.0 copy-start.4
  7.4 0.9 copy-done.4
  8.3 0.0 copy-start.6
  8.3 0.9 copy-done.6
  9.3 1.1 %shard_map.58 = f32[3,4,8,128]{3,2,1,0:T(8,128)} custom-call(f32[16,16,128]{2,1,0:T(8,128)S(1)} %copy-done.2, f32[16,16,128]{2,1,0:T(8,128)S(1)} %copy-done.4, f32[16,16,128]{2,1,0:T(8,128)S(1)} %copy-done.6), custom_call_target="tpu_custom_call" | custom-call | tf_op jit(solution)/shard_map/pallas_call | solution.py:449
  10.3 0.0 all-gather.4.cloned.1.call-update
  10.4 0.0 copy-start.3
  10.4 0.9 copy-done.3
  11.3 0.0 copy-start.5
  11.3 0.9 copy-done.5
  12.2 0.0 copy-start.7
  12.2 0.9 copy-done.7
  13.1 0.0 copy-start.9
  13.1 0.9 copy-done.9
  14.0 0.0 copy-start.10
  14.0 0.9 copy-done.10
  14.9 4.0 %collective-permute-start = (f32[5,4,16,128]{3,2,1,0:T(8,128)S(1)}, f32[5,4,16,128]{3,2,1,0:T(8,128)S(1)}, u32[]{:S(2)}, u32[]{:S(2)}) collective-permute-start(f32[5,4,16,128]{3,2,1,0:T(8,128)S(1)} %get-tuple-element.11), channel_id=1, source_target_pairs={{0,4},{4,8},{8,12},{12,16},{16,20},{20,24},{24,28},{1,5},{5,9},{9,... | collective-permute-start | bytes 491528 | tf_op jit(solution)/shard_map/ppermute | solution.py:466
  18.9 1.3 %collective-permute-start.1 = (f32[5,4,16,128]{3,2,1,0:T(8,128)S(1)}, f32[5,4,16,128]{3,2,1,0:T(8,128)S(1)}, u32[]{:S(2)}, u32[]{:S(2)}) collective-permute-start(f32[5,4,16,128]{3,2,1,0:T(8,128)S(1)} %get-tuple-element.12), channel_id=1, source_target_pairs={{4,0},{8,4},{12,8},{16,12},{20,16},{24,20},{28,24},{5,1},{9,5},{13... | collective-permute-start | bytes 491528 | tf_op jit(solution)/shard_map/ppermute | solution.py:466
  20.2 1.5 %collective-permute-done.refs_5_ = f32[5,4,16,128]{3,2,1,0:T(8,128)S(1)} collective-permute-done((f32[5,4,16,128]{3,2,1,0:T(8,128)S(1)}, f32[5,4,16,128]{3,2,1,0:T(8,128)S(1)}, u32[]{:S(2)}, u32[]{:S(2)}) %collective-permute-start) | collective-permute-done | bytes 163872 | tf_op jit(solution)/shard_map/ppermute | solution.py:466
  21.7 4.6 %collective-permute-done.1.refs_6_ = f32[5,4,16,128]{3,2,1,0:T(8,128)S(1)} collective-permute-done((f32[5,4,16,128]{3,2,1,0:T(8,128)S(1)}, f32[5,4,16,128]{3,2,1,0:T(8,128)S(1)}, u32[]{:S(2)}, u32[]{:S(2)}) %collective-permute-start.1) | collective-permute-done | bytes 163872 | tf_op jit(solution)/shard_map/ppermute | solution.py:466
  26.3 0.1 shard_map.56
  26.4 4.5 %collective-permute-start.2 = (f32[5,24,4,128]{3,2,1,0:T(4,128)S(1)}, f32[5,24,4,128]{3,2,1,0:T(4,128)S(1)}, u32[]{:S(2)}, u32[]{:S(2)}) collective-permute-start(f32[5,24,4,128]{3,2,1,0:T(4,128)S(1)} %get-tuple-element.13), channel_id=1, source_target_pairs={{0,1},{1,2},{2,3},{4,5},{5,6},{6,7},{8,9},{9,10},{10,11},{12,13},{... | collective-permute-start | bytes 737288 | tf_op jit(solution)/shard_map/ppermute | solution.py:466
  30.9 1.9 %collective-permute-start.3 = (f32[5,24,4,128]{3,2,1,0:T(4,128)S(1)}, f32[5,24,4,128]{3,2,1,0:T(4,128)S(1)}, u32[]{:S(2)}, u32[]{:S(2)}) collective-permute-start(f32[5,24,4,128]{3,2,1,0:T(4,128)S(1)} %get-tuple-element.14), channel_id=1, source_target_pairs={{1,0},{2,1},{3,2},{5,4},{6,5},{7,6},{9,8},{10,9},{11,10},{13,12},{... | collective-permute-start | bytes 737288 | tf_op jit(solution)/shard_map/ppermute | solution.py:466
  32.8 1.2 %collective-permute-done.2.refs_7_ = f32[5,24,4,128]{3,2,1,0:T(4,128)S(1)} collective-permute-done((f32[5,24,4,128]{3,2,1,0:T(4,128)S(1)}, f32[5,24,4,128]{3,2,1,0:T(4,128)S(1)}, u32[]{:S(2)}, u32[]{:S(2)}) %collective-permute-start.2) | collective-permute-done | bytes 245792 | tf_op jit(solution)/shard_map/ppermute | solution.py:466
  34.0 4.4 %collective-permute-done.3.refs_8_ = f32[5,24,4,128]{3,2,1,0:T(4,128)S(1)} collective-permute-done((f32[5,24,4,128]{3,2,1,0:T(4,128)S(1)}, f32[5,24,4,128]{3,2,1,0:T(4,128)S(1)}, u32[]{:S(2)}, u32[]{:S(2)}) %collective-permute-start.3) | collective-permute-done | bytes 245792 | tf_op jit(solution)/shard_map/ppermute | solution.py:466
  38.4 2.7 %shard_map.57 = (f32[8,24,40,128]{3,2,1,0:T(8,128)S(1)}, f32[4,8,128]{2,1,0:T(8,128)S(1)}) custom-call(f32[16,16,128]{2,1,0:T(8,128)S(1)} %copy-done.9, f32[16,16,128]{2,1,0:T(8,128)S(1)} %copy-done.10, f32[16,16,128]{2,1,0:T(8,128)S(1)} %copy-done.3, f32[16,16,128]{2,1,0:T(8,128)S(1)} %copy-done.5, f32[16,16,128]{2,1,0:T(8,128)S(1)} %copy-done.7, ...), custom_call_target="tpu_custom_call" | custom-call | tf_op jit(solution)/shard_map/pallas_call | solution.py:449
  41.0 0.0 copy-start
  41.0 1.9 %copy-done = f32[8,24,40,128]{3,2,1,0:T(8,128)} copy-done((f32[8,24,40,128]{3,2,1,0:T(8,128)}, f32[8,24,40,128]{3,2,1,0:T(8,128)S(1)}, u32[]{:S(2)}) %copy-start) | copy-done | bytes 3932184
  42.9 41.4 %all-gather = f32[128,8,128]{2,1,0:T(8,128)S(1)} all-gather(f32[4,8,128]{2,1,0:T(8,128)S(1)} %get-tuple-element.16), channel_id=2, replica_groups=mesh['gx'=8,'gy'=4] {'gx','gy'}, dimensions={0}, use_global_device_ids=true | all-gather | bytes 540672 | tf_op jit(solution)/shard_map/all_gather | solution.py:470
  84.4 0.0 all-gather.4.cloned.1.call-done
  84.4 0.0 copy-start.1
  84.4 2.1 %copy-done.1 = f32[8,24,40,128]{3,2,1,0:T(8,128)S(1)} copy-done((f32[8,24,40,128]{3,2,1,0:T(8,128)S(1)}, f32[8,24,40,128]{3,2,1,0:T(8,128)}, u32[]{:S(2)}) %copy-start.1) | copy-done | bytes 3932184
  86.5 0.0 copy-start.8
  86.5 1.4 %copy-done.8 = f32[96,4,8,128]{3,2,1,0:T(8,128)S(1)} copy-done((f32[96,4,8,128]{3,2,1,0:T(8,128)S(1)}, f32[96,4,8,128]{3,2,1,0:T(8,128)}, u32[]{:S(2)}) %copy-start.8) | copy-done | bytes 1572888
  87.9 14.2 %shard_map.59 = f32[16,16,128]{2,1,0:T(8,128)} custom-call(f32[8,24,40,128]{3,2,1,0:T(8,128)S(1)} %copy-done.1, f32[32,4,8,128]{3,2,1,0:T(8,128)S(1)} %bitcast.2, f32[32,3,4,8,128]{4,3,2,1,0:T(8,128)S(1)} %bitcast.3), custom_call_target="tpu_custom_call" | custom-call | tf_op jit(solution)/shard_map/pallas_call | solution.py:449
  (1 shorter events, 0.0 us)
Async XLA Ops:
  6.5 77.8 %all-gather.4.cloned.1.call-start = ((), (), s32[]{:S(2)}) async-start(), calls=%async_computation | async-start | bytes 1622016 | tf_op jit(solution)/shard_map/all_gather | solution.py:470
  6.5 0.9 copy-start.2
  7.4 0.9 copy-start.4
  8.3 0.9 copy-start.6
  10.4 0.9 copy-start.3
  11.3 0.9 copy-start.5
  12.2 0.9 copy-start.7
  13.1 0.9 copy-start.9
  14.0 0.9 copy-start.10
  14.9 6.8 %collective-permute-start = (f32[5,4,16,128]{3,2,1,0:T(8,128)S(1)}, f32[5,4,16,128]{3,2,1,0:T(8,128)S(1)}, u32[]{:S(2)}, u32[]{:S(2)}) collective-permute-start(f32[5,4,16,128]{3,2,1,0:T(8,128)S(1)} %get-tuple-element.11), channel_id=1, source_target_pairs={{0,4},{4,8},{8,12},{12,16},{16,20},{20,24},{24,28},{1,5},{5,9},{9,... | collective-permute-start | bytes 491528 | tf_op jit(solution)/shard_map/ppermute | solution.py:466
  18.9 7.4 %collective-permute-start.1 = (f32[5,4,16,128]{3,2,1,0:T(8,128)S(1)}, f32[5,4,16,128]{3,2,1,0:T(8,128)S(1)}, u32[]{:S(2)}, u32[]{:S(2)}) collective-permute-start(f32[5,4,16,128]{3,2,1,0:T(8,128)S(1)} %get-tuple-element.12), channel_id=1, source_target_pairs={{4,0},{8,4},{12,8},{16,12},{20,16},{24,20},{28,24},{5,1},{9,5},{13... | collective-permute-start | bytes 491528 | tf_op jit(solution)/shard_map/ppermute | solution.py:466
  26.4 7.6 %collective-permute-start.2 = (f32[5,24,4,128]{3,2,1,0:T(4,128)S(1)}, f32[5,24,4,128]{3,2,1,0:T(4,128)S(1)}, u32[]{:S(2)}, u32[]{:S(2)}) collective-permute-start(f32[5,24,4,128]{3,2,1,0:T(4,128)S(1)} %get-tuple-element.13), channel_id=1, source_target_pairs={{0,1},{1,2},{2,3},{4,5},{5,6},{6,7},{8,9},{9,10},{10,11},{12,13},{... | collective-permute-start | bytes 737288 | tf_op jit(solution)/shard_map/ppermute | solution.py:466
  30.9 7.5 %collective-permute-start.3 = (f32[5,24,4,128]{3,2,1,0:T(4,128)S(1)}, f32[5,24,4,128]{3,2,1,0:T(4,128)S(1)}, u32[]{:S(2)}, u32[]{:S(2)}) collective-permute-start(f32[5,24,4,128]{3,2,1,0:T(4,128)S(1)} %get-tuple-element.14), channel_id=1, source_target_pairs={{1,0},{2,1},{3,2},{5,4},{6,5},{7,6},{9,8},{10,9},{11,10},{13,12},{... | collective-permute-start | bytes 737288 | tf_op jit(solution)/shard_map/ppermute | solution.py:466
  41.0 1.9 %copy-start = (f32[8,24,40,128]{3,2,1,0:T(8,128)}, f32[8,24,40,128]{3,2,1,0:T(8,128)S(1)}, u32[]{:S(2)}) copy-start(f32[8,24,40,128]{3,2,1,0:T(8,128)S(1)} %get-tuple-element.15.top) | copy-start | bytes 11796484
  84.4 2.1 %copy-start.1 = (f32[8,24,40,128]{3,2,1,0:T(8,128)S(1)}, f32[8,24,40,128]{3,2,1,0:T(8,128)}, u32[]{:S(2)}) copy-start(f32[8,24,40,128]{3,2,1,0:T(8,128)} %copy-done) | copy-start | bytes 11796484
  86.5 1.4 %copy-start.8 = (f32[96,4,8,128]{3,2,1,0:T(8,128)S(1)}, f32[96,4,8,128]{3,2,1,0:T(8,128)}, u32[]{:S(2)}) copy-start(f32[96,4,8,128]{3,2,1,0:T(8,128)} %all-gather.4.cloned.1.call-done) | copy-start | bytes 4718596
Sparse Core Ops, SparseCore 0:
  10.5 58.2 all-gather.3

commit v2 on v1

--- a/solution.py
+++ b/solution.py
@@ -73,20 +73,24 @@
 
 
 def pack_x(*refs):
-    fields, (low, high) = refs[:5], refs[5:]
-    for index, ref in enumerate(fields):
-        low[index] = ref[:RIM]
-        high[index] = ref[ref.shape[0] - RIM :]
-
-
-def pack_y(*refs):
-    fields, (x_low, x_high, low, high) = refs[:5], refs[5:]
-    for index, ref in enumerate(fields):
-        nx, ny = ref.shape[:2]
+    fields, (own, low, high, done) = refs[:5], refs[5:]
+    copies = [pltpu.make_async_copy(ref, own.at[index], done.at[index]) for index, ref in enumerate(fields)]
+    for copy in copies:
+        copy.start()
+    nx = own.shape[1]
+    for index, copy in enumerate(copies):
+        copy.wait()
+        low[index] = own[index, :RIM]
+        high[index] = own[index, nx - RIM :]
+
+
+def pack_y(own, x_low, x_high, low, high):
+    count, nx, ny = own.shape[:3]
+    for index in range(count):
         for out, start in ((low, 0), (high, ny - RIM)):
             rows = slice(start, start + RIM)
             out[index, :RIM] = x_low[index, :, rows]
-            out[index, RIM : RIM + nx] = ref[:, rows]
+            out[index, RIM : RIM + nx] = own[index, :, rows]
             out[index, RIM + nx :] = x_high[index, :, rows]
 
 
@@ -96,7 +100,8 @@
     return values[:, 0], values[:, 1]
 
 
-def coarse_faces(fx, fy, fz, out, tmp):
+def coarse_faces(own, out, tmp):
+    fx, fy, fz = own.at[2], own.at[3], own.at[4]
     rows = fx.shape[1]
     tmp[...] = pair_slabs(fx)[0]
     out[0] = 0.25 * merge_lanes(even_rows(tmp, rows) + odd_rows(tmp, rows), LANES)
@@ -152,8 +157,8 @@
 
 
 def level_down(axes, *refs):
-    fields, (x_low, x_high, y_low, y_high, lev, chunk, other, tmp) = refs[:5], refs[5:]
-    nx, ny = fields[0].shape[:2]
+    own, x_low, x_high, y_low, y_high, lev, chunk, other, tmp = refs
+    nx, ny = own.shape[1:3]
     slabs, rows = nx + 2 * RIM, ny + 2 * RIM
     me_x, me_y = lax.axis_index(axes[0]), lax.axis_index(axes[1])
     for index, slot in enumerate((F, V, FX, FY, ZL)):
@@ -161,7 +166,7 @@
         lev[slot, :, PAD + rows :] = jnp.zeros((slabs, PAD, LANES), F32)
         inner = pl.ds(PAD + RIM, ny)
         lev[slot, :RIM, inner] = x_low[index]
-        lev[slot, RIM : RIM + nx, inner] = fields[index][...]
+        lev[slot, RIM : RIM + nx, inner] = own[index]
         lev[slot, RIM + nx :, inner] = x_high[index]
         lev[slot, :, PAD : PAD + RIM] = y_low[index]
         lev[slot, :, PAD + RIM + ny : PAD + rows] = y_high[index]
@@ -442,18 +447,17 @@
     run(nx, sixth, 2)
 
 
-def call(kernel, shapes, scratch=(), **kwargs):
+def call(kernel, shapes, scratch=(), space=pltpu.VMEM):
     vmem = pl.BlockSpec(memory_space=pltpu.VMEM)
 
     def launch(*args):
         return pl.pallas_call(
             kernel,
             out_shape=[jax.ShapeDtypeStruct(shape, F32) for shape in shapes],
-            in_specs=[vmem] * len(args),
+            in_specs=[pl.BlockSpec(memory_space=space)] * len(args),
             out_specs=[vmem] * len(shapes),
-            scratch_shapes=[pltpu.VMEM(shape, F32) for shape in scratch],
-            compiler_params=pltpu.CompilerParams(vmem_limit_bytes=48 * 2**20),
-            **kwargs,
+            scratch_shapes=[pltpu.VMEM(s, F32) if isinstance(s, tuple) else s for s in scratch],
+            compiler_params=pltpu.CompilerParams(vmem_limit_bytes=24 * 2**20),
         )(*args)
 
     return launch
@@ -466,29 +470,45 @@
     return lax.ppermute(high, axis, up), lax.ppermute(low, axis, down)
 
 
-def gathered(block):
-    return lax.all_gather(block, ("gx", "gy"), axis=0, tiled=False)
-
-
-def fused_cycle(source, guess, face_x, face_y, face_z):
+def summed(block):
+    count = lax.axis_size("gx") * lax.axis_size("gy")
+    index = lax.axis_index("gx") * lax.axis_size("gy") + lax.axis_index("gy")
+    zeros = jnp.zeros((count,) + block.shape, block.dtype)
+    start = (index,) + (0,) * block.ndim
+    return lax.psum(lax.dynamic_update_slice(zeros, block[None], start), ("gx", "gy"))
+
+
+def handed_out(block):
+    for axis in ("gx", "gy"):
+        copies = jnp.broadcast_to(block, (lax.axis_size(axis),) + block.shape)
+        block = lax.all_to_all(copies, axis, 0, 0)
+    block = jnp.swapaxes(block, 0, 1)
+    return block.reshape((-1,) + block.shape[2:])
+
+
+def fused_cycle(*fields):
     axes = ("gx", "gy")
     devices_x, devices_y = lax.axis_size("gx"), lax.axis_size("gy")
-    nx, ny, nz = source.shape
-    fields = (source, guess, face_x, face_y, face_z)
-    x_low, x_high = call(pack_x, [(5, RIM, ny, nz)] * 2)(*fields)
+    nx, ny, nz = fields[0].shape
+    parts = nx // 4
+    slabs, rows = nx + 2 * RIM, ny + 2 * RIM
+    own, x_low, x_high = call(
+        pack_x,
+        [(5, nx, ny, nz)] + [(5, RIM, ny, nz)] * 2,
+        [pltpu.SemaphoreType.DMA((5,))],
+        pl.ANY,
+    )(*fields)
     x_low, x_high = from_sides(x_low, x_high, "gx")
-    parts = nx // 4
-    (faces,) = call(coarse_faces, [(3, parts, ny // 2, LANES)], [(nx // 2, ny, LANES)])(face_x, face_y, face_z)
-    faces = gathered(faces)
-    slabs, rows = nx + 2 * RIM, ny + 2 * RIM
-    y_low, y_high = call(pack_y, [(5, slabs, RIM, nz)] * 2)(*fields, x_low, x_high)
+    (faces,) = call(coarse_faces, [(3, parts, ny // 2, LANES)], [(nx // 2, ny, LANES)])(own)
+    faces = handed_out(faces)
+    y_low, y_high = call(pack_y, [(5, slabs, RIM, nz)] * 2)(own, x_low, x_high)
     y_low, y_high = from_sides(y_low, y_high, "gy")
     top, chunk = call(
         functools.partial(level_down, axes),
         [(8, slabs, rows + 2 * PAD, LANES), (parts, ny // 2, LANES)],
         [(slabs, rows + 2 * PAD, LANES), (nx // 2, ny, LANES)],
-    )(*fields, x_low, x_high, y_low, y_high)
-    sources = gathered(chunk)
+    )(own, x_low, x_high, y_low, y_high)
+    sources = summed(chunk)
     count = devices_x * nx // 4
     rows_1 = devices_y * ny // 2
     coarsest = (devices_x * nx >> LEVELS - 1, devices_y * ny >> LEVELS - 1)

time: 109 us -> 216 us (1.98); the launches traced: 109 us -> 214 us
  waiting for transfers between devices: 11.7 us -> 137 us
  blocking collectives: 41.4 us -> 16.5 us
  starting transfers between devices: 11.6 us -> 16.5 us
    psum x0 -> x1, waiting for transfers between devices: none -> 125 us  [summed(): lax.psum(lax.dynamic_update_slice(zeros, block[None], start), ('gx', 'gy'))]
    all_gather x1 -> x0, blocking collectives: 41.4 us -> none  [gathered(): return lax.all_gather(block, ('gx', 'gy'), axis=0, tiled=False)]
    all_to_all x0 -> x1, blocking collectives: none -> 16.5 us  [handed_out(): block = lax.all_to_all(copies, axis, 0, 0)]
    all_to_all x0 -> x1, starting transfers between devices: none -> 6.23 us  [handed_out(): block = lax.all_to_all(copies, axis, 0, 0)]
    unnamed x22 -> x18, local copies, waits for them, and re-layouts: 12.6 us -> 10.3 us
  transfers between devices with their start and end apart: 5 -> 6, of which waited for: 4 -> 5; matrix products, arithmetic and copies ran while one was open for 0% -> 0% of each run, Pallas kernels for 3% -> 1%
where the time goes in v2:
time: 216 us; the launch traced here: 214 us
  waiting for transfers between devices  137 us (63%)
  Pallas kernels  18.3 us (8%)
  blocking collectives  16.5 us (8%)
  starting transfers between devices  16.5 us (8%)
  between operations  13.5 us (6%)
  local copies, waits for them, and re-layouts  12 us (6%)
    psum x1, waiting for transfers between devices, summed(): lax.psum(lax.dynamic_update_slice(zeros, block[None], start), ('gx', 'gy'))  125 us
    pallas_call x5, Pallas kernels, launch(): pl.pallas_call(kernel, out_shape=[jax.ShapeDtypeStruct(shape, F32) for sh...  18.3 us
    all_to_all x1, blocking collectives, handed_out(): block = lax.all_to_all(copies, axis, 0, 0)  16.5 us
    ppermute x4, waiting for transfers between devices, from_sides(): return (lax.ppermute(high, axis, up), lax.ppermute(low, axis, down))  11.6 us
    unnamed x18, local copies, waits for them, and re-layouts  10.3 us
    ppermute x4, starting transfers between devices, from_sides(): return (lax.ppermute(high, axis, up), lax.ppermute(low, axis, down))  10.3 us
    all_to_all x1, starting transfers between devices, handed_out(): block = lax.all_to_all(copies, axis, 0, 0)  6.23 us
  transfers between devices with their start and end apart: 6, of which 5 were waited for; matrix products, arithmetic and copies ran while one was open for 0% of the time, Pallas kernels for 1%

profile of v2, /device:TPU:1, one launch (start us, length us, event | category | flops | bytes accessed | tf_op | source)
XLA Modules:
  0.0 213.7 jit_solution(9679940139055079439)
XLA Ops:
  6.5 0.0 copy-start.3
  6.5 0.9 copy-done.3
  7.4 0.0 copy-start.4
  7.4 0.9 copy-done.4
  8.3 0.0 copy-start.5
  8.3 0.9 copy-done.5
  9.2 0.0 copy-start.6
  9.3 0.9 copy-done.6
  10.2 0.0 copy-start.7
  10.2 0.9 copy-done.7
  11.1 0.9 shard_map.55
  11.9 0.5 shard_map.58
  12.5 16.5 %all_to_all.10 = f32[8,3,4,8,128]{4,3,2,1,0:T(8,128)S(1)} all-to-all(f32[8,3,4,8,128]{4,3,2,1,0:T(8,128)S(1)} %broadcast_in_dim.14), channel_id=1, replica_groups=mesh['gx'=8,'gy'=4] {'gx'}, dimensions={0} | all-to-all | bytes 786432 | tf_op jit(solution)/shard_map/all_to_all | solution.py:484
  29.0 1.4 broadcast_in_dim.15
  30.4 6.2 %all-to-all-start.1 = ((f32[4,8,3,4,8,128]{5,4,3,2,1,0:T(8,128)}), f32[4,8,3,4,8,128]{5,4,3,2,1,0:T(8,128)S(1)}, u32[]{:S(2)}, u32[]{:S(2)}) async-start(f32[4,8,3,4,8,128]{5,4,3,2,1,0:T(8,128)} %broadcast_in_dim.15), calls=%async_computation.1 | async-start | bytes 3145728 | tf_op jit(solution)/shard_map/all_to_all | solution.py:484
  36.6 0.0 all-reduce.2.cloned.1.call-start
  36.6 2.7 %collective-permute-start = (f32[5,4,16,128]{3,2,1,0:T(8,128)S(1)}, f32[5,4,16,128]{3,2,1,0:T(8,128)S(1)}, u32[]{:S(2)}, u32[]{:S(2)}) collective-permute-start(f32[5,4,16,128]{3,2,1,0:T(8,128)S(1)} %get-tuple-element.13), channel_id=1, source_target_pairs={{0,4},{4,8},{8,12},{12,16},{16,20},{20,24},{24,28},{1,5},{5,9},{9,... | collective-permute-start | bytes 491528 | tf_op jit(solution)/shard_map/ppermute | solution.py:470
  39.3 1.3 collective-permute-start.1
  40.6 2.2 %collective-permute-done.x_low.refs_1_ = f32[5,4,16,128]{3,2,1,0:T(8,128)S(1)} collective-permute-done((f32[5,4,16,128]{3,2,1,0:T(8,128)S(1)}, f32[5,4,16,128]{3,2,1,0:T(8,128)S(1)}, u32[]{:S(2)}, u32[]{:S(2)}) %collective-permute-start) | collective-permute-done | bytes 163872 | tf_op jit(solution)/shard_map/ppermute | solution.py:470
  42.9 3.8 %collective-permute-done.1.x_high.refs_2_ = f32[5,4,16,128]{3,2,1,0:T(8,128)S(1)} collective-permute-done((f32[5,4,16,128]{3,2,1,0:T(8,128)S(1)}, f32[5,4,16,128]{3,2,1,0:T(8,128)S(1)}, u32[]{:S(2)}, u32[]{:S(2)}) %collective-permute-start.1) | collective-permute-done | bytes 163872 | tf_op jit(solution)/shard_map/ppermute | solution.py:470
  46.7 0.1 shard_map.56
  46.7 4.4 %collective-permute-start.2 = (f32[5,24,4,128]{3,2,1,0:T(4,128)S(1)}, f32[5,24,4,128]{3,2,1,0:T(4,128)S(1)}, u32[]{:S(2)}, u32[]{:S(2)}) collective-permute-start(f32[5,24,4,128]{3,2,1,0:T(4,128)S(1)} %get-tuple-element.15), channel_id=1, source_target_pairs={{0,1},{1,2},{2,3},{4,5},{5,6},{6,7},{8,9},{9,10},{10,11},{12,13},{... | collective-permute-start | bytes 737288 | tf_op jit(solution)/shard_map/ppermute | solution.py:470
  51.1 1.9 collective-permute-start.3
  53.0 3.8 %collective-permute-done.2.refs_3_ = f32[5,24,4,128]{3,2,1,0:T(4,128)S(1)} collective-permute-done((f32[5,24,4,128]{3,2,1,0:T(4,128)S(1)}, f32[5,24,4,128]{3,2,1,0:T(4,128)S(1)}, u32[]{:S(2)}, u32[]{:S(2)}) %collective-permute-start.2) | collective-permute-done | bytes 245792 | tf_op jit(solution)/shard_map/ppermute | solution.py:470
  56.8 1.8 collective-permute-done.3.refs_4_
  58.6 2.7 %shard_map.57 = (f32[8,24,40,128]{3,2,1,0:T(8,128)S(1)}, f32[4,8,128]{2,1,0:T(8,128)S(1)}) custom-call(f32[5,16,16,128]{3,2,1,0:T(8,128)S(1)} %get-tuple-element.12.own.refs_0_, f32[5,4,16,128]{3,2,1,0:T(8,128)S(1)} %collective-permute-done.x_low.refs_1_, f32[5,4,16,128]{3,2,1,0:T(8,128)S(1)} %collective-permute-done.1.x_high.refs_2_, ...), custom_call_target="tpu_custom_call" | custom-call | tf_op jit(solution)/shard_map/pallas_call | solution.py:454
  61.3 0.0 copy-start
  61.3 1.9 copy-done
  63.2 0.0 copy-start.8
  63.2 0.8 copy-done.8
  64.0 0.0 all-reduce.2.cloned.1.call-update
  64.1 0.0 all-to-all-done.1
  64.1 0.2 copy.6
  64.2 125.2 %all-reduce.2.cloned.1.call-done.sources = f32[32,4,8,128]{3,2,1,0:T(8,128)} async-done(((f32[32,4,8,128]{3,2,1,0:T(8,128)}), f32[32,4,8,128]{3,2,1,0:T(8,128)}) %all-reduce.2.cloned.1.call-update) | async-done | bytes 524304 | tf_op jit(solution)/shard_map/psum | solution.py:478
  189.5 0.0 copy-start.1
  189.5 2.1 copy-done.1
  191.6 0.0 copy-start.2
  191.6 1.0 copy-done.2
  192.6 14.2 %shard_map.59 = f32[16,16,128]{2,1,0:T(8,128)} custom-call(f32[8,24,40,128]{3,2,1,0:T(8,128)S(1)} %copy-done.1, f32[32,4,8,128]{3,2,1,0:T(8,128)S(1)} %copy-done.2, f32[32,3,4,8,128]{4,3,2,1,0:T(8,128)S(1)} %bitcast.4), custom_call_target="tpu_custom_call" | custom-call | tf_op jit(solution)/shard_map/pallas_call | solution.py:454
  (3 shorter events, 0.1 us)
Async XLA Ops:
  6.5 0.9 copy-start.3
  7.4 0.9 copy-start.4
  8.3 0.9 copy-start.5
  9.2 0.9 copy-start.6
  10.2 0.9 copy-start.7
  30.4 33.7 %all-to-all-start.1 = ((f32[4,8,3,4,8,128]{5,4,3,2,1,0:T(8,128)}), f32[4,8,3,4,8,128]{5,4,3,2,1,0:T(8,128)S(1)}, u32[]{:S(2)}, u32[]{:S(2)}) async-start(f32[4,8,3,4,8,128]{5,4,3,2,1,0:T(8,128)} %broadcast_in_dim.15), calls=%async_computation.1 | async-start | bytes 3145728 | tf_op jit(solution)/shard_map/all_to_all | solution.py:484
  36.6 152.9 %all-reduce.2.cloned.1.call-start = ((), (), s32[]{:S(2)}) async-start(), calls=%async_computation.2 | async-start | bytes 1048576 | tf_op jit(solution)/shard_map/psum | solution.py:478
  36.6 6.3 %collective-permute-start = (f32[5,4,16,128]{3,2,1,0:T(8,128)S(1)}, f32[5,4,16,128]{3,2,1,0:T(8,128)S(1)}, u32[]{:S(2)}, u32[]{:S(2)}) collective-permute-start(f32[5,4,16,128]{3,2,1,0:T(8,128)S(1)} %get-tuple-element.13), channel_id=1, source_target_pairs={{0,4},{4,8},{8,12},{12,16},{16,20},{20,24},{24,28},{1,5},{5,9},{9,... | collective-permute-start | bytes 491528 | tf_op jit(solution)/shard_map/ppermute | solution.py:470
  39.3 7.3 %collective-permute-start.1 = (f32[5,4,16,128]{3,2,1,0:T(8,128)S(1)}, f32[5,4,16,128]{3,2,1,0:T(8,128)S(1)}, u32[]{:S(2)}, u32[]{:S(2)}) collective-permute-start(f32[5,4,16,128]{3,2,1,0:T(8,128)S(1)} %get-tuple-element.14), channel_id=1, source_target_pairs={{4,0},{8,4},{12,8},{16,12},{20,16},{24,20},{28,24},{5,1},{9,5},{13... | collective-permute-start | bytes 491528 | tf_op jit(solution)/shard_map/ppermute | solution.py:470
  46.7 10.1 %collective-permute-start.2 = (f32[5,24,4,128]{3,2,1,0:T(4,128)S(1)}, f32[5,24,4,128]{3,2,1,0:T(4,128)S(1)}, u32[]{:S(2)}, u32[]{:S(2)}) collective-permute-start(f32[5,24,4,128]{3,2,1,0:T(4,128)S(1)} %get-tuple-element.15), channel_id=1, source_target_pairs={{0,1},{1,2},{2,3},{4,5},{5,6},{6,7},{8,9},{9,10},{10,11},{12,13},{... | collective-permute-start | bytes 737288 | tf_op jit(solution)/shard_map/ppermute | solution.py:470
  51.1 7.5 %collective-permute-start.3 = (f32[5,24,4,128]{3,2,1,0:T(4,128)S(1)}, f32[5,24,4,128]{3,2,1,0:T(4,128)S(1)}, u32[]{:S(2)}, u32[]{:S(2)}) collective-permute-start(f32[5,24,4,128]{3,2,1,0:T(4,128)S(1)} %get-tuple-element.16), channel_id=1, source_target_pairs={{1,0},{2,1},{3,2},{5,4},{6,5},{7,6},{9,8},{10,9},{11,10},{13,12},{... | collective-permute-start | bytes 737288 | tf_op jit(solution)/shard_map/ppermute | solution.py:470
  61.3 1.9 copy-start
  63.2 0.8 copy-start.8
  189.5 2.1 copy-start.1
  191.6 1.0 copy-start.2
Sparse Core Ops, SparseCore 0:
  64.2 125.2 all-reduce.1

commit v3 on v2

--- a/solution.py
+++ b/solution.py
@@ -157,7 +157,7 @@
 
 
 def level_down(axes, *refs):
-    own, x_low, x_high, y_low, y_high, lev, chunk, other, tmp = refs
+    own, x_low, x_high, y_low, y_high, top, chunk, lev, other, tmp, done = refs
     nx, ny = own.shape[1:3]
     slabs, rows = nx + 2 * RIM, ny + 2 * RIM
     me_x, me_y = lax.axis_index(axes[0]), lax.axis_index(axes[1])
@@ -182,12 +182,16 @@
         other[slab, main] = swept(lev, lev.at[V], slab, PAD, rows)
 
     run(slabs - 2, first, 2)
+    copies = [pltpu.make_async_copy(lev.at[slot], top.at[slot], done.at[slot]) for slot in range(D)]
+    for copy in copies[1:]:
+        copy.start()
 
     def second(index):
         slab = index + 2
         lev[V, slab, main] = swept(lev, other, slab, PAD, rows)
 
     run(slabs - 4, second, 2)
+    copies[0].start()
 
     def rest(slab):
         v, total = weighted(lev, lev.at[V], slab, PAD + RIM, ny)
@@ -199,6 +203,8 @@
 
     run(nx // 2, residual, 2)
     chunk[...] = 0.5 * merge_lanes(even_rows(tmp, ny) + odd_rows(tmp, ny), LANES)
+    for copy in copies:
+        copy.wait()
 
 
 def pair_rows(values, stride):
@@ -307,14 +313,16 @@
     ref[count + 1, main] = jnp.where(lane >= LANES - depth, 0.0, roll_lanes(first, -depth))
 
 
-def level_up(axes, grid, sweeps, top, sources, faces, out, lev, post, tmp, up):
+def level_up(axes, grid, sweeps, sources, faces, stored, out, lev, top, post, tmp, up, done):
     devices_x, devices_y = grid
+    fetch = pltpu.make_async_copy(stored, top, done.at[0])
+    fetch.start()
     me_x, me_y = lax.axis_index(axes[0]), lax.axis_index(axes[1])
     depth = LANES // 2
     count = lev.shape[1] - 2
     rows = lev.shape[2] - 2 * PAD
     main = pl.ds(PAD, rows)
-    parts = sources.shape[1]
+    parts = sources.shape[2]
     low_lanes = lanes_of((PAD, LANES)) < depth
     for slot in (V, U, FY):
         for start in (0, PAD + rows):
@@ -323,14 +331,19 @@
     def unpack(index):
         for y in range(devices_y):
             here = pl.ds(PAD + y * PAD, PAD)
-            near = index * devices_y + y
-            far = (index + devices_x // 2) * devices_y + y
-            for slot, ref, place in ((F, sources, ()), (FX, faces, (0,)), (FY, faces, (1,)), (ZL, faces, (2,))):
-                for part in range(parts):
-                    a, b = ref[(near,) + place + (part,)], ref[(far,) + place + (part,)]
-                    slab = 1 + index * 2 * parts + part
-                    lev[slot, slab, here] = jnp.where(low_lanes, a, roll_lanes(b, depth))
-                    lev[slot, slab + parts, here] = jnp.where(low_lanes, roll_lanes(a, depth), b)
+            near, far = index, index + devices_x // 2
+
+            def place(slot, part, a, b):
+                slab = 1 + index * 2 * parts + part
+                lev[slot, slab, here] = jnp.where(low_lanes, a, roll_lanes(b, depth))
+                lev[slot, slab + parts, here] = jnp.where(low_lanes, roll_lanes(a, depth), b)
+
+            for part in range(parts):
+                place(F, part, sources[y, near, part], sources[y, far, part])
+                a = (me_x - near + devices_x) % devices_x
+                b = (me_x - far + devices_x) % devices_x
+                for face, slot in enumerate((FX, FY, ZL)):
+                    place(slot, part, faces[y, a, face, part], faces[y, b, face, part])
 
     run(devices_x // 2, unpack)
     wrap_slabs(lev.at[FX], count, depth, main)
@@ -425,6 +438,7 @@
     for odd in range(2):
         up[:, pl.ds(odd, fine_rows // 2, stride=2), :] = fine
     body = pl.ds(PAD, fine_rows)
+    fetch.wait()
     for slot in (0, 1):
         for start in (0, PAD + fine_rows):
             post[slot, :, start : start + PAD] = jnp.zeros((post.shape[1], PAD, LANES), F32)
@@ -447,17 +461,19 @@
     run(nx, sixth, 2)
 
 
-def call(kernel, shapes, scratch=(), space=pltpu.VMEM):
-    vmem = pl.BlockSpec(memory_space=pltpu.VMEM)
-
+IN_VMEM = pl.BlockSpec(memory_space=pltpu.VMEM)
+ANYWHERE = pl.BlockSpec(memory_space=pl.ANY)
+
+
+def call(kernel, ins, outs, scratch=(), limit=24 * 2**20):
     def launch(*args):
         return pl.pallas_call(
             kernel,
-            out_shape=[jax.ShapeDtypeStruct(shape, F32) for shape in shapes],
-            in_specs=[pl.BlockSpec(memory_space=space)] * len(args),
-            out_specs=[vmem] * len(shapes),
+            out_shape=[jax.ShapeDtypeStruct(shape, F32) for shape, _ in outs],
+            in_specs=ins,
+            out_specs=[spec for _, spec in outs],
             scratch_shapes=[pltpu.VMEM(s, F32) if isinstance(s, tuple) else s for s in scratch],
-            compiler_params=pltpu.CompilerParams(vmem_limit_bytes=24 * 2**20),
+            compiler_params=pltpu.CompilerParams(vmem_limit_bytes=limit),
         )(*args)
 
     return launch
@@ -470,20 +486,17 @@
     return lax.ppermute(high, axis, up), lax.ppermute(low, axis, down)
 
 
-def summed(block):
-    count = lax.axis_size("gx") * lax.axis_size("gy")
-    index = lax.axis_index("gx") * lax.axis_size("gy") + lax.axis_index("gy")
-    zeros = jnp.zeros((count,) + block.shape, block.dtype)
-    start = (index,) + (0,) * block.ndim
-    return lax.psum(lax.dynamic_update_slice(zeros, block[None], start), ("gx", "gy"))
-
-
-def handed_out(block):
-    for axis in ("gx", "gy"):
-        copies = jnp.broadcast_to(block, (lax.axis_size(axis),) + block.shape)
-        block = lax.all_to_all(copies, axis, 0, 0)
-    block = jnp.swapaxes(block, 0, 1)
-    return block.reshape((-1,) + block.shape[2:])
+def handed_out(block, axis):
+    copies = jnp.broadcast_to(block, (lax.axis_size(axis),) + block.shape)
+    return lax.all_to_all(copies, axis, 0, 0)
+
+
+def passed_round(block, axis):
+    count = lax.axis_size(axis)
+    blocks = [block]
+    for distance in range(1, count):
+        blocks.append(lax.ppermute(block, axis, [(i, (i + distance) % count) for i in range(count)]))
+    return jnp.stack(blocks)
 
 
 def fused_cycle(*fields):
@@ -494,34 +507,42 @@
     slabs, rows = nx + 2 * RIM, ny + 2 * RIM
     own, x_low, x_high = call(
         pack_x,
-        [(5, nx, ny, nz)] + [(5, RIM, ny, nz)] * 2,
+        [ANYWHERE] * 5,
+        [((5, nx, ny, nz), IN_VMEM), ((5, RIM, ny, nz), IN_VMEM), ((5, RIM, ny, nz), IN_VMEM)],
         [pltpu.SemaphoreType.DMA((5,))],
-        pl.ANY,
+        None,
     )(*fields)
     x_low, x_high = from_sides(x_low, x_high, "gx")
-    (faces,) = call(coarse_faces, [(3, parts, ny // 2, LANES)], [(nx // 2, ny, LANES)])(own)
-    faces = handed_out(faces)
-    y_low, y_high = call(pack_y, [(5, slabs, RIM, nz)] * 2)(own, x_low, x_high)
+    (faces,) = call(
+        coarse_faces, [IN_VMEM], [((3, parts, ny // 2, LANES), IN_VMEM)], [(nx // 2, ny, LANES)]
+    )(own)
+    faces = handed_out(passed_round(faces, "gx"), "gy")
+    y_low, y_high = call(pack_y, [IN_VMEM] * 3, [((5, slabs, RIM, nz), IN_VMEM)] * 2)(own, x_low, x_high)
     y_low, y_high = from_sides(y_low, y_high, "gy")
+    stack = (slabs, rows + 2 * PAD, LANES)
     top, chunk = call(
         functools.partial(level_down, axes),
-        [(8, slabs, rows + 2 * PAD, LANES), (parts, ny // 2, LANES)],
-        [(slabs, rows + 2 * PAD, LANES), (nx // 2, ny, LANES)],
+        [IN_VMEM] * 5,
+        [((D,) + stack, ANYWHERE), ((parts, ny // 2, LANES), IN_VMEM)],
+        [(D + 1,) + stack, stack, (nx // 2, ny, LANES), pltpu.SemaphoreType.DMA((D,))],
     )(own, x_low, x_high, y_low, y_high)
-    sources = summed(chunk)
+    sources = handed_out(handed_out(chunk, "gx"), "gy")
     count = devices_x * nx // 4
     rows_1 = devices_y * ny // 2
     coarsest = (devices_x * nx >> LEVELS - 1, devices_y * ny >> LEVELS - 1)
     (out,) = call(
         functools.partial(level_up, axes, (devices_x, devices_y), 4 * max(coarsest)),
-        [(nx, ny, nz)],
+        [IN_VMEM, IN_VMEM, ANYWHERE],
+        [((nx, ny, nz), IN_VMEM)],
         [
             (9, count + 2, rows_1 + 2 * PAD, LANES),
-            (2, slabs, rows + 2 * PAD, LANES),
+            (D,) + stack,
+            (2,) + stack,
             (count // 2, rows_1, LANES),
             (nx // 2 + 2, rows, LANES),
+            pltpu.SemaphoreType.DMA((1,)),
         ],
-    )(top, sources, faces)
+    )(sources, faces, top)
     return out
 
 

time: 216 us -> 106 us (0.49)
  waiting for transfers between devices: 137 us -> 19.1 us
  between operations: 13.5 us -> 0.19 us
  starting transfers between devices: 16.5 us -> 28.5 us
  blocking collectives: 16.5 us -> 23.6 us
  Pallas kernels: 18.3 us -> 23.2 us
  local copies, waits for them, and re-layouts: 12 us -> 9.57 us
    psum x1 -> x0, waiting for transfers between devices: 125 us -> none  [summed(): lax.psum(lax.dynamic_update_slice(zeros, block[None], start), ('gx', 'gy'))]
    ppermute x0 -> x7, starting transfers between devices: none -> 7.9 us  [passed_round(): lax.ppermute(block, axis, [(i, (i + distance) % count) for i in range(cou...]
    all_to_all x1, blocking collectives: 16.5 us -> 23.6 us  [handed_out(): return lax.all_to_all(copies, axis, 0, 0)]
    all_to_all x1 -> x2, waiting for transfers between devices: 0.01 us -> 6.7 us  [handed_out(): return lax.all_to_all(copies, axis, 0, 0)]
    unnamed x18 -> x11, local copies, waits for them, and re-layouts: 10.3 us -> 5.35 us
    pallas_call x5, Pallas kernels: 18.3 us -> 23.2 us  [launch(): pl.pallas_call(kernel, out_shape=[jax.ShapeDtypeStruct(shape, F32) for sh...]
    ppermute x0 -> x7, waiting for transfers between devices: none -> 2.66 us  [passed_round(): lax.ppermute(block, axis, [(i, (i + distance) % count) for i in range(cou...]
    ppermute x4, starting transfers between devices: 10.3 us -> 12.5 us  [from_sides(): return (lax.ppermute(high, axis, up), lax.ppermute(low, axis, down))]
  transfers between devices with their start and end apart: 6 -> 13, of which waited for: 5 -> 6; matrix products, arithmetic and copies ran while one was open for 0% -> 7% of each run, Pallas kernels for 1% -> 5%
where the time goes in v3:
time: 106 us; the launch traced here: 104 us
  starting transfers between devices  28.5 us (27%)
  blocking collectives  23.6 us (22%)
  Pallas kernels  23.2 us (22%)
  waiting for transfers between devices  19.1 us (18%)
  local copies, waits for them, and re-layouts  9.57 us (9%)
    all_to_all x1, blocking collectives, handed_out(): return lax.all_to_all(copies, axis, 0, 0)  23.6 us
    pallas_call x5, Pallas kernels, launch(): pl.pallas_call(kernel, out_shape=[jax.ShapeDtypeStruct(shape, F32) for sh...  23.2 us
    ppermute x4, starting transfers between devices, from_sides(): return (lax.ppermute(high, axis, up), lax.ppermute(low, axis, down))  12.5 us
    ppermute x4, waiting for transfers between devices, from_sides(): return (lax.ppermute(high, axis, up), lax.ppermute(low, axis, down))  9.71 us
    all_to_all x2, starting transfers between devices, handed_out(): return lax.all_to_all(copies, axis, 0, 0)  8.12 us
    ppermute x7, starting transfers between devices, passed_round(): lax.ppermute(block, axis, [(i, (i + distance) % count) for i in range(cou...  7.9 us
    all_to_all x2, waiting for transfers between devices, handed_out(): return lax.all_to_all(copies, axis, 0, 0)  6.7 us
    unnamed x11, local copies, waits for them, and re-layouts  5.35 us
  transfers between devices with their start and end apart: 13, of which 6 were waited for; matrix products, arithmetic and copies ran while one was open for 7% of the time, Pallas kernels for 5%

profile of v3, /device:TPU:1, one launch (start us, length us, event | category | flops | bytes accessed | tf_op | source)
XLA Modules:
  0.0 104.1 jit_solution(13934897335980091091)
XLA Ops:
  0.0 2.2 %shard_map.55 = (f32[5,16,16,128]{3,2,1,0:T(8,128)}, f32[5,4,16,128]{3,2,1,0:T(8,128)}, f32[5,4,16,128]{3,2,1,0:T(8,128)}) custom-call(f32[16,16,128]{2,1,0:T(8,128)} %refs_0_.1, f32[16,16,128]{2,1,0:T(8,128)} %refs_1_.1, f32[16,16,128]{2,1,0:T(8,128)} %refs_2_.1, f32[16,16,128]{2,1,0:T(8,128)} %refs_3_.1, f32[16,16,128]{2,1,0:T(8,128)} %refs_4_.1), custom_call_target="tpu_custom_call" | custom-call | tf_op jit(solution)/shard_map/pallas_call | solution.py:470
  2.2 0.0 copy-start
  2.2 1.1 %copy-done = f32[5,16,16,128]{3,2,1,0:T(8,128)S(1)} copy-done((f32[5,16,16,128]{3,2,1,0:T(8,128)S(1)}, f32[5,16,16,128]{3,2,1,0:T(8,128)}, u32[]{:S(2)}) %copy-start) | copy-done | bytes 655384
  3.3 0.5 shard_map.58
  3.7 5.1 %collective-permute-start.10 = (f32[3,4,8,128]{3,2,1,0:T(8,128)S(1)}, f32[3,4,8,128]{3,2,1,0:T(8,128)S(1)}, u32[]{:S(2)}, u32[]{:S(2)}) collective-permute-start(f32[3,4,8,128]{3,2,1,0:T(8,128)S(1)} %shard_map.58), channel_id=1, source_target_pairs={{0,28},{4,0},{8,4},{12,8},{16,12},{20,16},{24,20},{28,24},{1,29},{... | collective-permute-start | bytes 147464 | tf_op jit(solution)/shard_map/ppermute | solution.py:498
  8.9 0.2 collective-permute-start.9
  9.0 1.3 %collective-permute-start.5 = (f32[3,4,8,128]{3,2,1,0:T(8,128)S(1)}, f32[3,4,8,128]{3,2,1,0:T(8,128)S(1)}, u32[]{:S(2)}, u32[]{:S(2)}) collective-permute-start(f32[3,4,8,128]{3,2,1,0:T(8,128)S(1)} %shard_map.58), channel_id=1, source_target_pairs={{0,8},{4,12},{8,16},{12,20},{16,24},{20,28},{24,0},{28,4},{1,9},{5... | collective-permute-start | bytes 147464 | tf_op jit(solution)/shard_map/ppermute | solution.py:498
  10.3 0.0 collective-permute-start.4
  10.3 3.1 %collective-permute-start = (f32[5,4,16,128]{3,2,1,0:T(8,128)}, f32[5,4,16,128]{3,2,1,0:T(8,128)S(1)}, u32[]{:S(2)}, u32[]{:S(2)}) collective-permute-start(f32[5,4,16,128]{3,2,1,0:T(8,128)} %get-tuple-element.13), channel_id=1, source_target_pairs={{0,4},{4,8},{8,12},{12,16},{16,20},{20,24},{24,28},{1,5},{5,9},{9,... | collective-permute-start | bytes 491528 | tf_op jit(solution)/shard_map/ppermute | solution.py:486
  13.4 2.6 %collective-permute-done.4 = f32[3,4,8,128]{3,2,1,0:T(8,128)S(1)} collective-permute-done((f32[3,4,8,128]{3,2,1,0:T(8,128)S(1)}, f32[3,4,8,128]{3,2,1,0:T(8,128)S(1)}, u32[]{:S(2)}, u32[]{:S(2)}) %collective-permute-start.4) | collective-permute-done | bytes 49184 | tf_op jit(solution)/shard_map/ppermute | solution.py:498
  16.1 1.3 %collective-permute-start.1 = (f32[5,4,16,128]{3,2,1,0:T(8,128)}, f32[5,4,16,128]{3,2,1,0:T(8,128)S(1)}, u32[]{:S(2)}, u32[]{:S(2)}) collective-permute-start(f32[5,4,16,128]{3,2,1,0:T(8,128)} %get-tuple-element.14), channel_id=1, source_target_pairs={{4,0},{8,4},{12,8},{16,12},{20,16},{24,20},{28,24},{5,1},{9,5},{13... | collective-permute-start | bytes 491528 | tf_op jit(solution)/shard_map/ppermute | solution.py:486
  17.4 0.0 collective-permute-done.x_low.refs_1_
  17.4 0.3 collective-permute-start.6
  17.7 5.2 %collective-permute-done.1.x_high.refs_2_ = f32[5,4,16,128]{3,2,1,0:T(8,128)S(1)} collective-permute-done((f32[5,4,16,128]{3,2,1,0:T(8,128)}, f32[5,4,16,128]{3,2,1,0:T(8,128)S(1)}, u32[]{:S(2)}, u32[]{:S(2)}) %collective-permute-start.1) | collective-permute-done | bytes 163872 | tf_op jit(solution)/shard_map/ppermute | solution.py:486
  22.9 0.1 shard_map.56
  23.0 6.2 %collective-permute-start.2 = (f32[5,24,4,128]{3,2,1,0:T(4,128)S(1)}, f32[5,24,4,128]{3,2,1,0:T(4,128)S(1)}, u32[]{:S(2)}, u32[]{:S(2)}) collective-permute-start(f32[5,24,4,128]{3,2,1,0:T(4,128)S(1)} %get-tuple-element.15), channel_id=1, source_target_pairs={{0,1},{1,2},{2,3},{4,5},{5,6},{6,7},{8,9},{9,10},{10,11},{12,13},{... | collective-permute-start | bytes 737288 | tf_op jit(solution)/shard_map/ppermute | solution.py:486
  29.2 0.0 collective-permute-done.5
  29.2 1.9 %collective-permute-start.3 = (f32[5,24,4,128]{3,2,1,0:T(4,128)S(1)}, f32[5,24,4,128]{3,2,1,0:T(4,128)S(1)}, u32[]{:S(2)}, u32[]{:S(2)}) collective-permute-start(f32[5,24,4,128]{3,2,1,0:T(4,128)S(1)} %get-tuple-element.16), channel_id=1, source_target_pairs={{1,0},{2,1},{3,2},{5,4},{6,5},{7,6},{9,8},{10,9},{11,10},{13,12},{... | collective-permute-start | bytes 737288 | tf_op jit(solution)/shard_map/ppermute | solution.py:486
  31.1 0.0 collective-permute-done.6
  31.1 0.1 collective-permute-start.7
  31.2 0.0 copy-start.1
  31.2 1.1 %collective-permute-done.2.refs_3_ = f32[5,24,4,128]{3,2,1,0:T(4,128)S(1)} collective-permute-done((f32[5,24,4,128]{3,2,1,0:T(4,128)S(1)}, f32[5,24,4,128]{3,2,1,0:T(4,128)S(1)}, u32[]{:S(2)}, u32[]{:S(2)}) %collective-permute-start.2) | collective-permute-done | bytes 245792 | tf_op jit(solution)/shard_map/ppermute | solution.py:486
  32.3 0.9 collective-permute-start.8
  33.2 3.5 %collective-permute-done.3.refs_4_ = f32[5,24,4,128]{3,2,1,0:T(4,128)S(1)} collective-permute-done((f32[5,24,4,128]{3,2,1,0:T(4,128)S(1)}, f32[5,24,4,128]{3,2,1,0:T(4,128)S(1)}, u32[]{:S(2)}, u32[]{:S(2)}) %collective-permute-start.3) | collective-permute-done | bytes 245792 | tf_op jit(solution)/shard_map/ppermute | solution.py:486
  36.7 4.9 %shard_map.57 = (f32[7,24,40,128]{3,2,1,0:T(8,128)S(1)}, f32[4,8,128]{2,1,0:T(8,128)S(1)}) custom-call(f32[5,16,16,128]{3,2,1,0:T(8,128)S(1)} %copy-done, f32[5,4,16,128]{3,2,1,0:T(8,128)S(1)} %collective-permute-done.x_low.refs_1_, f32[5,4,16,128]{3,2,1,0:T(8,128)S(1)} %collective-permute-done.1.x_high.refs_2_, ...), custom_call_target="tpu_custom_call" | custom-call | tf_op jit(solution)/shard_map/pallas_call | solution.py:470
  41.6 0.0 copy-done.1
  41.6 0.7 broadcast_in_dim.9
  42.3 4.0 %all-to-all-start = ((f32[8,4,8,128]{3,2,1,0:T(8,128)}), f32[8,4,8,128]{3,2,1,0:T(8,128)}, u32[]{:S(2)}, u32[]{:S(2)}) async-start(f32[8,4,8,128]{3,2,1,0:T(8,128)} %broadcast_in_dim.9), calls=%async_computation | async-start | bytes 262144 | tf_op jit(solution)/shard_map/all_to_all | solution.py:491
  46.3 0.0 collective-permute-done.7
  46.3 1.4 %bitcast_dynamic-update-slice_fusion.3 = f32[8,3,4,8,128]{4,3,2,1,0:T(8,128)} fusion(f32[8,3,4,8,128]{4,3,2,1,0:T(8,128)} %copy-done.1, f32[3,4,8,128]{3,2,1,0:T(8,128)} %collective-permute-done.7), kind=kLoop, calls=%fused_computation.3 | loop fusion | bytes 98304
  47.7 0.0 collective-permute-done.8
  47.7 1.4 %bitcast_dynamic-update-slice_fusion.2 = f32[8,3,4,8,128]{4,3,2,1,0:T(8,128)} fusion(f32[8,3,4,8,128]{4,3,2,1,0:T(8,128)} %bitcast_dynamic-update-slice_fusion.3, f32[3,4,8,128]{3,2,1,0:T(8,128)} %collective-permute-done.8), kind=kLoop, calls=%fused_computation.2 | loop fusion | bytes 98304
  49.1 3.4 %all-to-all-done = f32[8,4,8,128]{3,2,1,0:T(8,128)} async-done(((f32[8,4,8,128]{3,2,1,0:T(8,128)}), f32[8,4,8,128]{3,2,1,0:T(8,128)}, u32[]{:S(2)}, u32[]{:S(2)}) %all-to-all-start) | async-done | bytes 131104 | tf_op jit(solution)/shard_map/all_to_all | solution.py:491
  52.5 1.8 %broadcast_in_dim.10 = f32[4,8,4,8,128]{4,3,2,1,0:T(8,128)} broadcast(f32[8,4,8,128]{3,2,1,0:T(8,128)} %all-to-all-done), dimensions={1,2,3,4} | broadcast | bytes 655360 | tf_op jit(solution)/shard_map/broadcast_in_dim | solution.py:490
  54.3 4.1 %all-to-all-start.1 = ((f32[4,8,4,8,128]{4,3,2,1,0:T(8,128)}), f32[4,8,4,8,128]{4,3,2,1,0:T(8,128)}, u32[]{:S(2)}, u32[]{:S(2)}) async-start(f32[4,8,4,8,128]{4,3,2,1,0:T(8,128)} %broadcast_in_dim.10), calls=%async_computation.1 | async-start | bytes 1048576 | tf_op jit(solution)/shard_map/all_to_all | solution.py:491
  58.4 0.0 collective-permute-done.9
  58.4 1.4 %bitcast_dynamic-update-slice_fusion.1 = f32[8,3,4,8,128]{4,3,2,1,0:T(8,128)} fusion(f32[8,3,4,8,128]{4,3,2,1,0:T(8,128)} %bitcast_dynamic-update-slice_fusion.2, f32[3,4,8,128]{3,2,1,0:T(8,128)} %collective-permute-done.9), kind=kLoop, calls=%fused_computation.1 | loop fusion | bytes 98304
  59.8 0.0 collective-permute-done.10
  59.8 0.6 bitcast_dynamic-update-slice_fusion
  60.5 3.3 %all-to-all-done.1.sources = f32[4,8,4,8,128]{4,3,2,1,0:T(8,128)} async-done(((f32[4,8,4,8,128]{4,3,2,1,0:T(8,128)}), f32[4,8,4,8,128]{4,3,2,1,0:T(8,128)}, u32[]{:S(2)}, u32[]{:S(2)}) %all-to-all-start.1) | async-done | bytes 524320 | tf_op jit(solution)/shard_map/all_to_all | solution.py:491
  63.8 1.2 %broadcast_in_dim.11 = f32[4,8,3,4,8,128]{5,4,3,2,1,0:T(8,128)S(1)} broadcast(f32[8,3,4,8,128]{4,3,2,1,0:T(8,128)} %bitcast_dynamic-update-slice_fusion), dimensions={1,2,3,4,5} | broadcast | bytes 1966080 | tf_op jit(solution)/shard_map/broadcast_in_dim | solution.py:490
  65.0 23.6 %all_to_all.15.faces = f32[4,8,3,4,8,128]{5,4,3,2,1,0:T(8,128)S(1)} all-to-all(f32[4,8,3,4,8,128]{5,4,3,2,1,0:T(8,128)S(1)} %broadcast_in_dim.11), channel_id=1, replica_groups=mesh['gx'=8,'gy'=4] {'gy'}, dimensions={0} | all-to-all | bytes 3145728 | tf_op jit(solution)/shard_map/all_to_all | solution.py:491
  88.6 15.6 %shard_map.59 = f32[16,16,128]{2,1,0:T(8,128)} custom-call(f32[4,8,4,8,128]{4,3,2,1,0:T(8,128)} %all-to-all-done.1.sources, f32[4,8,3,4,8,128]{5,4,3,2,1,0:T(8,128)S(1)} %all_to_all.15.faces, f32[7,24,40,128]{3,2,1,0:T(8,128)S(1)} %get-tuple-element.18.stored), custom_call_target="tpu_custom_call" | custom-call | tf_op jit(solution)/shard_map/pallas_call | solution.py:470
  (4 shorter events, 0.0 us)
Async XLA Ops:
  2.2 1.1 %copy-start = (f32[5,16,16,128]{3,2,1,0:T(8,128)S(1)}, f32[5,16,16,128]{3,2,1,0:T(8,128)}, u32[]{:S(2)}) copy-start(f32[5,16,16,128]{3,2,1,0:T(8,128)} %get-tuple-element.12.own.refs_0_) | copy-start | bytes 1966084
  3.7 56.1 %collective-permute-start.10 = (f32[3,4,8,128]{3,2,1,0:T(8,128)S(1)}, f32[3,4,8,128]{3,2,1,0:T(8,128)S(1)}, u32[]{:S(2)}, u32[]{:S(2)}) collective-permute-start(f32[3,4,8,128]{3,2,1,0:T(8,128)S(1)} %shard_map.58), channel_id=1, source_target_pairs={{0,28},{4,0},{8,4},{12,8},{16,12},{20,16},{24,20},{28,24},{1,29},{... | collective-permute-start | bytes 147464 | tf_op jit(solution)/shard_map/ppermute | solution.py:498
  8.9 49.5 %collective-permute-start.9 = (f32[3,4,8,128]{3,2,1,0:T(8,128)S(1)}, f32[3,4,8,128]{3,2,1,0:T(8,128)}, u32[]{:S(2)}, u32[]{:S(2)}) collective-permute-start(f32[3,4,8,128]{3,2,1,0:T(8,128)S(1)} %shard_map.58), channel_id=1, source_target_pairs={{0,24},{4,28},{8,0},{12,4},{16,8},{20,12},{24,16},{28,20},{1,25},{... | collective-permute-start | bytes 147464 | tf_op jit(solution)/shard_map/ppermute | solution.py:498
  9.0 20.1 %collective-permute-start.5 = (f32[3,4,8,128]{3,2,1,0:T(8,128)S(1)}, f32[3,4,8,128]{3,2,1,0:T(8,128)S(1)}, u32[]{:S(2)}, u32[]{:S(2)}) collective-permute-start(f32[3,4,8,128]{3,2,1,0:T(8,128)S(1)} %shard_map.58), channel_id=1, source_target_pairs={{0,8},{4,12},{8,16},{12,20},{16,24},{20,28},{24,0},{28,4},{1,9},{5... | collective-permute-start | bytes 147464 | tf_op jit(solution)/shard_map/ppermute | solution.py:498
  10.3 5.7 %collective-permute-start.4 = (f32[3,4,8,128]{3,2,1,0:T(8,128)S(1)}, f32[3,4,8,128]{3,2,1,0:T(8,128)S(1)}, u32[]{:S(2)}, u32[]{:S(2)}) collective-permute-start(f32[3,4,8,128]{3,2,1,0:T(8,128)S(1)} %shard_map.58), channel_id=1, source_target_pairs={{0,4},{4,8},{8,12},{12,16},{16,20},{20,24},{24,28},{28,0},{1,5},{5... | collective-permute-start | bytes 147464 | tf_op jit(solution)/shard_map/ppermute | solution.py:498
  10.3 7.1 %collective-permute-start = (f32[5,4,16,128]{3,2,1,0:T(8,128)}, f32[5,4,16,128]{3,2,1,0:T(8,128)S(1)}, u32[]{:S(2)}, u32[]{:S(2)}) collective-permute-start(f32[5,4,16,128]{3,2,1,0:T(8,128)} %get-tuple-element.13), channel_id=1, source_target_pairs={{0,4},{4,8},{8,12},{12,16},{16,20},{20,24},{24,28},{1,5},{5,9},{9,... | collective-permute-start | bytes 491528 | tf_op jit(solution)/shard_map/ppermute | solution.py:486
  16.1 6.8 %collective-permute-start.1 = (f32[5,4,16,128]{3,2,1,0:T(8,128)}, f32[5,4,16,128]{3,2,1,0:T(8,128)S(1)}, u32[]{:S(2)}, u32[]{:S(2)}) collective-permute-start(f32[5,4,16,128]{3,2,1,0:T(8,128)} %get-tuple-element.14), channel_id=1, source_target_pairs={{4,0},{8,4},{12,8},{16,12},{20,16},{24,20},{28,24},{5,1},{9,5},{13... | collective-permute-start | bytes 491528 | tf_op jit(solution)/shard_map/ppermute | solution.py:486
  17.4 13.7 %collective-permute-start.6 = (f32[3,4,8,128]{3,2,1,0:T(8,128)S(1)}, f32[3,4,8,128]{3,2,1,0:T(8,128)S(1)}, u32[]{:S(2)}, u32[]{:S(2)}) collective-permute-start(f32[3,4,8,128]{3,2,1,0:T(8,128)S(1)} %shard_map.58), channel_id=1, source_target_pairs={{0,12},{4,16},{8,20},{12,24},{16,28},{20,0},{24,4},{28,8},{1,13},{... | collective-permute-start | bytes 147464 | tf_op jit(solution)/shard_map/ppermute | solution.py:498
  23.0 9.3 %collective-permute-start.2 = (f32[5,24,4,128]{3,2,1,0:T(4,128)S(1)}, f32[5,24,4,128]{3,2,1,0:T(4,128)S(1)}, u32[]{:S(2)}, u32[]{:S(2)}) collective-permute-start(f32[5,24,4,128]{3,2,1,0:T(4,128)S(1)} %get-tuple-element.15), channel_id=1, source_target_pairs={{0,1},{1,2},{2,3},{4,5},{5,6},{6,7},{8,9},{9,10},{10,11},{12,13},{... | collective-permute-start | bytes 737288 | tf_op jit(solution)/shard_map/ppermute | solution.py:486
  29.2 7.5 %collective-permute-start.3 = (f32[5,24,4,128]{3,2,1,0:T(4,128)S(1)}, f32[5,24,4,128]{3,2,1,0:T(4,128)S(1)}, u32[]{:S(2)}, u32[]{:S(2)}) collective-permute-start(f32[5,24,4,128]{3,2,1,0:T(4,128)S(1)} %get-tuple-element.16), channel_id=1, source_target_pairs={{1,0},{2,1},{3,2},{5,4},{6,5},{7,6},{9,8},{10,9},{11,10},{13,12},{... | collective-permute-start | bytes 737288 | tf_op jit(solution)/shard_map/ppermute | solution.py:486
  31.1 15.2 %collective-permute-start.7 = (f32[3,4,8,128]{3,2,1,0:T(8,128)S(1)}, f32[3,4,8,128]{3,2,1,0:T(8,128)}, u32[]{:S(2)}, u32[]{:S(2)}) collective-permute-start(f32[3,4,8,128]{3,2,1,0:T(8,128)S(1)} %shard_map.58), channel_id=1, source_target_pairs={{0,16},{4,20},{8,24},{12,28},{16,0},{20,4},{24,8},{28,12},{1,17},{... | collective-permute-start | bytes 147464 | tf_op jit(solution)/shard_map/ppermute | solution.py:498
  31.2 10.4 %copy-start.1 = (f32[8,3,4,8,128]{4,3,2,1,0:T(8,128)}, f32[8,3,4,8,128]{4,3,2,1,0:T(8,128)S(1)}, u32[]{:S(2)}) copy-start(f32[8,3,4,8,128]{4,3,2,1,0:T(8,128)S(1)} %bitcast_dynamic-update-slice_fusion.4) | copy-start | bytes 1179652
  32.3 15.4 %collective-permute-start.8 = (f32[3,4,8,128]{3,2,1,0:T(8,128)S(1)}, f32[3,4,8,128]{3,2,1,0:T(8,128)}, u32[]{:S(2)}, u32[]{:S(2)}) collective-permute-start(f32[3,4,8,128]{3,2,1,0:T(8,128)S(1)} %shard_map.58), channel_id=1, source_target_pairs={{0,20},{4,24},{8,28},{12,0},{16,4},{20,8},{24,12},{28,16},{1,21},{... | collective-permute-start | bytes 147464 | tf_op jit(solution)/shard_map/ppermute | solution.py:498
  42.3 10.2 %all-to-all-start = ((f32[8,4,8,128]{3,2,1,0:T(8,128)}), f32[8,4,8,128]{3,2,1,0:T(8,128)}, u32[]{:S(2)}, u32[]{:S(2)}) async-start(f32[8,4,8,128]{3,2,1,0:T(8,128)} %broadcast_in_dim.9), calls=%async_computation | async-start | bytes 262144 | tf_op jit(solution)/shard_map/all_to_all | solution.py:491
  54.3 9.5 %all-to-all-start.1 = ((f32[4,8,4,8,128]{4,3,2,1,0:T(8,128)}), f32[4,8,4,8,128]{4,3,2,1,0:T(8,128)}, u32[]{:S(2)}, u32[]{:S(2)}) async-start(f32[4,8,4,8,128]{4,3,2,1,0:T(8,128)} %broadcast_in_dim.10), calls=%async_computation.1 | async-start | bytes 1048576 | tf_op jit(solution)/shard_map/all_to_all | solution.py:491

commit v4 on v3

--- a/solution.py
+++ b/solution.py
@@ -72,26 +72,69 @@
     return ref[:, pl.ds(1, rows // 2, stride=2), :]
 
 
-def pack_x(*refs):
-    fields, (own, low, high, done) = refs[:5], refs[5:]
+HALF = LANES // 2
+
+
+def low_half(values):
+    return jnp.where(lanes_of(values.shape) < HALF, values, 0.0)
+
+
+def two_in_one(first, second):
+    return first + roll_lanes(second, HALF)
+
+
+def one_of_two(values):
+    return low_half(values), low_half(roll_lanes(values, HALF))
+
+
+def x_rows(nx, ny):
+    return 5 * RIM * ny, 3 * RIM // 2 * (ny // 2)
+
+
+def y_rows(nx, ny):
+    return 5 * (nx + 2 * RIM) * RIM, 3 * (nx // 2 + 2 * RIM) // 2 * RIM
+
+
+def start_pack(*refs):
+    fields, (x_low, x_high, y_low, y_high, faces, own, tmp, done) = refs[:5], refs[5:]
     copies = [pltpu.make_async_copy(ref, own.at[index], done.at[index]) for index, ref in enumerate(fields)]
     for copy in copies:
         copy.start()
-    nx = own.shape[1]
+    nx, ny = own.shape[1:3]
     for index, copy in enumerate(copies):
         copy.wait()
-        low[index] = own[index, :RIM]
-        high[index] = own[index, nx - RIM :]
-
-
-def pack_y(own, x_low, x_high, low, high):
-    count, nx, ny = own.shape[:3]
-    for index in range(count):
-        for out, start in ((low, 0), (high, ny - RIM)):
-            rows = slice(start, start + RIM)
-            out[index, :RIM] = x_low[index, :, rows]
-            out[index, RIM : RIM + nx] = own[index, :, rows]
-            out[index, RIM + nx :] = x_high[index, :, rows]
+        for layer in range(RIM):
+            rows = pl.ds((index * RIM + layer) * ny, ny)
+            x_low[rows] = own[index, layer]
+            x_high[rows] = own[index, nx - RIM + layer]
+        for slab in range(nx):
+            rows = pl.ds((index * nx + slab) * RIM, RIM)
+            y_low[rows] = own[index, slab, :RIM]
+            y_high[rows] = own[index, slab, ny - RIM :]
+    fx, fy, fz = own.at[2], own.at[3], own.at[4]
+    halve = compact(LANES, 0)
+
+    def stored(index, values, matrix):
+        count, rows, _ = values.shape
+        flat = exact_dot(values.reshape(count * rows, LANES), matrix)
+        faces[index] = 0.25 * flat.reshape(count, rows, LANES)
+
+    tmp[...] = pair_slabs(fx)[0]
+    stored(0, even_rows(tmp, ny) + odd_rows(tmp, ny), halve)
+    first, second = pair_slabs(fy)
+    tmp[...] = first + second
+    stored(1, even_rows(tmp, ny), halve)
+    first, second = pair_slabs(fz)
+    tmp[...] = first + second
+    stored(2, even_rows(tmp, ny) + odd_rows(tmp, ny), compact(LANES, 0, True))
+    base = x_rows(nx, ny)[0]
+    coarse_rows = ny // 2
+    for face in range(3):
+        for layer in range(RIM // 2):
+            rows = pl.ds(base + (face * (RIM // 2) + layer) * coarse_rows, coarse_rows)
+            top = nx // 2 - RIM + layer
+            x_low[rows] = two_in_one(faces[face, layer], faces[face, layer + RIM // 2])
+            x_high[rows] = two_in_one(faces[face, top], faces[face, top + RIM // 2])
 
 
 def pair_slabs(ref):
@@ -100,17 +143,75 @@
     return values[:, 0], values[:, 1]
 
 
-def coarse_faces(own, out, tmp):
-    fx, fy, fz = own.at[2], own.at[3], own.at[4]
-    rows = fx.shape[1]
+def wide_slab(slab, from_low, own, from_high):
+    count = own.shape[0]
+    if slab < RIM:
+        return from_low(slab)
+    if slab < RIM + count:
+        return own[slab - RIM]
+    return from_high(slab - RIM - count)
+
+
+def rim_slab(ref, base, rows, layer):
+    place = pl.ds(base + layer % (RIM // 2) * rows, rows)
+    return one_of_two(ref[place])[layer // (RIM // 2)]
+
+
+def pack_y(faces, y_own_low, y_own_high, x_low, x_high, low, high):
+    coarse_x, coarse_y = faces.shape[1:3]
+    nx, ny = 2 * coarse_x, 2 * coarse_y
+    for out, own, start in ((low, y_own_low, 0), (high, y_own_high, ny - RIM)):
+        for index in range(5):
+            base = index * (nx + 2 * RIM) * RIM
+            out[pl.ds(base + RIM * RIM, nx * RIM)] = own[pl.ds(index * nx * RIM, nx * RIM)]
+            for layer in range(RIM):
+                rows = pl.ds((index * RIM + layer) * ny + start, RIM)
+                out[pl.ds(base + layer * RIM, RIM)] = x_low[rows]
+                out[pl.ds(base + (RIM + nx + layer) * RIM, RIM)] = x_high[rows]
+    base_x, base_y = x_rows(nx, ny)[0], y_rows(nx, ny)[0]
+    half = (coarse_x + 2 * RIM) // 2
+    for face in range(3):
+        place = base_x + face * (RIM // 2) * coarse_y
+        slabs = [
+            wide_slab(
+                slab,
+                lambda layer: rim_slab(x_low, place, coarse_y, layer),
+                faces.at[face],
+                lambda layer: rim_slab(x_high, place, coarse_y, layer),
+            )
+            for slab in range(2 * half)
+        ]
+        for slab in range(half):
+            both = two_in_one(slabs[slab], slabs[slab + half])
+            rows = pl.ds(base_y + (face * half + slab) * RIM, RIM)
+            low[rows] = both[:RIM]
+            high[rows] = both[coarse_y - RIM :]
+
+
+def fold_four(slabs, even_only=False):
+    out = None
+    for part in range(2):
+        term = exact_dot(two_in_one(slabs[part], slabs[2 + part]), compact(HALF, part, even_only))
+        out = term if out is None else out + term
+    return out
+
+
+def coarse_faces(faces, out, tmp):
+    rows = faces.shape[2]
+    coarse = rows // 2
+    fx, fy, fz = faces.at[0], faces.at[1], faces.at[2]
     tmp[...] = pair_slabs(fx)[0]
-    out[0] = 0.25 * merge_lanes(even_rows(tmp, rows) + odd_rows(tmp, rows), LANES)
+    x = even_rows(tmp, rows) + odd_rows(tmp, rows)
     first, second = pair_slabs(fy)
     tmp[...] = first + second
-    out[1] = 0.25 * merge_lanes(even_rows(tmp, rows), LANES)
+    y = even_rows(tmp, rows)
     first, second = pair_slabs(fz)
     tmp[...] = first + second
-    out[2] = 0.25 * merge_lanes(even_rows(tmp, rows) + odd_rows(tmp, rows), LANES, True)
+    z = even_rows(tmp, rows) + odd_rows(tmp, rows)
+    out[...] = jnp.zeros(out.shape, F32)
+    out[:coarse] = 0.25 * fold_four([x[i] for i in range(4)])
+    out[coarse : 2 * coarse] = 0.25 * fold_four([y[i] for i in range(4)])
+    out[2 * coarse : 3 * coarse] = 0.25 * fold_four([z[i] for i in range(4)], True)
 
 
 def weighted(lev, src, slab, start, rows):
@@ -156,55 +257,133 @@
     lax.fori_loop(0, count, step, 0, unroll=unroll)
 
 
+def clear_pads(ref, rows):
+    for start in (0, RIM + rows):
+        ref[:, start : start + RIM] = jnp.zeros((ref.shape[0], RIM, LANES), F32)
+
+
 def level_down(axes, *refs):
-    own, x_low, x_high, y_low, y_high, top, chunk, lev, other, tmp, done = refs
-    nx, ny = own.shape[1:3]
+    fields = refs[:5]
+    faces, coefficients, x_low, x_high, y_low, y_high, top, mid, chunk, v_low, v_high, other, tmp, one, two = refs[5:]
+    nx, ny = fields[0].shape[:2]
     slabs, rows = nx + 2 * RIM, ny + 2 * RIM
     me_x, me_y = lax.axis_index(axes[0]), lax.axis_index(axes[1])
+    inner = pl.ds(2 * RIM, ny)
     for index, slot in enumerate((F, V, FX, FY, ZL)):
-        lev[slot, :, :PAD] = jnp.zeros((slabs, PAD, LANES), F32)
-        lev[slot, :, PAD + rows :] = jnp.zeros((slabs, PAD, LANES), F32)
-        inner = pl.ds(PAD + RIM, ny)
-        lev[slot, :RIM, inner] = x_low[index]
-        lev[slot, RIM : RIM + nx, inner] = own[index]
-        lev[slot, RIM + nx :, inner] = x_high[index]
-        lev[slot, :, PAD : PAD + RIM] = y_low[index]
-        lev[slot, :, PAD + RIM + ny : PAD + rows] = y_high[index]
-    other[:, :PAD] = jnp.zeros((slabs, PAD, LANES), F32)
-    other[:, PAD + rows :] = jnp.zeros((slabs, PAD, LANES), F32)
+        clear_pads(top.at[slot], rows)
+        top[slot, RIM : RIM + nx, inner] = fields[index][...]
+        for layer in range(RIM):
+            place = pl.ds((index * RIM + layer) * ny, ny)
+            top[slot, layer, inner] = x_low[place]
+            top[slot, RIM + nx + layer, inner] = x_high[place]
+        for slab in range(slabs):
+            place = pl.ds((index * slabs + slab) * RIM, RIM)
+            top[slot, slab, RIM : 2 * RIM] = y_low[place]
+            top[slot, slab, 2 * RIM + ny : RIM + rows] = y_high[place]
+    clear_pads(other, rows)
     row_inside = (rows_of((rows, LANES)) >= RIM) | (me_y > 0)
-    main = pl.ds(PAD, rows)
+    main = pl.ds(RIM, rows)
 
     def first(index):
         slab = index + 1
         inside = row_inside & ((slab >= RIM) | (me_x > 0))
-        set_weights(lev, slab, PAD, rows, LANES, inside)
-        other[slab, main] = swept(lev, lev.at[V], slab, PAD, rows)
-
+        set_weights(top, slab, RIM, rows, LANES, inside)
+        other[slab, main] = swept(top, other_v, slab, RIM, rows)
+
+    other_v = top.at[V]
     run(slabs - 2, first, 2)
-    copies = [pltpu.make_async_copy(lev.at[slot], top.at[slot], done.at[slot]) for slot in range(D)]
-    for copy in copies[1:]:
-        copy.start()
 
     def second(index):
         slab = index + 2
-        lev[V, slab, main] = swept(lev, other, slab, PAD, rows)
+        top[V, slab, main] = swept(top, other, slab, RIM, rows)
 
     run(slabs - 4, second, 2)
-    copies[0].start()
 
     def rest(slab):
-        v, total = weighted(lev, lev.at[V], slab, PAD + RIM, ny)
-        return total - lev[D, slab, pl.ds(PAD + RIM, ny)] * v
+        v, total = weighted(top, top.at[V], slab, 2 * RIM, ny)
+        return total - top[D, slab, inner] * v
 
     def residual(index):
         slab = RIM + 2 * index
         tmp[index] = rest(slab) + rest(slab + 1)
 
     run(nx // 2, residual, 2)
-    chunk[...] = 0.5 * merge_lanes(even_rows(tmp, ny) + odd_rows(tmp, ny), LANES)
-    for copy in copies:
-        copy.wait()
+
+    coarse_x, coarse_y = nx // 2, ny // 2
+    slabs, rows = coarse_x + 2 * RIM, coarse_y + 2 * RIM
+    half = slabs // 2
+    inner = pl.ds(2 * RIM, coarse_y)
+    main = pl.ds(RIM, rows)
+    base_x, base_y = x_rows(nx, ny)[0], y_rows(nx, ny)[0]
+    for face, slot in enumerate((FX, FY, ZL)):
+        clear_pads(mid.at[slot], rows)
+        mid[slot, RIM : RIM + coarse_x, inner] = faces[face]
+        place = base_x + face * (RIM // 2) * coarse_y
+        for layer in range(RIM):
+            mid[slot, layer, inner] = rim_slab(x_low, place, coarse_y, layer)
+            mid[slot, RIM + coarse_x + layer, inner] = rim_slab(x_high, place, coarse_y, layer)
+        for slab in range(half):
+            place = pl.ds(base_y + (face * half + slab) * RIM, RIM)
+            for message, row in ((y_low, RIM), (y_high, 2 * RIM + coarse_y)):
+                pair = one_of_two(message[place])
+                mid[slot, slab, row : row + RIM] = pair[0]
+                mid[slot, slab + half, row : row + RIM] = pair[1]
+    row_inside = (rows_of((rows, LANES)) >= RIM) | (me_y > 0)
+    for slab in range(slabs - 1):
+        inside = row_inside & (me_x > 0) if slab < RIM else row_inside
+        set_weights(mid, slab, RIM, rows, HALF, inside)
+
+    source = even_rows(tmp, ny) + odd_rows(tmp, ny)
+    source = 0.5 * exact_dot(source.reshape(coarse_x * coarse_y, LANES), compact(LANES, 0))
+    for ref in (mid.at[F], mid.at[V], one):
+        ref[...] = jnp.zeros(ref.shape, F32)
+    mid[F, RIM : RIM + coarse_x, inner] = source.reshape(coarse_x, coarse_y, LANES)
+    for slab in range(RIM, RIM + coarse_x):
+        mid[V, slab, inner] = mid[W, slab, inner] * mid[F, slab, inner]
+    for layer in range(RIM // 2):
+        near, far = RIM + layer, coarse_x + layer
+        v_low[layer * coarse_y : (layer + 1) * coarse_y] = two_in_one(
+            mid[V, near, inner], mid[V, near + RIM // 2, inner]
+        )
+        v_high[layer * coarse_y : (layer + 1) * coarse_y] = two_in_one(
+            mid[V, far, inner], mid[V, far + RIM // 2, inner]
+        )
+    for slab in range(RIM - 1, RIM + coarse_x + 1):
+        one[slab, main] = swept(mid, mid.at[V], slab, RIM, rows)
+
+    def rest_1(slab):
+        v, total = weighted(mid, one, slab, RIM, rows)
+        return total - mid[D, slab, main] * v
+
+    two[...] = jnp.zeros(two.shape, F32)
+    for pair in range(1, half - 1):
+        two[pair] = rest_1(2 * pair) + rest_1(2 * pair + 1)
+    pieces = even_rows(two, rows) + odd_rows(two, rows)
+    for part in range(half // 4):
+        folded = fold_four([pieces[4 * part + i] for i in range(4)])
+        chunk[part * rows // 2 : (part + 1) * rows // 2] = 0.5 * folded
+    chunk[half // 4 * rows // 2 :] = coefficients[...]
+
+
+def pack_v(mid_v, x_low, x_high, low, high):
+    slabs = mid_v.shape[1]
+    coarse_x = slabs - 2 * RIM
+    coarse_y = mid_v.shape[2] - 4 * RIM
+    half = slabs // 2
+    own = mid_v[V, RIM : RIM + coarse_x, 2 * RIM : 2 * RIM + coarse_y]
+    values = [
+        wide_slab(
+            slab,
+            lambda layer: rim_slab(x_low, 0, coarse_y, layer),
+            own,
+            lambda layer: rim_slab(x_high, 0, coarse_y, layer),
+        )
+        for slab in range(slabs)
+    ]
+    for slab in range(half):
+        both = two_in_one(values[slab], values[slab + half])
+        low[slab * RIM : (slab + 1) * RIM] = both[:RIM]
+        high[slab * RIM : (slab + 1) * RIM] = both[coarse_y - RIM :]
 
 
 def pair_rows(values, stride):
@@ -306,157 +485,153 @@
     return level.sweep(level.sweep(v, f), f)
 
 
-def wrap_slabs(ref, count, depth, main):
-    first, last = ref[1, main], ref[count, main]
-    lane = lanes_of(first.shape)
-    ref[0, main] = jnp.where(lane < depth, 0.0, roll_lanes(last, depth))
-    ref[count + 1, main] = jnp.where(lane >= LANES - depth, 0.0, roll_lanes(first, -depth))
-
-
-def level_up(axes, grid, sweeps, sources, faces, stored, out, lev, top, post, tmp, up, done):
+def level_up(axes, grid, sweeps, pieces, top, mid, x_low, x_high, y_low, y_high, out, wide, one, two, tall, post, up):
     devices_x, devices_y = grid
-    fetch = pltpu.make_async_copy(stored, top, done.at[0])
-    fetch.start()
     me_x, me_y = lax.axis_index(axes[0]), lax.axis_index(axes[1])
-    depth = LANES // 2
-    count = lev.shape[1] - 2
-    rows = lev.shape[2] - 2 * PAD
+    coarse_x, coarse_y = mid.shape[1] - 2 * RIM, mid.shape[2] - 4 * RIM
+    own_x, own_y = coarse_x // 2, coarse_y // 2
+    quarter = LANES // 4
+    reach = RIM // 2
+    blocks = 4
+    count = devices_x * own_x // blocks
+    rows = devices_y * own_y
     main = pl.ds(PAD, rows)
-    parts = sources.shape[2]
-    low_lanes = lanes_of((PAD, LANES)) < depth
-    for slot in (V, U, FY):
-        for start in (0, PAD + rows):
-            lev[slot, :, start : start + PAD] = jnp.zeros((count + 2, PAD, LANES), F32)
-
-    def unpack(index):
-        for y in range(devices_y):
-            here = pl.ds(PAD + y * PAD, PAD)
-            near, far = index, index + devices_x // 2
-
-            def place(slot, part, a, b):
-                slab = 1 + index * 2 * parts + part
-                lev[slot, slab, here] = jnp.where(low_lanes, a, roll_lanes(b, depth))
-                lev[slot, slab + parts, here] = jnp.where(low_lanes, roll_lanes(a, depth), b)
-
-            for part in range(parts):
-                place(F, part, sources[y, near, part], sources[y, far, part])
-                a = (me_x - near + devices_x) % devices_x
-                b = (me_x - far + devices_x) % devices_x
-                for face, slot in enumerate((FX, FY, ZL)):
-                    place(slot, part, faces[y, a, face, part], faces[y, b, face, part])
-
-    run(devices_x // 2, unpack)
-    wrap_slabs(lev.at[FX], count, depth, main)
-
-    half = count // 2
-
-    def pairs(slot, combine):
-        def pair(index):
-            tmp[index] = combine(lev[slot, 1 + 2 * index, main], lev[slot, 2 + 2 * index, main])
-
-        run(half, pair, 2)
-
-    def slabs_of(values):
-        return [values[s] for s in range(half // 2)]
-
-    pairs(FX, lambda a, b: a)
-    fx = 0.25 * merge_lanes(even_rows(tmp, rows) + odd_rows(tmp, rows), depth)
-    pairs(FY, lambda a, b: a + b)
-    fy = 0.25 * merge_lanes(even_rows(tmp, rows), depth)
-    pairs(ZL, lambda a, b: a + b)
-    fz = 0.25 * merge_lanes(even_rows(tmp, rows) + odd_rows(tmp, rows), depth, True)
-    levels = [Listed(slabs_of(fx), slabs_of(fy), slabs_of(fz), 1, depth // 2)]
+    window = own_y + RIM
+
+    def piece(gx, gy):
+        slow = (me_x // 2 - gx // 2 + devices_x // 2) % (devices_x // 2)
+        far = (me_y // 2 - gy // 2 + devices_y // 2) % (devices_y // 2)
+        return ((me_y + gy) % 2, far, (me_x + gx) % 2, slow)
+
+    for ref in (wide, tall):
+        ref[...] = jnp.zeros(ref.shape, F32)
+    lane = lanes_of((window, LANES))
+    for gy in range(devices_y):
+        sums = [None] * count
+        for gx in range(devices_x):
+            where = piece(gx, gy)
+            layers = [pieces[where + (pl.ds(part * window, window),)] for part in range(2)]
+            for local in range(1, 2 * blocks - 1):
+                x = own_x * gx - reach + local
+                if not 0 <= x < devices_x * own_x:
+                    continue
+                block, slab = x // count, x % count
+                moved = roll_lanes(layers[local // blocks], (block - local % blocks) * quarter)
+                moved = jnp.where(lane // quarter == block, moved, 0.0)
+                sums[slab] = moved if sums[slab] is None else sums[slab] + moved
+        place = pl.ds(PAD + own_y * gy - reach, window)
+        for slab in range(count):
+            tall[slab, place] = tall[slab, place] + sums[slab]
+    f = [tall[slab, main] for slab in range(count)]
+
+    lane = lanes_of((rows, LANES))
+    for gx in range(devices_x):
+        for gy in range(devices_y):
+            where = piece(gx, gy)
+            for face in range(3):
+                values = pieces[where + (pl.ds(2 * window + face * own_y, own_y),)]
+                wide[face, gx, gy * own_y : (gy + 1) * own_y] = values
+    faces = []
+    for face in range(3):
+        slabs = [None] * count
+        for gx in range(devices_x):
+            values = wide[face, gx]
+            for local in range(own_x):
+                x = own_x * gx + local
+                block, slab = x // count, x % count
+                moved = roll_lanes(values, (block - local) * quarter)
+                moved = jnp.where(lane // quarter == block, moved, 0.0)
+                slabs[slab] = moved if slabs[slab] is None else slabs[slab] + moved
+        faces.append(slabs)
+    levels = [Listed(*faces, 1, quarter)]
     while len(levels) < LEVELS - 2:
         levels.append(levels[-1].coarser())
-
-    def first(index):
-        slab = index + 1
-        set_weights(lev, slab, PAD, rows, depth)
-        lev[V, slab, main] = lev[W, slab, main] * lev[F, slab, main]
-
-    run(count, first, 2)
-    wrap_slabs(lev.at[V], count, depth, main)
-
-    def second(index):
-        slab = index + 1
-        lev[U, slab, main] = swept(lev, lev.at[V], slab, PAD, rows)
-
-    run(count, second, 2)
-    wrap_slabs(lev.at[U], count, depth, main)
-
-    def rest(slab):
-        v, total = weighted(lev, lev.at[U], slab, PAD, rows)
-        return total - lev[D, slab, main] * v
-
-    def residual(index):
-        tmp[index] = rest(1 + 2 * index) + rest(2 + 2 * index)
-
-    run(half, residual)
-    coarse = 0.5 * merge_lanes(even_rows(tmp, rows) + odd_rows(tmp, rows), depth)
-    e = listed_cycle(levels, sweeps, slabs_of(coarse))
-
-    flat = jnp.stack(e).reshape(half // 2 * rows // 2, LANES)
-    for part in range(2):
-        fine = exact_dot(flat, expand(depth, part)).reshape(half // 2, rows // 2, LANES)
-        for odd in range(2):
-            tmp[part * half // 2 : (part + 1) * half // 2, pl.ds(odd, rows // 2, stride=2), :] = fine
-
-    def correct(index):
-        for slab in (1 + 2 * index, 2 + 2 * index):
-            lev[U, slab, main] = lev[U, slab, main] + tmp[index]
-
-    run(half, correct, 2)
-    wrap_slabs(lev.at[U], count, depth, main)
-
-    near = 2 * parts
-    base = me_x % (devices_x // 2) * near
-
-    def third(index):
-        slab = (base + index - 2 + count) % count + 1
-        lev[V, slab, main] = swept(lev, lev.at[U], slab, PAD, rows)
-
-    run(near + 4, third, 2)
-    wrap_slabs(lev.at[V], count, depth, main)
-
-    def fourth(index):
-        slab = (base + index - 1 + count) % count + 1
-        lev[U, slab, main] = swept(lev, lev.at[V], slab, PAD, rows)
-
-    run(near + 2, fourth, 2)
-    wrap_slabs(lev.at[U], count, depth, main)
-
-    slabs = near + 2
+    e = listed_cycle(levels, sweeps, f)
+
+    slabs, high = coarse_x + 2 * RIM, coarse_y + 2 * RIM
+    half = slabs // 2
+    inner = pl.ds(2 * RIM, coarse_y)
+    body = pl.ds(RIM, high)
+    one[...] = mid[V]
+    clear_pads(two, high)
+    for layer in range(RIM):
+        one[layer, inner] = rim_slab(x_low, 0, coarse_y, layer)
+        one[RIM + coarse_x + layer, inner] = rim_slab(x_high, 0, coarse_y, layer)
+    for slab in range(half):
+        place = pl.ds(slab * RIM, RIM)
+        for message, row in ((y_low, RIM), (y_high, 2 * RIM + coarse_y)):
+            pair = one_of_two(message[place])
+            one[slab, row : row + RIM] = pair[0]
+            one[slab + half, row : row + RIM] = pair[1]
+    row = rows_of((high, LANES))
+    own_row = (row >= RIM) & (row < RIM + coarse_y)
+    for slab in range(1, slabs - 1):
+        f_rim = one[slab, body] * mid[D, slab, body] * (1.0 / OMEGA)
+        if RIM <= slab < RIM + coarse_x:
+            f_rim = jnp.where(own_row, mid[F, slab, body], f_rim)
+        mid[F, slab, body] = f_rim
+        two[slab, body] = swept(mid, one, slab, RIM, high)
+
+    extra = reach
+    tall[:, :PAD] = jnp.zeros((count + 2 * extra, PAD, LANES), F32)
+    tall[:, PAD + rows :] = jnp.zeros((count + 2 * extra, PAD, LANES), F32)
+    for slab in range(count):
+        tall[extra + slab, main] = e[slab]
+    for slab in range(extra):
+        tall[slab, main] = jnp.where(lane < quarter, 0.0, roll_lanes(e[count - extra + slab], quarter))
+        tall[extra + count + slab, main] = jnp.where(
+            lane >= LANES - quarter, 0.0, roll_lanes(e[slab], -quarter)
+        )
+    per_block = count // own_x
+    base = me_x % per_block * own_x
+    mine = None
+    for gy in range(devices_y):
+        place = pl.ds(PAD + gy * own_y - reach, window)
+        values = tall[pl.ds(base, half), place, :]
+        values = jnp.where(me_y == gy, values, 0.0)
+        mine = values if mine is None else mine + values
+    source = lax.broadcasted_iota(jnp.int32, (LANES, LANES), 0)
+    target = lax.broadcasted_iota(jnp.int32, (LANES, LANES), 1)
+    hit = (source == me_x // per_block * quarter + target // 2) & (target < HALF)
+    fine = exact_dot(mine.reshape(half * window, LANES), jnp.where(hit, 1.0, 0.0).astype(F32))
+    fine = fine.reshape(half, window, LANES)
+    for odd in range(2):
+        up[:half, pl.ds(odd, window, stride=2), :] = fine
+    for pair in range(half):
+        for slab in (2 * pair, 2 * pair + 1):
+            if 1 <= slab < slabs - 1:
+                two[slab, body] = two[slab, body] + up[pair, :high]
+    for slab in range(2, slabs - 2):
+        one[slab, body] = swept(mid, two, slab, RIM, high)
+    for slab in range(3, slabs - 3):
+        two[slab, body] = swept(mid, one, slab, RIM, high)
+
     nx, ny = out.shape[:2]
+    steps = coarse_x + 2
     fine_rows = ny + 2 * RIM
-    window = ny // 2 + 2 * PAD
-    top_row = pl.multiple_of(me_y * (ny // 2), PAD)
-    e = lev[U, pl.ds(base, slabs), pl.ds(top_row, window), :]
-    side = me_x // (devices_x // 2)
-    fine = exact_dot(e.reshape(slabs * window, LANES), expand(LANES, side)).reshape(slabs, window, LANES)
-    skip = PAD - RIM // 2
-    fine = fine[:, skip : skip + fine_rows // 2]
+    e = two[RIM - 1 : RIM - 1 + steps, body]
+    fine = exact_dot(e.reshape(steps * high, LANES), expand(LANES, 0)).reshape(steps, high, LANES)
+    fine = fine[:, reach : reach + fine_rows // 2]
     for odd in range(2):
         up[:, pl.ds(odd, fine_rows // 2, stride=2), :] = fine
-    body = pl.ds(PAD, fine_rows)
-    fetch.wait()
+    body = pl.ds(RIM, fine_rows)
     for slot in (0, 1):
-        for start in (0, PAD + fine_rows):
-            post[slot, :, start : start + PAD] = jnp.zeros((post.shape[1], PAD, LANES), F32)
+        clear_pads(post.at[slot], fine_rows)
 
     def raise_level(index):
         for slab in (RIM - 2 + 2 * index, RIM - 1 + 2 * index):
             post[0, slab, body] = top[V, slab, body] + up[index]
 
-    run(slabs, raise_level, 2)
+    run(steps, raise_level, 2)
 
     def fifth(index):
         slab = RIM - 1 + index
-        post[1, slab, body] = swept(top, post.at[0], slab, PAD, fine_rows)
+        post[1, slab, body] = swept(top, post.at[0], slab, RIM, fine_rows)
 
     run(nx + 2, fifth, 2)
 
     def sixth(index):
-        out[index] = swept(top, post.at[1], RIM + index, PAD + RIM, ny)
+        out[index] = swept(top, post.at[1], RIM + index, 2 * RIM, ny)
 
     run(nx, sixth, 2)
 
@@ -486,63 +661,81 @@
     return lax.ppermute(high, axis, up), lax.ppermute(low, axis, down)
 
 
-def handed_out(block, axis):
-    copies = jnp.broadcast_to(block, (lax.axis_size(axis),) + block.shape)
-    return lax.all_to_all(copies, axis, 0, 0)
-
-
-def passed_round(block, axis):
+def paired(block, axis, stride):
+    count = lax.axis_size(axis)
+    return jnp.stack((block, lax.ppermute(block, axis, [(i, i ^ stride) for i in range(count)])))
+
+
+def passed_round(block, axis, stride):
     count = lax.axis_size(axis)
     blocks = [block]
-    for distance in range(1, count):
+    for distance in range(stride, count, stride):
         blocks.append(lax.ppermute(block, axis, [(i, (i + distance) % count) for i in range(count)]))
     return jnp.stack(blocks)
+
+
+def gathered(block):
+    block = passed_round(block, "gx", 2)
+    block = paired(block, "gx", 1)
+    block = passed_round(block, "gy", 2)
+    return paired(block, "gy", 1)
 
 
 def fused_cycle(*fields):
     axes = ("gx", "gy")
     devices_x, devices_y = lax.axis_size("gx"), lax.axis_size("gy")
     nx, ny, nz = fields[0].shape
-    parts = nx // 4
-    slabs, rows = nx + 2 * RIM, ny + 2 * RIM
-    own, x_low, x_high = call(
-        pack_x,
+    coarse_x, coarse_y = nx // 2, ny // 2
+    x_shape = (sum(x_rows(nx, ny)), LANES)
+    y_shape = (sum(y_rows(nx, ny)), LANES)
+    x_low, x_high, y_own_low, y_own_high, faces = call(
+        start_pack,
         [ANYWHERE] * 5,
-        [((5, nx, ny, nz), IN_VMEM), ((5, RIM, ny, nz), IN_VMEM), ((5, RIM, ny, nz), IN_VMEM)],
-        [pltpu.SemaphoreType.DMA((5,))],
+        [(shape, IN_VMEM) for shape in (x_shape, x_shape) + ((5 * nx * RIM, LANES),) * 2 + ((3, coarse_x, coarse_y, LANES),)],
+        [(5, nx, ny, LANES), (coarse_x, ny, LANES), pltpu.SemaphoreType.DMA((5,))],
         None,
     )(*fields)
     x_low, x_high = from_sides(x_low, x_high, "gx")
-    (faces,) = call(
-        coarse_faces, [IN_VMEM], [((3, parts, ny // 2, LANES), IN_VMEM)], [(nx // 2, ny, LANES)]
-    )(own)
-    faces = handed_out(passed_round(faces, "gx"), "gy")
-    y_low, y_high = call(pack_y, [IN_VMEM] * 3, [((5, slabs, RIM, nz), IN_VMEM)] * 2)(own, x_low, x_high)
+    (coefficients,) = call(
+        coarse_faces, [IN_VMEM], [((16, LANES), IN_VMEM)], [(coarse_x // 2, coarse_y, LANES)]
+    )(faces)
+    y_low, y_high = call(pack_y, [IN_VMEM] * 5, [(y_shape, IN_VMEM)] * 2)(
+        faces, y_own_low, y_own_high, x_low, x_high
+    )
     y_low, y_high = from_sides(y_low, y_high, "gy")
-    stack = (slabs, rows + 2 * PAD, LANES)
-    top, chunk = call(
+    stack = (nx + 2 * RIM, ny + 4 * RIM, LANES)
+    stack_1 = (coarse_x + 2 * RIM, coarse_y + 4 * RIM, LANES)
+    half = stack_1[0] // 2
+    v_shape = (RIM // 2 * coarse_y, LANES)
+    top, mid, chunk, v_low, v_high = call(
         functools.partial(level_down, axes),
-        [IN_VMEM] * 5,
-        [((D,) + stack, ANYWHERE), ((parts, ny // 2, LANES), IN_VMEM)],
-        [(D + 1,) + stack, stack, (nx // 2, ny, LANES), pltpu.SemaphoreType.DMA((D,))],
-    )(own, x_low, x_high, y_low, y_high)
-    sources = handed_out(handed_out(chunk, "gx"), "gy")
-    count = devices_x * nx // 4
-    rows_1 = devices_y * ny // 2
+        [IN_VMEM] * 11,
+        [
+            (shape, IN_VMEM)
+            for shape in ((D + 1,) + stack, (D + 1,) + stack_1, (32, LANES), v_shape, v_shape)
+        ],
+        [stack, (nx // 2, ny, LANES), stack_1, (half, coarse_y + 2 * RIM, LANES)],
+    )(*fields, faces, coefficients, x_low, x_high, y_low, y_high)
+    pieces = gathered(chunk)
+    v_low, v_high = from_sides(v_low, v_high, "gx")
+    w_low, w_high = call(pack_v, [IN_VMEM] * 3, [((half * RIM, LANES), IN_VMEM)] * 2)(mid, v_low, v_high)
+    w_low, w_high = from_sides(w_low, w_high, "gy")
+    count = devices_x * nx // 16
+    rows = devices_y * ny // 4
     coarsest = (devices_x * nx >> LEVELS - 1, devices_y * ny >> LEVELS - 1)
     (out,) = call(
         functools.partial(level_up, axes, (devices_x, devices_y), 4 * max(coarsest)),
-        [IN_VMEM, IN_VMEM, ANYWHERE],
+        [IN_VMEM] * 7,
         [((nx, ny, nz), IN_VMEM)],
         [
-            (9, count + 2, rows_1 + 2 * PAD, LANES),
-            (D,) + stack,
+            (3, devices_x, rows, LANES),
+            stack_1,
+            stack_1,
+            (count + RIM, rows + 2 * PAD, LANES),
             (2,) + stack,
-            (count // 2, rows_1, LANES),
-            (nx // 2 + 2, rows, LANES),
-            pltpu.SemaphoreType.DMA((1,)),
+            (coarse_x + 2, ny + 2 * RIM, LANES),
         ],
-    )(sources, faces, top)
+    )(pieces, top, mid, v_low, v_high, w_low, w_high)
     return out
 
 
@@ -711,7 +904,8 @@
 
 def fits(nx, ny, nz, devices_x, devices_y):
     cells = devices_x * nx * devices_y * ny * nz // 8
-    return cells <= 2**18 and devices_x % 2 == 0 and (nx, ny, nz) == (16, 16, LANES)
+    even = devices_x % 8 == 0 and devices_y % 4 == 0
+    return cells <= 2**18 and even and (nx, ny, nz) == (16, 16, LANES)
 
 
 def local(source_term, initial_guess, face_x, face_y, face_z):

time: 106 us -> 79.9 us (0.75); the launches traced: 104 us -> 79.4 us
  blocking collectives: 23.6 us -> 0 us
  Pallas kernels: 23.2 us -> 12.6 us
  waiting for transfers between devices: 19.1 us -> 29.1 us
  local copies, waits for them, and re-layouts: 9.57 us -> 8.13 us
    all_to_all x1 -> x0, blocking collectives: 23.6 us -> none  [handed_out(): return lax.all_to_all(copies, axis, 0, 0)]
    pallas_call x5 -> x6, Pallas kernels: 23.2 us -> 12.6 us  [launch(): pl.pallas_call(kernel, out_shape=[jax.ShapeDtypeStruct(shape, F32) for sh...]
    ppermute x4 -> x8, starting transfers between devices: 12.5 us -> 21.8 us  [from_sides(): return (lax.ppermute(high, axis, up), lax.ppermute(low, axis, down))]
    ppermute x4 -> x8, waiting for transfers between devices: 9.71 us -> 17.9 us  [from_sides(): return (lax.ppermute(high, axis, up), lax.ppermute(low, axis, down))]
    all_to_all x2 -> x0, starting transfers between devices: 8.12 us -> none  [handed_out(): return lax.all_to_all(copies, axis, 0, 0)]
    all_to_all x2 -> x0, waiting for transfers between devices: 6.7 us -> none  [handed_out(): return lax.all_to_all(copies, axis, 0, 0)]
    ppermute x7 -> x4, waiting for transfers between devices: 2.66 us -> 8.15 us  [passed_round(): lax.ppermute(block, axis, [(i, (i + distance) % count) for i in range(cou...]
    broadcast_in_dim x3 -> x0, local copies, waits for them, and re-layouts: 3.61 us -> none  [handed_out(): copies = jnp.broadcast_to(block, (lax.axis_size(axis),) + block.shape)]
  transfers between devices with their start and end apart: 13 -> 14, of which waited for: 6 -> 11; matrix products, arithmetic and copies ran while one was open for 7% -> 0% of each run, Pallas kernels for 5% -> 1%
where the time goes in v4:
time: 79.9 us; the launch traced here: 79.4 us
  starting transfers between devices  29.3 us (37%)
  waiting for transfers between devices  29.1 us (36%)
  Pallas kernels  12.6 us (16%)
  local copies, waits for them, and re-layouts  8.13 us (10%)
    ppermute x8, starting transfers between devices, from_sides(): return (lax.ppermute(high, axis, up), lax.ppermute(low, axis, down))  21.8 us
    ppermute x8, waiting for transfers between devices, from_sides(): return (lax.ppermute(high, axis, up), lax.ppermute(low, axis, down))  17.9 us
    pallas_call x6, Pallas kernels, launch(): pl.pallas_call(kernel, out_shape=[jax.ShapeDtypeStruct(shape, F32) for sh...  12.6 us
    ppermute x4, waiting for transfers between devices, passed_round(): lax.ppermute(block, axis, [(i, (i + distance) % count) for i in range(cou...  8.15 us
    unnamed x18, local copies, waits for them, and re-layouts  8.13 us
    ppermute x4, starting transfers between devices, passed_round(): lax.ppermute(block, axis, [(i, (i + distance) % count) for i in range(cou...  5.65 us
    ppermute x2, waiting for transfers between devices, paired(): lax.ppermute(block, axis, [(i, i ^ stride) for i in range(count)])  3.11 us
    ppermute x2, starting transfers between devices, paired(): lax.ppermute(block, axis, [(i, i ^ stride) for i in range(count)])  1.82 us
  transfers between devices with their start and end apart: 14, of which 11 were waited for; matrix products, arithmetic and copies ran while one was open for 0% of the time, Pallas kernels for 1%

profile of v4, /device:TPU:1, one launch (start us, length us, event | category | flops | bytes accessed | tf_op | source)
XLA Modules:
  0.0 79.4 jit_solution(13797256873239144213)
XLA Ops:
  0.0 2.4 %shard_map.55 = (f32[368,128]{1,0:T(8,128)}, f32[368,128]{1,0:T(8,128)}, f32[320,128]{1,0:T(8,128)}, f32[320,128]{1,0:T(8,128)}, f32[3,8,8,128]{3,2,1,0:T(8,128)}) custom-call(f32[16,16,128]{2,1,0:T(8,128)} %refs_0_.3, f32[16,16,128]{2,1,0:T(8,128)} %refs_1_.3, f32[16,16,128]{2,1,0:T(8,128)} %refs_2_.3, f32[16,16,128]{2,1,0:T(8,128)} %refs_3_.3, ...), custom_call_target="tpu_custom_call" | custom-call | tf_op jit(solution)/shard_map/pallas_call | solution.py:645
  2.4 4.0 %collective-permute-start = (f32[368,128]{1,0:T(8,128)}, f32[368,128]{1,0:T(8,128)S(1)}, u32[]{:S(2)}, u32[]{:S(2)}) collective-permute-start(f32[368,128]{1,0:T(8,128)} %get-tuple-element.20), channel_id=1, source_target_pairs={{0,4},{4,8},{8,12},{12,16},{16,20},{20,24},{24,28},{1,5},{5,9},{9,... | collective-permute-start | bytes 565256 | tf_op jit(solution)/shard_map/ppermute | solution.py:661
  6.3 1.3 %collective-permute-start.1 = (f32[368,128]{1,0:T(8,128)}, f32[368,128]{1,0:T(8,128)S(1)}, u32[]{:S(2)}, u32[]{:S(2)}) collective-permute-start(f32[368,128]{1,0:T(8,128)} %get-tuple-element.21), channel_id=1, source_target_pairs={{4,0},{8,4},{12,8},{16,12},{20,16},{24,20},{28,24},{5,1},{9,5},{13... | collective-permute-start | bytes 565256 | tf_op jit(solution)/shard_map/ppermute | solution.py:661
  7.6 2.4 %collective-permute-done.x_low.refs_7_ = f32[368,128]{1,0:T(8,128)S(1)} collective-permute-done((f32[368,128]{1,0:T(8,128)}, f32[368,128]{1,0:T(8,128)S(1)}, u32[]{:S(2)}, u32[]{:S(2)}) %collective-permute-start) | collective-permute-done | bytes 188448 | tf_op jit(solution)/shard_map/ppermute | solution.py:661
  10.0 3.7 %collective-permute-done.1.x_high.refs_8_ = f32[368,128]{1,0:T(8,128)S(1)} collective-permute-done((f32[368,128]{1,0:T(8,128)}, f32[368,128]{1,0:T(8,128)S(1)}, u32[]{:S(2)}, u32[]{:S(2)}) %collective-permute-start.1) | collective-permute-done | bytes 188448 | tf_op jit(solution)/shard_map/ppermute | solution.py:661
  13.7 0.0 copy-start
  13.7 0.9 %copy-done = f32[3,8,8,128]{3,2,1,0:T(8,128)S(1)} copy-done((f32[3,8,8,128]{3,2,1,0:T(8,128)S(1)}, f32[3,8,8,128]{3,2,1,0:T(8,128)}, u32[]{:S(2)}) %copy-start) | copy-done | bytes 98328
  14.6 0.0 copy-start.7
  14.6 0.9 %copy-done.7 = f32[320,128]{1,0:T(8,128)S(1)} copy-done((f32[320,128]{1,0:T(8,128)S(1)}, f32[320,128]{1,0:T(8,128)}, u32[]{:S(2)}) %copy-start.7) | copy-done | bytes 163864
  15.5 0.0 copy-start.8
  15.5 0.9 %copy-done.8 = f32[320,128]{1,0:T(8,128)S(1)} copy-done((f32[320,128]{1,0:T(8,128)S(1)}, f32[320,128]{1,0:T(8,128)}, u32[]{:S(2)}) %copy-start.8) | copy-done | bytes 163864
  16.5 0.2 shard_map.57
  16.6 4.9 %collective-permute-start.2 = (f32[576,128]{1,0:T(8,128)S(1)}, f32[576,128]{1,0:T(8,128)S(1)}, u32[]{:S(2)}, u32[]{:S(2)}) collective-permute-start(f32[576,128]{1,0:T(8,128)S(1)} %get-tuple-element.24), channel_id=1, source_target_pairs={{0,1},{1,2},{2,3},{4,5},{5,6},{6,7},{8,9},{9,10},{10,11},{12,13},{... | collective-permute-start | bytes 884744 | tf_op jit(solution)/shard_map/ppermute | solution.py:661
  21.5 1.9 %collective-permute-start.3 = (f32[576,128]{1,0:T(8,128)S(1)}, f32[576,128]{1,0:T(8,128)S(1)}, u32[]{:S(2)}, u32[]{:S(2)}) collective-permute-start(f32[576,128]{1,0:T(8,128)S(1)} %get-tuple-element.25), channel_id=1, source_target_pairs={{1,0},{2,1},{3,2},{5,4},{6,5},{7,6},{9,8},{10,9},{11,10},{13,12},{... | collective-permute-start | bytes 884744 | tf_op jit(solution)/shard_map/ppermute | solution.py:661
  23.4 0.5 shard_map.56.refs_6_
  23.9 1.2 %collective-permute-done.2.refs_9_ = f32[576,128]{1,0:T(8,128)S(1)} collective-permute-done((f32[576,128]{1,0:T(8,128)S(1)}, f32[576,128]{1,0:T(8,128)S(1)}, u32[]{:S(2)}, u32[]{:S(2)}) %collective-permute-start.2) | collective-permute-done | bytes 294944 | tf_op jit(solution)/shard_map/ppermute | solution.py:661
  25.1 4.4 %collective-permute-done.3.refs_10_ = f32[576,128]{1,0:T(8,128)S(1)} collective-permute-done((f32[576,128]{1,0:T(8,128)S(1)}, f32[576,128]{1,0:T(8,128)S(1)}, u32[]{:S(2)}, u32[]{:S(2)}) %collective-permute-start.3) | collective-permute-done | bytes 294944 | tf_op jit(solution)/shard_map/ppermute | solution.py:661
  29.5 0.0 copy-start.1
  29.5 0.9 %copy-done.1 = f32[3,8,8,128]{3,2,1,0:T(8,128)S(1)} copy-done((f32[3,8,8,128]{3,2,1,0:T(8,128)S(1)}, f32[3,8,8,128]{3,2,1,0:T(8,128)}, u32[]{:S(2)}) %copy-start.1) | copy-done | bytes 98328
  30.4 0.9 %copy-done.2 = f32[16,16,128]{2,1,0:T(8,128)S(1)} copy-done((f32[16,16,128]{2,1,0:T(8,128)S(1)}, f32[16,16,128]{2,1,0:T(8,128)}, u32[]{:S(2)}) %copy-start.2) | copy-done | bytes 131096
  31.3 0.9 %copy-done.3 = f32[16,16,128]{2,1,0:T(8,128)S(1)} copy-done((f32[16,16,128]{2,1,0:T(8,128)S(1)}, f32[16,16,128]{2,1,0:T(8,128)}, u32[]{:S(2)}) %copy-start.3) | copy-done | bytes 131096
  32.3 0.9 %copy-done.4 = f32[16,16,128]{2,1,0:T(8,128)S(1)} copy-done((f32[16,16,128]{2,1,0:T(8,128)S(1)}, f32[16,16,128]{2,1,0:T(8,128)}, u32[]{:S(2)}) %copy-start.4) | copy-done | bytes 131096
  33.2 0.9 %copy-done.5 = f32[16,16,128]{2,1,0:T(8,128)S(1)} copy-done((f32[16,16,128]{2,1,0:T(8,128)S(1)}, f32[16,16,128]{2,1,0:T(8,128)}, u32[]{:S(2)}) %copy-start.5) | copy-done | bytes 131096
  34.1 0.9 %copy-done.6 = f32[16,16,128]{2,1,0:T(8,128)S(1)} copy-done((f32[16,16,128]{2,1,0:T(8,128)S(1)}, f32[16,16,128]{2,1,0:T(8,128)}, u32[]{:S(2)}) %copy-start.6) | copy-done | bytes 131096
  35.0 3.4 %shard_map.58 = (f32[8,24,32,128]{3,2,1,0:T(8,128)S(1)}, f32[8,16,24,128]{3,2,1,0:T(8,128)S(1)}, f32[32,128]{1,0:T(8,128)S(1)}, f32[16,128]{1,0:T(8,128)S(1)}, f32[16,128]{1,0:T(8,128)S(1)}) custom-call(f32[16,16,128]{2,1,0:T(8,128)S(1)} %copy-done.2, f32[16,16,128]{2,1,0:T(8,128)S(1)} %copy-done.3, f32[16,16,128]{2,1,0:T(8,128)S(1)} %copy-done.4, ...), custom_call_target="tpu_custom_call" | custom-call | tf_op jit(solution)/shard_map/pallas_call | solution.py:645
  38.4 5.1 %collective-permute-start.6 = (f32[32,128]{1,0:T(8,128)S(1)}, f32[32,128]{1,0:T(8,128)S(1)}, u32[]{:S(2)}, u32[]{:S(2)}) collective-permute-start(f32[32,128]{1,0:T(8,128)S(1)} %get-tuple-element.26), channel_id=1, source_target_pairs={{0,24},{4,28},{8,0},{12,4},{16,8},{20,12},{24,16},{28,20},{1,25},{... | collective-permute-start | bytes 49160 | tf_op jit(solution)/shard_map/ppermute | solution.py:673
  43.5 0.0 collective-permute-start.5
  43.5 0.5 collective-permute-start.4
  44.0 0.4 collective-permute-done.6
  44.4 2.6 %collective-permute-done.5 = f32[32,128]{1,0:T(8,128)S(1)} collective-permute-done((f32[32,128]{1,0:T(8,128)S(1)}, f32[32,128]{1,0:T(8,128)S(1)}, u32[]{:S(2)}, u32[]{:S(2)}) %collective-permute-start.5) | collective-permute-done | bytes 16416 | tf_op jit(solution)/shard_map/ppermute | solution.py:673
  47.0 0.9 %collective-permute-done.4 = f32[32,128]{1,0:T(8,128)S(1)} collective-permute-done((f32[32,128]{1,0:T(8,128)S(1)}, f32[32,128]{1,0:T(8,128)S(1)}, u32[]{:S(2)}, u32[]{:S(2)}) %collective-permute-start.4) | collective-permute-done | bytes 16416 | tf_op jit(solution)/shard_map/ppermute | solution.py:673
  47.9 0.1 collective-permute-start.7
  48.0 3.1 %collective-permute-done.7 = f32[4,32,128]{2,1,0:T(8,128)S(1)} collective-permute-done((f32[4,32,128]{2,1,0:T(8,128)S(1)}, f32[4,32,128]{2,1,0:T(8,128)S(1)}, u32[]{:S(2)}, u32[]{:S(2)}) %collective-permute-start.7) | collective-permute-done | bytes 65568 | tf_op jit(solution)/shard_map/ppermute | solution.py:666
  51.1 0.1 collective-permute-start.8
  51.2 4.2 %collective-permute-done.8 = f32[2,4,32,128]{3,2,1,0:T(8,128)S(1)} collective-permute-done((f32[2,4,32,128]{3,2,1,0:T(8,128)S(1)}, f32[2,4,32,128]{3,2,1,0:T(8,128)S(1)}, u32[]{:S(2)}, u32[]{:S(2)}) %collective-permute-start.8) | collective-permute-done | bytes 131104 | tf_op jit(solution)/shard_map/ppermute | solution.py:673
  55.4 0.1 fusion.2
  55.5 1.7 %collective-permute-start.9 = (f32[2,2,4,32,128]{4,3,2,1,0:T(8,128)S(1)}, f32[2,2,4,32,128]{4,3,2,1,0:T(8,128)S(1)}, u32[]{:S(2)}, u32[]{:S(2)}) collective-permute-start(f32[2,2,4,32,128]{4,3,2,1,0:T(8,128)S(1)} %get-tuple-element.34), channel_id=1, source_target_pairs={{0,1},{1,0},{2,3},{3,2},{4,5},{5,4},{6,7},{7,6},{8,9},{9,8},{10,11... | collective-permute-start | bytes 786440 | tf_op jit(solution)/shard_map/ppermute | solution.py:666
  57.2 1.9 %collective-permute-start.10 = (f32[16,128]{1,0:T(8,128)S(1)}, f32[16,128]{1,0:T(8,128)S(1)}, u32[]{:S(2)}, u32[]{:S(2)}) collective-permute-start(f32[16,128]{1,0:T(8,128)S(1)} %get-tuple-element.29), channel_id=1, source_target_pairs={{0,4},{4,8},{8,12},{12,16},{16,20},{20,24},{24,28},{1,5},{5,9},{9,... | collective-permute-start | bytes 24584 | tf_op jit(solution)/shard_map/ppermute | solution.py:661
  59.1 1.3 %collective-permute-start.11 = (f32[16,128]{1,0:T(8,128)S(1)}, f32[16,128]{1,0:T(8,128)S(1)}, u32[]{:S(2)}, u32[]{:S(2)}) collective-permute-start(f32[16,128]{1,0:T(8,128)S(1)} %get-tuple-element.30), channel_id=1, source_target_pairs={{4,0},{8,4},{12,8},{16,12},{20,16},{24,20},{28,24},{5,1},{9,5},{13... | collective-permute-start | bytes 24584 | tf_op jit(solution)/shard_map/ppermute | solution.py:661
  60.4 0.0 collective-permute-done.10.x_low
  60.4 3.1 %collective-permute-done.11.x_high = f32[16,128]{1,0:T(8,128)S(1)} collective-permute-done((f32[16,128]{1,0:T(8,128)S(1)}, f32[16,128]{1,0:T(8,128)S(1)}, u32[]{:S(2)}, u32[]{:S(2)}) %collective-permute-start.11) | collective-permute-done | bytes 8224 | tf_op jit(solution)/shard_map/ppermute | solution.py:661
  63.5 0.1 shard_map.59
  63.7 4.6 %collective-permute-start.12 = (f32[32,128]{1,0:T(8,128)S(1)}, f32[32,128]{1,0:T(8,128)S(1)}, u32[]{:S(2)}, u32[]{:S(2)}) collective-permute-start(f32[32,128]{1,0:T(8,128)S(1)} %get-tuple-element.31), channel_id=1, source_target_pairs={{0,1},{1,2},{2,3},{4,5},{5,6},{6,7},{8,9},{9,10},{10,11},{12,13},{... | collective-permute-start | bytes 49160 | tf_op jit(solution)/shard_map/ppermute | solution.py:661
  68.3 1.9 %collective-permute-start.13 = (f32[32,128]{1,0:T(8,128)S(1)}, f32[32,128]{1,0:T(8,128)S(1)}, u32[]{:S(2)}, u32[]{:S(2)}) collective-permute-start(f32[32,128]{1,0:T(8,128)S(1)} %get-tuple-element.32), channel_id=1, source_target_pairs={{1,0},{2,1},{3,2},{5,4},{6,5},{7,6},{9,8},{10,9},{11,10},{13,12},{... | collective-permute-start | bytes 49160 | tf_op jit(solution)/shard_map/ppermute | solution.py:661
  70.2 0.0 collective-permute-done.9
  70.3 0.0 collective-permute-done.12.y_low
  70.3 3.1 %collective-permute-done.13.y_high = f32[32,128]{1,0:T(8,128)S(1)} collective-permute-done((f32[32,128]{1,0:T(8,128)S(1)}, f32[32,128]{1,0:T(8,128)S(1)}, u32[]{:S(2)}, u32[]{:S(2)}) %collective-permute-start.13) | collective-permute-done | bytes 16416 | tf_op jit(solution)/shard_map/ppermute | solution.py:661
  73.3 6.0 %shard_map.60 = f32[16,16,128]{2,1,0:T(8,128)} custom-call(f32[2,2,2,4,32,128]{5,4,3,2,1,0:T(8,128)S(1)} %pad_maximum_fusion.pieces, f32[8,24,32,128]{3,2,1,0:T(8,128)S(1)} %get-tuple-element.27.top, f32[8,16,24,128]{3,2,1,0:T(8,128)S(1)} %get-tuple-element.28.mid_v.mid, f32[16,128]{1,0:T(8,128)S(1)} %collective-permute-done.10.x_low, ...), custom_call_target="tpu_custom_call" | custom-call | tf_op jit(solution)/shard_map/pallas_call | solution.py:645
  (8 shorter events, 0.1 us)
Async XLA Ops:
  2.4 7.6 %collective-permute-start = (f32[368,128]{1,0:T(8,128)}, f32[368,128]{1,0:T(8,128)S(1)}, u32[]{:S(2)}, u32[]{:S(2)}) collective-permute-start(f32[368,128]{1,0:T(8,128)} %get-tuple-element.20), channel_id=1, source_target_pairs={{0,4},{4,8},{8,12},{12,16},{16,20},{20,24},{24,28},{1,5},{5,9},{9,... | collective-permute-start | bytes 565256 | tf_op jit(solution)/shard_map/ppermute | solution.py:661
  6.3 7.4 %collective-permute-start.1 = (f32[368,128]{1,0:T(8,128)}, f32[368,128]{1,0:T(8,128)S(1)}, u32[]{:S(2)}, u32[]{:S(2)}) collective-permute-start(f32[368,128]{1,0:T(8,128)} %get-tuple-element.21), channel_id=1, source_target_pairs={{4,0},{8,4},{12,8},{16,12},{20,16},{24,20},{28,24},{5,1},{9,5},{13... | collective-permute-start | bytes 565256 | tf_op jit(solution)/shard_map/ppermute | solution.py:661
  13.7 0.9 %copy-start = (f32[3,8,8,128]{3,2,1,0:T(8,128)S(1)}, f32[3,8,8,128]{3,2,1,0:T(8,128)}, u32[]{:S(2)}) copy-start(f32[3,8,8,128]{3,2,1,0:T(8,128)} %get-tuple-element.19.faces.refs_5_) | copy-start | bytes 294916
  14.6 0.9 %copy-start.7 = (f32[320,128]{1,0:T(8,128)S(1)}, f32[320,128]{1,0:T(8,128)}, u32[]{:S(2)}) copy-start(f32[320,128]{1,0:T(8,128)} %get-tuple-element.22.y_own_low) | copy-start | bytes 491524
  15.5 0.9 %copy-start.8 = (f32[320,128]{1,0:T(8,128)S(1)}, f32[320,128]{1,0:T(8,128)}, u32[]{:S(2)}) copy-start(f32[320,128]{1,0:T(8,128)} %get-tuple-element.23.y_own_high) | copy-start | bytes 491524
  16.6 8.5 %collective-permute-start.2 = (f32[576,128]{1,0:T(8,128)S(1)}, f32[576,128]{1,0:T(8,128)S(1)}, u32[]{:S(2)}, u32[]{:S(2)}) collective-permute-start(f32[576,128]{1,0:T(8,128)S(1)} %get-tuple-element.24), channel_id=1, source_target_pairs={{0,1},{1,2},{2,3},{4,5},{5,6},{6,7},{8,9},{9,10},{10,11},{12,13},{... | collective-permute-start | bytes 884744 | tf_op jit(solution)/shard_map/ppermute | solution.py:661
  21.5 8.0 %collective-permute-start.3 = (f32[576,128]{1,0:T(8,128)S(1)}, f32[576,128]{1,0:T(8,128)S(1)}, u32[]{:S(2)}, u32[]{:S(2)}) collective-permute-start(f32[576,128]{1,0:T(8,128)S(1)} %get-tuple-element.25), channel_id=1, source_target_pairs={{1,0},{2,1},{3,2},{5,4},{6,5},{7,6},{9,8},{10,9},{11,10},{13,12},{... | collective-permute-start | bytes 884744 | tf_op jit(solution)/shard_map/ppermute | solution.py:661
  29.5 0.9 %copy-start.1 = (f32[3,8,8,128]{3,2,1,0:T(8,128)S(1)}, f32[3,8,8,128]{3,2,1,0:T(8,128)}, u32[]{:S(2)}) copy-start(f32[3,8,8,128]{3,2,1,0:T(8,128)} %get-tuple-element.19.faces.refs_5_) | copy-start | bytes 294916
  30.4 0.9 %copy-start.2 = (f32[16,16,128]{2,1,0:T(8,128)S(1)}, f32[16,16,128]{2,1,0:T(8,128)}, u32[]{:S(2)}) copy-start(f32[16,16,128]{2,1,0:T(8,128)} %refs_0_.3) | copy-start | bytes 393220
  31.3 0.9 %copy-start.3 = (f32[16,16,128]{2,1,0:T(8,128)S(1)}, f32[16,16,128]{2,1,0:T(8,128)}, u32[]{:S(2)}) copy-start(f32[16,16,128]{2,1,0:T(8,128)} %refs_1_.3) | copy-start | bytes 393220
  32.2 0.9 %copy-start.4 = (f32[16,16,128]{2,1,0:T(8,128)S(1)}, f32[16,16,128]{2,1,0:T(8,128)}, u32[]{:S(2)}) copy-start(f32[16,16,128]{2,1,0:T(8,128)} %refs_2_.3) | copy-start | bytes 393220
  33.2 0.9 %copy-start.5 = (f32[16,16,128]{2,1,0:T(8,128)S(1)}, f32[16,16,128]{2,1,0:T(8,128)}, u32[]{:S(2)}) copy-start(f32[16,16,128]{2,1,0:T(8,128)} %refs_3_.3) | copy-start | bytes 393220
  34.1 0.9 %copy-start.6 = (f32[16,16,128]{2,1,0:T(8,128)S(1)}, f32[16,16,128]{2,1,0:T(8,128)}, u32[]{:S(2)}) copy-start(f32[16,16,128]{2,1,0:T(8,128)} %refs_4_.3) | copy-start | bytes 393220
  38.4 6.0 %collective-permute-start.6 = (f32[32,128]{1,0:T(8,128)S(1)}, f32[32,128]{1,0:T(8,128)S(1)}, u32[]{:S(2)}, u32[]{:S(2)}) collective-permute-start(f32[32,128]{1,0:T(8,128)S(1)} %get-tuple-element.26), channel_id=1, source_target_pairs={{0,24},{4,28},{8,0},{12,4},{16,8},{20,12},{24,16},{28,20},{1,25},{... | collective-permute-start | bytes 49160 | tf_op jit(solution)/shard_map/ppermute | solution.py:673
  43.5 3.5 %collective-permute-start.5 = (f32[32,128]{1,0:T(8,128)S(1)}, f32[32,128]{1,0:T(8,128)S(1)}, u32[]{:S(2)}, u32[]{:S(2)}) collective-permute-start(f32[32,128]{1,0:T(8,128)S(1)} %get-tuple-element.26), channel_id=1, source_target_pairs={{0,16},{4,20},{8,24},{12,28},{16,0},{20,4},{24,8},{28,12},{1,17},{... | collective-permute-start | bytes 49160 | tf_op jit(solution)/shard_map/ppermute | solution.py:673
  43.5 4.4 %collective-permute-start.4 = (f32[32,128]{1,0:T(8,128)S(1)}, f32[32,128]{1,0:T(8,128)S(1)}, u32[]{:S(2)}, u32[]{:S(2)}) collective-permute-start(f32[32,128]{1,0:T(8,128)S(1)} %get-tuple-element.26), channel_id=1, source_target_pairs={{0,8},{4,12},{8,16},{12,20},{16,24},{20,28},{24,0},{28,4},{1,9},{5... | collective-permute-start | bytes 49160 | tf_op jit(solution)/shard_map/ppermute | solution.py:673
  47.9 3.2 %collective-permute-start.7 = (f32[4,32,128]{2,1,0:T(8,128)S(1)}, f32[4,32,128]{2,1,0:T(8,128)S(1)}, u32[]{:S(2)}, u32[]{:S(2)}) collective-permute-start(f32[4,32,128]{2,1,0:T(8,128)S(1)} %get-tuple-element.38), channel_id=1, source_target_pairs={{0,4},{4,0},{8,12},{12,8},{16,20},{20,16},{24,28},{28,24},{1,5},{5... | collective-permute-start | bytes 196616 | tf_op jit(solution)/shard_map/ppermute | solution.py:666
  51.1 4.3 %collective-permute-start.8 = (f32[2,4,32,128]{3,2,1,0:T(8,128)S(1)}, f32[2,4,32,128]{3,2,1,0:T(8,128)S(1)}, u32[]{:S(2)}, u32[]{:S(2)}) collective-permute-start(f32[2,4,32,128]{3,2,1,0:T(8,128)S(1)} %get-tuple-element.36), channel_id=1, source_target_pairs={{0,2},{1,3},{2,0},{3,1},{4,6},{5,7},{6,4},{7,5},{8,10},{9,11},{10,... | collective-permute-start | bytes 393224 | tf_op jit(solution)/shard_map/ppermute | solution.py:673
  55.5 14.7 %collective-permute-start.9 = (f32[2,2,4,32,128]{4,3,2,1,0:T(8,128)S(1)}, f32[2,2,4,32,128]{4,3,2,1,0:T(8,128)S(1)}, u32[]{:S(2)}, u32[]{:S(2)}) collective-permute-start(f32[2,2,4,32,128]{4,3,2,1,0:T(8,128)S(1)} %get-tuple-element.34), channel_id=1, source_target_pairs={{0,1},{1,0},{2,3},{3,2},{4,5},{5,4},{6,7},{7,6},{8,9},{9,8},{10,11... | collective-permute-start | bytes 786440 | tf_op jit(solution)/shard_map/ppermute | solution.py:666
  57.2 3.2 %collective-permute-start.10 = (f32[16,128]{1,0:T(8,128)S(1)}, f32[16,128]{1,0:T(8,128)S(1)}, u32[]{:S(2)}, u32[]{:S(2)}) collective-permute-start(f32[16,128]{1,0:T(8,128)S(1)} %get-tuple-element.29), channel_id=1, source_target_pairs={{0,4},{4,8},{8,12},{12,16},{16,20},{20,24},{24,28},{1,5},{5,9},{9,... | collective-permute-start | bytes 24584 | tf_op jit(solution)/shard_map/ppermute | solution.py:661
  59.1 4.4 %collective-permute-start.11 = (f32[16,128]{1,0:T(8,128)S(1)}, f32[16,128]{1,0:T(8,128)S(1)}, u32[]{:S(2)}, u32[]{:S(2)}) collective-permute-start(f32[16,128]{1,0:T(8,128)S(1)} %get-tuple-element.30), channel_id=1, source_target_pairs={{4,0},{8,4},{12,8},{16,12},{20,16},{24,20},{28,24},{5,1},{9,5},{13... | collective-permute-start | bytes 24584 | tf_op jit(solution)/shard_map/ppermute | solution.py:661
  63.7 6.6 %collective-permute-start.12 = (f32[32,128]{1,0:T(8,128)S(1)}, f32[32,128]{1,0:T(8,128)S(1)}, u32[]{:S(2)}, u32[]{:S(2)}) collective-permute-start(f32[32,128]{1,0:T(8,128)S(1)} %get-tuple-element.31), channel_id=1, source_target_pairs={{0,1},{1,2},{2,3},{4,5},{5,6},{6,7},{8,9},{9,10},{10,11},{12,13},{... | collective-permute-start | bytes 49160 | tf_op jit(solution)/shard_map/ppermute | solution.py:661
  68.3 5.1 %collective-permute-start.13 = (f32[32,128]{1,0:T(8,128)S(1)}, f32[32,128]{1,0:T(8,128)S(1)}, u32[]{:S(2)}, u32[]{:S(2)}) collective-permute-start(f32[32,128]{1,0:T(8,128)S(1)} %get-tuple-element.32), channel_id=1, source_target_pairs={{1,0},{2,1},{3,2},{5,4},{6,5},{7,6},{9,8},{10,9},{11,10},{13,12},{... | collective-permute-start | bytes 49160 | tf_op jit(solution)/shard_map/ppermute | solution.py:661

commit v5 on v4

--- a/solution.py
+++ b/solution.py
@@ -11,10 +11,14 @@
 OMEGA = 0.8
 LANES = 128
 RIM = 4
+EDGE = 3
 PAD = 8
 F32 = jnp.float32
 
-V, F, FX, FY, ZL, ZH, W, D, U = range(9)
+V, F, FX, FY, ZL, ZH, W, D = range(8)
+SLOTS = (F, V, FX, FY, ZL)
+X_LAYERS = (2, 3, 3, 2, 2)
+Y_LAYERS = (2, 3, 2, 3, 2)
 
 
 def lanes_of(shape):
@@ -88,29 +92,32 @@
 
 
 def x_rows(nx, ny):
-    return 5 * RIM * ny, 3 * RIM // 2 * (ny // 2)
+    return sum(X_LAYERS) * ny, 3 * RIM // 2 * (ny // 2)
 
 
 def y_rows(nx, ny):
-    return 5 * (nx + 2 * RIM) * RIM, 3 * (nx // 2 + 2 * RIM) // 2 * RIM
+    return sum(Y_LAYERS) * (nx + 2 * EDGE), 3 * (nx // 2 + 2 * RIM) // 2 * RIM
+
+
+def x_place(index, layer, ny):
+    return pl.ds((sum(X_LAYERS[:index]) + layer) * ny, ny)
+
+
+def y_place(index, slab, slabs):
+    return pl.ds(sum(Y_LAYERS[:index]) * slabs + slab * Y_LAYERS[index], Y_LAYERS[index])
 
 
 def start_pack(*refs):
-    fields, (x_low, x_high, y_low, y_high, faces, own, tmp, done) = refs[:5], refs[5:]
+    fields, (own, x_low, x_high, faces, tmp, done) = refs[:5], refs[5:]
     copies = [pltpu.make_async_copy(ref, own.at[index], done.at[index]) for index, ref in enumerate(fields)]
     for copy in copies:
         copy.start()
     nx, ny = own.shape[1:3]
     for index, copy in enumerate(copies):
         copy.wait()
-        for layer in range(RIM):
-            rows = pl.ds((index * RIM + layer) * ny, ny)
-            x_low[rows] = own[index, layer]
-            x_high[rows] = own[index, nx - RIM + layer]
-        for slab in range(nx):
-            rows = pl.ds((index * nx + slab) * RIM, RIM)
-            y_low[rows] = own[index, slab, :RIM]
-            y_high[rows] = own[index, slab, ny - RIM :]
+        for layer in range(X_LAYERS[index]):
+            x_low[x_place(index, layer, ny)] = own[index, layer]
+            x_high[x_place(index, layer, ny)] = own[index, nx - X_LAYERS[index] + layer]
     fx, fy, fz = own.at[2], own.at[3], own.at[4]
     halve = compact(LANES, 0)
 
@@ -157,17 +164,21 @@
     return one_of_two(ref[place])[layer // (RIM // 2)]
 
 
-def pack_y(faces, y_own_low, y_own_high, x_low, x_high, low, high):
+def pack_y(own, faces, x_low, x_high, low, high):
     coarse_x, coarse_y = faces.shape[1:3]
     nx, ny = 2 * coarse_x, 2 * coarse_y
-    for out, own, start in ((low, y_own_low, 0), (high, y_own_high, ny - RIM)):
-        for index in range(5):
-            base = index * (nx + 2 * RIM) * RIM
-            out[pl.ds(base + RIM * RIM, nx * RIM)] = own[pl.ds(index * nx * RIM, nx * RIM)]
-            for layer in range(RIM):
-                rows = pl.ds((index * RIM + layer) * ny + start, RIM)
-                out[pl.ds(base + layer * RIM, RIM)] = x_low[rows]
-                out[pl.ds(base + (RIM + nx + layer) * RIM, RIM)] = x_high[rows]
+    slabs = nx + 2 * EDGE
+    for index in range(5):
+        width, layers = Y_LAYERS[index], X_LAYERS[index]
+        for out, start in ((low, 0), (high, ny - width)):
+            for slab in range(nx):
+                out[y_place(index, EDGE + slab, slabs)] = own[index, slab, start : start + width]
+            for layer in range(EDGE):
+                near, far = layer + layers - EDGE, layer
+                rows = pl.ds(x_place(index, max(near, 0), ny).start + start, width)
+                out[y_place(index, layer, slabs)] = x_low[rows]
+                rows = pl.ds(x_place(index, min(far, layers - 1), ny).start + start, width)
+                out[y_place(index, EDGE + nx + layer, slabs)] = x_high[rows]
     base_x, base_y = x_rows(nx, ny)[0], y_rows(nx, ny)[0]
     half = (coarse_x + 2 * RIM) // 2
     for face in range(3):
@@ -262,35 +273,38 @@
         ref[:, start : start + RIM] = jnp.zeros((ref.shape[0], RIM, LANES), F32)
 
 
-def level_down(axes, *refs):
-    fields = refs[:5]
-    faces, coefficients, x_low, x_high, y_low, y_high, top, mid, chunk, v_low, v_high, other, tmp, one, two = refs[5:]
-    nx, ny = fields[0].shape[:2]
-    slabs, rows = nx + 2 * RIM, ny + 2 * RIM
+def level_down(axes, own, faces, coefficients, x_low, x_high, y_low, y_high, *refs):
+    top, mid, chunk, v_low, v_high, other, tmp, one, two = refs
+    nx, ny = own.shape[1:3]
+    slabs, rows = nx + 2 * EDGE, ny + 2 * RIM
     me_x, me_y = lax.axis_index(axes[0]), lax.axis_index(axes[1])
-    inner = pl.ds(2 * RIM, ny)
-    for index, slot in enumerate((F, V, FX, FY, ZL)):
-        clear_pads(top.at[slot], rows)
-        top[slot, RIM : RIM + nx, inner] = fields[index][...]
-        for layer in range(RIM):
-            place = pl.ds((index * RIM + layer) * ny, ny)
-            top[slot, layer, inner] = x_low[place]
-            top[slot, RIM + nx + layer, inner] = x_high[place]
+    inner = pl.ds(PAD, ny)
+    for index, slot in enumerate(SLOTS):
+        layers, width = X_LAYERS[index], Y_LAYERS[index]
+        top[slot, :, :PAD] = jnp.zeros((slabs, PAD, LANES), F32)
+        top[slot, :, PAD + ny :] = jnp.zeros((slabs, PAD, LANES), F32)
+        top[slot, EDGE : EDGE + nx, inner] = own[index]
+        for layer in range(EDGE):
+            if layer < layers:
+                top[slot, EDGE - layers + layer, inner] = x_low[x_place(index, layer, ny)]
+                top[slot, EDGE + nx + layer, inner] = x_high[x_place(index, layer, ny)]
+            else:
+                top[slot, EDGE - 1 - layer, inner] = jnp.zeros((ny, LANES), F32)
+                top[slot, EDGE + nx + layer, inner] = jnp.zeros((ny, LANES), F32)
         for slab in range(slabs):
-            place = pl.ds((index * slabs + slab) * RIM, RIM)
-            top[slot, slab, RIM : 2 * RIM] = y_low[place]
-            top[slot, slab, 2 * RIM + ny : RIM + rows] = y_high[place]
+            top[slot, slab, PAD - width : PAD] = y_low[y_place(index, slab, slabs)]
+            top[slot, slab, PAD + ny : PAD + ny + width] = y_high[y_place(index, slab, slabs)]
     clear_pads(other, rows)
     row_inside = (rows_of((rows, LANES)) >= RIM) | (me_y > 0)
     main = pl.ds(RIM, rows)
+    start_v = top.at[V]
 
     def first(index):
         slab = index + 1
-        inside = row_inside & ((slab >= RIM) | (me_x > 0))
+        inside = row_inside & ((slab >= EDGE) | (me_x > 0))
         set_weights(top, slab, RIM, rows, LANES, inside)
-        other[slab, main] = swept(top, other_v, slab, RIM, rows)
-
-    other_v = top.at[V]
+        other[slab, main] = swept(top, start_v, slab, RIM, rows)
+
     run(slabs - 2, first, 2)
 
     def second(index):
@@ -300,11 +314,11 @@
     run(slabs - 4, second, 2)
 
     def rest(slab):
-        v, total = weighted(top, top.at[V], slab, 2 * RIM, ny)
+        v, total = weighted(top, top.at[V], slab, PAD, ny)
         return total - top[D, slab, inner] * v
 
     def residual(index):
-        slab = RIM + 2 * index
+        slab = EDGE + 2 * index
         tmp[index] = rest(slab) + rest(slab + 1)
 
     run(nx // 2, residual, 2)
@@ -348,6 +362,11 @@
         v_high[layer * coarse_y : (layer + 1) * coarse_y] = two_in_one(
             mid[V, far, inner], mid[V, far + RIM // 2, inner]
         )
+    base = RIM // 2 * coarse_y
+    for layer in range(2):
+        place = pl.ds(base + layer * ny, ny)
+        v_low[place] = top[V, EDGE + layer, pl.ds(PAD, ny)]
+        v_high[place] = top[V, EDGE + nx - 2 + layer, pl.ds(PAD, ny)]
     for slab in range(RIM - 1, RIM + coarse_x + 1):
         one[slab, main] = swept(mid, mid.at[V], slab, RIM, rows)
 
@@ -365,12 +384,12 @@
     chunk[half // 4 * rows // 2 :] = coefficients[...]
 
 
-def pack_v(mid_v, x_low, x_high, low, high):
-    slabs = mid_v.shape[1]
+def pack_v(top, mid, x_low, x_high, low, high):
+    slabs = mid.shape[1]
     coarse_x = slabs - 2 * RIM
-    coarse_y = mid_v.shape[2] - 4 * RIM
+    coarse_y = mid.shape[2] - 4 * RIM
     half = slabs // 2
-    own = mid_v[V, RIM : RIM + coarse_x, 2 * RIM : 2 * RIM + coarse_y]
+    own = mid[V, RIM : RIM + coarse_x, 2 * RIM : 2 * RIM + coarse_y]
     values = [
         wide_slab(
             slab,
@@ -384,6 +403,21 @@
         both = two_in_one(values[slab], values[slab + half])
         low[slab * RIM : (slab + 1) * RIM] = both[:RIM]
         high[slab * RIM : (slab + 1) * RIM] = both[coarse_y - RIM :]
+    nx, ny = 2 * coarse_x, 2 * coarse_y
+    base_x, base_y = RIM // 2 * coarse_y, half * RIM
+    for out, start in ((low, 0), (high, ny - 2)):
+        for layer in range(2):
+            rows = pl.ds(base_x + layer * ny + start, 2)
+            out[pl.ds(base_y + 2 * layer, 2)] = x_low[rows]
+            out[pl.ds(base_y + 2 * (2 + nx + layer), 2)] = x_high[rows]
+        for slab in range(nx):
+            out[pl.ds(base_y + 2 * (2 + slab), 2)] = top[V, EDGE + slab, pl.ds(PAD + start, 2)]
+
+
+def stack_blocks(count, *refs):
+    out = refs[-1]
+    for index in range(count):
+        out[index] = refs[index][...]
 
 
 def pair_rows(values, stride):
@@ -617,38 +651,54 @@
     body = pl.ds(RIM, fine_rows)
     for slot in (0, 1):
         clear_pads(post.at[slot], fine_rows)
+    inner = pl.ds(PAD, ny)
+    post[0, EDGE : EDGE + nx, inner] = top[V, EDGE : EDGE + nx, inner]
+    base_x, base_y = RIM // 2 * coarse_y, half * RIM
+    for layer in range(2):
+        place = pl.ds(base_x + layer * ny, ny)
+        post[0, EDGE - 2 + layer, inner] = x_low[place]
+        post[0, EDGE + nx + layer, inner] = x_high[place]
+    for slab in range(nx + 4):
+        place = pl.ds(base_y + 2 * slab, 2)
+        post[0, slab + EDGE - 2, RIM:PAD] = jnp.zeros((RIM, LANES), F32)
+        post[0, slab + EDGE - 2, PAD + ny : PAD + ny + RIM] = jnp.zeros((RIM, LANES), F32)
+        post[0, slab + EDGE - 2, PAD - 2 : PAD] = y_low[place]
+        post[0, slab + EDGE - 2, PAD + ny : PAD + ny + 2] = y_high[place]
 
     def raise_level(index):
-        for slab in (RIM - 2 + 2 * index, RIM - 1 + 2 * index):
-            post[0, slab, body] = top[V, slab, body] + up[index]
+        for slab in (EDGE - 2 + 2 * index, EDGE - 1 + 2 * index):
+            post[0, slab, body] = post[0, slab, body] + up[index]
 
     run(steps, raise_level, 2)
 
     def fifth(index):
-        slab = RIM - 1 + index
+        slab = EDGE - 1 + index
         post[1, slab, body] = swept(top, post.at[0], slab, RIM, fine_rows)
 
     run(nx + 2, fifth, 2)
 
     def sixth(index):
-        out[index] = swept(top, post.at[1], RIM + index, 2 * RIM, ny)
+        out[index] = swept(top, post.at[1], EDGE + index, PAD, ny)
 
     run(nx, sixth, 2)
 
 
 IN_VMEM = pl.BlockSpec(memory_space=pltpu.VMEM)
-ANYWHERE = pl.BlockSpec(memory_space=pl.ANY)
-
-
-def call(kernel, ins, outs, scratch=(), limit=24 * 2**20):
+
+
+def call(kernel, outs, scratch=(), from_hbm=False):
+    ins = pl.BlockSpec(memory_space=pl.ANY) if from_hbm else IN_VMEM
+
     def launch(*args):
+        if from_hbm:
+            args = [pltpu.with_memory_space_constraint(arg, pltpu.HBM) for arg in args]
         return pl.pallas_call(
             kernel,
-            out_shape=[jax.ShapeDtypeStruct(shape, F32) for shape, _ in outs],
-            in_specs=ins,
-            out_specs=[spec for _, spec in outs],
+            out_shape=[pltpu.VMEM(shape, F32) for shape in outs],
+            in_specs=[ins] * len(args),
+            out_specs=[IN_VMEM] * len(outs),
             scratch_shapes=[pltpu.VMEM(s, F32) if isinstance(s, tuple) else s for s in scratch],
-            compiler_params=pltpu.CompilerParams(vmem_limit_bytes=limit),
+            compiler_params=pltpu.CompilerParams(vmem_limit_bytes=24 * 2**20),
         )(*args)
 
     return launch
@@ -671,14 +721,7 @@
     blocks = [block]
     for distance in range(stride, count, stride):
         blocks.append(lax.ppermute(block, axis, [(i, (i + distance) % count) for i in range(count)]))
-    return jnp.stack(blocks)
-
-
-def gathered(block):
-    block = passed_round(block, "gx", 2)
-    block = paired(block, "gx", 1)
-    block = passed_round(block, "gy", 2)
-    return paired(block, "gy", 1)
+    return blocks
 
 
 def fused_cycle(*fields):
@@ -688,53 +731,58 @@
     coarse_x, coarse_y = nx // 2, ny // 2
     x_shape = (sum(x_rows(nx, ny)), LANES)
     y_shape = (sum(y_rows(nx, ny)), LANES)
-    x_low, x_high, y_own_low, y_own_high, faces = call(
+    own, x_low, x_high, faces = call(
         start_pack,
-        [ANYWHERE] * 5,
-        [(shape, IN_VMEM) for shape in (x_shape, x_shape) + ((5 * nx * RIM, LANES),) * 2 + ((3, coarse_x, coarse_y, LANES),)],
-        [(5, nx, ny, LANES), (coarse_x, ny, LANES), pltpu.SemaphoreType.DMA((5,))],
-        None,
+        [(5, nx, ny, nz), x_shape, x_shape, (3, coarse_x, coarse_y, LANES)],
+        [(coarse_x, ny, LANES), pltpu.SemaphoreType.DMA((5,))],
+        True,
     )(*fields)
     x_low, x_high = from_sides(x_low, x_high, "gx")
-    (coefficients,) = call(
-        coarse_faces, [IN_VMEM], [((16, LANES), IN_VMEM)], [(coarse_x // 2, coarse_y, LANES)]
-    )(faces)
-    y_low, y_high = call(pack_y, [IN_VMEM] * 5, [(y_shape, IN_VMEM)] * 2)(
-        faces, y_own_low, y_own_high, x_low, x_high
-    )
+    (coefficients,) = call(coarse_faces, [(16, LANES)], [(coarse_x // 2, coarse_y, LANES)])(faces)
+    y_low, y_high = call(pack_y, [y_shape] * 2)(own, faces, x_low, x_high)
     y_low, y_high = from_sides(y_low, y_high, "gy")
-    stack = (nx + 2 * RIM, ny + 4 * RIM, LANES)
+    stack = (nx + 2 * EDGE, ny + 4 * RIM, LANES)
     stack_1 = (coarse_x + 2 * RIM, coarse_y + 4 * RIM, LANES)
     half = stack_1[0] // 2
-    v_shape = (RIM // 2 * coarse_y, LANES)
+    v_shape = (RIM // 2 * coarse_y + 2 * ny, LANES)
+    w_shape = (half * RIM + 2 * (nx + 4), LANES)
     top, mid, chunk, v_low, v_high = call(
         functools.partial(level_down, axes),
-        [IN_VMEM] * 11,
-        [
-            (shape, IN_VMEM)
-            for shape in ((D + 1,) + stack, (D + 1,) + stack_1, (32, LANES), v_shape, v_shape)
-        ],
+        [(D + 1,) + stack, (D + 1,) + stack_1, (32, LANES), v_shape, v_shape],
         [stack, (nx // 2, ny, LANES), stack_1, (half, coarse_y + 2 * RIM, LANES)],
-    )(*fields, faces, coefficients, x_low, x_high, y_low, y_high)
-    pieces = gathered(chunk)
+    )(own, faces, coefficients, x_low, x_high, y_low, y_high)
+
+    blocks = passed_round(chunk, "gx", 2)
     v_low, v_high = from_sides(v_low, v_high, "gx")
-    w_low, w_high = call(pack_v, [IN_VMEM] * 3, [((half * RIM, LANES), IN_VMEM)] * 2)(mid, v_low, v_high)
+    slow = (len(blocks),) + chunk.shape
+    (pieces,) = call(functools.partial(stack_blocks, len(blocks)), [slow])(*blocks, v_low, v_high)
+    w_low, w_high = call(pack_v, [w_shape] * 2)(top, mid, v_low, v_high)
+    pieces = paired(pieces, "gx", 1)
     w_low, w_high = from_sides(w_low, w_high, "gy")
+    blocks = passed_round(pieces, "gy", 2)
+    slow = (len(blocks),) + pieces.shape
+    (pieces,) = call(functools.partial(stack_blocks, len(blocks)), [slow])(*blocks, w_low, w_high)
+    pieces = paired(pieces, "gy", 1)
     count = devices_x * nx // 16
     rows = devices_y * ny // 4
     coarsest = (devices_x * nx >> LEVELS - 1, devices_y * ny >> LEVELS - 1)
-    (out,) = call(
+    out = pl.pallas_call(
         functools.partial(level_up, axes, (devices_x, devices_y), 4 * max(coarsest)),
-        [IN_VMEM] * 7,
-        [((nx, ny, nz), IN_VMEM)],
-        [
-            (3, devices_x, rows, LANES),
-            stack_1,
-            stack_1,
-            (count + RIM, rows + 2 * PAD, LANES),
-            (2,) + stack,
-            (coarse_x + 2, ny + 2 * RIM, LANES),
+        out_shape=jax.ShapeDtypeStruct((nx, ny, nz), F32),
+        in_specs=[IN_VMEM] * 7,
+        out_specs=IN_VMEM,
+        scratch_shapes=[
+            pltpu.VMEM(shape, F32)
+            for shape in (
+                (3, devices_x, rows, LANES),
+                stack_1,
+                stack_1,
+                (count + RIM, rows + 2 * PAD, LANES),
+                (2,) + stack,
+                (coarse_x + 2, ny + 2 * RIM, LANES),
+            )
         ],
+        compiler_params=pltpu.CompilerParams(vmem_limit_bytes=24 * 2**20),
     )(pieces, top, mid, v_low, v_high, w_low, w_high)
     return out
 

time: 79.9 us -> 62.3 us (0.78)
  waiting for transfers between devices: 29.1 us -> 20.6 us
  local copies, waits for them, and re-layouts: 8.13 us -> 0 us
  Pallas kernels: 12.6 us -> 11.5 us
    unnamed x18 -> x0, local copies, waits for them, and re-layouts: 8.13 us -> none
    ppermute x8, waiting for transfers between devices: 17.9 us -> 12.1 us  [from_sides(): return (lax.ppermute(high, axis, up), lax.ppermute(low, axis, down))]
    ppermute x4, waiting for transfers between devices: 8.15 us -> 3.94 us  [passed_round(): lax.ppermute(block, axis, [(i, (i + distance) % count) for i in range(cou...]
    ppermute x8, starting transfers between devices: 21.8 us -> 24.4 us  [from_sides(): return (lax.ppermute(high, axis, up), lax.ppermute(low, axis, down))]
    ppermute x2, starting transfers between devices: 1.82 us -> 0.25 us  [paired(): lax.ppermute(block, axis, [(i, i ^ stride) for i in range(count)])]
    ppermute x2, waiting for transfers between devices: 3.11 us -> 4.52 us  [paired(): lax.ppermute(block, axis, [(i, i ^ stride) for i in range(count)])]
    pallas_call x6 -> x8, Pallas kernels: 12.6 us -> 11.5 us  [the longest x1 5.95 us: fused_cycle(): pl.pallas_call(functools.partial(level_up, axes, (devices_x, devices_y),...]
  transfers between devices with their start and end apart: 14 -> 14, of which waited for: 11 -> 10; matrix products, arithmetic and copies ran while one was open for 0% -> 0% of each run, Pallas kernels for 1% -> 1%
where the time goes in v5:
time: 62.3 us; the launch traced here: 61.9 us
  starting transfers between devices  29.7 us (48%)
  waiting for transfers between devices  20.6 us (33%)
  Pallas kernels  11.5 us (18%)
    ppermute x8, starting transfers between devices, from_sides(): return (lax.ppermute(high, axis, up), lax.ppermute(low, axis, down))  24.4 us
    ppermute x8, waiting for transfers between devices, from_sides(): return (lax.ppermute(high, axis, up), lax.ppermute(low, axis, down))  12.1 us
    pallas_call x1, Pallas kernels, fused_cycle(): pl.pallas_call(functools.partial(level_up, axes, (devices_x, devices_y),...  5.95 us
    pallas_call x7, Pallas kernels, launch(): pl.pallas_call(kernel, out_shape=[pltpu.VMEM(shape, F32) for shape in out...  5.52 us
    ppermute x4, starting transfers between devices, passed_round(): lax.ppermute(block, axis, [(i, (i + distance) % count) for i in range(cou...  5.02 us
    ppermute x2, waiting for transfers between devices, paired(): lax.ppermute(block, axis, [(i, i ^ stride) for i in range(count)])  4.52 us
    ppermute x4, waiting for transfers between devices, passed_round(): lax.ppermute(block, axis, [(i, (i + distance) % count) for i in range(cou...  3.94 us
  transfers between devices with their start and end apart: 14, of which 10 were waited for; matrix products, arithmetic and copies ran while one was open for 0% of the time, Pallas kernels for 1%

profile of v5, /device:TPU:1, one launch (start us, length us, event | category | flops | bytes accessed | tf_op | source)
XLA Modules:
  0.0 61.9 jit_solution(11672249565011211696)
XLA Ops:
  0.0 1.6 %shard_map.55 = (f32[5,16,16,128]{3,2,1,0:T(8,128)S(1)}, f32[240,128]{1,0:T(8,128)S(1)}, f32[240,128]{1,0:T(8,128)S(1)}, f32[3,8,8,128]{3,2,1,0:T(8,128)S(1)}) custom-call(f32[16,16,128]{2,1,0:T(8,128)} %refs_0_.1, f32[16,16,128]{2,1,0:T(8,128)} %refs_1_.1, f32[16,16,128]{2,1,0:T(8,128)} %refs_2_.1, f32[16,16,128]{2,1,0:T(8,128)} %refs_3_.1, ...), custom_call_target="tpu_custom_call" | custom-call | tf_op jit(solution)/shard_map/pallas_call | solution.py:695
  1.6 4.0 %collective-permute-start = (f32[240,128]{1,0:T(8,128)S(1)}, f32[240,128]{1,0:T(8,128)S(1)}, u32[]{:S(2)}, u32[]{:S(2)}) collective-permute-start(f32[240,128]{1,0:T(8,128)S(1)} %get-tuple-element.20), channel_id=1, source_target_pairs={{0,4},{4,8},{8,12},{12,16},{16,20},{20,24},{24,28},{1,5},{5,9},{9,... | collective-permute-start | bytes 368648 | tf_op jit(solution)/shard_map/ppermute | solution.py:711
  5.5 1.3 %collective-permute-start.1 = (f32[240,128]{1,0:T(8,128)S(1)}, f32[240,128]{1,0:T(8,128)S(1)}, u32[]{:S(2)}, u32[]{:S(2)}) collective-permute-start(f32[240,128]{1,0:T(8,128)S(1)} %get-tuple-element.21), channel_id=1, source_target_pairs={{4,0},{8,4},{12,8},{16,12},{20,16},{24,20},{28,24},{5,1},{9,5},{13... | collective-permute-start | bytes 368648 | tf_op jit(solution)/shard_map/ppermute | solution.py:711
  6.8 0.5 collective-permute-done.x_low
  7.4 3.8 %collective-permute-done.1.x_high = f32[240,128]{1,0:T(8,128)S(1)} collective-permute-done((f32[240,128]{1,0:T(8,128)S(1)}, f32[240,128]{1,0:T(8,128)S(1)}, u32[]{:S(2)}, u32[]{:S(2)}) %collective-permute-start.1) | collective-permute-done | bytes 122912 | tf_op jit(solution)/shard_map/ppermute | solution.py:711
  11.2 0.1 shard_map.57
  11.3 5.1 %collective-permute-start.2 = (f32[360,128]{1,0:T(8,128)S(1)}, f32[360,128]{1,0:T(8,128)S(1)}, u32[]{:S(2)}, u32[]{:S(2)}) collective-permute-start(f32[360,128]{1,0:T(8,128)S(1)} %get-tuple-element.22), channel_id=1, source_target_pairs={{0,1},{1,2},{2,3},{4,5},{5,6},{6,7},{8,9},{9,10},{10,11},{12,13},{... | collective-permute-start | bytes 552968 | tf_op jit(solution)/shard_map/ppermute | solution.py:711
  16.5 1.9 %collective-permute-start.3 = (f32[360,128]{1,0:T(8,128)S(1)}, f32[360,128]{1,0:T(8,128)S(1)}, u32[]{:S(2)}, u32[]{:S(2)}) collective-permute-start(f32[360,128]{1,0:T(8,128)S(1)} %get-tuple-element.23), channel_id=1, source_target_pairs={{1,0},{2,1},{3,2},{5,4},{6,5},{7,6},{9,8},{10,9},{11,10},{13,12},{... | collective-permute-start | bytes 552968 | tf_op jit(solution)/shard_map/ppermute | solution.py:711
  18.4 0.5 shard_map.56.coefficients
  18.9 0.1 collective-permute-done.2.y_low
  18.9 4.4 %collective-permute-done.3.y_high = f32[360,128]{1,0:T(8,128)S(1)} collective-permute-done((f32[360,128]{1,0:T(8,128)S(1)}, f32[360,128]{1,0:T(8,128)S(1)}, u32[]{:S(2)}, u32[]{:S(2)}) %collective-permute-start.3) | collective-permute-done | bytes 184352 | tf_op jit(solution)/shard_map/ppermute | solution.py:711
  23.3 3.2 %shard_map.58 = (f32[8,22,32,128]{3,2,1,0:T(8,128)S(1)}, f32[8,16,24,128]{3,2,1,0:T(8,128)S(1)}, f32[32,128]{1,0:T(8,128)S(1)}, f32[48,128]{1,0:T(8,128)S(1)}, f32[48,128]{1,0:T(8,128)S(1)}) custom-call(f32[5,16,16,128]{3,2,1,0:T(8,128)S(1)} %get-tuple-element.18.own, f32[3,8,8,128]{3,2,1,0:T(8,128)S(1)} %get-tuple-element.19.faces, ...), custom_call_target="tpu_custom_call" | custom-call | tf_op jit(solution)/shard_map/pallas_call | solution.py:695
  26.5 4.1 %collective-permute-start.7 = (f32[48,128]{1,0:T(8,128)S(1)}, f32[48,128]{1,0:T(8,128)S(1)}, u32[]{:S(2)}, u32[]{:S(2)}) collective-permute-start(f32[48,128]{1,0:T(8,128)S(1)} %get-tuple-element.25), channel_id=1, source_target_pairs={{0,4},{4,8},{8,12},{12,16},{16,20},{20,24},{24,28},{1,5},{5,9},{9,... | collective-permute-start | bytes 73736 | tf_op jit(solution)/shard_map/ppermute | solution.py:711
  30.5 1.3 %collective-permute-start.8 = (f32[48,128]{1,0:T(8,128)S(1)}, f32[48,128]{1,0:T(8,128)S(1)}, u32[]{:S(2)}, u32[]{:S(2)}) collective-permute-start(f32[48,128]{1,0:T(8,128)S(1)} %get-tuple-element.26), channel_id=1, source_target_pairs={{4,0},{8,4},{12,8},{16,12},{20,16},{24,20},{28,24},{5,1},{9,5},{13... | collective-permute-start | bytes 73736 | tf_op jit(solution)/shard_map/ppermute | solution.py:711
  31.8 4.5 %collective-permute-start.6 = (f32[32,128]{1,0:T(8,128)S(1)}, f32[32,128]{1,0:T(8,128)S(1)}, u32[]{:S(2)}, u32[]{:S(2)}) collective-permute-start(f32[32,128]{1,0:T(8,128)S(1)} %get-tuple-element.24.refs_0_), channel_id=1, source_target_pairs={{0,24},{4,28},{8,0},{12,4},{16,8},{20,12},{24,16},{28,20},{1,25},{... | collective-permute-start | bytes 49160 | tf_op jit(solution)/shard_map/ppermute | solution.py:723
  36.3 0.0 collective-permute-start.5
  36.3 0.5 collective-permute-start.4
  36.8 0.4 collective-permute-done.6.refs_3_
  37.2 2.6 %collective-permute-done.5.refs_2_ = f32[32,128]{1,0:T(8,128)S(1)} collective-permute-done((f32[32,128]{1,0:T(8,128)S(1)}, f32[32,128]{1,0:T(8,128)S(1)}, u32[]{:S(2)}, u32[]{:S(2)}) %collective-permute-start.5) | collective-permute-done | bytes 16416 | tf_op jit(solution)/shard_map/ppermute | solution.py:723
  39.8 0.9 %collective-permute-done.4.refs_1_ = f32[32,128]{1,0:T(8,128)S(1)} collective-permute-done((f32[32,128]{1,0:T(8,128)S(1)}, f32[32,128]{1,0:T(8,128)S(1)}, u32[]{:S(2)}, u32[]{:S(2)}) %collective-permute-start.4) | collective-permute-done | bytes 16416 | tf_op jit(solution)/shard_map/ppermute | solution.py:723
  40.7 0.0 collective-permute-done.7.refs_4_.x_low
  40.7 0.0 collective-permute-done.8.refs_5_.x_high
  40.7 0.2 collective-permute-start.9
  40.9 3.0 %collective-permute-done.9 = f32[4,32,128]{2,1,0:T(8,128)S(1)} collective-permute-done((f32[4,32,128]{2,1,0:T(8,128)S(1)}, f32[4,32,128]{2,1,0:T(8,128)S(1)}, u32[]{:S(2)}, u32[]{:S(2)}) %collective-permute-start.9) | collective-permute-done | bytes 65568 | tf_op jit(solution)/shard_map/ppermute | solution.py:716
  43.9 0.1 collective-permute-start.10
  44.0 0.1 shard_map.60
  44.2 4.9 %collective-permute-start.11 = (f32[72,128]{1,0:T(8,128)S(1)}, f32[72,128]{1,0:T(8,128)S(1)}, u32[]{:S(2)}, u32[]{:S(2)}) collective-permute-start(f32[72,128]{1,0:T(8,128)S(1)} %get-tuple-element.29), channel_id=1, source_target_pairs={{0,1},{1,2},{2,3},{4,5},{5,6},{6,7},{8,9},{9,10},{10,11},{12,13},{... | collective-permute-start | bytes 110600 | tf_op jit(solution)/shard_map/ppermute | solution.py:711
  49.0 1.9 %collective-permute-start.12 = (f32[72,128]{1,0:T(8,128)S(1)}, f32[72,128]{1,0:T(8,128)S(1)}, u32[]{:S(2)}, u32[]{:S(2)}) collective-permute-start(f32[72,128]{1,0:T(8,128)S(1)} %get-tuple-element.30), channel_id=1, source_target_pairs={{1,0},{2,1},{3,2},{5,4},{6,5},{7,6},{9,8},{10,9},{11,10},{13,12},{... | collective-permute-start | bytes 110600 | tf_op jit(solution)/shard_map/ppermute | solution.py:711
  51.0 0.0 collective-permute-done.11.refs_2_.y_low
  51.0 3.3 %collective-permute-done.12.refs_3_.y_high = f32[72,128]{1,0:T(8,128)S(1)} collective-permute-done((f32[72,128]{1,0:T(8,128)S(1)}, f32[72,128]{1,0:T(8,128)S(1)}, u32[]{:S(2)}, u32[]{:S(2)}) %collective-permute-start.12) | collective-permute-done | bytes 36896 | tf_op jit(solution)/shard_map/ppermute | solution.py:711
  54.3 0.0 collective-permute-done.10.refs_1_
  54.3 0.1 collective-permute-start.13
  54.4 1.5 %collective-permute-done.13 = f32[2,2,4,32,128]{4,3,2,1,0:T(8,128)S(1)} collective-permute-done((f32[2,2,4,32,128]{4,3,2,1,0:T(8,128)S(1)}, f32[2,2,4,32,128]{4,3,2,1,0:T(8,128)S(1)}, u32[]{:S(2)}, u32[]{:S(2)}) %collective-permute-start.13) | collective-permute-done | bytes 262176 | tf_op jit(solution)/shard_map/ppermute | solution.py:716
  56.0 6.0 %shard_map.62 = f32[16,16,128]{2,1,0:T(8,128)} custom-call(f32[2,2,2,4,32,128]{5,4,3,2,1,0:T(8,128)S(1)} %pad_maximum_fusion.pieces, f32[8,22,32,128]{3,2,1,0:T(8,128)S(1)} %get-tuple-element.27.top, f32[8,16,24,128]{3,2,1,0:T(8,128)S(1)} %get-tuple-element.28.mid, f32[48,128]{1,0:T(8,128)S(1)} %collective-permute-done.7.refs_4_.x_low, ...), custom_call_target="tpu_custom_call" | custom-call | tf_op jit(solution)/shard_map/pallas_call | solution.py:769
  (4 shorter events, 0.1 us)
Async XLA Ops:
  1.6 5.8 %collective-permute-start = (f32[240,128]{1,0:T(8,128)S(1)}, f32[240,128]{1,0:T(8,128)S(1)}, u32[]{:S(2)}, u32[]{:S(2)}) collective-permute-start(f32[240,128]{1,0:T(8,128)S(1)} %get-tuple-element.20), channel_id=1, source_target_pairs={{0,4},{4,8},{8,12},{12,16},{16,20},{20,24},{24,28},{1,5},{5,9},{9,... | collective-permute-start | bytes 368648 | tf_op jit(solution)/shard_map/ppermute | solution.py:711
  5.5 5.6 %collective-permute-start.1 = (f32[240,128]{1,0:T(8,128)S(1)}, f32[240,128]{1,0:T(8,128)S(1)}, u32[]{:S(2)}, u32[]{:S(2)}) collective-permute-start(f32[240,128]{1,0:T(8,128)S(1)} %get-tuple-element.21), channel_id=1, source_target_pairs={{4,0},{8,4},{12,8},{16,12},{20,16},{24,20},{28,24},{5,1},{9,5},{13... | collective-permute-start | bytes 368648 | tf_op jit(solution)/shard_map/ppermute | solution.py:711
  11.3 7.6 %collective-permute-start.2 = (f32[360,128]{1,0:T(8,128)S(1)}, f32[360,128]{1,0:T(8,128)S(1)}, u32[]{:S(2)}, u32[]{:S(2)}) collective-permute-start(f32[360,128]{1,0:T(8,128)S(1)} %get-tuple-element.22), channel_id=1, source_target_pairs={{0,1},{1,2},{2,3},{4,5},{5,6},{6,7},{8,9},{9,10},{10,11},{12,13},{... | collective-permute-start | bytes 552968 | tf_op jit(solution)/shard_map/ppermute | solution.py:711
  16.5 6.9 %collective-permute-start.3 = (f32[360,128]{1,0:T(8,128)S(1)}, f32[360,128]{1,0:T(8,128)S(1)}, u32[]{:S(2)}, u32[]{:S(2)}) collective-permute-start(f32[360,128]{1,0:T(8,128)S(1)} %get-tuple-element.23), channel_id=1, source_target_pairs={{1,0},{2,1},{3,2},{5,4},{6,5},{7,6},{9,8},{10,9},{11,10},{13,12},{... | collective-permute-start | bytes 552968 | tf_op jit(solution)/shard_map/ppermute | solution.py:711
  26.5 14.3 %collective-permute-start.7 = (f32[48,128]{1,0:T(8,128)S(1)}, f32[48,128]{1,0:T(8,128)S(1)}, u32[]{:S(2)}, u32[]{:S(2)}) collective-permute-start(f32[48,128]{1,0:T(8,128)S(1)} %get-tuple-element.25), channel_id=1, source_target_pairs={{0,4},{4,8},{8,12},{12,16},{16,20},{20,24},{24,28},{1,5},{5,9},{9,... | collective-permute-start | bytes 73736 | tf_op jit(solution)/shard_map/ppermute | solution.py:711
  30.5 10.2 %collective-permute-start.8 = (f32[48,128]{1,0:T(8,128)S(1)}, f32[48,128]{1,0:T(8,128)S(1)}, u32[]{:S(2)}, u32[]{:S(2)}) collective-permute-start(f32[48,128]{1,0:T(8,128)S(1)} %get-tuple-element.26), channel_id=1, source_target_pairs={{4,0},{8,4},{12,8},{16,12},{20,16},{24,20},{28,24},{5,1},{9,5},{13... | collective-permute-start | bytes 73736 | tf_op jit(solution)/shard_map/ppermute | solution.py:711
  31.8 5.4 %collective-permute-start.6 = (f32[32,128]{1,0:T(8,128)S(1)}, f32[32,128]{1,0:T(8,128)S(1)}, u32[]{:S(2)}, u32[]{:S(2)}) collective-permute-start(f32[32,128]{1,0:T(8,128)S(1)} %get-tuple-element.24.refs_0_), channel_id=1, source_target_pairs={{0,24},{4,28},{8,0},{12,4},{16,8},{20,12},{24,16},{28,20},{1,25},{... | collective-permute-start | bytes 49160 | tf_op jit(solution)/shard_map/ppermute | solution.py:723
  36.3 3.5 %collective-permute-start.5 = (f32[32,128]{1,0:T(8,128)S(1)}, f32[32,128]{1,0:T(8,128)S(1)}, u32[]{:S(2)}, u32[]{:S(2)}) collective-permute-start(f32[32,128]{1,0:T(8,128)S(1)} %get-tuple-element.24.refs_0_), channel_id=1, source_target_pairs={{0,16},{4,20},{8,24},{12,28},{16,0},{20,4},{24,8},{28,12},{1,17},{... | collective-permute-start | bytes 49160 | tf_op jit(solution)/shard_map/ppermute | solution.py:723
  36.3 4.4 %collective-permute-start.4 = (f32[32,128]{1,0:T(8,128)S(1)}, f32[32,128]{1,0:T(8,128)S(1)}, u32[]{:S(2)}, u32[]{:S(2)}) collective-permute-start(f32[32,128]{1,0:T(8,128)S(1)} %get-tuple-element.24.refs_0_), channel_id=1, source_target_pairs={{0,8},{4,12},{8,16},{12,20},{16,24},{20,28},{24,0},{28,4},{1,9},{5... | collective-permute-start | bytes 49160 | tf_op jit(solution)/shard_map/ppermute | solution.py:723
  40.7 3.2 %collective-permute-start.9 = (f32[4,32,128]{2,1,0:T(8,128)S(1)}, f32[4,32,128]{2,1,0:T(8,128)S(1)}, u32[]{:S(2)}, u32[]{:S(2)}) collective-permute-start(f32[4,32,128]{2,1,0:T(8,128)S(1)} %shard_map.59), channel_id=1, source_target_pairs={{0,4},{4,0},{8,12},{12,8},{16,20},{20,16},{24,28},{28,24},{1,5},{5... | collective-permute-start | bytes 196616 | tf_op jit(solution)/shard_map/ppermute | solution.py:716
  43.9 10.4 %collective-permute-start.10 = (f32[2,4,32,128]{3,2,1,0:T(8,128)S(1)}, f32[2,4,32,128]{3,2,1,0:T(8,128)S(1)}, u32[]{:S(2)}, u32[]{:S(2)}) collective-permute-start(f32[2,4,32,128]{3,2,1,0:T(8,128)S(1)} %pad_maximum_fusion.1.refs_0_), channel_id=1, source_target_pairs={{0,2},{1,3},{2,0},{3,1},{4,6},{5,7},{6,4},{7,5},{8,10},{9,11},{10,... | collective-permute-start | bytes 393224 | tf_op jit(solution)/shard_map/ppermute | solution.py:723
  44.2 6.8 %collective-permute-start.11 = (f32[72,128]{1,0:T(8,128)S(1)}, f32[72,128]{1,0:T(8,128)S(1)}, u32[]{:S(2)}, u32[]{:S(2)}) collective-permute-start(f32[72,128]{1,0:T(8,128)S(1)} %get-tuple-element.29), channel_id=1, source_target_pairs={{0,1},{1,2},{2,3},{4,5},{5,6},{6,7},{8,9},{9,10},{10,11},{12,13},{... | collective-permute-start | bytes 110600 | tf_op jit(solution)/shard_map/ppermute | solution.py:711
  49.0 5.3 %collective-permute-start.12 = (f32[72,128]{1,0:T(8,128)S(1)}, f32[72,128]{1,0:T(8,128)S(1)}, u32[]{:S(2)}, u32[]{:S(2)}) collective-permute-start(f32[72,128]{1,0:T(8,128)S(1)} %get-tuple-element.30), channel_id=1, source_target_pairs={{1,0},{2,1},{3,2},{5,4},{6,5},{7,6},{9,8},{10,9},{11,10},{13,12},{... | collective-permute-start | bytes 110600 | tf_op jit(solution)/shard_map/ppermute | solution.py:711
  54.3 1.6 %collective-permute-start.13 = (f32[2,2,4,32,128]{4,3,2,1,0:T(8,128)S(1)}, f32[2,2,4,32,128]{4,3,2,1,0:T(8,128)S(1)}, u32[]{:S(2)}, u32[]{:S(2)}) collective-permute-start(f32[2,2,4,32,128]{4,3,2,1,0:T(8,128)S(1)} %shard_map.61), channel_id=1, source_target_pairs={{0,1},{1,0},{2,3},{3,2},{4,5},{5,4},{6,7},{7,6},{8,9},{9,8},{10,11... | collective-permute-start | bytes 786440 | tf_op jit(solution)/shard_map/ppermute | solution.py:716

commit v6 on v5

--- a/solution.py
+++ b/solution.py
@@ -225,12 +225,13 @@
     out[2 * coarse : 3 * coarse] = 0.25 * fold_four([z[i] for i in range(4)], True)
 
 
-def weighted(lev, src, slab, start, rows):
+def weighted(lev, src, slab, start, rows, f=None):
     here = pl.ds(start, rows)
     below = pl.ds(start - 1, rows)
     above = pl.ds(start + 1, rows)
     v = src[slab, here]
-    total = lev[F, slab, here] + lev[FX, slab, here] * src[slab - 1, here]
+    f = lev.at[F] if f is None else f
+    total = f[slab, here] + lev[FX, slab, here] * src[slab - 1, here]
     total = total + lev[FX, slab + 1, here] * src[slab + 1, here]
     total = total + lev[FY, slab, here] * src[slab, below]
     total = total + lev[FY, slab, above] * src[slab, above]
@@ -239,8 +240,8 @@
     return v, total
 
 
-def swept(lev, src, slab, start, rows):
-    v, total = weighted(lev, src, slab, start, rows)
+def swept(lev, src, slab, start, rows, f=None):
+    v, total = weighted(lev, src, slab, start, rows, f)
     return (1.0 - OMEGA) * v + lev[W, slab, pl.ds(start, rows)] * total
 
 
@@ -414,10 +415,12 @@
             out[pl.ds(base_y + 2 * (2 + slab), 2)] = top[V, EDGE + slab, pl.ds(PAD + start, 2)]
 
 
-def stack_blocks(count, *refs):
-    out = refs[-1]
-    for index in range(count):
-        out[index] = refs[index][...]
+def stack_blocks(count, blocks, *refs):
+    for index in range(blocks):
+        refs[count][index] = refs[index][...]
+    for index in range(blocks, count):
+        if index + 1 - blocks < len(refs) - count:
+            refs[count + 1 + index - blocks][...] = refs[index][...]
 
 
 def pair_rows(values, stride):
@@ -519,11 +522,10 @@
     return level.sweep(level.sweep(v, f), f)
 
 
-def level_up(axes, grid, sweeps, pieces, top, mid, x_low, x_high, y_low, y_high, out, wide, one, two, tall, post, up):
+def level_two(axes, grid, sweeps, shape, pieces, out, wide, tall):
     devices_x, devices_y = grid
     me_x, me_y = lax.axis_index(axes[0]), lax.axis_index(axes[1])
-    coarse_x, coarse_y = mid.shape[1] - 2 * RIM, mid.shape[2] - 4 * RIM
-    own_x, own_y = coarse_x // 2, coarse_y // 2
+    own_x, own_y = shape
     quarter = LANES // 4
     reach = RIM // 2
     blocks = 4
@@ -535,7 +537,7 @@
     def piece(gx, gy):
         slow = (me_x // 2 - gx // 2 + devices_x // 2) % (devices_x // 2)
         far = (me_y // 2 - gy // 2 + devices_y // 2) % (devices_y // 2)
-        return ((me_y + gy) % 2, far, (me_x + gx) % 2, slow)
+        return ((me_y + gy) % 2, (me_x + gx) % 2 * (devices_y // 2) + far, slow)
 
     for ref in (wide, tall):
         ref[...] = jnp.zeros(ref.shape, F32)
@@ -582,6 +584,26 @@
         levels.append(levels[-1].coarser())
     e = listed_cycle(levels, sweeps, f)
 
+    for slab in range(count):
+        out[reach + slab, main] = e[slab]
+    for slab in range(reach):
+        out[slab, main] = jnp.where(lane < quarter, 0.0, roll_lanes(e[count - reach + slab], quarter))
+        out[reach + count + slab, main] = jnp.where(
+            lane >= LANES - quarter, 0.0, roll_lanes(e[slab], -quarter)
+        )
+    out[:, :PAD] = jnp.zeros((count + 2 * reach, PAD, LANES), F32)
+    out[:, PAD + rows :] = jnp.zeros((count + 2 * reach, PAD, LANES), F32)
+
+
+def level_up(axes, grid, coarse, top, mid, x_low, x_high, y_low, y_high, out, one, two, right, post, up):
+    devices_x, devices_y = grid
+    me_x, me_y = lax.axis_index(axes[0]), lax.axis_index(axes[1])
+    coarse_x, coarse_y = mid.shape[1] - 2 * RIM, mid.shape[2] - 4 * RIM
+    own_x, own_y = coarse_x // 2, coarse_y // 2
+    quarter = LANES // 4
+    reach = RIM // 2
+    window = own_y + RIM
+
     slabs, high = coarse_x + 2 * RIM, coarse_y + 2 * RIM
     half = slabs // 2
     inner = pl.ds(2 * RIM, coarse_y)
@@ -603,26 +625,15 @@
         f_rim = one[slab, body] * mid[D, slab, body] * (1.0 / OMEGA)
         if RIM <= slab < RIM + coarse_x:
             f_rim = jnp.where(own_row, mid[F, slab, body], f_rim)
-        mid[F, slab, body] = f_rim
-        two[slab, body] = swept(mid, one, slab, RIM, high)
-
-    extra = reach
-    tall[:, :PAD] = jnp.zeros((count + 2 * extra, PAD, LANES), F32)
-    tall[:, PAD + rows :] = jnp.zeros((count + 2 * extra, PAD, LANES), F32)
-    for slab in range(count):
-        tall[extra + slab, main] = e[slab]
-    for slab in range(extra):
-        tall[slab, main] = jnp.where(lane < quarter, 0.0, roll_lanes(e[count - extra + slab], quarter))
-        tall[extra + count + slab, main] = jnp.where(
-            lane >= LANES - quarter, 0.0, roll_lanes(e[slab], -quarter)
-        )
-    per_block = count // own_x
+        right[slab, body] = f_rim
+        two[slab, body] = swept(mid, one, slab, RIM, high, right)
+
+    per_block = (coarse.shape[0] - 2 * reach) // own_x
     base = me_x % per_block * own_x
     mine = None
     for gy in range(devices_y):
         place = pl.ds(PAD + gy * own_y - reach, window)
-        values = tall[pl.ds(base, half), place, :]
-        values = jnp.where(me_y == gy, values, 0.0)
+        values = jnp.where(me_y == gy, coarse[pl.ds(base, half), place, :], 0.0)
         mine = values if mine is None else mine + values
     source = lax.broadcasted_iota(jnp.int32, (LANES, LANES), 0)
     target = lax.broadcasted_iota(jnp.int32, (LANES, LANES), 1)
@@ -636,9 +647,9 @@
             if 1 <= slab < slabs - 1:
                 two[slab, body] = two[slab, body] + up[pair, :high]
     for slab in range(2, slabs - 2):
-        one[slab, body] = swept(mid, two, slab, RIM, high)
+        one[slab, body] = swept(mid, two, slab, RIM, high, right)
     for slab in range(3, slabs - 3):
-        two[slab, body] = swept(mid, one, slab, RIM, high)
+        two[slab, body] = swept(mid, one, slab, RIM, high, right)
 
     nx, ny = out.shape[:2]
     steps = coarse_x + 2
@@ -721,6 +732,21 @@
     blocks = [block]
     for distance in range(stride, count, stride):
         blocks.append(lax.ppermute(block, axis, [(i, (i + distance) % count) for i in range(count)]))
+    return blocks
+
+
+def passed_across(block):
+    count, size = lax.axis_size("gx"), lax.axis_size("gy")
+    blocks = []
+    for side in range(2):
+        for distance in range(0, size, 2):
+            route = [
+                (x * size + y, (x ^ side) * size + (y + distance) % size)
+                for x in range(count)
+                for y in range(size)
+            ]
+            moved = side + distance > 0
+            blocks.append(lax.ppermute(block, ("gx", "gy"), route) if moved else block)
     return blocks
 
 
@@ -753,38 +779,40 @@
     )(own, faces, coefficients, x_low, x_high, y_low, y_high)
 
     blocks = passed_round(chunk, "gx", 2)
+    slow = (len(blocks),) + chunk.shape
+    pieces, v_low, v_high = call(
+        functools.partial(stack_blocks, len(blocks) + 2, len(blocks)), [slow, v_shape, v_shape]
+    )(*blocks, v_low, v_high)
+    blocks = passed_across(pieces)
     v_low, v_high = from_sides(v_low, v_high, "gx")
-    slow = (len(blocks),) + chunk.shape
-    (pieces,) = call(functools.partial(stack_blocks, len(blocks)), [slow])(*blocks, v_low, v_high)
+    slow = (len(blocks),) + pieces.shape
+    (pieces,) = call(functools.partial(stack_blocks, len(blocks) + 2, len(blocks)), [slow])(
+        *blocks, v_low, v_high
+    )
+    pieces = paired(pieces, "gy", 1)
     w_low, w_high = call(pack_v, [w_shape] * 2)(top, mid, v_low, v_high)
-    pieces = paired(pieces, "gx", 1)
     w_low, w_high = from_sides(w_low, w_high, "gy")
-    blocks = passed_round(pieces, "gy", 2)
-    slow = (len(blocks),) + pieces.shape
-    (pieces,) = call(functools.partial(stack_blocks, len(blocks)), [slow])(*blocks, w_low, w_high)
-    pieces = paired(pieces, "gy", 1)
     count = devices_x * nx // 16
     rows = devices_y * ny // 4
+    grid = (devices_x, devices_y)
     coarsest = (devices_x * nx >> LEVELS - 1, devices_y * ny >> LEVELS - 1)
-    out = pl.pallas_call(
-        functools.partial(level_up, axes, (devices_x, devices_y), 4 * max(coarsest)),
+    wide = (count + RIM, rows + 2 * PAD, LANES)
+    (coarse,) = call(
+        functools.partial(level_two, axes, grid, 4 * max(coarsest), (nx // 4, ny // 4)),
+        [wide],
+        [(3, devices_x, rows, LANES), wide],
+    )(pieces)
+    return pl.pallas_call(
+        functools.partial(level_up, axes, grid),
         out_shape=jax.ShapeDtypeStruct((nx, ny, nz), F32),
         in_specs=[IN_VMEM] * 7,
         out_specs=IN_VMEM,
         scratch_shapes=[
             pltpu.VMEM(shape, F32)
-            for shape in (
-                (3, devices_x, rows, LANES),
-                stack_1,
-                stack_1,
-                (count + RIM, rows + 2 * PAD, LANES),
-                (2,) + stack,
-                (coarse_x + 2, ny + 2 * RIM, LANES),
-            )
+            for shape in (stack_1, stack_1, stack_1, (2,) + stack, (coarse_x + 2, ny + 2 * RIM, LANES))
         ],
         compiler_params=pltpu.CompilerParams(vmem_limit_bytes=24 * 2**20),
-    )(pieces, top, mid, v_low, v_high, w_low, w_high)
-    return out
+    )(coarse, top, mid, v_low, v_high, w_low, w_high)
 
 
 def with_halo(block, sides, width):

time: 62.3 us -> 59.1 us (0.949)
  waiting for transfers between devices: 20.6 us -> 16.1 us
  starting transfers between devices: 29.7 us -> 31 us
    ppermute x2 -> x1, waiting for transfers between devices: 4.52 us -> 0.01 us  [paired(): lax.ppermute(block, axis, [(i, i ^ stride) for i in range(count)])]
    pallas_call x7 -> x8, Pallas kernels: 5.52 us -> 8.7 us  [launch(): pl.pallas_call(kernel, out_shape=[pltpu.VMEM(shape, F32) for shape in out...]
    pallas_call x1, Pallas kernels: 5.95 us -> 2.85 us  [fused_cycle(): pl.pallas_call(functools.partial(level_up, axes, grid), out_shape=jax.Sha...]
    ppermute x0 -> x3, starting transfers between devices: none -> 2.73 us  [passed_across(): blocks.append(lax.ppermute(block, ('gx', 'gy'), route) if moved else block)]
    ppermute x8, starting transfers between devices: 24.4 us -> 21.9 us  [from_sides(): return (lax.ppermute(high, axis, up), lax.ppermute(low, axis, down))]
    ppermute x2 -> x1, starting transfers between devices: 0.25 us -> 2.26 us  [paired(): lax.ppermute(block, axis, [(i, i ^ stride) for i in range(count)])]
    ppermute x4 -> x3, starting transfers between devices: 5.02 us -> 4.08 us  [passed_round(): lax.ppermute(block, axis, [(i, (i + distance) % count) for i in range(cou...]
    ppermute x4 -> x3, waiting for transfers between devices: 3.94 us -> 3.93 us  [passed_round(): lax.ppermute(block, axis, [(i, (i + distance) % count) for i in range(cou...]
  transfers between devices with their start and end apart: 14 -> 15, of which waited for: 10 -> 9; matrix products, arithmetic and copies ran while one was open for 0% -> 0% of each run, Pallas kernels for 1% -> 6%
where the time goes in v6:
time: 59.1 us; the launch traced here: 58.8 us
  starting transfers between devices  31 us (52%)
  waiting for transfers between devices  16.1 us (27%)
  Pallas kernels  11.5 us (19%)
    ppermute x8, starting transfers between devices, from_sides(): return (lax.ppermute(high, axis, up), lax.ppermute(low, axis, down))  21.9 us
    ppermute x8, waiting for transfers between devices, from_sides(): return (lax.ppermute(high, axis, up), lax.ppermute(low, axis, down))  12.2 us
    pallas_call x8, Pallas kernels, launch(): pl.pallas_call(kernel, out_shape=[pltpu.VMEM(shape, F32) for shape in out...  8.7 us
    ppermute x3, starting transfers between devices, passed_round(): lax.ppermute(block, axis, [(i, (i + distance) % count) for i in range(cou...  4.08 us
    ppermute x3, waiting for transfers between devices, passed_round(): lax.ppermute(block, axis, [(i, (i + distance) % count) for i in range(cou...  3.93 us
    pallas_call x1, Pallas kernels, fused_cycle(): pl.pallas_call(functools.partial(level_up, axes, grid), out_shape=jax.Sha...  2.85 us
    ppermute x3, starting transfers between devices, passed_across(): blocks.append(lax.ppermute(block, ('gx', 'gy'), route) if moved else block)  2.73 us
    ppermute x1, starting transfers between devices, paired(): lax.ppermute(block, axis, [(i, i ^ stride) for i in range(count)])  2.26 us
  transfers between devices with their start and end apart: 15, of which 9 were waited for; matrix products, arithmetic and copies ran while one was open for 0% of the time, Pallas kernels for 6%

profile of v6, /device:TPU:1, one launch (start us, length us, event | category | flops | bytes accessed | tf_op | source)
XLA Modules:
  0.0 58.8 jit_solution(10135118828041450561)
XLA Ops:
  0.0 1.6 %shard_map.55 = (f32[5,16,16,128]{3,2,1,0:T(8,128)S(1)}, f32[240,128]{1,0:T(8,128)S(1)}, f32[240,128]{1,0:T(8,128)S(1)}, f32[3,8,8,128]{3,2,1,0:T(8,128)S(1)}) custom-call(f32[16,16,128]{2,1,0:T(8,128)} %refs_0_.1, f32[16,16,128]{2,1,0:T(8,128)} %refs_1_.1, f32[16,16,128]{2,1,0:T(8,128)} %refs_2_.1, f32[16,16,128]{2,1,0:T(8,128)} %refs_3_.1, ...), custom_call_target="tpu_custom_call" | custom-call | tf_op jit(solution)/shard_map/pallas_call | solution.py:706
  1.6 4.0 %collective-permute-start = (f32[240,128]{1,0:T(8,128)S(1)}, f32[240,128]{1,0:T(8,128)S(1)}, u32[]{:S(2)}, u32[]{:S(2)}) collective-permute-start(f32[240,128]{1,0:T(8,128)S(1)} %get-tuple-element.23), channel_id=1, source_target_pairs={{0,4},{4,8},{8,12},{12,16},{16,20},{20,24},{24,28},{1,5},{5,9},{9,... | collective-permute-start | bytes 368648 | tf_op jit(solution)/shard_map/ppermute | solution.py:722
  5.5 1.3 %collective-permute-start.1 = (f32[240,128]{1,0:T(8,128)S(1)}, f32[240,128]{1,0:T(8,128)S(1)}, u32[]{:S(2)}, u32[]{:S(2)}) collective-permute-start(f32[240,128]{1,0:T(8,128)S(1)} %get-tuple-element.24), channel_id=1, source_target_pairs={{4,0},{8,4},{12,8},{16,12},{20,16},{24,20},{28,24},{5,1},{9,5},{13... | collective-permute-start | bytes 368648 | tf_op jit(solution)/shard_map/ppermute | solution.py:722
  6.8 0.5 collective-permute-done.x_low
  7.4 3.8 %collective-permute-done.1.x_high = f32[240,128]{1,0:T(8,128)S(1)} collective-permute-done((f32[240,128]{1,0:T(8,128)S(1)}, f32[240,128]{1,0:T(8,128)S(1)}, u32[]{:S(2)}, u32[]{:S(2)}) %collective-permute-start.1) | collective-permute-done | bytes 122912 | tf_op jit(solution)/shard_map/ppermute | solution.py:722
  11.2 0.1 shard_map.57
  11.3 5.1 %collective-permute-start.2 = (f32[360,128]{1,0:T(8,128)S(1)}, f32[360,128]{1,0:T(8,128)S(1)}, u32[]{:S(2)}, u32[]{:S(2)}) collective-permute-start(f32[360,128]{1,0:T(8,128)S(1)} %get-tuple-element.25), channel_id=1, source_target_pairs={{0,1},{1,2},{2,3},{4,5},{5,6},{6,7},{8,9},{9,10},{10,11},{12,13},{... | collective-permute-start | bytes 552968 | tf_op jit(solution)/shard_map/ppermute | solution.py:722
  16.5 1.9 %collective-permute-start.3 = (f32[360,128]{1,0:T(8,128)S(1)}, f32[360,128]{1,0:T(8,128)S(1)}, u32[]{:S(2)}, u32[]{:S(2)}) collective-permute-start(f32[360,128]{1,0:T(8,128)S(1)} %get-tuple-element.26), channel_id=1, source_target_pairs={{1,0},{2,1},{3,2},{5,4},{6,5},{7,6},{9,8},{10,9},{11,10},{13,12},{... | collective-permute-start | bytes 552968 | tf_op jit(solution)/shard_map/ppermute | solution.py:722
  18.4 0.5 shard_map.56.coefficients
  18.9 0.1 collective-permute-done.2.y_low
  18.9 4.4 %collective-permute-done.3.y_high = f32[360,128]{1,0:T(8,128)S(1)} collective-permute-done((f32[360,128]{1,0:T(8,128)S(1)}, f32[360,128]{1,0:T(8,128)S(1)}, u32[]{:S(2)}, u32[]{:S(2)}) %collective-permute-start.3) | collective-permute-done | bytes 184352 | tf_op jit(solution)/shard_map/ppermute | solution.py:722
  23.3 3.2 %shard_map.58 = (f32[8,22,32,128]{3,2,1,0:T(8,128)S(1)}, f32[8,16,24,128]{3,2,1,0:T(8,128)S(1)}, f32[32,128]{1,0:T(8,128)S(1)}, f32[48,128]{1,0:T(8,128)S(1)}, f32[48,128]{1,0:T(8,128)S(1)}) custom-call(f32[5,16,16,128]{3,2,1,0:T(8,128)S(1)} %get-tuple-element.21.own, f32[3,8,8,128]{3,2,1,0:T(8,128)S(1)} %get-tuple-element.22.faces, ...), custom_call_target="tpu_custom_call" | custom-call | tf_op jit(solution)/shard_map/pallas_call | solution.py:706
  26.5 3.6 %collective-permute-start.6 = (f32[32,128]{1,0:T(8,128)S(1)}, f32[32,128]{1,0:T(8,128)S(1)}, u32[]{:S(2)}, u32[]{:S(2)}) collective-permute-start(f32[32,128]{1,0:T(8,128)S(1)} %get-tuple-element.27.refs_0_), channel_id=1, source_target_pairs={{0,24},{4,28},{8,0},{12,4},{16,8},{20,12},{24,16},{28,20},{1,25},{... | collective-permute-start | bytes 49160 | tf_op jit(solution)/shard_map/ppermute | solution.py:734
  30.1 0.0 collective-permute-start.5
  30.1 0.5 collective-permute-start.4
  30.6 0.4 collective-permute-done.6.refs_3_
  31.0 2.6 %collective-permute-done.5.refs_2_ = f32[32,128]{1,0:T(8,128)S(1)} collective-permute-done((f32[32,128]{1,0:T(8,128)S(1)}, f32[32,128]{1,0:T(8,128)S(1)}, u32[]{:S(2)}, u32[]{:S(2)}) %collective-permute-start.5) | collective-permute-done | bytes 16416 | tf_op jit(solution)/shard_map/ppermute | solution.py:734
  33.6 0.9 %collective-permute-done.4.refs_1_ = f32[32,128]{1,0:T(8,128)S(1)} collective-permute-done((f32[32,128]{1,0:T(8,128)S(1)}, f32[32,128]{1,0:T(8,128)S(1)}, u32[]{:S(2)}, u32[]{:S(2)}) %collective-permute-start.4) | collective-permute-done | bytes 16416 | tf_op jit(solution)/shard_map/ppermute | solution.py:734
  34.5 0.1 collective-permute-start.9
  34.6 1.1 %collective-permute-start.8 = (f32[4,32,128]{2,1,0:T(8,128)S(1)}, f32[4,32,128]{2,1,0:T(8,128)S(1)}, u32[]{:S(2)}, u32[]{:S(2)}) collective-permute-start(f32[4,32,128]{2,1,0:T(8,128)S(1)} %get-tuple-element.30.refs_0_), channel_id=1, source_target_pairs={{0,4},{1,5},{2,6},{3,7},{4,0},{5,1},{6,2},{7,3},{8,12},{9,13},{10,... | collective-permute-start | bytes 196616 | tf_op jit(solution)/shard_map/ppermute | solution.py:749
  35.7 1.6 %collective-permute-start.7 = (f32[4,32,128]{2,1,0:T(8,128)S(1)}, f32[4,32,128]{2,1,0:T(8,128)S(1)}, u32[]{:S(2)}, u32[]{:S(2)}) collective-permute-start(f32[4,32,128]{2,1,0:T(8,128)S(1)} %get-tuple-element.30.refs_0_), channel_id=1, source_target_pairs={{0,2},{1,3},{2,0},{3,1},{4,6},{5,7},{6,4},{7,5},{8,10},{9,11},{10,... | collective-permute-start | bytes 196616 | tf_op jit(solution)/shard_map/ppermute | solution.py:749
  37.2 2.9 %collective-permute-start.10 = (f32[48,128]{1,0:T(8,128)S(1)}, f32[48,128]{1,0:T(8,128)S(1)}, u32[]{:S(2)}, u32[]{:S(2)}) collective-permute-start(f32[48,128]{1,0:T(8,128)S(1)} %get-tuple-element.31), channel_id=1, source_target_pairs={{0,4},{4,8},{8,12},{12,16},{16,20},{20,24},{24,28},{1,5},{5,9},{9,... | collective-permute-start | bytes 73736 | tf_op jit(solution)/shard_map/ppermute | solution.py:722
  40.1 1.3 %collective-permute-start.11 = (f32[48,128]{1,0:T(8,128)S(1)}, f32[48,128]{1,0:T(8,128)S(1)}, u32[]{:S(2)}, u32[]{:S(2)}) collective-permute-start(f32[48,128]{1,0:T(8,128)S(1)} %get-tuple-element.32), channel_id=1, source_target_pairs={{4,0},{8,4},{12,8},{16,12},{20,16},{24,20},{28,24},{5,1},{9,5},{13... | collective-permute-start | bytes 73736 | tf_op jit(solution)/shard_map/ppermute | solution.py:722
  41.4 0.0 collective-permute-done.10.refs_4_.x_low
  41.4 3.3 %collective-permute-done.11.refs_5_.x_high = f32[48,128]{1,0:T(8,128)S(1)} collective-permute-done((f32[48,128]{1,0:T(8,128)S(1)}, f32[48,128]{1,0:T(8,128)S(1)}, u32[]{:S(2)}, u32[]{:S(2)}) %collective-permute-start.11) | collective-permute-done | bytes 24608 | tf_op jit(solution)/shard_map/ppermute | solution.py:722
  44.7 0.0 collective-permute-done.9.refs_3_
  44.7 0.0 collective-permute-done.8.refs_2_
  44.7 0.0 collective-permute-done.7.refs_1_
  44.7 2.3 %collective-permute-start.12 = (f32[4,4,32,128]{3,2,1,0:T(8,128)S(1)}, f32[4,4,32,128]{3,2,1,0:T(8,128)S(1)}, u32[]{:S(2)}, u32[]{:S(2)}) collective-permute-start(f32[4,4,32,128]{3,2,1,0:T(8,128)S(1)} %shard_map.60), channel_id=1, source_target_pairs={{0,1},{1,0},{2,3},{3,2},{4,5},{5,4},{6,7},{7,6},{8,9},{9,8},{10,11... | collective-permute-start | bytes 786440 | tf_op jit(solution)/shard_map/ppermute | solution.py:727
  47.0 0.1 shard_map.62
  47.1 3.5 %collective-permute-start.13 = (f32[72,128]{1,0:T(8,128)S(1)}, f32[72,128]{1,0:T(8,128)S(1)}, u32[]{:S(2)}, u32[]{:S(2)}) collective-permute-start(f32[72,128]{1,0:T(8,128)S(1)} %get-tuple-element.35), channel_id=1, source_target_pairs={{0,1},{1,2},{2,3},{4,5},{5,6},{6,7},{8,9},{9,10},{10,11},{12,13},{... | collective-permute-start | bytes 110600 | tf_op jit(solution)/shard_map/ppermute | solution.py:722
  50.7 1.9 %collective-permute-start.14 = (f32[72,128]{1,0:T(8,128)S(1)}, f32[72,128]{1,0:T(8,128)S(1)}, u32[]{:S(2)}, u32[]{:S(2)}) collective-permute-start(f32[72,128]{1,0:T(8,128)S(1)} %get-tuple-element.36), channel_id=1, source_target_pairs={{1,0},{2,1},{3,2},{5,4},{6,5},{7,6},{9,8},{10,9},{11,10},{13,12},{... | collective-permute-start | bytes 110600 | tf_op jit(solution)/shard_map/ppermute | solution.py:722
  52.6 0.0 collective-permute-done.12
  52.7 3.2 %shard_map.61.coarse = f32[12,32,128]{2,1,0:T(8,128)S(1)} custom-call(f32[2,4,4,32,128]{4,3,2,1,0:T(8,128)S(1)} %pad_maximum_fusion.pieces), custom_call_target="tpu_custom_call" | custom-call | tf_op jit(solution)/shard_map/pallas_call | solution.py:706
  55.8 0.0 collective-permute-done.13.y_low
  55.9 0.1 collective-permute-done.14.y_high
  56.0 2.8 %shard_map.63 = f32[16,16,128]{2,1,0:T(8,128)} custom-call(f32[12,32,128]{2,1,0:T(8,128)S(1)} %shard_map.61.coarse, f32[8,22,32,128]{3,2,1,0:T(8,128)S(1)} %get-tuple-element.33.top, f32[8,16,24,128]{3,2,1,0:T(8,128)S(1)} %get-tuple-element.34.mid, f32[48,128]{1,0:T(8,128)S(1)} %collective-permute-done.10.refs_4_.x_low, ...), custom_call_target="tpu_custom_call" | custom-call | tf_op jit(solution)/shard_map/pallas_call | solution.py:805
  (3 shorter events, 0.1 us)
Async XLA Ops:
  1.6 5.8 %collective-permute-start = (f32[240,128]{1,0:T(8,128)S(1)}, f32[240,128]{1,0:T(8,128)S(1)}, u32[]{:S(2)}, u32[]{:S(2)}) collective-permute-start(f32[240,128]{1,0:T(8,128)S(1)} %get-tuple-element.23), channel_id=1, source_target_pairs={{0,4},{4,8},{8,12},{12,16},{16,20},{20,24},{24,28},{1,5},{5,9},{9,... | collective-permute-start | bytes 368648 | tf_op jit(solution)/shard_map/ppermute | solution.py:722
  5.5 5.6 %collective-permute-start.1 = (f32[240,128]{1,0:T(8,128)S(1)}, f32[240,128]{1,0:T(8,128)S(1)}, u32[]{:S(2)}, u32[]{:S(2)}) collective-permute-start(f32[240,128]{1,0:T(8,128)S(1)} %get-tuple-element.24), channel_id=1, source_target_pairs={{4,0},{8,4},{12,8},{16,12},{20,16},{24,20},{28,24},{5,1},{9,5},{13... | collective-permute-start | bytes 368648 | tf_op jit(solution)/shard_map/ppermute | solution.py:722
  11.3 7.6 %collective-permute-start.2 = (f32[360,128]{1,0:T(8,128)S(1)}, f32[360,128]{1,0:T(8,128)S(1)}, u32[]{:S(2)}, u32[]{:S(2)}) collective-permute-start(f32[360,128]{1,0:T(8,128)S(1)} %get-tuple-element.25), channel_id=1, source_target_pairs={{0,1},{1,2},{2,3},{4,5},{5,6},{6,7},{8,9},{9,10},{10,11},{12,13},{... | collective-permute-start | bytes 552968 | tf_op jit(solution)/shard_map/ppermute | solution.py:722
  16.5 6.9 %collective-permute-start.3 = (f32[360,128]{1,0:T(8,128)S(1)}, f32[360,128]{1,0:T(8,128)S(1)}, u32[]{:S(2)}, u32[]{:S(2)}) collective-permute-start(f32[360,128]{1,0:T(8,128)S(1)} %get-tuple-element.26), channel_id=1, source_target_pairs={{1,0},{2,1},{3,2},{5,4},{6,5},{7,6},{9,8},{10,9},{11,10},{13,12},{... | collective-permute-start | bytes 552968 | tf_op jit(solution)/shard_map/ppermute | solution.py:722
  26.5 4.5 %collective-permute-start.6 = (f32[32,128]{1,0:T(8,128)S(1)}, f32[32,128]{1,0:T(8,128)S(1)}, u32[]{:S(2)}, u32[]{:S(2)}) collective-permute-start(f32[32,128]{1,0:T(8,128)S(1)} %get-tuple-element.27.refs_0_), channel_id=1, source_target_pairs={{0,24},{4,28},{8,0},{12,4},{16,8},{20,12},{24,16},{28,20},{1,25},{... | collective-permute-start | bytes 49160 | tf_op jit(solution)/shard_map/ppermute | solution.py:734
  30.1 3.5 %collective-permute-start.5 = (f32[32,128]{1,0:T(8,128)S(1)}, f32[32,128]{1,0:T(8,128)S(1)}, u32[]{:S(2)}, u32[]{:S(2)}) collective-permute-start(f32[32,128]{1,0:T(8,128)S(1)} %get-tuple-element.27.refs_0_), channel_id=1, source_target_pairs={{0,16},{4,20},{8,24},{12,28},{16,0},{20,4},{24,8},{28,12},{1,17},{... | collective-permute-start | bytes 49160 | tf_op jit(solution)/shard_map/ppermute | solution.py:734
  30.1 4.4 %collective-permute-start.4 = (f32[32,128]{1,0:T(8,128)S(1)}, f32[32,128]{1,0:T(8,128)S(1)}, u32[]{:S(2)}, u32[]{:S(2)}) collective-permute-start(f32[32,128]{1,0:T(8,128)S(1)} %get-tuple-element.27.refs_0_), channel_id=1, source_target_pairs={{0,8},{4,12},{8,16},{12,20},{16,24},{20,28},{24,0},{28,4},{1,9},{5... | collective-permute-start | bytes 49160 | tf_op jit(solution)/shard_map/ppermute | solution.py:734
  34.5 10.2 %collective-permute-start.9 = (f32[4,32,128]{2,1,0:T(8,128)S(1)}, f32[4,32,128]{2,1,0:T(8,128)S(1)}, u32[]{:S(2)}, u32[]{:S(2)}) collective-permute-start(f32[4,32,128]{2,1,0:T(8,128)S(1)} %get-tuple-element.30.refs_0_), channel_id=1, source_target_pairs={{0,6},{1,7},{2,4},{3,5},{4,2},{5,3},{6,0},{7,1},{8,14},{9,15},{10,... | collective-permute-start | bytes 196616 | tf_op jit(solution)/shard_map/ppermute | solution.py:749
  34.6 10.1 %collective-permute-start.8 = (f32[4,32,128]{2,1,0:T(8,128)S(1)}, f32[4,32,128]{2,1,0:T(8,128)S(1)}, u32[]{:S(2)}, u32[]{:S(2)}) collective-permute-start(f32[4,32,128]{2,1,0:T(8,128)S(1)} %get-tuple-element.30.refs_0_), channel_id=1, source_target_pairs={{0,4},{1,5},{2,6},{3,7},{4,0},{5,1},{6,2},{7,3},{8,12},{9,13},{10,... | collective-permute-start | bytes 196616 | tf_op jit(solution)/shard_map/ppermute | solution.py:749
  35.7 9.1 %collective-permute-start.7 = (f32[4,32,128]{2,1,0:T(8,128)S(1)}, f32[4,32,128]{2,1,0:T(8,128)S(1)}, u32[]{:S(2)}, u32[]{:S(2)}) collective-permute-start(f32[4,32,128]{2,1,0:T(8,128)S(1)} %get-tuple-element.30.refs_0_), channel_id=1, source_target_pairs={{0,2},{1,3},{2,0},{3,1},{4,6},{5,7},{6,4},{7,5},{8,10},{9,11},{10,... | collective-permute-start | bytes 196616 | tf_op jit(solution)/shard_map/ppermute | solution.py:749
  37.2 4.2 %collective-permute-start.10 = (f32[48,128]{1,0:T(8,128)S(1)}, f32[48,128]{1,0:T(8,128)S(1)}, u32[]{:S(2)}, u32[]{:S(2)}) collective-permute-start(f32[48,128]{1,0:T(8,128)S(1)} %get-tuple-element.31), channel_id=1, source_target_pairs={{0,4},{4,8},{8,12},{12,16},{16,20},{20,24},{24,28},{1,5},{5,9},{9,... | collective-permute-start | bytes 73736 | tf_op jit(solution)/shard_map/ppermute | solution.py:722
  40.1 4.6 %collective-permute-start.11 = (f32[48,128]{1,0:T(8,128)S(1)}, f32[48,128]{1,0:T(8,128)S(1)}, u32[]{:S(2)}, u32[]{:S(2)}) collective-permute-start(f32[48,128]{1,0:T(8,128)S(1)} %get-tuple-element.32), channel_id=1, source_target_pairs={{4,0},{8,4},{12,8},{16,12},{20,16},{24,20},{28,24},{5,1},{9,5},{13... | collective-permute-start | bytes 73736 | tf_op jit(solution)/shard_map/ppermute | solution.py:722
  44.7 7.9 %collective-permute-start.12 = (f32[4,4,32,128]{3,2,1,0:T(8,128)S(1)}, f32[4,4,32,128]{3,2,1,0:T(8,128)S(1)}, u32[]{:S(2)}, u32[]{:S(2)}) collective-permute-start(f32[4,4,32,128]{3,2,1,0:T(8,128)S(1)} %shard_map.60), channel_id=1, source_target_pairs={{0,1},{1,0},{2,3},{3,2},{4,5},{5,4},{6,7},{7,6},{8,9},{9,8},{10,11... | collective-permute-start | bytes 786440 | tf_op jit(solution)/shard_map/ppermute | solution.py:727
  47.1 8.7 %collective-permute-start.13 = (f32[72,128]{1,0:T(8,128)S(1)}, f32[72,128]{1,0:T(8,128)S(1)}, u32[]{:S(2)}, u32[]{:S(2)}) collective-permute-start(f32[72,128]{1,0:T(8,128)S(1)} %get-tuple-element.35), channel_id=1, source_target_pairs={{0,1},{1,2},{2,3},{4,5},{5,6},{6,7},{8,9},{9,10},{10,11},{12,13},{... | collective-permute-start | bytes 110600 | tf_op jit(solution)/shard_map/ppermute | solution.py:722
  50.7 5.3 %collective-permute-start.14 = (f32[72,128]{1,0:T(8,128)S(1)}, f32[72,128]{1,0:T(8,128)S(1)}, u32[]{:S(2)}, u32[]{:S(2)}) collective-permute-start(f32[72,128]{1,0:T(8,128)S(1)} %get-tuple-element.36), channel_id=1, source_target_pairs={{1,0},{2,1},{3,2},{5,4},{6,5},{7,6},{9,8},{10,9},{11,10},{13,12},{... | collective-permute-start | bytes 110600 | tf_op jit(solution)/shard_map/ppermute | solution.py:722

commit v7 on v6

--- a/solution.py
+++ b/solution.py
@@ -535,8 +535,7 @@
     window = own_y + RIM
 
     def piece(gx, gy):
-        slow = (me_x // 2 - gx // 2 + devices_x // 2) % (devices_x // 2)
-        far = (me_y // 2 - gy // 2 + devices_y // 2) % (devices_y // 2)
+        slow, far = (me_x // 2) ^ (gx // 2), (me_y // 2) ^ (gy // 2)
         return ((me_y + gy) % 2, (me_x + gx) % 2 * (devices_y // 2) + far, slow)
 
     for ref in (wide, tall):
@@ -715,39 +714,51 @@
     return launch
 
 
+def pair_route(axis):
+    return [(i, i ^ 1) for i in range(lax.axis_size(axis))]
+
+
+def swap_route(axis):
+    count = lax.axis_size(axis)
+    return [(i, (i + 1 ^ 1) - 1) for i in range(1, count - 1)]
+
+
+def by_partner(low, high, axis):
+    odd = lax.axis_index(axis) % 2 == 1
+    return jnp.where(odd, low, high), jnp.where(odd, high, low)
+
+
 def from_sides(low, high, axis):
-    count = lax.axis_size(axis)
-    up = [(i, i + 1) for i in range(count - 1)]
-    down = [(target, source) for source, target in up]
-    return lax.ppermute(high, axis, up), lax.ppermute(low, axis, down)
-
-
-def paired(block, axis, stride):
-    count = lax.axis_size(axis)
-    return jnp.stack((block, lax.ppermute(block, axis, [(i, i ^ stride) for i in range(count)])))
+    pair, swap = by_partner(low, high, axis)
+    pair = lax.ppermute(pair, axis, pair_route(axis))
+    swap = lax.ppermute(swap, axis, swap_route(axis))
+    return by_partner(pair, swap, axis)
 
 
 def passed_round(block, axis, stride):
     count = lax.axis_size(axis)
+    return [block] + [
+        lax.ppermute(block, axis, [(i, i ^ distance) for i in range(count)])
+        for distance in range(stride, count, stride)
+    ]
+
+
+def passed_across(block, rider):
+    count, size = lax.axis_size("gx"), lax.axis_size("gy")
+    rows = block.shape[0]
     blocks = [block]
-    for distance in range(stride, count, stride):
-        blocks.append(lax.ppermute(block, axis, [(i, (i + distance) % count) for i in range(count)]))
-    return blocks
-
-
-def passed_across(block):
-    count, size = lax.axis_size("gx"), lax.axis_size("gy")
-    blocks = []
     for side in range(2):
         for distance in range(0, size, 2):
             route = [
-                (x * size + y, (x ^ side) * size + (y + distance) % size)
-                for x in range(count)
-                for y in range(size)
+                (x * size + y, (x ^ side) * size + (y ^ distance)) for x in range(count) for y in range(size)
             ]
-            moved = side + distance > 0
-            blocks.append(lax.ppermute(block, ("gx", "gy"), route) if moved else block)
-    return blocks
+            if side == 1 and distance == 0:
+                both = lax.ppermute(jnp.concatenate((block, rider)), ("gx", "gy"), route)
+                blocks.append(both[:rows])
+                rider = both[rows:]
+            elif distance > 0:
+                blocks.append(lax.ppermute(block, ("gx", "gy"), route))
+    return blocks, rider
 
 
 def fused_cycle(*fields):
@@ -783,15 +794,18 @@
     pieces, v_low, v_high = call(
         functools.partial(stack_blocks, len(blocks) + 2, len(blocks)), [slow, v_shape, v_shape]
     )(*blocks, v_low, v_high)
-    blocks = passed_across(pieces)
-    v_low, v_high = from_sides(v_low, v_high, "gx")
-    slow = (len(blocks),) + pieces.shape
-    (pieces,) = call(functools.partial(stack_blocks, len(blocks) + 2, len(blocks)), [slow])(
-        *blocks, v_low, v_high
-    )
-    pieces = paired(pieces, "gy", 1)
+    pair, swap = by_partner(v_low, v_high, "gx")
+    swap = lax.ppermute(swap, "gx", swap_route("gx"))
+    blocks, pair = passed_across(pieces.reshape(-1, LANES), pair)
+    v_low, v_high = by_partner(pair, swap, "gx")
     w_low, w_high = call(pack_v, [w_shape] * 2)(top, mid, v_low, v_high)
-    w_low, w_high = from_sides(w_low, w_high, "gy")
+    pair, swap = by_partner(w_low, w_high, "gy")
+    message = jnp.concatenate(blocks + [pair])
+    swap = lax.ppermute(swap, "gy", swap_route("gy"))
+    other = lax.ppermute(message, "gy", pair_route("gy"))
+    rows = message.shape[0] - w_shape[0]
+    pieces = jnp.stack((message[:rows], other[:rows])).reshape((2, len(blocks)) + slow)
+    w_low, w_high = by_partner(other[rows:], swap, "gy")
     count = devices_x * nx // 16
     rows = devices_y * ny // 4
     grid = (devices_x, devices_y)
@@ -981,6 +995,7 @@
 def fits(nx, ny, nz, devices_x, devices_y):
     cells = devices_x * nx * devices_y * ny * nz // 8
     even = devices_x % 8 == 0 and devices_y % 4 == 0
+    even = even and devices_x & (devices_x - 1) == 0 and devices_y & (devices_y - 1) == 0
     return cells <= 2**18 and even and (nx, ny, nz) == (16, 16, LANES)
 
 

time: 59.1 us -> 50.9 us (0.86)
  starting transfers between devices: 31 us -> 24.9 us
  waiting for transfers between devices: 16.1 us -> 13.7 us
    ppermute x15 -> x13, starting transfers between devices: 31 us -> 24.9 us  [the longest x2 4.69 us: from_sides(): pair = lax.ppermute(pair, axis, pair_route(axis))]
    ppermute x15 -> x13, waiting for transfers between devices: 16.1 us -> 13.7 us  [the longest x2 5.22 us: from_sides(): pair = lax.ppermute(pair, axis, pair_route(axis))]
    pallas_call x8 -> x7, Pallas kernels: 8.7 us -> 8.67 us  [launch(): pl.pallas_call(kernel, out_shape=[pltpu.VMEM(shape, F32) for shape in out...]
  transfers between devices with their start and end apart: 15 -> 13, of which waited for: 9 -> 5; matrix products, arithmetic and copies ran while one was open for 0% -> 0% of each run, Pallas kernels for 6% -> 7%
where the time goes in v7:
time: 50.9 us; the launch traced here: 50.5 us
  starting transfers between devices  24.9 us (49%)
  waiting for transfers between devices  13.7 us (27%)
  Pallas kernels  11.5 us (23%)
    pallas_call x7, Pallas kernels, launch(): pl.pallas_call(kernel, out_shape=[pltpu.VMEM(shape, F32) for shape in out...  8.67 us
    ppermute x2, waiting for transfers between devices, from_sides(): pair = lax.ppermute(pair, axis, pair_route(axis))  5.22 us
    ppermute x2, starting transfers between devices, from_sides(): pair = lax.ppermute(pair, axis, pair_route(axis))  4.69 us
    ppermute x3, starting transfers between devices, passed_round(): lax.ppermute(block, axis, [(i, i ^ distance) for i in range(count)])  4.64 us
    ppermute x2, starting transfers between devices, from_sides(): swap = lax.ppermute(swap, axis, swap_route(axis))  4.19 us
    ppermute x1, starting transfers between devices, fused_cycle(): swap = lax.ppermute(swap, 'gy', swap_route('gy'))  3.54 us
    ppermute x1, starting transfers between devices, passed_across(): both = lax.ppermute(jnp.concatenate((block, rider)), ('gx', 'gy'), route)  3.44 us
    ppermute x3, waiting for transfers between devices, passed_round(): lax.ppermute(block, axis, [(i, i ^ distance) for i in range(count)])  3.17 us
  transfers between devices with their start and end apart: 13, of which 5 were waited for; matrix products, arithmetic and copies ran while one was open for 0% of the time, Pallas kernels for 7%

profile of v7, /device:TPU:1, one launch (start us, length us, event | category | flops | bytes accessed | tf_op | source)
XLA Modules:
  0.0 50.5 jit_solution(10806401181200477019)
XLA Ops:
  0.0 1.6 %shard_map.55 = (f32[5,16,16,128]{3,2,1,0:T(8,128)S(1)}, f32[240,128]{1,0:T(8,128)S(1)}, f32[240,128]{1,0:T(8,128)S(1)}, f32[3,8,8,128]{3,2,1,0:T(8,128)S(1)}) custom-call(f32[16,16,128]{2,1,0:T(8,128)} %refs_0_.1, f32[16,16,128]{2,1,0:T(8,128)} %refs_1_.1, f32[16,16,128]{2,1,0:T(8,128)} %refs_2_.1, f32[16,16,128]{2,1,0:T(8,128)} %refs_3_.1, ...), custom_call_target="tpu_custom_call" | custom-call | tf_op jit(solution)/shard_map/pallas_call | solution.py:705
  1.6 0.7 %collective-permute-start.1 = (f32[240,128]{1,0:T(8,128)S(1)}, f32[240,128]{1,0:T(8,128)S(1)}, u32[]{:S(2)}, u32[]{:S(2)}) collective-permute-start(f32[240,128]{1,0:T(8,128)S(1)} %get-tuple-element.45), channel_id=1, source_target_pairs={{4,8},{8,4},{12,16},{16,12},{20,24},{24,20},{5,9},{9,5},{13,17},{1... | collective-permute-start | bytes 368648 | tf_op jit(solution)/shard_map/ppermute | solution.py:734
  2.3 4.6 %collective-permute-start = (f32[240,128]{1,0:T(8,128)S(1)}, f32[240,128]{1,0:T(8,128)S(1)}, u32[]{:S(2)}, u32[]{:S(2)}) collective-permute-start(f32[240,128]{1,0:T(8,128)S(1)} %get-tuple-element.46), channel_id=1, source_target_pairs={{0,4},{4,0},{8,12},{12,8},{16,20},{20,16},{24,28},{28,24},{1,5},{5... | collective-permute-start | bytes 368648 | tf_op jit(solution)/shard_map/ppermute | solution.py:733
  6.9 0.0 collective-permute-done.1
  6.9 5.2 %collective-permute-done = f32[240,128]{1,0:T(8,128)S(1)} collective-permute-done((f32[240,128]{1,0:T(8,128)S(1)}, f32[240,128]{1,0:T(8,128)S(1)}, u32[]{:S(2)}, u32[]{:S(2)}) %collective-permute-start) | collective-permute-done | bytes 122912 | tf_op jit(solution)/shard_map/ppermute | solution.py:733
  12.1 0.2 shard_map.57
  12.3 3.5 %collective-permute-start.3 = (f32[360,128]{1,0:T(8,128)S(1)}, f32[360,128]{1,0:T(8,128)S(1)}, u32[]{:S(2)}, u32[]{:S(2)}) collective-permute-start(f32[360,128]{1,0:T(8,128)S(1)} %get-tuple-element.39), channel_id=1, source_target_pairs={{1,2},{2,1},{5,6},{6,5},{9,10},{10,9},{13,14},{14,13},{17,18},{18,... | collective-permute-start | bytes 552968 | tf_op jit(solution)/shard_map/ppermute | solution.py:734
  15.9 0.1 collective-permute-start.2
  15.9 0.5 shard_map.56.coefficients
  16.4 2.8 %collective-permute-done.3 = f32[360,128]{1,0:T(8,128)S(1)} collective-permute-done((f32[360,128]{1,0:T(8,128)S(1)}, f32[360,128]{1,0:T(8,128)S(1)}, u32[]{:S(2)}, u32[]{:S(2)}) %collective-permute-start.3) | collective-permute-done | bytes 184352 | tf_op jit(solution)/shard_map/ppermute | solution.py:734
  19.2 0.0 collective-permute-done.2
  19.2 3.2 %shard_map.58 = (f32[8,22,32,128]{3,2,1,0:T(8,128)S(1)}, f32[8,16,24,128]{3,2,1,0:T(8,128)S(1)}, f32[32,128]{1,0:T(8,128)S(1)}, f32[48,128]{1,0:T(8,128)S(1)}, f32[48,128]{1,0:T(8,128)S(1)}) custom-call(f32[5,16,16,128]{3,2,1,0:T(8,128)S(1)} %get-tuple-element.21.own, f32[3,8,8,128]{3,2,1,0:T(8,128)S(1)} %get-tuple-element.22.faces, ...), custom_call_target="tpu_custom_call" | custom-call | tf_op jit(solution)/shard_map/pallas_call | solution.py:705
  22.4 4.3 %collective-permute-start.6 = (f32[32,128]{1,0:T(8,128)S(1)}, f32[32,128]{1,0:T(8,128)S(1)}, u32[]{:S(2)}, u32[]{:S(2)}) collective-permute-start(f32[32,128]{1,0:T(8,128)S(1)} %get-tuple-element.27.refs_0_), channel_id=1, source_target_pairs={{0,24},{4,28},{8,16},{12,20},{16,8},{20,12},{24,0},{28,4},{1,25},{... | collective-permute-start | bytes 49160 | tf_op jit(solution)/shard_map/ppermute | solution.py:741
  26.7 0.0 collective-permute-start.5
  26.7 0.3 collective-permute-start.4
  27.0 0.8 %collective-permute-done.6.refs_3_ = f32[32,128]{1,0:T(8,128)S(1)} collective-permute-done((f32[32,128]{1,0:T(8,128)S(1)}, f32[32,128]{1,0:T(8,128)S(1)}, u32[]{:S(2)}, u32[]{:S(2)}) %collective-permute-start.6) | collective-permute-done | bytes 16416 | tf_op jit(solution)/shard_map/ppermute | solution.py:741
  27.8 2.4 %collective-permute-done.5.refs_2_ = f32[32,128]{1,0:T(8,128)S(1)} collective-permute-done((f32[32,128]{1,0:T(8,128)S(1)}, f32[32,128]{1,0:T(8,128)S(1)}, u32[]{:S(2)}, u32[]{:S(2)}) %collective-permute-start.5) | collective-permute-done | bytes 16416 | tf_op jit(solution)/shard_map/ppermute | solution.py:741
  30.2 0.0 collective-permute-done.4.refs_1_
  30.2 0.1 collective-permute-start.9
  30.3 0.8 %collective-permute-start.7 = (f32[128,128]{1,0:T(8,128)S(1)}, f32[128,128]{1,0:T(8,128)S(1)}, u32[]{:S(2)}, u32[]{:S(2)}) collective-permute-start(f32[128,128]{1,0:T(8,128)S(1)} %bitcast.4), channel_id=1, source_target_pairs={{0,2},{1,3},{2,0},{3,1},{4,6},{5,7},{6,4},{7,5},{8,10},{9,11},{10,... | collective-permute-start | bytes 196616 | tf_op jit(solution)/shard_map/ppermute | solution.py:760
  31.0 0.7 %collective-permute-start.10 = (f32[48,128]{1,0:T(8,128)S(1)}, f32[48,128]{1,0:T(8,128)S(1)}, u32[]{:S(2)}, u32[]{:S(2)}) collective-permute-start(f32[48,128]{1,0:T(8,128)S(1)} %get-tuple-element.53), channel_id=1, source_target_pairs={{4,8},{8,4},{12,16},{16,12},{20,24},{24,20},{5,9},{9,5},{13,17},{1... | collective-permute-start | bytes 73736 | tf_op jit(solution)/shard_map/ppermute | solution.py:798
  31.7 3.4 %collective-permute-start.8 = (f32[176,128]{1,0:T(8,128)S(1)}, f32[176,128]{1,0:T(8,128)S(1)}, u32[]{:S(2)}, u32[]{:S(2)}) collective-permute-start(f32[176,128]{1,0:T(8,128)S(1)} %pad_maximum_fusion.2), channel_id=1, source_target_pairs={{0,4},{1,5},{2,6},{3,7},{4,0},{5,1},{6,2},{7,3},{8,12},{9,13},{10,... | collective-permute-start | bytes 270344 | tf_op jit(solution)/shard_map/ppermute | solution.py:756
  35.2 0.0 collective-permute-done.7
  35.2 2.5 %collective-permute-done.8 = f32[176,128]{1,0:T(8,128)S(1)} collective-permute-done((f32[176,128]{1,0:T(8,128)S(1)}, f32[176,128]{1,0:T(8,128)S(1)}, u32[]{:S(2)}, u32[]{:S(2)}) %collective-permute-start.8) | collective-permute-done | bytes 90144 | tf_op jit(solution)/shard_map/ppermute | solution.py:756
  37.7 0.0 collective-permute-done.10
  37.7 0.1 shard_map.60
  37.9 0.0 collective-permute-done.9
  37.9 2.9 %collective-permute-start.11 = (f32[584,128]{1,0:T(8,128)S(1)}, f32[584,128]{1,0:T(8,128)S(1)}, u32[]{:S(2)}, u32[]{:S(2)}) collective-permute-start(f32[584,128]{1,0:T(8,128)S(1)} %get-tuple-element.52), channel_id=1, source_target_pairs={{0,1},{1,0},{2,3},{3,2},{4,5},{5,4},{6,7},{7,6},{8,9},{9,8},{10,11... | collective-permute-start | bytes 897032 | tf_op jit(solution)/shard_map/ppermute | solution.py:805
  40.8 3.5 %collective-permute-start.12 = (f32[72,128]{1,0:T(8,128)S(1)}, f32[72,128]{1,0:T(8,128)S(1)}, u32[]{:S(2)}, u32[]{:S(2)}) collective-permute-start(f32[72,128]{1,0:T(8,128)S(1)} %get-tuple-element.51), channel_id=1, source_target_pairs={{1,2},{2,1},{5,6},{6,5},{9,10},{10,9},{13,14},{14,13},{17,18},{18,... | collective-permute-start | bytes 110600 | tf_op jit(solution)/shard_map/ppermute | solution.py:804
  44.4 0.0 collective-permute-done.11
  44.4 3.2 %shard_map.61.coarse = f32[12,32,128]{2,1,0:T(8,128)S(1)} custom-call(f32[2,4,4,32,128]{4,3,2,1,0:T(8,128)S(1)} %pad_maximum_fusion.pieces), custom_call_target="tpu_custom_call" | custom-call | tf_op jit(solution)/shard_map/pallas_call | solution.py:705
  47.6 0.0 collective-permute-done.12
  47.6 2.8 %shard_map.62 = f32[16,16,128]{2,1,0:T(8,128)} custom-call(f32[12,32,128]{2,1,0:T(8,128)S(1)} %shard_map.61.coarse, f32[8,22,32,128]{3,2,1,0:T(8,128)S(1)} %get-tuple-element.33.top, f32[8,16,24,128]{3,2,1,0:T(8,128)S(1)} %get-tuple-element.34.mid, f32[48,128]{1,0:T(8,128)S(1)} %get-tuple-element.48.x_low, f32[48,128]{1,0:T(8,128)S(1)} %get-tuple-element.47.x_high, ...), custom_call_target="tpu_custom_call" | custom-call | tf_op jit(solution)/shard_map/pallas_call | solution.py:819
  (17 shorter events, 0.3 us)
Async XLA Ops:
  1.6 5.3 %collective-permute-start.1 = (f32[240,128]{1,0:T(8,128)S(1)}, f32[240,128]{1,0:T(8,128)S(1)}, u32[]{:S(2)}, u32[]{:S(2)}) collective-permute-start(f32[240,128]{1,0:T(8,128)S(1)} %get-tuple-element.45), channel_id=1, source_target_pairs={{4,8},{8,4},{12,16},{16,12},{20,24},{24,20},{5,9},{9,5},{13,17},{1... | collective-permute-start | bytes 368648 | tf_op jit(solution)/shard_map/ppermute | solution.py:734
  2.3 9.8 %collective-permute-start = (f32[240,128]{1,0:T(8,128)S(1)}, f32[240,128]{1,0:T(8,128)S(1)}, u32[]{:S(2)}, u32[]{:S(2)}) collective-permute-start(f32[240,128]{1,0:T(8,128)S(1)} %get-tuple-element.46), channel_id=1, source_target_pairs={{0,4},{4,0},{8,12},{12,8},{16,20},{20,16},{24,28},{28,24},{1,5},{5... | collective-permute-start | bytes 368648 | tf_op jit(solution)/shard_map/ppermute | solution.py:733
  12.3 6.9 %collective-permute-start.3 = (f32[360,128]{1,0:T(8,128)S(1)}, f32[360,128]{1,0:T(8,128)S(1)}, u32[]{:S(2)}, u32[]{:S(2)}) collective-permute-start(f32[360,128]{1,0:T(8,128)S(1)} %get-tuple-element.39), channel_id=1, source_target_pairs={{1,2},{2,1},{5,6},{6,5},{9,10},{10,9},{13,14},{14,13},{17,18},{18,... | collective-permute-start | bytes 552968 | tf_op jit(solution)/shard_map/ppermute | solution.py:734
  15.9 3.3 %collective-permute-start.2 = (f32[360,128]{1,0:T(8,128)S(1)}, f32[360,128]{1,0:T(8,128)S(1)}, u32[]{:S(2)}, u32[]{:S(2)}) collective-permute-start(f32[360,128]{1,0:T(8,128)S(1)} %get-tuple-element.40), channel_id=1, source_target_pairs={{0,1},{1,0},{2,3},{3,2},{4,5},{5,4},{6,7},{7,6},{8,9},{9,8},{10,11... | collective-permute-start | bytes 552968 | tf_op jit(solution)/shard_map/ppermute | solution.py:733
  22.4 5.4 %collective-permute-start.6 = (f32[32,128]{1,0:T(8,128)S(1)}, f32[32,128]{1,0:T(8,128)S(1)}, u32[]{:S(2)}, u32[]{:S(2)}) collective-permute-start(f32[32,128]{1,0:T(8,128)S(1)} %get-tuple-element.27.refs_0_), channel_id=1, source_target_pairs={{0,24},{4,28},{8,16},{12,20},{16,8},{20,12},{24,0},{28,4},{1,25},{... | collective-permute-start | bytes 49160 | tf_op jit(solution)/shard_map/ppermute | solution.py:741
  26.7 3.5 %collective-permute-start.5 = (f32[32,128]{1,0:T(8,128)S(1)}, f32[32,128]{1,0:T(8,128)S(1)}, u32[]{:S(2)}, u32[]{:S(2)}) collective-permute-start(f32[32,128]{1,0:T(8,128)S(1)} %get-tuple-element.27.refs_0_), channel_id=1, source_target_pairs={{0,16},{4,20},{8,24},{12,28},{16,0},{20,4},{24,8},{28,12},{1,17},{... | collective-permute-start | bytes 49160 | tf_op jit(solution)/shard_map/ppermute | solution.py:741
  26.7 3.5 %collective-permute-start.4 = (f32[32,128]{1,0:T(8,128)S(1)}, f32[32,128]{1,0:T(8,128)S(1)}, u32[]{:S(2)}, u32[]{:S(2)}) collective-permute-start(f32[32,128]{1,0:T(8,128)S(1)} %get-tuple-element.27.refs_0_), channel_id=1, source_target_pairs={{0,8},{4,12},{8,0},{12,4},{16,24},{20,28},{24,16},{28,20},{1,9},{5... | collective-permute-start | bytes 49160 | tf_op jit(solution)/shard_map/ppermute | solution.py:741
  30.2 7.7 %collective-permute-start.9 = (f32[128,128]{1,0:T(8,128)S(1)}, f32[128,128]{1,0:T(8,128)S(1)}, u32[]{:S(2)}, u32[]{:S(2)}) collective-permute-start(f32[128,128]{1,0:T(8,128)S(1)} %bitcast.3), channel_id=1, source_target_pairs={{0,6},{1,7},{2,4},{3,5},{4,2},{5,3},{6,0},{7,1},{8,14},{9,15},{10,... | collective-permute-start | bytes 196616 | tf_op jit(solution)/shard_map/ppermute | solution.py:760
  30.3 4.9 %collective-permute-start.7 = (f32[128,128]{1,0:T(8,128)S(1)}, f32[128,128]{1,0:T(8,128)S(1)}, u32[]{:S(2)}, u32[]{:S(2)}) collective-permute-start(f32[128,128]{1,0:T(8,128)S(1)} %bitcast.4), channel_id=1, source_target_pairs={{0,2},{1,3},{2,0},{3,1},{4,6},{5,7},{6,4},{7,5},{8,10},{9,11},{10,... | collective-permute-start | bytes 196616 | tf_op jit(solution)/shard_map/ppermute | solution.py:760
  31.0 6.7 %collective-permute-start.10 = (f32[48,128]{1,0:T(8,128)S(1)}, f32[48,128]{1,0:T(8,128)S(1)}, u32[]{:S(2)}, u32[]{:S(2)}) collective-permute-start(f32[48,128]{1,0:T(8,128)S(1)} %get-tuple-element.53), channel_id=1, source_target_pairs={{4,8},{8,4},{12,16},{16,12},{20,24},{24,20},{5,9},{9,5},{13,17},{1... | collective-permute-start | bytes 73736 | tf_op jit(solution)/shard_map/ppermute | solution.py:798
  31.7 6.0 %collective-permute-start.8 = (f32[176,128]{1,0:T(8,128)S(1)}, f32[176,128]{1,0:T(8,128)S(1)}, u32[]{:S(2)}, u32[]{:S(2)}) collective-permute-start(f32[176,128]{1,0:T(8,128)S(1)} %pad_maximum_fusion.2), channel_id=1, source_target_pairs={{0,4},{1,5},{2,6},{3,7},{4,0},{5,1},{6,2},{7,3},{8,12},{9,13},{10,... | collective-permute-start | bytes 270344 | tf_op jit(solution)/shard_map/ppermute | solution.py:756
  37.9 6.5 %collective-permute-start.11 = (f32[584,128]{1,0:T(8,128)S(1)}, f32[584,128]{1,0:T(8,128)S(1)}, u32[]{:S(2)}, u32[]{:S(2)}) collective-permute-start(f32[584,128]{1,0:T(8,128)S(1)} %get-tuple-element.52), channel_id=1, source_target_pairs={{0,1},{1,0},{2,3},{3,2},{4,5},{5,4},{6,7},{7,6},{8,9},{9,8},{10,11... | collective-permute-start | bytes 897032 | tf_op jit(solution)/shard_map/ppermute | solution.py:805
  40.8 6.8 %collective-permute-start.12 = (f32[72,128]{1,0:T(8,128)S(1)}, f32[72,128]{1,0:T(8,128)S(1)}, u32[]{:S(2)}, u32[]{:S(2)}) collective-permute-start(f32[72,128]{1,0:T(8,128)S(1)} %get-tuple-element.51), channel_id=1, source_target_pairs={{1,2},{2,1},{5,6},{6,5},{9,10},{10,9},{13,14},{14,13},{17,18},{18,... | collective-permute-start | bytes 110600 | tf_op jit(solution)/shard_map/ppermute | solution.py:804

commit v8 on v7

--- a/solution.py
+++ b/solution.py
@@ -96,28 +96,46 @@
 
 
 def y_rows(nx, ny):
-    return sum(Y_LAYERS) * (nx + 2 * EDGE), 3 * (nx // 2 + 2 * RIM) // 2 * RIM
+    return sum(Y_LAYERS) * nx, 3 * (nx // 4) * RIM
+
+
+def corner_rows():
+    return sum(x * y for x, y in zip(X_LAYERS, Y_LAYERS)) + 3, 3 * RIM // 2 * RIM
 
 
 def x_place(index, layer, ny):
     return pl.ds((sum(X_LAYERS[:index]) + layer) * ny, ny)
 
 
-def y_place(index, slab, slabs):
-    return pl.ds(sum(Y_LAYERS[:index]) * slabs + slab * Y_LAYERS[index], Y_LAYERS[index])
+def y_place(index, slab, nx):
+    return pl.ds(sum(Y_LAYERS[:index]) * nx + slab * Y_LAYERS[index], Y_LAYERS[index])
+
+
+def corner_place(index, layer):
+    start = sum(x * y for x, y in zip(X_LAYERS[:index], Y_LAYERS[:index]))
+    return pl.ds(start + layer * Y_LAYERS[index], Y_LAYERS[index])
 
 
 def start_pack(*refs):
-    fields, (own, x_low, x_high, faces, tmp, done) = refs[:5], refs[5:]
+    fields, (own, x_low, x_high, y_low, y_high, *corners, faces, tmp, done) = refs[:5], refs[5:]
     copies = [pltpu.make_async_copy(ref, own.at[index], done.at[index]) for index, ref in enumerate(fields)]
     for copy in copies:
         copy.start()
     nx, ny = own.shape[1:3]
     for index, copy in enumerate(copies):
         copy.wait()
-        for layer in range(X_LAYERS[index]):
+        layers, width = X_LAYERS[index], Y_LAYERS[index]
+        for layer in range(layers):
             x_low[x_place(index, layer, ny)] = own[index, layer]
-            x_high[x_place(index, layer, ny)] = own[index, nx - X_LAYERS[index] + layer]
+            x_high[x_place(index, layer, ny)] = own[index, nx - layers + layer]
+        for slab in range(nx):
+            y_low[y_place(index, slab, nx)] = own[index, slab, :width]
+            y_high[y_place(index, slab, nx)] = own[index, slab, ny - width :]
+        for side_x, first in enumerate((0, nx - layers)):
+            for side_y, start in enumerate((0, ny - width)):
+                for layer in range(layers):
+                    rows = own[index, first + layer, start : start + width]
+                    corners[2 * side_x + side_y][corner_place(index, layer)] = rows
     fx, fy, fz = own.at[2], own.at[3], own.at[4]
     halve = compact(LANES, 0)
 
@@ -134,14 +152,26 @@
     first, second = pair_slabs(fz)
     tmp[...] = first + second
     stored(2, even_rows(tmp, ny) + odd_rows(tmp, ny), compact(LANES, 0, True))
-    base = x_rows(nx, ny)[0]
-    coarse_rows = ny // 2
+    base, base_y, base_c = x_rows(nx, ny)[0], y_rows(nx, ny)[0], corner_rows()[0]
+    coarse_x, coarse_y = nx // 2, ny // 2
+    pairs = RIM // 2
     for face in range(3):
-        for layer in range(RIM // 2):
-            rows = pl.ds(base + (face * (RIM // 2) + layer) * coarse_rows, coarse_rows)
-            top = nx // 2 - RIM + layer
-            x_low[rows] = two_in_one(faces[face, layer], faces[face, layer + RIM // 2])
-            x_high[rows] = two_in_one(faces[face, top], faces[face, top + RIM // 2])
+        low = [two_in_one(faces[face, i], faces[face, i + pairs]) for i in range(pairs)]
+        top = coarse_x - RIM
+        high = [two_in_one(faces[face, top + i], faces[face, top + i + pairs]) for i in range(pairs)]
+        for layer in range(pairs):
+            rows = pl.ds(base + (face * pairs + layer) * coarse_y, coarse_y)
+            x_low[rows] = low[layer]
+            x_high[rows] = high[layer]
+            rows = pl.ds(base_c + (face * pairs + layer) * RIM, RIM)
+            for side_x, both in enumerate((low[layer], high[layer])):
+                corners[2 * side_x][rows] = both[:RIM]
+                corners[2 * side_x + 1][rows] = both[coarse_y - RIM :]
+        for slab in range(coarse_x // 2):
+            both = two_in_one(faces[face, slab], faces[face, slab + coarse_x // 2])
+            rows = pl.ds(base_y + (face * (coarse_x // 2) + slab) * RIM, RIM)
+            y_low[rows] = both[:RIM]
+            y_high[rows] = both[coarse_y - RIM :]
 
 
 def pair_slabs(ref):
@@ -162,41 +192,6 @@
 def rim_slab(ref, base, rows, layer):
     place = pl.ds(base + layer % (RIM // 2) * rows, rows)
     return one_of_two(ref[place])[layer // (RIM // 2)]
-
-
-def pack_y(own, faces, x_low, x_high, low, high):
-    coarse_x, coarse_y = faces.shape[1:3]
-    nx, ny = 2 * coarse_x, 2 * coarse_y
-    slabs = nx + 2 * EDGE
-    for index in range(5):
-        width, layers = Y_LAYERS[index], X_LAYERS[index]
-        for out, start in ((low, 0), (high, ny - width)):
-            for slab in range(nx):
-                out[y_place(index, EDGE + slab, slabs)] = own[index, slab, start : start + width]
-            for layer in range(EDGE):
-                near, far = layer + layers - EDGE, layer
-                rows = pl.ds(x_place(index, max(near, 0), ny).start + start, width)
-                out[y_place(index, layer, slabs)] = x_low[rows]
-                rows = pl.ds(x_place(index, min(far, layers - 1), ny).start + start, width)
-                out[y_place(index, EDGE + nx + layer, slabs)] = x_high[rows]
-    base_x, base_y = x_rows(nx, ny)[0], y_rows(nx, ny)[0]
-    half = (coarse_x + 2 * RIM) // 2
-    for face in range(3):
-        place = base_x + face * (RIM // 2) * coarse_y
-        slabs = [
-            wide_slab(
-                slab,
-                lambda layer: rim_slab(x_low, place, coarse_y, layer),
-                faces.at[face],
-                lambda layer: rim_slab(x_high, place, coarse_y, layer),
-            )
-            for slab in range(2 * half)
-        ]
-        for slab in range(half):
-            both = two_in_one(slabs[slab], slabs[slab + half])
-            rows = pl.ds(base_y + (face * half + slab) * RIM, RIM)
-            low[rows] = both[:RIM]
-            high[rows] = both[coarse_y - RIM :]
 
 
 def fold_four(slabs, even_only=False):
@@ -245,6 +240,12 @@
     return (1.0 - OMEGA) * v + lev[W, slab, pl.ds(start, rows)] * total
 
 
+def omega_over(values):
+    inverse = pl.reciprocal(values, approx=True)
+    inverse = inverse * (2.0 - values * inverse)
+    return OMEGA * inverse * (2.0 - values * inverse)
+
+
 def set_weights(lev, slab, start, rows, depth, inside=None):
     here = pl.ds(start, rows)
     fz = lev[ZL, slab, here]
@@ -258,7 +259,7 @@
     lev[ZL, slab, here] = jnp.where(z == 0, 0.0, fz)
     lev[ZH, slab, here] = upper
     lev[D, slab, here] = diagonal
-    lev[W, slab, here] = jnp.where(valid, OMEGA / jnp.where(valid, diagonal, 1.0), 0.0)
+    lev[W, slab, here] = jnp.where(valid, omega_over(jnp.where(valid, diagonal, 1.0)), 0.0)
 
 
 def run(count, body, unroll=1):
@@ -275,6 +276,7 @@
 
 
 def level_down(axes, own, faces, coefficients, x_low, x_high, y_low, y_high, *refs):
+    corners, refs = refs[:4], refs[4:]
     top, mid, chunk, v_low, v_high, other, tmp, one, two = refs
     nx, ny = own.shape[1:3]
     slabs, rows = nx + 2 * EDGE, ny + 2 * RIM
@@ -292,9 +294,14 @@
             else:
                 top[slot, EDGE - 1 - layer, inner] = jnp.zeros((ny, LANES), F32)
                 top[slot, EDGE + nx + layer, inner] = jnp.zeros((ny, LANES), F32)
-        for slab in range(slabs):
-            top[slot, slab, PAD - width : PAD] = y_low[y_place(index, slab, slabs)]
-            top[slot, slab, PAD + ny : PAD + ny + width] = y_high[y_place(index, slab, slabs)]
+        for slab in range(nx):
+            top[slot, EDGE + slab, PAD - width : PAD] = y_low[y_place(index, slab, nx)]
+            top[slot, EDGE + slab, PAD + ny : PAD + ny + width] = y_high[y_place(index, slab, nx)]
+        for side_x, start in enumerate((EDGE - layers, EDGE + nx)):
+            for layer in range(layers):
+                place = corner_place(index, layer)
+                top[slot, start + layer, PAD - width : PAD] = corners[2 * side_x][place]
+                top[slot, start + layer, PAD + ny : PAD + ny + width] = corners[2 * side_x + 1][place]
     clear_pads(other, rows)
     row_inside = (rows_of((rows, LANES)) >= RIM) | (me_y > 0)
     main = pl.ds(RIM, rows)
@@ -337,12 +344,19 @@
         for layer in range(RIM):
             mid[slot, layer, inner] = rim_slab(x_low, place, coarse_y, layer)
             mid[slot, RIM + coarse_x + layer, inner] = rim_slab(x_high, place, coarse_y, layer)
-        for slab in range(half):
-            place = pl.ds(base_y + (face * half + slab) * RIM, RIM)
+        parts = coarse_x // 2
+        for slab in range(parts):
+            place = pl.ds(base_y + (face * parts + slab) * RIM, RIM)
             for message, row in ((y_low, RIM), (y_high, 2 * RIM + coarse_y)):
                 pair = one_of_two(message[place])
-                mid[slot, slab, row : row + RIM] = pair[0]
-                mid[slot, slab + half, row : row + RIM] = pair[1]
+                mid[slot, RIM + slab, row : row + RIM] = pair[0]
+                mid[slot, RIM + slab + parts, row : row + RIM] = pair[1]
+        for side_x, start in enumerate((0, RIM + coarse_x)):
+            for side_y, row in enumerate((RIM, 2 * RIM + coarse_y)):
+                place = corner_rows()[0] + face * (RIM // 2) * RIM
+                for layer in range(RIM):
+                    values = rim_slab(corners[2 * side_x + side_y], place, RIM, layer)
+                    mid[slot, start + layer, row : row + RIM] = values
     row_inside = (rows_of((rows, LANES)) >= RIM) | (me_y > 0)
     for slab in range(slabs - 1):
         inside = row_inside & (me_x > 0) if slab < RIM else row_inside
@@ -451,7 +465,7 @@
         self.d = [
             fx[s] + self.x_high[s] + fy[s] + self.y_high[s] + fz[s] + self.z_high[s] for s in range(count)
         ]
-        self.w = [jnp.where(d > 0.0, OMEGA / jnp.where(d > 0.0, d, 1.0), 0.0) for d in self.d]
+        self.w = [jnp.where(d > 0.0, omega_over(jnp.where(d > 0.0, d, 1.0)), 0.0) for d in self.d]
 
     def weighted(self, v, f):
         count = self.count
@@ -728,11 +742,37 @@
     return jnp.where(odd, low, high), jnp.where(odd, high, low)
 
 
-def from_sides(low, high, axis):
-    pair, swap = by_partner(low, high, axis)
-    pair = lax.ppermute(pair, axis, pair_route(axis))
-    swap = lax.ppermute(swap, axis, swap_route(axis))
-    return by_partner(pair, swap, axis)
+def partner(kind, index, count):
+    other = index if kind is None else index ^ 1 if kind == 0 else (index + 1 ^ 1) - 1
+    return other if 0 <= other < count else None
+
+
+def across(block, kind_x, kind_y):
+    count, size = lax.axis_size("gx"), lax.axis_size("gy")
+    route = []
+    for x in range(count):
+        for y in range(size):
+            to_x, to_y = partner(kind_x, x, count), partner(kind_y, y, size)
+            if to_x is not None and to_y is not None:
+                route.append((x * size + y, to_x * size + to_y))
+    return lax.ppermute(block, ("gx", "gy"), route)
+
+
+def by_partners(corners):
+    low = by_partner(corners[0], corners[2], "gx")
+    high = by_partner(corners[1], corners[3], "gx")
+    out = [by_partner(low[kind], high[kind], "gy") for kind in range(2)]
+    return [out[0][0], out[0][1], out[1][0], out[1][1]]
+
+
+def from_around(x_low, x_high, y_low, y_high, corners):
+    x = by_partner(x_low, x_high, "gx")
+    y = by_partner(y_low, y_high, "gy")
+    corners = by_partners(corners)
+    x = [across(x[kind], kind, None) for kind in (1, 0)]
+    corners = [across(corners[2 * kx + ky], kx, ky) for kx in range(2) for ky in range(2)]
+    y = [across(y[kind], None, kind) for kind in (1, 0)]
+    return by_partner(x[1], x[0], "gx") + by_partner(y[1], y[0], "gy") + tuple(by_partners(corners))
 
 
 def passed_round(block, axis, stride):
@@ -768,16 +808,17 @@
     coarse_x, coarse_y = nx // 2, ny // 2
     x_shape = (sum(x_rows(nx, ny)), LANES)
     y_shape = (sum(y_rows(nx, ny)), LANES)
-    own, x_low, x_high, faces = call(
+    corner_shape = (sum(corner_rows()), LANES)
+    own, x_low, x_high, y_low, y_high, *corners, faces = call(
         start_pack,
-        [(5, nx, ny, nz), x_shape, x_shape, (3, coarse_x, coarse_y, LANES)],
+        [(5, nx, ny, nz), x_shape, x_shape, y_shape, y_shape]
+        + [corner_shape] * 4
+        + [(3, coarse_x, coarse_y, LANES)],
         [(coarse_x, ny, LANES), pltpu.SemaphoreType.DMA((5,))],
         True,
     )(*fields)
-    x_low, x_high = from_sides(x_low, x_high, "gx")
+    around = from_around(x_low, x_high, y_low, y_high, corners)
     (coefficients,) = call(coarse_faces, [(16, LANES)], [(coarse_x // 2, coarse_y, LANES)])(faces)
-    y_low, y_high = call(pack_y, [y_shape] * 2)(own, faces, x_low, x_high)
-    y_low, y_high = from_sides(y_low, y_high, "gy")
     stack = (nx + 2 * EDGE, ny + 4 * RIM, LANES)
     stack_1 = (coarse_x + 2 * RIM, coarse_y + 4 * RIM, LANES)
     half = stack_1[0] // 2
@@ -787,7 +828,7 @@
         functools.partial(level_down, axes),
         [(D + 1,) + stack, (D + 1,) + stack_1, (32, LANES), v_shape, v_shape],
         [stack, (nx // 2, ny, LANES), stack_1, (half, coarse_y + 2 * RIM, LANES)],
-    )(own, faces, coefficients, x_low, x_high, y_low, y_high)
+    )(own, faces, coefficients, *around)
 
     blocks = passed_round(chunk, "gx", 2)
     slow = (len(blocks),) + chunk.shape

time: 50.9 us -> 53.3 us (1.047)
  starting transfers between devices: 24.9 us -> 34.6 us
  waiting for transfers between devices: 13.7 us -> 6.25 us
    ppermute x4 -> x8, starting transfers between devices: 8.88 us -> 19 us  [across(): return lax.ppermute(block, ('gx', 'gy'), route)]
    ppermute x4 -> x8, waiting for transfers between devices: 7.99 us -> 2.41 us  [across(): return lax.ppermute(block, ('gx', 'gy'), route)]
    ppermute x3, waiting for transfers between devices: 3.17 us -> 1.52 us  [passed_round(): lax.ppermute(block, axis, [(i, i ^ distance) for i in range(count)])]
    ppermute x2, starting transfers between devices: 0.83 us -> 2.05 us  [passed_across(): blocks.append(lax.ppermute(block, ('gx', 'gy'), route))]
    ppermute x3, starting transfers between devices: 4.64 us -> 3.55 us  [passed_round(): lax.ppermute(block, axis, [(i, i ^ distance) for i in range(count)])]
    ppermute x1, starting transfers between devices: 3.44 us -> 2.84 us  [passed_across(): both = lax.ppermute(jnp.concatenate((block, rider)), ('gx', 'gy'), route)]
    ppermute x1, starting transfers between devices: 2.88 us -> 3.45 us  [fused_cycle(): other = lax.ppermute(message, 'gy', pair_route('gy'))]
    pallas_call x7 -> x6, Pallas kernels: 8.67 us -> 8.59 us  [launch(): pl.pallas_call(kernel, out_shape=[pltpu.VMEM(shape, F32) for shape in out...]
  transfers between devices with their start and end apart: 13 -> 17, of which waited for: 5 -> 6; matrix products, arithmetic and copies ran while one was open for 0% -> 0% of each run, Pallas kernels for 7% -> 7%
where the time goes in v8:
time: 53.3 us; the launch traced here: 52.9 us
  starting transfers between devices  34.6 us (65%)
  Pallas kernels  11.5 us (22%)
  waiting for transfers between devices  6.25 us (12%)
    ppermute x8, starting transfers between devices, across(): return lax.ppermute(block, ('gx', 'gy'), route)  19 us
    pallas_call x6, Pallas kernels, launch(): pl.pallas_call(kernel, out_shape=[pltpu.VMEM(shape, F32) for shape in out...  8.59 us
    ppermute x3, starting transfers between devices, passed_round(): lax.ppermute(block, axis, [(i, i ^ distance) for i in range(count)])  3.55 us
    ppermute x1, starting transfers between devices, fused_cycle(): other = lax.ppermute(message, 'gy', pair_route('gy'))  3.45 us
    ppermute x1, starting transfers between devices, fused_cycle(): swap = lax.ppermute(swap, 'gy', swap_route('gy'))  3.04 us
    pallas_call x1, Pallas kernels, fused_cycle(): pl.pallas_call(functools.partial(level_up, axes, grid), out_shape=jax.Sha...  2.91 us
    ppermute x1, starting transfers between devices, passed_across(): both = lax.ppermute(jnp.concatenate((block, rider)), ('gx', 'gy'), route)  2.84 us
    ppermute x8, waiting for transfers between devices, across(): return lax.ppermute(block, ('gx', 'gy'), route)  2.41 us
  transfers between devices with their start and end apart: 17, of which 6 were waited for; matrix products, arithmetic and copies ran while one was open for 0% of the time, Pallas kernels for 7%

profile of v8, /device:TPU:1, one launch (start us, length us, event | category | flops | bytes accessed | tf_op | source)
XLA Modules:
  0.0 52.9 jit_solution(1948854263354055548)
XLA Ops:
  0.0 1.6 %shard_map.55 = (f32[5,16,16,128]{3,2,1,0:T(8,128)S(1)}, f32[240,128]{1,0:T(8,128)S(1)}, f32[240,128]{1,0:T(8,128)S(1)}, f32[240,128]{1,0:T(8,128)S(1)}, f32[240...) custom-call(f32[16,16,128]{2,1,0:T(8,128)} %refs_0_.1, ...), custom_call_target="tpu_custom_call" | custom-call | tf_op jit(solution)/shard_map/pallas_call | solution.py:719
  1.6 0.7 %collective-permute-start.7 = (f32[56,128]{1,0:T(8,128)S(1)}, f32[56,128]{1,0:T(8,128)S(1)}, u32[]{:S(2)}, u32[]{:S(2)}) collective-permute-start(f32[56,128]{1,0:T(8,128)S(1)} %get-tuple-element.61), channel_id=1, source_target_pairs={{5,10},{6,9},{9,6},{10,5},{13,18},{14,17},{17,14},{18,13},{21,26},... | collective-permute-start | bytes 86024 | tf_op jit(solution)/shard_map/ppermute | solution.py:758
  2.3 0.7 %collective-permute-start.5 = (f32[56,128]{1,0:T(8,128)S(1)}, f32[56,128]{1,0:T(8,128)S(1)}, u32[]{:S(2)}, u32[]{:S(2)}) collective-permute-start(f32[56,128]{1,0:T(8,128)S(1)} %get-tuple-element.62), channel_id=1, source_target_pairs={{4,9},{5,8},{6,11},{7,10},{8,5},{9,4},{10,7},{11,6},{12,17},{13,16... | collective-permute-start | bytes 86024 | tf_op jit(solution)/shard_map/ppermute | solution.py:758
  3.0 8.9 %collective-permute-start.6 = (f32[56,128]{1,0:T(8,128)S(1)}, f32[56,128]{1,0:T(8,128)S(1)}, u32[]{:S(2)}, u32[]{:S(2)}) collective-permute-start(f32[56,128]{1,0:T(8,128)S(1)} %get-tuple-element.63), channel_id=1, source_target_pairs={{1,6},{2,5},{5,2},{6,1},{9,14},{10,13},{13,10},{14,9},{17,22},{18,... | collective-permute-start | bytes 86024 | tf_op jit(solution)/shard_map/ppermute | solution.py:758
  11.9 0.5 collective-permute-start.4
  12.4 0.7 %collective-permute-start.1 = (f32[240,128]{1,0:T(8,128)S(1)}, f32[240,128]{1,0:T(8,128)S(1)}, u32[]{:S(2)}, u32[]{:S(2)}) collective-permute-start(f32[240,128]{1,0:T(8,128)S(1)} %get-tuple-element.53), channel_id=1, source_target_pairs={{4,8},{5,9},{6,10},{7,11},{8,4},{9,5},{10,6},{11,7},{12,16},{13,17... | collective-permute-start | bytes 368648 | tf_op jit(solution)/shard_map/ppermute | solution.py:758
  13.1 0.5 shard_map.56.coefficients
  13.6 0.0 collective-permute-done.7
  13.6 3.7 %collective-permute-start = (f32[240,128]{1,0:T(8,128)S(1)}, f32[240,128]{1,0:T(8,128)S(1)}, u32[]{:S(2)}, u32[]{:S(2)}) collective-permute-start(f32[240,128]{1,0:T(8,128)S(1)} %get-tuple-element.54), channel_id=1, source_target_pairs={{0,4},{1,5},{2,6},{3,7},{4,0},{5,1},{6,2},{7,3},{8,12},{9,13},{10,... | collective-permute-start | bytes 368648 | tf_op jit(solution)/shard_map/ppermute | solution.py:758
  17.3 0.0 collective-permute-done.5
  17.4 3.8 %collective-permute-start.3 = (f32[240,128]{1,0:T(8,128)S(1)}, f32[240,128]{1,0:T(8,128)S(1)}, u32[]{:S(2)}, u32[]{:S(2)}) collective-permute-start(f32[240,128]{1,0:T(8,128)S(1)} %get-tuple-element.49), channel_id=1, source_target_pairs={{1,2},{2,1},{5,6},{6,5},{9,10},{10,9},{13,14},{14,13},{17,18},{18,... | collective-permute-start | bytes 368648 | tf_op jit(solution)/shard_map/ppermute | solution.py:758
  21.2 0.0 collective-permute-done.6
  21.2 0.1 collective-permute-start.2
  21.3 0.0 collective-permute-done.4
  21.3 0.0 collective-permute-done.1
  21.3 0.1 collective-permute-done
  21.5 2.3 %collective-permute-done.3 = f32[240,128]{1,0:T(8,128)S(1)} collective-permute-done((f32[240,128]{1,0:T(8,128)S(1)}, f32[240,128]{1,0:T(8,128)S(1)}, u32[]{:S(2)}, u32[]{:S(2)}) %collective-permute-start.3) | collective-permute-done | bytes 122912 | tf_op jit(solution)/shard_map/ppermute | solution.py:758
  23.7 0.0 collective-permute-done.2
  23.8 3.2 %shard_map.57 = (f32[8,22,32,128]{3,2,1,0:T(8,128)S(1)}, f32[8,16,24,128]{3,2,1,0:T(8,128)S(1)}, f32[32,128]{1,0:T(8,128)S(1)}, f32[48,128]{1,0:T(8,128)S(1)}, f32[48,128]{1,0:T(8,128)S(1)}) custom-call(f32[5,16,16,128]{3,2,1,0:T(8,128)S(1)} %get-tuple-element.25.own, f32[3,8,8,128]{3,2,1,0:T(8,128)S(1)} %get-tuple-element.26.faces, ...), custom_call_target="tpu_custom_call" | custom-call | tf_op jit(solution)/shard_map/pallas_call | solution.py:719
  27.0 1.1 %collective-permute-start.10 = (f32[32,128]{1,0:T(8,128)S(1)}, f32[32,128]{1,0:T(8,128)S(1)}, u32[]{:S(2)}, u32[]{:S(2)}) collective-permute-start(f32[32,128]{1,0:T(8,128)S(1)} %get-tuple-element.35.refs_0_), channel_id=1, source_target_pairs={{0,24},{4,28},{8,16},{12,20},{16,8},{20,12},{24,0},{28,4},{1,25},{... | collective-permute-start | bytes 49160 | tf_op jit(solution)/shard_map/ppermute | solution.py:781
  28.1 1.4 %collective-permute-start.9 = (f32[32,128]{1,0:T(8,128)S(1)}, f32[32,128]{1,0:T(8,128)S(1)}, u32[]{:S(2)}, u32[]{:S(2)}) collective-permute-start(f32[32,128]{1,0:T(8,128)S(1)} %get-tuple-element.35.refs_0_), channel_id=1, source_target_pairs={{0,16},{4,20},{8,24},{12,28},{16,0},{20,4},{24,8},{28,12},{1,17},{... | collective-permute-start | bytes 49160 | tf_op jit(solution)/shard_map/ppermute | solution.py:781
  29.4 1.1 %collective-permute-start.8 = (f32[32,128]{1,0:T(8,128)S(1)}, f32[32,128]{1,0:T(8,128)S(1)}, u32[]{:S(2)}, u32[]{:S(2)}) collective-permute-start(f32[32,128]{1,0:T(8,128)S(1)} %get-tuple-element.35.refs_0_), channel_id=1, source_target_pairs={{0,8},{4,12},{8,0},{12,4},{16,24},{20,28},{24,16},{28,20},{1,9},{5... | collective-permute-start | bytes 49160 | tf_op jit(solution)/shard_map/ppermute | solution.py:781
  30.5 0.8 %collective-permute-done.10.refs_3_ = f32[32,128]{1,0:T(8,128)S(1)} collective-permute-done((f32[32,128]{1,0:T(8,128)S(1)}, f32[32,128]{1,0:T(8,128)S(1)}, u32[]{:S(2)}, u32[]{:S(2)}) %collective-permute-start.10) | collective-permute-done | bytes 16416 | tf_op jit(solution)/shard_map/ppermute | solution.py:781
  31.3 0.2 collective-permute-done.9.refs_2_
  31.5 0.5 collective-permute-done.8.refs_1_
  32.0 1.6 %collective-permute-start.13 = (f32[128,128]{1,0:T(8,128)S(1)}, f32[128,128]{1,0:T(8,128)S(1)}, u32[]{:S(2)}, u32[]{:S(2)}) collective-permute-start(f32[128,128]{1,0:T(8,128)S(1)} %bitcast.3), channel_id=1, source_target_pairs={{0,6},{1,7},{2,4},{3,5},{4,2},{5,3},{6,0},{7,1},{8,14},{9,15},{10,... | collective-permute-start | bytes 196616 | tf_op jit(solution)/shard_map/ppermute | solution.py:800
  33.6 0.5 collective-permute-start.11
  34.1 0.7 %collective-permute-start.14 = (f32[48,128]{1,0:T(8,128)S(1)}, f32[48,128]{1,0:T(8,128)S(1)}, u32[]{:S(2)}, u32[]{:S(2)}) collective-permute-start(f32[48,128]{1,0:T(8,128)S(1)} %get-tuple-element.69), channel_id=1, source_target_pairs={{4,8},{8,4},{12,16},{16,12},{20,24},{24,20},{5,9},{9,5},{13,17},{1... | collective-permute-start | bytes 73736 | tf_op jit(solution)/shard_map/ppermute | solution.py:839
  34.8 2.8 %collective-permute-start.12 = (f32[176,128]{1,0:T(8,128)S(1)}, f32[176,128]{1,0:T(8,128)S(1)}, u32[]{:S(2)}, u32[]{:S(2)}) collective-permute-start(f32[176,128]{1,0:T(8,128)S(1)} %pad_maximum_fusion.2), channel_id=1, source_target_pairs={{0,4},{1,5},{2,6},{3,7},{4,0},{5,1},{6,2},{7,3},{8,12},{9,13},{10,... | collective-permute-start | bytes 270344 | tf_op jit(solution)/shard_map/ppermute | solution.py:796
  37.6 0.0 collective-permute-done.11
  37.6 2.3 %collective-permute-done.12 = f32[176,128]{1,0:T(8,128)S(1)} collective-permute-done((f32[176,128]{1,0:T(8,128)S(1)}, f32[176,128]{1,0:T(8,128)S(1)}, u32[]{:S(2)}, u32[]{:S(2)}) %collective-permute-start.12) | collective-permute-done | bytes 90144 | tf_op jit(solution)/shard_map/ppermute | solution.py:796
  40.0 0.0 collective-permute-done.14
  40.0 0.1 shard_map.59
  40.1 0.0 collective-permute-done.13
  40.2 3.4 %collective-permute-start.15 = (f32[584,128]{1,0:T(8,128)S(1)}, f32[584,128]{1,0:T(8,128)S(1)}, u32[]{:S(2)}, u32[]{:S(2)}) collective-permute-start(f32[584,128]{1,0:T(8,128)S(1)} %get-tuple-element.68), channel_id=1, source_target_pairs={{0,1},{1,0},{2,3},{3,2},{4,5},{5,4},{6,7},{7,6},{8,9},{9,8},{10,11... | collective-permute-start | bytes 897032 | tf_op jit(solution)/shard_map/ppermute | solution.py:846
  43.6 3.0 %collective-permute-start.16 = (f32[72,128]{1,0:T(8,128)S(1)}, f32[72,128]{1,0:T(8,128)S(1)}, u32[]{:S(2)}, u32[]{:S(2)}) collective-permute-start(f32[72,128]{1,0:T(8,128)S(1)} %get-tuple-element.67), channel_id=1, source_target_pairs={{1,2},{2,1},{5,6},{6,5},{9,10},{10,9},{13,14},{14,13},{17,18},{18,... | collective-permute-start | bytes 110600 | tf_op jit(solution)/shard_map/ppermute | solution.py:845
  46.7 0.0 collective-permute-done.15
  46.8 3.2 %shard_map.60.coarse = f32[12,32,128]{2,1,0:T(8,128)S(1)} custom-call(f32[2,4,4,32,128]{4,3,2,1,0:T(8,128)S(1)} %pad_maximum_fusion.pieces), custom_call_target="tpu_custom_call" | custom-call | tf_op jit(solution)/shard_map/pallas_call | solution.py:719
  49.9 0.0 collective-permute-done.16
  50.0 2.9 %shard_map.61 = f32[16,16,128]{2,1,0:T(8,128)} custom-call(f32[12,32,128]{2,1,0:T(8,128)S(1)} %shard_map.60.coarse, f32[8,22,32,128]{3,2,1,0:T(8,128)S(1)} %get-tuple-element.41.top, f32[8,16,24,128]{3,2,1,0:T(8,128)S(1)} %get-tuple-element.42.mid, f32[48,128]{1,0:T(8,128)S(1)} %get-tuple-element.56.x_low, f32[48,128]{1,0:T(8,128)S(1)} %get-tuple-element.55.x_high, ...), custom_call_target="tpu_custom_call" | custom-call | tf_op jit(solution)/shard_map/pallas_call | solution.py:860
  (19 shorter events, 0.3 us)
Async XLA Ops:
  1.6 12.0 %collective-permute-start.7 = (f32[56,128]{1,0:T(8,128)S(1)}, f32[56,128]{1,0:T(8,128)S(1)}, u32[]{:S(2)}, u32[]{:S(2)}) collective-permute-start(f32[56,128]{1,0:T(8,128)S(1)} %get-tuple-element.61), channel_id=1, source_target_pairs={{5,10},{6,9},{9,6},{10,5},{13,18},{14,17},{17,14},{18,13},{21,26},... | collective-permute-start | bytes 86024 | tf_op jit(solution)/shard_map/ppermute | solution.py:758
  2.3 15.0 %collective-permute-start.5 = (f32[56,128]{1,0:T(8,128)S(1)}, f32[56,128]{1,0:T(8,128)S(1)}, u32[]{:S(2)}, u32[]{:S(2)}) collective-permute-start(f32[56,128]{1,0:T(8,128)S(1)} %get-tuple-element.62), channel_id=1, source_target_pairs={{4,9},{5,8},{6,11},{7,10},{8,5},{9,4},{10,7},{11,6},{12,17},{13,16... | collective-permute-start | bytes 86024 | tf_op jit(solution)/shard_map/ppermute | solution.py:758
  3.0 18.2 %collective-permute-start.6 = (f32[56,128]{1,0:T(8,128)S(1)}, f32[56,128]{1,0:T(8,128)S(1)}, u32[]{:S(2)}, u32[]{:S(2)}) collective-permute-start(f32[56,128]{1,0:T(8,128)S(1)} %get-tuple-element.63), channel_id=1, source_target_pairs={{1,6},{2,5},{5,2},{6,1},{9,14},{10,13},{13,10},{14,9},{17,22},{18,... | collective-permute-start | bytes 86024 | tf_op jit(solution)/shard_map/ppermute | solution.py:758
  11.9 9.4 %collective-permute-start.4 = (f32[56,128]{1,0:T(8,128)S(1)}, f32[56,128]{1,0:T(8,128)S(1)}, u32[]{:S(2)}, u32[]{:S(2)}) collective-permute-start(f32[56,128]{1,0:T(8,128)S(1)} %get-tuple-element.64), channel_id=1, source_target_pairs={{0,5},{1,4},{2,7},{3,6},{4,1},{5,0},{6,3},{7,2},{8,13},{9,12},{10,... | collective-permute-start | bytes 86024 | tf_op jit(solution)/shard_map/ppermute | solution.py:758
  12.4 8.9 %collective-permute-start.1 = (f32[240,128]{1,0:T(8,128)S(1)}, f32[240,128]{1,0:T(8,128)S(1)}, u32[]{:S(2)}, u32[]{:S(2)}) collective-permute-start(f32[240,128]{1,0:T(8,128)S(1)} %get-tuple-element.53), channel_id=1, source_target_pairs={{4,8},{5,9},{6,10},{7,11},{8,4},{9,5},{10,6},{11,7},{12,16},{13,17... | collective-permute-start | bytes 368648 | tf_op jit(solution)/shard_map/ppermute | solution.py:758
  13.6 7.8 %collective-permute-start = (f32[240,128]{1,0:T(8,128)S(1)}, f32[240,128]{1,0:T(8,128)S(1)}, u32[]{:S(2)}, u32[]{:S(2)}) collective-permute-start(f32[240,128]{1,0:T(8,128)S(1)} %get-tuple-element.54), channel_id=1, source_target_pairs={{0,4},{1,5},{2,6},{3,7},{4,0},{5,1},{6,2},{7,3},{8,12},{9,13},{10,... | collective-permute-start | bytes 368648 | tf_op jit(solution)/shard_map/ppermute | solution.py:758
  17.4 6.4 %collective-permute-start.3 = (f32[240,128]{1,0:T(8,128)S(1)}, f32[240,128]{1,0:T(8,128)S(1)}, u32[]{:S(2)}, u32[]{:S(2)}) collective-permute-start(f32[240,128]{1,0:T(8,128)S(1)} %get-tuple-element.49), channel_id=1, source_target_pairs={{1,2},{2,1},{5,6},{6,5},{9,10},{10,9},{13,14},{14,13},{17,18},{18,... | collective-permute-start | bytes 368648 | tf_op jit(solution)/shard_map/ppermute | solution.py:758
  21.2 2.5 %collective-permute-start.2 = (f32[240,128]{1,0:T(8,128)S(1)}, f32[240,128]{1,0:T(8,128)S(1)}, u32[]{:S(2)}, u32[]{:S(2)}) collective-permute-start(f32[240,128]{1,0:T(8,128)S(1)} %get-tuple-element.50), channel_id=1, source_target_pairs={{0,1},{1,0},{2,3},{3,2},{4,5},{5,4},{6,7},{7,6},{8,9},{9,8},{10,11... | collective-permute-start | bytes 368648 | tf_op jit(solution)/shard_map/ppermute | solution.py:758
  27.0 4.4 %collective-permute-start.10 = (f32[32,128]{1,0:T(8,128)S(1)}, f32[32,128]{1,0:T(8,128)S(1)}, u32[]{:S(2)}, u32[]{:S(2)}) collective-permute-start(f32[32,128]{1,0:T(8,128)S(1)} %get-tuple-element.35.refs_0_), channel_id=1, source_target_pairs={{0,24},{4,28},{8,16},{12,20},{16,8},{20,12},{24,0},{28,4},{1,25},{... | collective-permute-start | bytes 49160 | tf_op jit(solution)/shard_map/ppermute | solution.py:781
  28.1 3.5 %collective-permute-start.9 = (f32[32,128]{1,0:T(8,128)S(1)}, f32[32,128]{1,0:T(8,128)S(1)}, u32[]{:S(2)}, u32[]{:S(2)}) collective-permute-start(f32[32,128]{1,0:T(8,128)S(1)} %get-tuple-element.35.refs_0_), channel_id=1, source_target_pairs={{0,16},{4,20},{8,24},{12,28},{16,0},{20,4},{24,8},{28,12},{1,17},{... | collective-permute-start | bytes 49160 | tf_op jit(solution)/shard_map/ppermute | solution.py:781
  29.4 2.6 %collective-permute-start.8 = (f32[32,128]{1,0:T(8,128)S(1)}, f32[32,128]{1,0:T(8,128)S(1)}, u32[]{:S(2)}, u32[]{:S(2)}) collective-permute-start(f32[32,128]{1,0:T(8,128)S(1)} %get-tuple-element.35.refs_0_), channel_id=1, source_target_pairs={{0,8},{4,12},{8,0},{12,4},{16,24},{20,28},{24,16},{28,20},{1,9},{5... | collective-permute-start | bytes 49160 | tf_op jit(solution)/shard_map/ppermute | solution.py:781
  32.0 8.1 %collective-permute-start.13 = (f32[128,128]{1,0:T(8,128)S(1)}, f32[128,128]{1,0:T(8,128)S(1)}, u32[]{:S(2)}, u32[]{:S(2)}) collective-permute-start(f32[128,128]{1,0:T(8,128)S(1)} %bitcast.3), channel_id=1, source_target_pairs={{0,6},{1,7},{2,4},{3,5},{4,2},{5,3},{6,0},{7,1},{8,14},{9,15},{10,... | collective-permute-start | bytes 196616 | tf_op jit(solution)/shard_map/ppermute | solution.py:800
  33.6 4.0 %collective-permute-start.11 = (f32[128,128]{1,0:T(8,128)S(1)}, f32[128,128]{1,0:T(8,128)S(1)}, u32[]{:S(2)}, u32[]{:S(2)}) collective-permute-start(f32[128,128]{1,0:T(8,128)S(1)} %bitcast.4), channel_id=1, source_target_pairs={{0,2},{1,3},{2,0},{3,1},{4,6},{5,7},{6,4},{7,5},{8,10},{9,11},{10,... | collective-permute-start | bytes 196616 | tf_op jit(solution)/shard_map/ppermute | solution.py:800
  34.1 5.9 %collective-permute-start.14 = (f32[48,128]{1,0:T(8,128)S(1)}, f32[48,128]{1,0:T(8,128)S(1)}, u32[]{:S(2)}, u32[]{:S(2)}) collective-permute-start(f32[48,128]{1,0:T(8,128)S(1)} %get-tuple-element.69), channel_id=1, source_target_pairs={{4,8},{8,4},{12,16},{16,12},{20,24},{24,20},{5,9},{9,5},{13,17},{1... | collective-permute-start | bytes 73736 | tf_op jit(solution)/shard_map/ppermute | solution.py:839
  34.8 5.2 %collective-permute-start.12 = (f32[176,128]{1,0:T(8,128)S(1)}, f32[176,128]{1,0:T(8,128)S(1)}, u32[]{:S(2)}, u32[]{:S(2)}) collective-permute-start(f32[176,128]{1,0:T(8,128)S(1)} %pad_maximum_fusion.2), channel_id=1, source_target_pairs={{0,4},{1,5},{2,6},{3,7},{4,0},{5,1},{6,2},{7,3},{8,12},{9,13},{10,... | collective-permute-start | bytes 270344 | tf_op jit(solution)/shard_map/ppermute | solution.py:796
  40.2 6.5 %collective-permute-start.15 = (f32[584,128]{1,0:T(8,128)S(1)}, f32[584,128]{1,0:T(8,128)S(1)}, u32[]{:S(2)}, u32[]{:S(2)}) collective-permute-start(f32[584,128]{1,0:T(8,128)S(1)} %get-tuple-element.68), channel_id=1, source_target_pairs={{0,1},{1,0},{2,3},{3,2},{4,5},{5,4},{6,7},{7,6},{8,9},{9,8},{10,11... | collective-permute-start | bytes 897032 | tf_op jit(solution)/shard_map/ppermute | solution.py:846
  43.6 6.3 %collective-permute-start.16 = (f32[72,128]{1,0:T(8,128)S(1)}, f32[72,128]{1,0:T(8,128)S(1)}, u32[]{:S(2)}, u32[]{:S(2)}) collective-permute-start(f32[72,128]{1,0:T(8,128)S(1)} %get-tuple-element.67), channel_id=1, source_target_pairs={{1,2},{2,1},{5,6},{6,5},{9,10},{10,9},{13,14},{14,13},{17,18},{18,... | collective-permute-start | bytes 110600 | tf_op jit(solution)/shard_map/ppermute | solution.py:845

commit v9 on v7

--- a/solution.py
+++ b/solution.py
@@ -13,6 +13,7 @@
 RIM = 4
 EDGE = 3
 PAD = 8
+BLOCK_ROWS = 24
 F32 = jnp.float32
 
 V, F, FX, FY, ZL, ZH, W, D = range(8)
@@ -231,12 +232,10 @@
     above = pl.ds(start + 1, rows)
     v = src[slab, here]
     f = lev.at[F] if f is None else f
-    total = f[slab, here] + lev[FX, slab, here] * src[slab - 1, here]
-    total = total + lev[FX, slab + 1, here] * src[slab + 1, here]
-    total = total + lev[FY, slab, here] * src[slab, below]
-    total = total + lev[FY, slab, above] * src[slab, above]
-    total = total + lev[ZL, slab, here] * roll_lanes(v, 1)
-    total = total + lev[ZH, slab, here] * roll_lanes(v, -1)
+    x = lev[FX, slab, here] * src[slab - 1, here] + lev[FX, slab + 1, here] * src[slab + 1, here]
+    y = lev[FY, slab, here] * src[slab, below] + lev[FY, slab, above] * src[slab, above]
+    z = lev[ZL, slab, here] * roll_lanes(v, 1) + lev[ZH, slab, here] * roll_lanes(v, -1)
+    total = ((x + y) + f[slab, here]) + z
     return v, total
 
 
@@ -261,12 +260,9 @@
     lev[W, slab, here] = jnp.where(valid, OMEGA / jnp.where(valid, diagonal, 1.0), 0.0)
 
 
-def run(count, body, unroll=1):
-    def step(index, carry):
+def run(count, body):
+    for index in range(count):
         body(index)
-        return carry
-
-    lax.fori_loop(0, count, step, 0, unroll=unroll)
 
 
 def clear_pads(ref, rows):
@@ -306,13 +302,13 @@
         set_weights(top, slab, RIM, rows, LANES, inside)
         other[slab, main] = swept(top, start_v, slab, RIM, rows)
 
-    run(slabs - 2, first, 2)
+    run(slabs - 2, first)
 
     def second(index):
         slab = index + 2
         top[V, slab, main] = swept(top, other, slab, RIM, rows)
 
-    run(slabs - 4, second, 2)
+    run(slabs - 4, second)
 
     def rest(slab):
         v, total = weighted(top, top.at[V], slab, PAD, ny)
@@ -322,7 +318,7 @@
         slab = EDGE + 2 * index
         tmp[index] = rest(slab) + rest(slab + 1)
 
-    run(nx // 2, residual, 2)
+    run(nx // 2, residual)
 
     coarse_x, coarse_y = nx // 2, ny // 2
     slabs, rows = coarse_x + 2 * RIM, coarse_y + 2 * RIM
@@ -379,10 +375,11 @@
     for pair in range(1, half - 1):
         two[pair] = rest_1(2 * pair) + rest_1(2 * pair + 1)
     pieces = even_rows(two, rows) + odd_rows(two, rows)
-    for part in range(half // 4):
-        folded = fold_four([pieces[4 * part + i] for i in range(4)])
-        chunk[part * rows // 2 : (part + 1) * rows // 2] = 0.5 * folded
-    chunk[half // 4 * rows // 2 :] = coefficients[...]
+    coarse_rows, quarter_rows = rows // 2, rows // 4
+    chunk[:coarse_rows] = 0.5 * fold_four([pieces[1 + i] for i in range(4)])
+    rest_of = [pieces[5 + i // 2][i % 2 * quarter_rows :][:quarter_rows] for i in range(4)]
+    chunk[coarse_rows : coarse_rows + quarter_rows] = 0.5 * fold_four(rest_of)
+    chunk[coarse_rows + quarter_rows :] = coefficients[:BLOCK_ROWS - coarse_rows - quarter_rows]
 
 
 def pack_v(top, mid, x_low, x_high, low, high):
@@ -459,17 +456,37 @@
         for s in range(count):
             low = v[s - 1] if s > 0 else roll_lanes(v[count - 1], self.depth)
             high = v[s + 1] if s + 1 < count else roll_lanes(v[0], -self.depth)
-            total = f[s] + self.x_low[s] * low + self.x_high[s] * high
-            total = total + self.y_low[s] * roll_rows(v[s], self.stride)
-            total = total + self.y_high[s] * roll_rows(v[s], -self.stride)
-            total = total + self.z_low[s] * roll_lanes(v[s], self.stride)
-            total = total + self.z_high[s] * roll_lanes(v[s], -self.stride)
+            x = self.x_low[s] * low + self.x_high[s] * high
+            y = self.y_low[s] * roll_rows(v[s], self.stride) + self.y_high[s] * roll_rows(v[s], -self.stride)
+            z = self.z_low[s] * roll_lanes(v[s], self.stride) + self.z_high[s] * roll_lanes(v[s], -self.stride)
+            total = (f[s] + y) + (x + z)
             out.append(total)
         return out
 
     def sweep(self, v, f):
         totals = self.weighted(v, f)
         return [(1.0 - OMEGA) * v[s] + self.w[s] * totals[s] for s in range(self.count)]
+
+    def sweeps(self, count, f):
+        folded = [
+            [w * c for w, c in zip(self.w, coefficients)]
+            for coefficients in (self.x_low, self.x_high, self.y_low, self.y_high, self.z_low, self.z_high)
+        ]
+        scaled = self.start(f)
+        slabs = self.count
+
+        def step(index, v):
+            out = []
+            for s in range(slabs):
+                low = v[s - 1] if s > 0 else roll_lanes(v[slabs - 1], self.depth)
+                high = v[s + 1] if s + 1 < slabs else roll_lanes(v[0], -self.depth)
+                x = folded[0][s] * low + folded[1][s] * high
+                y = folded[2][s] * roll_rows(v[s], self.stride) + folded[3][s] * roll_rows(v[s], -self.stride)
+                z = folded[4][s] * roll_lanes(v[s], self.stride) + folded[5][s] * roll_lanes(v[s], -self.stride)
+                out.append((((1.0 - OMEGA) * v[s] + scaled[s]) + y) + (x + z))
+            return out
+
+        return lax.fori_loop(1, count, step, scaled)
 
     def start(self, f):
         return [self.w[s] * f[s] for s in range(self.count)]
@@ -513,10 +530,9 @@
 
 def listed_cycle(levels, sweeps, f):
     level = levels[0]
-    v = level.start(f)
     if len(levels) == 1:
-        return lax.fori_loop(0, sweeps - 1, lambda index, values: level.sweep(values, f), v)
-    v = level.sweep(v, f)
+        return level.sweeps(sweeps, f)
+    v = level.sweep(level.start(f), f)
     e = listed_cycle(levels[1:], sweeps, level.restrict(level.residual(v, f)))
     v = [a + b for a, b in zip(v, level.prolong(e))]
     return level.sweep(level.sweep(v, f), f)
@@ -545,13 +561,19 @@
         sums = [None] * count
         for gx in range(devices_x):
             where = piece(gx, gy)
-            layers = [pieces[where + (pl.ds(part * window, window),)] for part in range(2)]
+            first = pieces[where + (pl.ds(0, window),)]
+            second = pieces[where + (pl.ds(window, window // 2),)]
             for local in range(1, 2 * blocks - 1):
                 x = own_x * gx - reach + local
                 if not 0 <= x < devices_x * own_x:
                     continue
                 block, slab = x // count, x % count
-                moved = roll_lanes(layers[local // blocks], (block - local % blocks) * quarter)
+                if local <= blocks:
+                    moved = roll_lanes(first, (block - local + 1) * quarter)
+                else:
+                    at = 2 * (local - blocks - 1)
+                    halves = [roll_lanes(second, (block - at - odd) * quarter) for odd in range(2)]
+                    moved = jnp.concatenate(halves)
                 moved = jnp.where(lane // quarter == block, moved, 0.0)
                 sums[slab] = moved if sums[slab] is None else sums[slab] + moved
         place = pl.ds(PAD + own_y * gy - reach, window)
@@ -564,7 +586,7 @@
         for gy in range(devices_y):
             where = piece(gx, gy)
             for face in range(3):
-                values = pieces[where + (pl.ds(2 * window + face * own_y, own_y),)]
+                values = pieces[where + (pl.ds(window + window // 2 + face * own_y, own_y),)]
                 wide[face, gx, gy * own_y : (gy + 1) * own_y] = values
     faces = []
     for face in range(3):
@@ -679,18 +701,18 @@
         for slab in (EDGE - 2 + 2 * index, EDGE - 1 + 2 * index):
             post[0, slab, body] = post[0, slab, body] + up[index]
 
-    run(steps, raise_level, 2)
+    run(steps, raise_level)
 
     def fifth(index):
         slab = EDGE - 1 + index
         post[1, slab, body] = swept(top, post.at[0], slab, RIM, fine_rows)
 
-    run(nx + 2, fifth, 2)
+    run(nx + 2, fifth)
 
     def sixth(index):
         out[index] = swept(top, post.at[1], EDGE + index, PAD, ny)
 
-    run(nx, sixth, 2)
+    run(nx, sixth)
 
 
 IN_VMEM = pl.BlockSpec(memory_space=pltpu.VMEM)
@@ -785,7 +807,7 @@
     w_shape = (half * RIM + 2 * (nx + 4), LANES)
     top, mid, chunk, v_low, v_high = call(
         functools.partial(level_down, axes),
-        [(D + 1,) + stack, (D + 1,) + stack_1, (32, LANES), v_shape, v_shape],
+        [(D + 1,) + stack, (D + 1,) + stack_1, (BLOCK_ROWS, LANES), v_shape, v_shape],
         [stack, (nx // 2, ny, LANES), stack_1, (half, coarse_y + 2 * RIM, LANES)],
     )(own, faces, coefficients, x_low, x_high, y_low, y_high)
 

time: 50.9 us -> 48.3 us (0.949)
  Pallas kernels: 11.5 us -> 9.06 us
    pallas_call x7, Pallas kernels: 8.67 us -> 7.33 us  [launch(): pl.pallas_call(kernel, out_shape=[pltpu.VMEM(shape, F32) for shape in out...]
    pallas_call x1, Pallas kernels: 2.85 us -> 1.73 us  [fused_cycle(): pl.pallas_call(functools.partial(level_up, axes, grid), out_shape=jax.Sha...]
  transfers between devices with their start and end apart: 13 -> 13, of which waited for: 5 -> 5; matrix products, arithmetic and copies ran while one was open for 0% -> 0% of each run, Pallas kernels for 7% -> 8%
where the time goes in v9:
time: 48.3 us; the launch traced here: 47.8 us
  starting transfers between devices  25.1 us (52%)
  waiting for transfers between devices  13.3 us (28%)
  Pallas kernels  9.06 us (19%)
    pallas_call x7, Pallas kernels, launch(): pl.pallas_call(kernel, out_shape=[pltpu.VMEM(shape, F32) for shape in out...  7.33 us
    ppermute x2, waiting for transfers between devices, from_sides(): pair = lax.ppermute(pair, axis, pair_route(axis))  5.22 us
    ppermute x2, starting transfers between devices, from_sides(): pair = lax.ppermute(pair, axis, pair_route(axis))  4.69 us
    ppermute x3, starting transfers between devices, passed_round(): lax.ppermute(block, axis, [(i, i ^ distance) for i in range(count)])  4.64 us
    ppermute x2, starting transfers between devices, from_sides(): swap = lax.ppermute(swap, axis, swap_route(axis))  4.19 us
    ppermute x1, starting transfers between devices, fused_cycle(): swap = lax.ppermute(swap, 'gy', swap_route('gy'))  3.55 us
    ppermute x1, starting transfers between devices, passed_across(): both = lax.ppermute(jnp.concatenate((block, rider)), ('gx', 'gy'), route)  3.5 us
    ppermute x3, waiting for transfers between devices, passed_round(): lax.ppermute(block, axis, [(i, i ^ distance) for i in range(count)])  3.12 us
  transfers between devices with their start and end apart: 13, of which 5 were waited for; matrix products, arithmetic and copies ran while one was open for 0% of the time, Pallas kernels for 8%

profile of v9, /device:TPU:1, one launch (start us, length us, event | category | flops | bytes accessed | tf_op | source)
XLA Modules:
  0.0 47.8 jit_solution(7075317855794163524)
XLA Ops:
  0.0 1.6 %shard_map.55 = (f32[5,16,16,128]{3,2,1,0:T(8,128)S(1)}, f32[240,128]{1,0:T(8,128)S(1)}, f32[240,128]{1,0:T(8,128)S(1)}, f32[3,8,8,128]{3,2,1,0:T(8,128)S(1)}) custom-call(f32[16,16,128]{2,1,0:T(8,128)} %refs_0_.1, f32[16,16,128]{2,1,0:T(8,128)} %refs_1_.1, f32[16,16,128]{2,1,0:T(8,128)} %refs_2_.1, f32[16,16,128]{2,1,0:T(8,128)} %refs_3_.1, ...), custom_call_target="tpu_custom_call" | custom-call | tf_op jit(solution)/shard_map/pallas_call | solution.py:727
  1.6 0.7 %collective-permute-start.1 = (f32[240,128]{1,0:T(8,128)S(1)}, f32[240,128]{1,0:T(8,128)S(1)}, u32[]{:S(2)}, u32[]{:S(2)}) collective-permute-start(f32[240,128]{1,0:T(8,128)S(1)} %get-tuple-element.45), channel_id=1, source_target_pairs={{4,8},{8,4},{12,16},{16,12},{20,24},{24,20},{5,9},{9,5},{13,17},{1... | collective-permute-start | bytes 368648 | tf_op jit(solution)/shard_map/ppermute | solution.py:756
  2.3 4.6 %collective-permute-start = (f32[240,128]{1,0:T(8,128)S(1)}, f32[240,128]{1,0:T(8,128)S(1)}, u32[]{:S(2)}, u32[]{:S(2)}) collective-permute-start(f32[240,128]{1,0:T(8,128)S(1)} %get-tuple-element.46), channel_id=1, source_target_pairs={{0,4},{4,0},{8,12},{12,8},{16,20},{20,16},{24,28},{28,24},{1,5},{5... | collective-permute-start | bytes 368648 | tf_op jit(solution)/shard_map/ppermute | solution.py:755
  6.9 0.0 collective-permute-done.1
  6.9 5.2 %collective-permute-done = f32[240,128]{1,0:T(8,128)S(1)} collective-permute-done((f32[240,128]{1,0:T(8,128)S(1)}, f32[240,128]{1,0:T(8,128)S(1)}, u32[]{:S(2)}, u32[]{:S(2)}) %collective-permute-start) | collective-permute-done | bytes 122912 | tf_op jit(solution)/shard_map/ppermute | solution.py:755
  12.1 0.2 shard_map.57
  12.3 3.5 %collective-permute-start.3 = (f32[360,128]{1,0:T(8,128)S(1)}, f32[360,128]{1,0:T(8,128)S(1)}, u32[]{:S(2)}, u32[]{:S(2)}) collective-permute-start(f32[360,128]{1,0:T(8,128)S(1)} %get-tuple-element.39), channel_id=1, source_target_pairs={{1,2},{2,1},{5,6},{6,5},{9,10},{10,9},{13,14},{14,13},{17,18},{18,... | collective-permute-start | bytes 552968 | tf_op jit(solution)/shard_map/ppermute | solution.py:756
  15.9 0.1 collective-permute-start.2
  15.9 0.5 shard_map.56.coefficients
  16.4 2.8 %collective-permute-done.3 = f32[360,128]{1,0:T(8,128)S(1)} collective-permute-done((f32[360,128]{1,0:T(8,128)S(1)}, f32[360,128]{1,0:T(8,128)S(1)}, u32[]{:S(2)}, u32[]{:S(2)}) %collective-permute-start.3) | collective-permute-done | bytes 184352 | tf_op jit(solution)/shard_map/ppermute | solution.py:756
  19.2 0.0 collective-permute-done.2
  19.2 1.7 %shard_map.58 = (f32[8,22,32,128]{3,2,1,0:T(8,128)S(1)}, f32[8,16,24,128]{3,2,1,0:T(8,128)S(1)}, f32[24,128]{1,0:T(8,128)S(1)}, f32[48,128]{1,0:T(8,128)S(1)}, f32[48,128]{1,0:T(8,128)S(1)}) custom-call(f32[5,16,16,128]{3,2,1,0:T(8,128)S(1)} %get-tuple-element.21.own, f32[3,8,8,128]{3,2,1,0:T(8,128)S(1)} %get-tuple-element.22.faces, ...), custom_call_target="tpu_custom_call" | custom-call | tf_op jit(solution)/shard_map/pallas_call | solution.py:727
  20.9 4.3 %collective-permute-start.6 = (f32[24,128]{1,0:T(8,128)S(1)}, f32[24,128]{1,0:T(8,128)S(1)}, u32[]{:S(2)}, u32[]{:S(2)}) collective-permute-start(f32[24,128]{1,0:T(8,128)S(1)} %get-tuple-element.27.refs_0_), channel_id=1, source_target_pairs={{0,24},{4,28},{8,16},{12,20},{16,8},{20,12},{24,0},{28,4},{1,25},{... | collective-permute-start | bytes 36872 | tf_op jit(solution)/shard_map/ppermute | solution.py:763
  25.3 0.0 collective-permute-start.5
  25.3 0.3 collective-permute-start.4
  25.6 0.8 %collective-permute-done.6.refs_3_ = f32[24,128]{1,0:T(8,128)S(1)} collective-permute-done((f32[24,128]{1,0:T(8,128)S(1)}, f32[24,128]{1,0:T(8,128)S(1)}, u32[]{:S(2)}, u32[]{:S(2)}) %collective-permute-start.6) | collective-permute-done | bytes 12320 | tf_op jit(solution)/shard_map/ppermute | solution.py:763
  26.3 2.4 %collective-permute-done.5.refs_2_ = f32[24,128]{1,0:T(8,128)S(1)} collective-permute-done((f32[24,128]{1,0:T(8,128)S(1)}, f32[24,128]{1,0:T(8,128)S(1)}, u32[]{:S(2)}, u32[]{:S(2)}) %collective-permute-start.5) | collective-permute-done | bytes 12320 | tf_op jit(solution)/shard_map/ppermute | solution.py:763
  28.7 0.0 collective-permute-done.4.refs_1_
  28.7 0.1 collective-permute-start.9
  28.8 0.7 %collective-permute-start.7 = (f32[96,128]{1,0:T(8,128)S(1)}, f32[96,128]{1,0:T(8,128)S(1)}, u32[]{:S(2)}, u32[]{:S(2)}) collective-permute-start(f32[96,128]{1,0:T(8,128)S(1)} %bitcast.4), channel_id=1, source_target_pairs={{0,2},{1,3},{2,0},{3,1},{4,6},{5,7},{6,4},{7,5},{8,10},{9,11},{10,... | collective-permute-start | bytes 147464 | tf_op jit(solution)/shard_map/ppermute | solution.py:782
  29.5 0.7 %collective-permute-start.10 = (f32[48,128]{1,0:T(8,128)S(1)}, f32[48,128]{1,0:T(8,128)S(1)}, u32[]{:S(2)}, u32[]{:S(2)}) collective-permute-start(f32[48,128]{1,0:T(8,128)S(1)} %get-tuple-element.53), channel_id=1, source_target_pairs={{4,8},{8,4},{12,16},{16,12},{20,24},{24,20},{5,9},{9,5},{13,17},{1... | collective-permute-start | bytes 73736 | tf_op jit(solution)/shard_map/ppermute | solution.py:820
  30.2 3.5 %collective-permute-start.8 = (f32[144,128]{1,0:T(8,128)S(1)}, f32[144,128]{1,0:T(8,128)S(1)}, u32[]{:S(2)}, u32[]{:S(2)}) collective-permute-start(f32[144,128]{1,0:T(8,128)S(1)} %pad_maximum_fusion.2), channel_id=1, source_target_pairs={{0,4},{1,5},{2,6},{3,7},{4,0},{5,1},{6,2},{7,3},{8,12},{9,13},{10,... | collective-permute-start | bytes 221192 | tf_op jit(solution)/shard_map/ppermute | solution.py:778
  33.7 0.0 collective-permute-done.7
  33.7 2.1 %collective-permute-done.8 = f32[144,128]{1,0:T(8,128)S(1)} collective-permute-done((f32[144,128]{1,0:T(8,128)S(1)}, f32[144,128]{1,0:T(8,128)S(1)}, u32[]{:S(2)}, u32[]{:S(2)}) %collective-permute-start.8) | collective-permute-done | bytes 73760 | tf_op jit(solution)/shard_map/ppermute | solution.py:778
  35.9 0.0 collective-permute-done.10
  35.9 0.1 shard_map.60
  36.0 0.0 collective-permute-done.9
  36.1 3.1 %collective-permute-start.11 = (f32[456,128]{1,0:T(8,128)S(1)}, f32[456,128]{1,0:T(8,128)S(1)}, u32[]{:S(2)}, u32[]{:S(2)}) collective-permute-start(f32[456,128]{1,0:T(8,128)S(1)} %get-tuple-element.50), channel_id=1, source_target_pairs={{0,1},{1,0},{2,3},{3,2},{4,5},{5,4},{6,7},{7,6},{8,9},{9,8},{10,11... | collective-permute-start | bytes 700424 | tf_op jit(solution)/shard_map/ppermute | solution.py:827
  39.1 3.5 %collective-permute-start.12 = (f32[72,128]{1,0:T(8,128)S(1)}, f32[72,128]{1,0:T(8,128)S(1)}, u32[]{:S(2)}, u32[]{:S(2)}) collective-permute-start(f32[72,128]{1,0:T(8,128)S(1)} %get-tuple-element.49), channel_id=1, source_target_pairs={{1,2},{2,1},{5,6},{6,5},{9,10},{10,9},{13,14},{14,13},{17,18},{18,... | collective-permute-start | bytes 110600 | tf_op jit(solution)/shard_map/ppermute | solution.py:826
  42.7 0.0 collective-permute-done.11
  42.8 3.3 %shard_map.61.coarse = f32[12,32,128]{2,1,0:T(8,128)S(1)} custom-call(f32[2,4,4,24,128]{4,3,2,1,0:T(8,128)S(1)} %pad_maximum_fusion.pieces), custom_call_target="tpu_custom_call" | custom-call | tf_op jit(solution)/shard_map/pallas_call | solution.py:727
  46.0 0.0 collective-permute-done.12
  46.1 1.7 %shard_map.62 = f32[16,16,128]{2,1,0:T(8,128)} custom-call(f32[12,32,128]{2,1,0:T(8,128)S(1)} %shard_map.61.coarse, f32[8,22,32,128]{3,2,1,0:T(8,128)S(1)} %get-tuple-element.33.top, f32[8,16,24,128]{3,2,1,0:T(8,128)S(1)} %get-tuple-element.34.mid, f32[48,128]{1,0:T(8,128)S(1)} %get-tuple-element.48.x_low, f32[48,128]{1,0:T(8,128)S(1)} %get-tuple-element.47.x_high, ...), custom_call_target="tpu_custom_call" | custom-call | tf_op jit(solution)/shard_map/pallas_call | solution.py:841
  (17 shorter events, 0.2 us)
Async XLA Ops:
  1.6 5.3 %collective-permute-start.1 = (f32[240,128]{1,0:T(8,128)S(1)}, f32[240,128]{1,0:T(8,128)S(1)}, u32[]{:S(2)}, u32[]{:S(2)}) collective-permute-start(f32[240,128]{1,0:T(8,128)S(1)} %get-tuple-element.45), channel_id=1, source_target_pairs={{4,8},{8,4},{12,16},{16,12},{20,24},{24,20},{5,9},{9,5},{13,17},{1... | collective-permute-start | bytes 368648 | tf_op jit(solution)/shard_map/ppermute | solution.py:756
  2.3 9.8 %collective-permute-start = (f32[240,128]{1,0:T(8,128)S(1)}, f32[240,128]{1,0:T(8,128)S(1)}, u32[]{:S(2)}, u32[]{:S(2)}) collective-permute-start(f32[240,128]{1,0:T(8,128)S(1)} %get-tuple-element.46), channel_id=1, source_target_pairs={{0,4},{4,0},{8,12},{12,8},{16,20},{20,16},{24,28},{28,24},{1,5},{5... | collective-permute-start | bytes 368648 | tf_op jit(solution)/shard_map/ppermute | solution.py:755
  12.3 6.9 %collective-permute-start.3 = (f32[360,128]{1,0:T(8,128)S(1)}, f32[360,128]{1,0:T(8,128)S(1)}, u32[]{:S(2)}, u32[]{:S(2)}) collective-permute-start(f32[360,128]{1,0:T(8,128)S(1)} %get-tuple-element.39), channel_id=1, source_target_pairs={{1,2},{2,1},{5,6},{6,5},{9,10},{10,9},{13,14},{14,13},{17,18},{18,... | collective-permute-start | bytes 552968 | tf_op jit(solution)/shard_map/ppermute | solution.py:756
  15.9 3.3 %collective-permute-start.2 = (f32[360,128]{1,0:T(8,128)S(1)}, f32[360,128]{1,0:T(8,128)S(1)}, u32[]{:S(2)}, u32[]{:S(2)}) collective-permute-start(f32[360,128]{1,0:T(8,128)S(1)} %get-tuple-element.40), channel_id=1, source_target_pairs={{0,1},{1,0},{2,3},{3,2},{4,5},{5,4},{6,7},{7,6},{8,9},{9,8},{10,11... | collective-permute-start | bytes 552968 | tf_op jit(solution)/shard_map/ppermute | solution.py:755
  20.9 5.4 %collective-permute-start.6 = (f32[24,128]{1,0:T(8,128)S(1)}, f32[24,128]{1,0:T(8,128)S(1)}, u32[]{:S(2)}, u32[]{:S(2)}) collective-permute-start(f32[24,128]{1,0:T(8,128)S(1)} %get-tuple-element.27.refs_0_), channel_id=1, source_target_pairs={{0,24},{4,28},{8,16},{12,20},{16,8},{20,12},{24,0},{28,4},{1,25},{... | collective-permute-start | bytes 36872 | tf_op jit(solution)/shard_map/ppermute | solution.py:763
  25.3 3.4 %collective-permute-start.5 = (f32[24,128]{1,0:T(8,128)S(1)}, f32[24,128]{1,0:T(8,128)S(1)}, u32[]{:S(2)}, u32[]{:S(2)}) collective-permute-start(f32[24,128]{1,0:T(8,128)S(1)} %get-tuple-element.27.refs_0_), channel_id=1, source_target_pairs={{0,16},{4,20},{8,24},{12,28},{16,0},{20,4},{24,8},{28,12},{1,17},{... | collective-permute-start | bytes 36872 | tf_op jit(solution)/shard_map/ppermute | solution.py:763
  25.3 3.4 %collective-permute-start.4 = (f32[24,128]{1,0:T(8,128)S(1)}, f32[24,128]{1,0:T(8,128)S(1)}, u32[]{:S(2)}, u32[]{:S(2)}) collective-permute-start(f32[24,128]{1,0:T(8,128)S(1)} %get-tuple-element.27.refs_0_), channel_id=1, source_target_pairs={{0,8},{4,12},{8,0},{12,4},{16,24},{20,28},{24,16},{28,20},{1,9},{5... | collective-permute-start | bytes 36872 | tf_op jit(solution)/shard_map/ppermute | solution.py:763
  28.7 7.3 %collective-permute-start.9 = (f32[96,128]{1,0:T(8,128)S(1)}, f32[96,128]{1,0:T(8,128)S(1)}, u32[]{:S(2)}, u32[]{:S(2)}) collective-permute-start(f32[96,128]{1,0:T(8,128)S(1)} %bitcast.3), channel_id=1, source_target_pairs={{0,6},{1,7},{2,4},{3,5},{4,2},{5,3},{6,0},{7,1},{8,14},{9,15},{10,... | collective-permute-start | bytes 147464 | tf_op jit(solution)/shard_map/ppermute | solution.py:782
  28.8 4.9 %collective-permute-start.7 = (f32[96,128]{1,0:T(8,128)S(1)}, f32[96,128]{1,0:T(8,128)S(1)}, u32[]{:S(2)}, u32[]{:S(2)}) collective-permute-start(f32[96,128]{1,0:T(8,128)S(1)} %bitcast.4), channel_id=1, source_target_pairs={{0,2},{1,3},{2,0},{3,1},{4,6},{5,7},{6,4},{7,5},{8,10},{9,11},{10,... | collective-permute-start | bytes 147464 | tf_op jit(solution)/shard_map/ppermute | solution.py:782
  29.5 6.4 %collective-permute-start.10 = (f32[48,128]{1,0:T(8,128)S(1)}, f32[48,128]{1,0:T(8,128)S(1)}, u32[]{:S(2)}, u32[]{:S(2)}) collective-permute-start(f32[48,128]{1,0:T(8,128)S(1)} %get-tuple-element.53), channel_id=1, source_target_pairs={{4,8},{8,4},{12,16},{16,12},{20,24},{24,20},{5,9},{9,5},{13,17},{1... | collective-permute-start | bytes 73736 | tf_op jit(solution)/shard_map/ppermute | solution.py:820
  30.2 5.7 %collective-permute-start.8 = (f32[144,128]{1,0:T(8,128)S(1)}, f32[144,128]{1,0:T(8,128)S(1)}, u32[]{:S(2)}, u32[]{:S(2)}) collective-permute-start(f32[144,128]{1,0:T(8,128)S(1)} %pad_maximum_fusion.2), channel_id=1, source_target_pairs={{0,4},{1,5},{2,6},{3,7},{4,0},{5,1},{6,2},{7,3},{8,12},{9,13},{10,... | collective-permute-start | bytes 221192 | tf_op jit(solution)/shard_map/ppermute | solution.py:778
  36.1 6.6 %collective-permute-start.11 = (f32[456,128]{1,0:T(8,128)S(1)}, f32[456,128]{1,0:T(8,128)S(1)}, u32[]{:S(2)}, u32[]{:S(2)}) collective-permute-start(f32[456,128]{1,0:T(8,128)S(1)} %get-tuple-element.50), channel_id=1, source_target_pairs={{0,1},{1,0},{2,3},{3,2},{4,5},{5,4},{6,7},{7,6},{8,9},{9,8},{10,11... | collective-permute-start | bytes 700424 | tf_op jit(solution)/shard_map/ppermute | solution.py:827
  39.1 6.9 %collective-permute-start.12 = (f32[72,128]{1,0:T(8,128)S(1)}, f32[72,128]{1,0:T(8,128)S(1)}, u32[]{:S(2)}, u32[]{:S(2)}) collective-permute-start(f32[72,128]{1,0:T(8,128)S(1)} %get-tuple-element.49), channel_id=1, source_target_pairs={{1,2},{2,1},{5,6},{6,5},{9,10},{10,9},{13,14},{14,13},{17,18},{18,... | collective-permute-start | bytes 110600 | tf_op jit(solution)/shard_map/ppermute | solution.py:826

commit v10 on v9

--- a/solution.py
+++ b/solution.py
@@ -20,6 +20,7 @@
 SLOTS = (F, V, FX, FY, ZL)
 X_LAYERS = (2, 3, 3, 2, 2)
 Y_LAYERS = (2, 3, 2, 3, 2)
+Y_REACH = (1, 2, 2, 2, 1)
 
 
 def lanes_of(shape):
@@ -97,15 +98,18 @@
 
 
 def y_rows(nx, ny):
-    return sum(Y_LAYERS) * (nx + 2 * EDGE), 3 * (nx // 2 + 2 * RIM) // 2 * RIM
+    fine = sum(layers * (nx + 2 * reach) for layers, reach in zip(Y_LAYERS, Y_REACH))
+    return fine, 3 * (nx // 2 + 2 * RIM) // 2 * RIM
 
 
 def x_place(index, layer, ny):
     return pl.ds((sum(X_LAYERS[:index]) + layer) * ny, ny)
 
 
-def y_place(index, slab, slabs):
-    return pl.ds(sum(Y_LAYERS[:index]) * slabs + slab * Y_LAYERS[index], Y_LAYERS[index])
+def y_place(index, slab, nx):
+    before = zip(Y_LAYERS[:index], Y_REACH[:index])
+    start = sum(layers * (nx + 2 * reach) for layers, reach in before)
+    return pl.ds(start + (Y_REACH[index] + slab) * Y_LAYERS[index], Y_LAYERS[index])
 
 
 def start_pack(*refs):
@@ -168,18 +172,16 @@
 def pack_y(own, faces, x_low, x_high, low, high):
     coarse_x, coarse_y = faces.shape[1:3]
     nx, ny = 2 * coarse_x, 2 * coarse_y
-    slabs = nx + 2 * EDGE
     for index in range(5):
-        width, layers = Y_LAYERS[index], X_LAYERS[index]
+        width, layers, reach = Y_LAYERS[index], X_LAYERS[index], Y_REACH[index]
         for out, start in ((low, 0), (high, ny - width)):
             for slab in range(nx):
-                out[y_place(index, EDGE + slab, slabs)] = own[index, slab, start : start + width]
-            for layer in range(EDGE):
-                near, far = layer + layers - EDGE, layer
-                rows = pl.ds(x_place(index, max(near, 0), ny).start + start, width)
-                out[y_place(index, layer, slabs)] = x_low[rows]
-                rows = pl.ds(x_place(index, min(far, layers - 1), ny).start + start, width)
-                out[y_place(index, EDGE + nx + layer, slabs)] = x_high[rows]
+                out[y_place(index, slab, nx)] = own[index, slab, start : start + width]
+            for layer in range(reach):
+                rows = pl.ds(x_place(index, layers - reach + layer, ny).start + start, width)
+                out[y_place(index, layer - reach, nx)] = x_low[rows]
+                rows = pl.ds(x_place(index, layer, ny).start + start, width)
+                out[y_place(index, nx + layer, nx)] = x_high[rows]
     base_x, base_y = x_rows(nx, ny)[0], y_rows(nx, ny)[0]
     half = (coarse_x + 2 * RIM) // 2
     for face in range(3):
@@ -288,9 +290,9 @@
             else:
                 top[slot, EDGE - 1 - layer, inner] = jnp.zeros((ny, LANES), F32)
                 top[slot, EDGE + nx + layer, inner] = jnp.zeros((ny, LANES), F32)
-        for slab in range(slabs):
-            top[slot, slab, PAD - width : PAD] = y_low[y_place(index, slab, slabs)]
-            top[slot, slab, PAD + ny : PAD + ny + width] = y_high[y_place(index, slab, slabs)]
+        for slab in range(-Y_REACH[index], nx + Y_REACH[index]):
+            top[slot, EDGE + slab, PAD - width : PAD] = y_low[y_place(index, slab, nx)]
+            top[slot, EDGE + slab, PAD + ny : PAD + ny + width] = y_high[y_place(index, slab, nx)]
     clear_pads(other, rows)
     row_inside = (rows_of((rows, LANES)) >= RIM) | (me_y > 0)
     main = pl.ds(RIM, rows)
@@ -412,12 +414,9 @@
             out[pl.ds(base_y + 2 * (2 + slab), 2)] = top[V, EDGE + slab, pl.ds(PAD + start, 2)]
 
 
-def stack_blocks(count, blocks, *refs):
-    for index in range(blocks):
-        refs[count][index] = refs[index][...]
-    for index in range(blocks, count):
-        if index + 1 - blocks < len(refs) - count:
-            refs[count + 1 + index - blocks][...] = refs[index][...]
+def stack_blocks(*refs):
+    for index, ref in enumerate(refs[:-3]):
+        refs[-1][index] = ref[...]
 
 
 def pair_rows(values, stride):
@@ -765,22 +764,17 @@
     ]
 
 
-def passed_across(block, rider):
+def passed_across(block):
     count, size = lax.axis_size("gx"), lax.axis_size("gy")
-    rows = block.shape[0]
-    blocks = [block]
+    blocks = []
     for side in range(2):
         for distance in range(0, size, 2):
             route = [
                 (x * size + y, (x ^ side) * size + (y ^ distance)) for x in range(count) for y in range(size)
             ]
-            if side == 1 and distance == 0:
-                both = lax.ppermute(jnp.concatenate((block, rider)), ("gx", "gy"), route)
-                blocks.append(both[:rows])
-                rider = both[rows:]
-            elif distance > 0:
-                blocks.append(lax.ppermute(block, ("gx", "gy"), route))
-    return blocks, rider
+            moved = side + distance > 0
+            blocks.append(lax.ppermute(block, ("gx", "gy"), route) if moved else block)
+    return blocks
 
 
 def fused_cycle(*fields):
@@ -812,14 +806,10 @@
     )(own, faces, coefficients, x_low, x_high, y_low, y_high)
 
     blocks = passed_round(chunk, "gx", 2)
+    v_low, v_high = from_sides(v_low, v_high, "gx")
     slow = (len(blocks),) + chunk.shape
-    pieces, v_low, v_high = call(
-        functools.partial(stack_blocks, len(blocks) + 2, len(blocks)), [slow, v_shape, v_shape]
-    )(*blocks, v_low, v_high)
-    pair, swap = by_partner(v_low, v_high, "gx")
-    swap = lax.ppermute(swap, "gx", swap_route("gx"))
-    blocks, pair = passed_across(pieces.reshape(-1, LANES), pair)
-    v_low, v_high = by_partner(pair, swap, "gx")
+    (pieces,) = call(stack_blocks, [slow])(*blocks, v_low, v_high)
+    blocks = passed_across(pieces.reshape(-1, LANES))
     w_low, w_high = call(pack_v, [w_shape] * 2)(top, mid, v_low, v_high)
     pair, swap = by_partner(w_low, w_high, "gy")
     message = jnp.concatenate(blocks + [pair])

time: 48.3 us -> 48.6 us (level)
  starting transfers between devices: 25.1 us -> 27.5 us
  waiting for transfers between devices: 13.3 us -> 11.4 us
    ppermute x2 -> x3, starting transfers between devices: 4.69 us -> 9.47 us  [from_sides(): pair = lax.ppermute(pair, axis, pair_route(axis))]
    ppermute x4 -> x3, starting transfers between devices: 4.93 us -> 2.69 us  [passed_across(): blocks.append(lax.ppermute(block, ('gx', 'gy'), route) if moved else block)]
    ppermute x1, starting transfers between devices: 3.06 us -> 4.94 us  [fused_cycle(): other = lax.ppermute(message, 'gy', pair_route('gy'))]
    ppermute x1, starting transfers between devices: 3.55 us -> 2.03 us  [fused_cycle(): swap = lax.ppermute(swap, 'gy', swap_route('gy'))]
    ppermute x3, waiting for transfers between devices: 3.12 us -> 1.93 us  [passed_round(): lax.ppermute(block, axis, [(i, i ^ distance) for i in range(count)])]
    ppermute x3, starting transfers between devices: 4.64 us -> 3.55 us  [passed_round(): lax.ppermute(block, axis, [(i, i ^ distance) for i in range(count)])]
    ppermute x2 -> x3, starting transfers between devices: 4.19 us -> 4.85 us  [from_sides(): swap = lax.ppermute(swap, axis, swap_route(axis))]
    ppermute x4 -> x3, waiting for transfers between devices: 2.16 us -> 1.66 us  [passed_across(): blocks.append(lax.ppermute(block, ('gx', 'gy'), route) if moved else block)]
  transfers between devices with their start and end apart: 13 -> 14, of which waited for: 5 -> 5; matrix products, arithmetic and copies ran while one was open for 0% -> 0% of each run, Pallas kernels for 8% -> 8%
where the time goes in v10:
time: 48.6 us; the launch traced here: 48.4 us
  starting transfers between devices  27.5 us (57%)
  waiting for transfers between devices  11.4 us (23%)
  Pallas kernels  9.05 us (19%)
    ppermute x3, starting transfers between devices, from_sides(): pair = lax.ppermute(pair, axis, pair_route(axis))  9.47 us
    pallas_call x7, Pallas kernels, launch(): pl.pallas_call(kernel, out_shape=[pltpu.VMEM(shape, F32) for shape in out...  7.32 us
    ppermute x3, waiting for transfers between devices, from_sides(): pair = lax.ppermute(pair, axis, pair_route(axis))  5.22 us
    ppermute x1, starting transfers between devices, fused_cycle(): other = lax.ppermute(message, 'gy', pair_route('gy'))  4.94 us
    ppermute x3, starting transfers between devices, from_sides(): swap = lax.ppermute(swap, axis, swap_route(axis))  4.85 us
    ppermute x3, starting transfers between devices, passed_round(): lax.ppermute(block, axis, [(i, i ^ distance) for i in range(count)])  3.55 us
    ppermute x3, starting transfers between devices, passed_across(): blocks.append(lax.ppermute(block, ('gx', 'gy'), route) if moved else block)  2.69 us
    ppermute x3, waiting for transfers between devices, from_sides(): swap = lax.ppermute(swap, axis, swap_route(axis))  2.6 us
  transfers between devices with their start and end apart: 14, of which 5 were waited for; matrix products, arithmetic and copies ran while one was open for 0% of the time, Pallas kernels for 8%

profile of v10, /device:TPU:1, one launch (start us, length us, event | category | flops | bytes accessed | tf_op | source)
XLA Modules:
  0.0 48.4 jit_solution(10220213020821666870)
XLA Ops:
  0.0 1.6 %shard_map.55 = (f32[5,16,16,128]{3,2,1,0:T(8,128)S(1)}, f32[240,128]{1,0:T(8,128)S(1)}, f32[240,128]{1,0:T(8,128)S(1)}, f32[3,8,8,128]{3,2,1,0:T(8,128)S(1)}) custom-call(f32[16,16,128]{2,1,0:T(8,128)} %refs_0_.1, f32[16,16,128]{2,1,0:T(8,128)} %refs_1_.1, f32[16,16,128]{2,1,0:T(8,128)} %refs_2_.1, f32[16,16,128]{2,1,0:T(8,128)} %refs_3_.1, ...), custom_call_target="tpu_custom_call" | custom-call | tf_op jit(solution)/shard_map/pallas_call | solution.py:726
  1.6 0.7 %collective-permute-start.1 = (f32[240,128]{1,0:T(8,128)S(1)}, f32[240,128]{1,0:T(8,128)S(1)}, u32[]{:S(2)}, u32[]{:S(2)}) collective-permute-start(f32[240,128]{1,0:T(8,128)S(1)} %get-tuple-element.39), channel_id=1, source_target_pairs={{4,8},{8,4},{12,16},{16,12},{20,24},{24,20},{5,9},{9,5},{13,17},{1... | collective-permute-start | bytes 368648 | tf_op jit(solution)/shard_map/ppermute | solution.py:755
  2.3 4.6 %collective-permute-start = (f32[240,128]{1,0:T(8,128)S(1)}, f32[240,128]{1,0:T(8,128)S(1)}, u32[]{:S(2)}, u32[]{:S(2)}) collective-permute-start(f32[240,128]{1,0:T(8,128)S(1)} %get-tuple-element.40), channel_id=1, source_target_pairs={{0,4},{4,0},{8,12},{12,8},{16,20},{20,16},{24,28},{28,24},{1,5},{5... | collective-permute-start | bytes 368648 | tf_op jit(solution)/shard_map/ppermute | solution.py:754
  6.9 0.0 collective-permute-done.1
  6.9 5.2 %collective-permute-done = f32[240,128]{1,0:T(8,128)S(1)} collective-permute-done((f32[240,128]{1,0:T(8,128)S(1)}, f32[240,128]{1,0:T(8,128)S(1)}, u32[]{:S(2)}, u32[]{:S(2)}) %collective-permute-start) | collective-permute-done | bytes 122912 | tf_op jit(solution)/shard_map/ppermute | solution.py:754
  12.1 0.1 shard_map.57
  12.3 3.5 %collective-permute-start.3 = (f32[328,128]{1,0:T(8,128)S(1)}, f32[328,128]{1,0:T(8,128)S(1)}, u32[]{:S(2)}, u32[]{:S(2)}) collective-permute-start(f32[328,128]{1,0:T(8,128)S(1)} %get-tuple-element.33), channel_id=1, source_target_pairs={{1,2},{2,1},{5,6},{6,5},{9,10},{10,9},{13,14},{14,13},{17,18},{18,... | collective-permute-start | bytes 503816 | tf_op jit(solution)/shard_map/ppermute | solution.py:755
  15.9 0.1 collective-permute-start.2
  15.9 0.5 shard_map.56.coefficients
  16.4 2.6 %collective-permute-done.3 = f32[328,128]{1,0:T(8,128)S(1)} collective-permute-done((f32[328,128]{1,0:T(8,128)S(1)}, f32[328,128]{1,0:T(8,128)S(1)}, u32[]{:S(2)}, u32[]{:S(2)}) %collective-permute-start.3) | collective-permute-done | bytes 167968 | tf_op jit(solution)/shard_map/ppermute | solution.py:755
  19.0 0.0 collective-permute-done.2
  19.0 1.7 %shard_map.58 = (f32[8,22,32,128]{3,2,1,0:T(8,128)S(1)}, f32[8,16,24,128]{3,2,1,0:T(8,128)S(1)}, f32[24,128]{1,0:T(8,128)S(1)}, f32[48,128]{1,0:T(8,128)S(1)}, f32[48,128]{1,0:T(8,128)S(1)}) custom-call(f32[5,16,16,128]{3,2,1,0:T(8,128)S(1)} %get-tuple-element.18.own, f32[3,8,8,128]{3,2,1,0:T(8,128)S(1)} %get-tuple-element.19.faces, ...), custom_call_target="tpu_custom_call" | custom-call | tf_op jit(solution)/shard_map/pallas_call | solution.py:726
  20.8 0.7 %collective-permute-start.8 = (f32[48,128]{1,0:T(8,128)S(1)}, f32[48,128]{1,0:T(8,128)S(1)}, u32[]{:S(2)}, u32[]{:S(2)}) collective-permute-start(f32[48,128]{1,0:T(8,128)S(1)} %get-tuple-element.45), channel_id=1, source_target_pairs={{4,8},{8,4},{12,16},{16,12},{20,24},{24,20},{5,9},{9,5},{13,17},{1... | collective-permute-start | bytes 73736 | tf_op jit(solution)/shard_map/ppermute | solution.py:755
  21.4 4.8 %collective-permute-start.7 = (f32[48,128]{1,0:T(8,128)S(1)}, f32[48,128]{1,0:T(8,128)S(1)}, u32[]{:S(2)}, u32[]{:S(2)}) collective-permute-start(f32[48,128]{1,0:T(8,128)S(1)} %get-tuple-element.46), channel_id=1, source_target_pairs={{0,4},{4,0},{8,12},{12,8},{16,20},{20,16},{24,28},{28,24},{1,5},{5... | collective-permute-start | bytes 73736 | tf_op jit(solution)/shard_map/ppermute | solution.py:754
  26.2 2.0 %collective-permute-start.6 = (f32[24,128]{1,0:T(8,128)S(1)}, f32[24,128]{1,0:T(8,128)S(1)}, u32[]{:S(2)}, u32[]{:S(2)}) collective-permute-start(f32[24,128]{1,0:T(8,128)S(1)} %get-tuple-element.24.refs_0_), channel_id=1, source_target_pairs={{0,24},{4,28},{8,16},{12,20},{16,8},{20,12},{24,0},{28,4},{1,25},{... | collective-permute-start | bytes 36872 | tf_op jit(solution)/shard_map/ppermute | solution.py:762
  28.2 0.5 collective-permute-start.5
  28.7 1.1 %collective-permute-start.4 = (f32[24,128]{1,0:T(8,128)S(1)}, f32[24,128]{1,0:T(8,128)S(1)}, u32[]{:S(2)}, u32[]{:S(2)}) collective-permute-start(f32[24,128]{1,0:T(8,128)S(1)} %get-tuple-element.24.refs_0_), channel_id=1, source_target_pairs={{0,8},{4,12},{8,0},{12,4},{16,24},{20,28},{24,16},{28,20},{1,9},{5... | collective-permute-start | bytes 36872 | tf_op jit(solution)/shard_map/ppermute | solution.py:762
  29.8 0.0 collective-permute-done.8
  29.8 0.0 collective-permute-done.7
  29.8 0.8 %collective-permute-done.6.refs_3_ = f32[24,128]{1,0:T(8,128)S(1)} collective-permute-done((f32[24,128]{1,0:T(8,128)S(1)}, f32[24,128]{1,0:T(8,128)S(1)}, u32[]{:S(2)}, u32[]{:S(2)}) %collective-permute-start.6) | collective-permute-done | bytes 12320 | tf_op jit(solution)/shard_map/ppermute | solution.py:762
  30.6 1.1 %collective-permute-done.5.refs_2_ = f32[24,128]{1,0:T(8,128)S(1)} collective-permute-done((f32[24,128]{1,0:T(8,128)S(1)}, f32[24,128]{1,0:T(8,128)S(1)}, u32[]{:S(2)}, u32[]{:S(2)}) %collective-permute-start.5) | collective-permute-done | bytes 12320 | tf_op jit(solution)/shard_map/ppermute | solution.py:762
  31.7 0.0 collective-permute-done.4.refs_1_
  31.7 0.1 collective-permute-start.11
  31.8 1.5 %collective-permute-start.10 = (f32[96,128]{1,0:T(8,128)S(1)}, f32[96,128]{1,0:T(8,128)S(1)}, u32[]{:S(2)}, u32[]{:S(2)}) collective-permute-start(f32[96,128]{1,0:T(8,128)S(1)} %bitcast.4), channel_id=1, source_target_pairs={{0,4},{1,5},{2,6},{3,7},{4,0},{5,1},{6,2},{7,3},{8,12},{9,13},{10,... | collective-permute-start | bytes 147464 | tf_op jit(solution)/shard_map/ppermute | solution.py:776
  33.3 1.1 %collective-permute-start.9 = (f32[96,128]{1,0:T(8,128)S(1)}, f32[96,128]{1,0:T(8,128)S(1)}, u32[]{:S(2)}, u32[]{:S(2)}) collective-permute-start(f32[96,128]{1,0:T(8,128)S(1)} %bitcast.5), channel_id=1, source_target_pairs={{0,2},{1,3},{2,0},{3,1},{4,6},{5,7},{6,4},{7,5},{8,10},{9,11},{10,... | collective-permute-start | bytes 147464 | tf_op jit(solution)/shard_map/ppermute | solution.py:776
  34.4 0.1 shard_map.60
  34.6 1.7 %collective-permute-done.9 = f32[96,128]{1,0:T(8,128)S(1)} collective-permute-done((f32[96,128]{1,0:T(8,128)S(1)}, f32[96,128]{1,0:T(8,128)S(1)}, u32[]{:S(2)}, u32[]{:S(2)}) %collective-permute-start.9) | collective-permute-done | bytes 49184 | tf_op jit(solution)/shard_map/ppermute | solution.py:776
  36.2 0.0 collective-permute-done.10
  36.2 0.0 collective-permute-done.11
  36.3 4.9 %collective-permute-start.12 = (f32[456,128]{1,0:T(8,128)S(1)}, f32[456,128]{1,0:T(8,128)S(1)}, u32[]{:S(2)}, u32[]{:S(2)}) collective-permute-start(f32[456,128]{1,0:T(8,128)S(1)} %get-tuple-element.42), channel_id=1, source_target_pairs={{0,1},{1,0},{2,3},{3,2},{4,5},{5,4},{6,7},{7,6},{8,9},{9,8},{10,11... | collective-permute-start | bytes 700424 | tf_op jit(solution)/shard_map/ppermute | solution.py:817
  41.2 2.0 %collective-permute-start.13 = (f32[72,128]{1,0:T(8,128)S(1)}, f32[72,128]{1,0:T(8,128)S(1)}, u32[]{:S(2)}, u32[]{:S(2)}) collective-permute-start(f32[72,128]{1,0:T(8,128)S(1)} %get-tuple-element.41), channel_id=1, source_target_pairs={{1,2},{2,1},{5,6},{6,5},{9,10},{10,9},{13,14},{14,13},{17,18},{18,... | collective-permute-start | bytes 110600 | tf_op jit(solution)/shard_map/ppermute | solution.py:816
  43.3 0.0 collective-permute-done.12
  43.3 3.3 %shard_map.61.coarse = f32[12,32,128]{2,1,0:T(8,128)S(1)} custom-call(f32[2,4,4,24,128]{4,3,2,1,0:T(8,128)S(1)} %pad_maximum_fusion.pieces), custom_call_target="tpu_custom_call" | custom-call | tf_op jit(solution)/shard_map/pallas_call | solution.py:726
  46.6 0.0 collective-permute-done.13
  46.6 1.7 %shard_map.62 = f32[16,16,128]{2,1,0:T(8,128)} custom-call(f32[12,32,128]{2,1,0:T(8,128)S(1)} %shard_map.61.coarse, f32[8,22,32,128]{3,2,1,0:T(8,128)S(1)} %get-tuple-element.27.top, f32[8,16,24,128]{3,2,1,0:T(8,128)S(1)} %get-tuple-element.28.mid, f32[48,128]{1,0:T(8,128)S(1)} %get-tuple-element.44.refs_4_.x_low, ...), custom_call_target="tpu_custom_call" | custom-call | tf_op jit(solution)/shard_map/pallas_call | solution.py:831
  (16 shorter events, 0.2 us)
Async XLA Ops:
  1.6 5.3 %collective-permute-start.1 = (f32[240,128]{1,0:T(8,128)S(1)}, f32[240,128]{1,0:T(8,128)S(1)}, u32[]{:S(2)}, u32[]{:S(2)}) collective-permute-start(f32[240,128]{1,0:T(8,128)S(1)} %get-tuple-element.39), channel_id=1, source_target_pairs={{4,8},{8,4},{12,16},{16,12},{20,24},{24,20},{5,9},{9,5},{13,17},{1... | collective-permute-start | bytes 368648 | tf_op jit(solution)/shard_map/ppermute | solution.py:755
  2.3 9.8 %collective-permute-start = (f32[240,128]{1,0:T(8,128)S(1)}, f32[240,128]{1,0:T(8,128)S(1)}, u32[]{:S(2)}, u32[]{:S(2)}) collective-permute-start(f32[240,128]{1,0:T(8,128)S(1)} %get-tuple-element.40), channel_id=1, source_target_pairs={{0,4},{4,0},{8,12},{12,8},{16,20},{20,16},{24,28},{28,24},{1,5},{5... | collective-permute-start | bytes 368648 | tf_op jit(solution)/shard_map/ppermute | solution.py:754
  12.3 6.7 %collective-permute-start.3 = (f32[328,128]{1,0:T(8,128)S(1)}, f32[328,128]{1,0:T(8,128)S(1)}, u32[]{:S(2)}, u32[]{:S(2)}) collective-permute-start(f32[328,128]{1,0:T(8,128)S(1)} %get-tuple-element.33), channel_id=1, source_target_pairs={{1,2},{2,1},{5,6},{6,5},{9,10},{10,9},{13,14},{14,13},{17,18},{18,... | collective-permute-start | bytes 503816 | tf_op jit(solution)/shard_map/ppermute | solution.py:755
  15.9 3.2 %collective-permute-start.2 = (f32[328,128]{1,0:T(8,128)S(1)}, f32[328,128]{1,0:T(8,128)S(1)}, u32[]{:S(2)}, u32[]{:S(2)}) collective-permute-start(f32[328,128]{1,0:T(8,128)S(1)} %get-tuple-element.34), channel_id=1, source_target_pairs={{0,1},{1,0},{2,3},{3,2},{4,5},{5,4},{6,7},{7,6},{8,9},{9,8},{10,11... | collective-permute-start | bytes 503816 | tf_op jit(solution)/shard_map/ppermute | solution.py:754
  20.8 9.0 %collective-permute-start.8 = (f32[48,128]{1,0:T(8,128)S(1)}, f32[48,128]{1,0:T(8,128)S(1)}, u32[]{:S(2)}, u32[]{:S(2)}) collective-permute-start(f32[48,128]{1,0:T(8,128)S(1)} %get-tuple-element.45), channel_id=1, source_target_pairs={{4,8},{8,4},{12,16},{16,12},{20,24},{24,20},{5,9},{9,5},{13,17},{1... | collective-permute-start | bytes 73736 | tf_op jit(solution)/shard_map/ppermute | solution.py:755
  21.4 8.3 %collective-permute-start.7 = (f32[48,128]{1,0:T(8,128)S(1)}, f32[48,128]{1,0:T(8,128)S(1)}, u32[]{:S(2)}, u32[]{:S(2)}) collective-permute-start(f32[48,128]{1,0:T(8,128)S(1)} %get-tuple-element.46), channel_id=1, source_target_pairs={{0,4},{4,0},{8,12},{12,8},{16,20},{20,16},{24,28},{28,24},{1,5},{5... | collective-permute-start | bytes 73736 | tf_op jit(solution)/shard_map/ppermute | solution.py:754
  26.2 4.3 %collective-permute-start.6 = (f32[24,128]{1,0:T(8,128)S(1)}, f32[24,128]{1,0:T(8,128)S(1)}, u32[]{:S(2)}, u32[]{:S(2)}) collective-permute-start(f32[24,128]{1,0:T(8,128)S(1)} %get-tuple-element.24.refs_0_), channel_id=1, source_target_pairs={{0,24},{4,28},{8,16},{12,20},{16,8},{20,12},{24,0},{28,4},{1,25},{... | collective-permute-start | bytes 36872 | tf_op jit(solution)/shard_map/ppermute | solution.py:762
  28.2 3.5 %collective-permute-start.5 = (f32[24,128]{1,0:T(8,128)S(1)}, f32[24,128]{1,0:T(8,128)S(1)}, u32[]{:S(2)}, u32[]{:S(2)}) collective-permute-start(f32[24,128]{1,0:T(8,128)S(1)} %get-tuple-element.24.refs_0_), channel_id=1, source_target_pairs={{0,16},{4,20},{8,24},{12,28},{16,0},{20,4},{24,8},{28,12},{1,17},{... | collective-permute-start | bytes 36872 | tf_op jit(solution)/shard_map/ppermute | solution.py:762
  28.7 3.0 %collective-permute-start.4 = (f32[24,128]{1,0:T(8,128)S(1)}, f32[24,128]{1,0:T(8,128)S(1)}, u32[]{:S(2)}, u32[]{:S(2)}) collective-permute-start(f32[24,128]{1,0:T(8,128)S(1)} %get-tuple-element.24.refs_0_), channel_id=1, source_target_pairs={{0,8},{4,12},{8,0},{12,4},{16,24},{20,28},{24,16},{28,20},{1,9},{5... | collective-permute-start | bytes 36872 | tf_op jit(solution)/shard_map/ppermute | solution.py:762
  31.7 4.5 %collective-permute-start.11 = (f32[96,128]{1,0:T(8,128)S(1)}, f32[96,128]{1,0:T(8,128)S(1)}, u32[]{:S(2)}, u32[]{:S(2)}) collective-permute-start(f32[96,128]{1,0:T(8,128)S(1)} %bitcast.3), channel_id=1, source_target_pairs={{0,6},{1,7},{2,4},{3,5},{4,2},{5,3},{6,0},{7,1},{8,14},{9,15},{10,... | collective-permute-start | bytes 147464 | tf_op jit(solution)/shard_map/ppermute | solution.py:776
  31.8 4.4 %collective-permute-start.10 = (f32[96,128]{1,0:T(8,128)S(1)}, f32[96,128]{1,0:T(8,128)S(1)}, u32[]{:S(2)}, u32[]{:S(2)}) collective-permute-start(f32[96,128]{1,0:T(8,128)S(1)} %bitcast.4), channel_id=1, source_target_pairs={{0,4},{1,5},{2,6},{3,7},{4,0},{5,1},{6,2},{7,3},{8,12},{9,13},{10,... | collective-permute-start | bytes 147464 | tf_op jit(solution)/shard_map/ppermute | solution.py:776
  33.3 2.9 %collective-permute-start.9 = (f32[96,128]{1,0:T(8,128)S(1)}, f32[96,128]{1,0:T(8,128)S(1)}, u32[]{:S(2)}, u32[]{:S(2)}) collective-permute-start(f32[96,128]{1,0:T(8,128)S(1)} %bitcast.5), channel_id=1, source_target_pairs={{0,2},{1,3},{2,0},{3,1},{4,6},{5,7},{6,4},{7,5},{8,10},{9,11},{10,... | collective-permute-start | bytes 147464 | tf_op jit(solution)/shard_map/ppermute | solution.py:776
  36.3 7.0 %collective-permute-start.12 = (f32[456,128]{1,0:T(8,128)S(1)}, f32[456,128]{1,0:T(8,128)S(1)}, u32[]{:S(2)}, u32[]{:S(2)}) collective-permute-start(f32[456,128]{1,0:T(8,128)S(1)} %get-tuple-element.42), channel_id=1, source_target_pairs={{0,1},{1,0},{2,3},{3,2},{4,5},{5,4},{6,7},{7,6},{8,9},{9,8},{10,11... | collective-permute-start | bytes 700424 | tf_op jit(solution)/shard_map/ppermute | solution.py:817
  41.2 5.4 %collective-permute-start.13 = (f32[72,128]{1,0:T(8,128)S(1)}, f32[72,128]{1,0:T(8,128)S(1)}, u32[]{:S(2)}, u32[]{:S(2)}) collective-permute-start(f32[72,128]{1,0:T(8,128)S(1)} %get-tuple-element.41), channel_id=1, source_target_pairs={{1,2},{2,1},{5,6},{6,5},{9,10},{10,9},{13,14},{14,13},{17,18},{18,... | collective-permute-start | bytes 110600 | tf_op jit(solution)/shard_map/ppermute | solution.py:816

commit v11 on v10

--- a/solution.py
+++ b/solution.py
@@ -94,12 +94,21 @@
 
 
 def x_rows(nx, ny):
-    return sum(X_LAYERS) * ny, 3 * RIM // 2 * (ny // 2)
+    return sum(X_LAYERS) * ny
 
 
 def y_rows(nx, ny):
-    fine = sum(layers * (nx + 2 * reach) for layers, reach in zip(Y_LAYERS, Y_REACH))
-    return fine, 3 * (nx // 2 + 2 * RIM) // 2 * RIM
+    return sum(layers * (nx + 2 * reach) for layers, reach in zip(Y_LAYERS, Y_REACH))
+
+
+def rim_rows_x(nx, ny):
+    slab = RIM // 2 * (ny // 2)
+    return slab, 2 * ny, 3 * slab
+
+
+def rim_rows_y(nx, ny):
+    slabs = (nx // 2 + 2 * RIM) // 2 * RIM
+    return slabs, 2 * (nx + 4), 3 * slabs
 
 
 def x_place(index, layer, ny):
@@ -113,7 +122,7 @@
 
 
 def start_pack(*refs):
-    fields, (own, x_low, x_high, faces, tmp, done) = refs[:5], refs[5:]
+    fields, (own, x_low, x_high, done) = refs[:5], refs[5:]
     copies = [pltpu.make_async_copy(ref, own.at[index], done.at[index]) for index, ref in enumerate(fields)]
     for copy in copies:
         copy.start()
@@ -123,30 +132,6 @@
         for layer in range(X_LAYERS[index]):
             x_low[x_place(index, layer, ny)] = own[index, layer]
             x_high[x_place(index, layer, ny)] = own[index, nx - X_LAYERS[index] + layer]
-    fx, fy, fz = own.at[2], own.at[3], own.at[4]
-    halve = compact(LANES, 0)
-
-    def stored(index, values, matrix):
-        count, rows, _ = values.shape
-        flat = exact_dot(values.reshape(count * rows, LANES), matrix)
-        faces[index] = 0.25 * flat.reshape(count, rows, LANES)
-
-    tmp[...] = pair_slabs(fx)[0]
-    stored(0, even_rows(tmp, ny) + odd_rows(tmp, ny), halve)
-    first, second = pair_slabs(fy)
-    tmp[...] = first + second
-    stored(1, even_rows(tmp, ny), halve)
-    first, second = pair_slabs(fz)
-    tmp[...] = first + second
-    stored(2, even_rows(tmp, ny) + odd_rows(tmp, ny), compact(LANES, 0, True))
-    base = x_rows(nx, ny)[0]
-    coarse_rows = ny // 2
-    for face in range(3):
-        for layer in range(RIM // 2):
-            rows = pl.ds(base + (face * (RIM // 2) + layer) * coarse_rows, coarse_rows)
-            top = nx // 2 - RIM + layer
-            x_low[rows] = two_in_one(faces[face, layer], faces[face, layer + RIM // 2])
-            x_high[rows] = two_in_one(faces[face, top], faces[face, top + RIM // 2])
 
 
 def pair_slabs(ref):
@@ -169,9 +154,8 @@
     return one_of_two(ref[place])[layer // (RIM // 2)]
 
 
-def pack_y(own, faces, x_low, x_high, low, high):
-    coarse_x, coarse_y = faces.shape[1:3]
-    nx, ny = 2 * coarse_x, 2 * coarse_y
+def pack_y(own, x_low, x_high, low, high):
+    nx, ny = own.shape[1:3]
     for index in range(5):
         width, layers, reach = Y_LAYERS[index], X_LAYERS[index], Y_REACH[index]
         for out, start in ((low, 0), (high, ny - width)):
@@ -182,24 +166,6 @@
                 out[y_place(index, layer - reach, nx)] = x_low[rows]
                 rows = pl.ds(x_place(index, layer, ny).start + start, width)
                 out[y_place(index, nx + layer, nx)] = x_high[rows]
-    base_x, base_y = x_rows(nx, ny)[0], y_rows(nx, ny)[0]
-    half = (coarse_x + 2 * RIM) // 2
-    for face in range(3):
-        place = base_x + face * (RIM // 2) * coarse_y
-        slabs = [
-            wide_slab(
-                slab,
-                lambda layer: rim_slab(x_low, place, coarse_y, layer),
-                faces.at[face],
-                lambda layer: rim_slab(x_high, place, coarse_y, layer),
-            )
-            for slab in range(2 * half)
-        ]
-        for slab in range(half):
-            both = two_in_one(slabs[slab], slabs[slab + half])
-            rows = pl.ds(base_y + (face * half + slab) * RIM, RIM)
-            low[rows] = both[:RIM]
-            high[rows] = both[coarse_y - RIM :]
 
 
 def fold_four(slabs, even_only=False):
@@ -210,7 +176,31 @@
     return out
 
 
-def coarse_faces(faces, out, tmp):
+def coarse_slab_sums(ref_x, ref_y, ref_z, count, first, tmp):
+    extra = tmp.shape[0]
+    rows = tmp.shape[1]
+    for index in range(extra):
+        tmp[index] = ref_x[first + 2 * index]
+    x = even_rows(tmp, rows) + odd_rows(tmp, rows)
+    for index in range(count):
+        tmp[index] = ref_y[first + 2 * index] + ref_y[first + 2 * index + 1]
+    y = even_rows(tmp, rows)[:count]
+    for index in range(count):
+        tmp[index] = ref_z[first + 2 * index] + ref_z[first + 2 * index + 1]
+    return x, y, (even_rows(tmp, rows) + odd_rows(tmp, rows))[:count]
+
+
+def halved(values, even_only=False):
+    count, rows, _ = values.shape
+    flat = exact_dot(values.reshape(count * rows, LANES), compact(LANES, 0, even_only))
+    return 0.25 * flat.reshape(count, rows, LANES)
+
+
+def coarse_faces(own, faces, out, fine, tmp):
+    x, y, z = coarse_slab_sums(own.at[2], own.at[3], own.at[4], own.shape[1] // 2, 0, fine)
+    faces[0] = halved(x)
+    faces[1] = halved(y)
+    faces[2] = halved(z, True)
     rows = faces.shape[2]
     coarse = rows // 2
     fx, fy, fz = faces.at[0], faces.at[1], faces.at[2]
@@ -273,7 +263,7 @@
 
 
 def level_down(axes, own, faces, coefficients, x_low, x_high, y_low, y_high, *refs):
-    top, mid, chunk, v_low, v_high, other, tmp, one, two = refs
+    top, kept, chunk, v_low, v_high, other, tmp, one, two, mid, wide = refs
     nx, ny = own.shape[1:3]
     slabs, rows = nx + 2 * EDGE, ny + 2 * RIM
     me_x, me_y = lax.axis_index(axes[0]), lax.axis_index(axes[1])
@@ -294,6 +284,16 @@
             top[slot, EDGE + slab, PAD - width : PAD] = y_low[y_place(index, slab, nx)]
             top[slot, EDGE + slab, PAD + ny : PAD + ny + width] = y_high[y_place(index, slab, nx)]
     clear_pads(other, rows)
+
+    coarse_x, coarse_y = nx // 2, ny // 2
+    near = RIM - 1
+    for slot in (FX, FY, ZL, ZH, W, D):
+        mid[slot] = jnp.zeros(mid.shape[1:], F32)
+    x, y, z = coarse_slab_sums(top.at[FX], top.at[FY], top.at[ZL], coarse_x + 2, EDGE - 2, wide)
+    mid[FX, near : near + coarse_x + 3, RIM : 3 * RIM + coarse_y] = halved(x)
+    mid[FY, near : near + coarse_x + 2, RIM : 3 * RIM + coarse_y] = halved(y)
+    mid[ZL, near : near + coarse_x + 2, RIM : 3 * RIM + coarse_y] = halved(z, True)
+
     row_inside = (rows_of((rows, LANES)) >= RIM) | (me_y > 0)
     main = pl.ds(RIM, rows)
     start_v = top.at[V]
@@ -322,27 +322,12 @@
 
     run(nx // 2, residual)
 
-    coarse_x, coarse_y = nx // 2, ny // 2
     slabs, rows = coarse_x + 2 * RIM, coarse_y + 2 * RIM
     half = slabs // 2
     inner = pl.ds(2 * RIM, coarse_y)
     main = pl.ds(RIM, rows)
-    base_x, base_y = x_rows(nx, ny)[0], y_rows(nx, ny)[0]
-    for face, slot in enumerate((FX, FY, ZL)):
-        clear_pads(mid.at[slot], rows)
-        mid[slot, RIM : RIM + coarse_x, inner] = faces[face]
-        place = base_x + face * (RIM // 2) * coarse_y
-        for layer in range(RIM):
-            mid[slot, layer, inner] = rim_slab(x_low, place, coarse_y, layer)
-            mid[slot, RIM + coarse_x + layer, inner] = rim_slab(x_high, place, coarse_y, layer)
-        for slab in range(half):
-            place = pl.ds(base_y + (face * half + slab) * RIM, RIM)
-            for message, row in ((y_low, RIM), (y_high, 2 * RIM + coarse_y)):
-                pair = one_of_two(message[place])
-                mid[slot, slab, row : row + RIM] = pair[0]
-                mid[slot, slab + half, row : row + RIM] = pair[1]
     row_inside = (rows_of((rows, LANES)) >= RIM) | (me_y > 0)
-    for slab in range(slabs - 1):
+    for slab in range(near, near + coarse_x + 2):
         inside = row_inside & (me_x > 0) if slab < RIM else row_inside
         set_weights(mid, slab, RIM, rows, HALF, inside)
 
@@ -361,7 +346,16 @@
         v_high[layer * coarse_y : (layer + 1) * coarse_y] = two_in_one(
             mid[V, far, inner], mid[V, far + RIM // 2, inner]
         )
-    base = RIM // 2 * coarse_y
+    kept[0] = mid[F, RIM : RIM + coarse_x, inner]
+    kept[1] = mid[V, RIM : RIM + coarse_x, inner]
+    base, after, _ = rim_rows_x(nx, ny)
+    pairs = RIM // 2
+    for face in range(3):
+        for layer in range(pairs):
+            place = pl.ds(base + after + (face * pairs + layer) * coarse_y, coarse_y)
+            far = coarse_x - RIM + layer
+            v_low[place] = two_in_one(faces[face, layer], faces[face, layer + pairs])
+            v_high[place] = two_in_one(faces[face, far], faces[face, far + pairs])
     for layer in range(2):
         place = pl.ds(base + layer * ny, ny)
         v_low[place] = top[V, EDGE + layer, pl.ds(PAD, ny)]
@@ -384,27 +378,37 @@
     chunk[coarse_rows + quarter_rows :] = coefficients[:BLOCK_ROWS - coarse_rows - quarter_rows]
 
 
-def pack_v(top, mid, x_low, x_high, low, high):
-    slabs = mid.shape[1]
-    coarse_x = slabs - 2 * RIM
-    coarse_y = mid.shape[2] - 4 * RIM
+def pack_v(top, kept, faces, x_low, x_high, low, high):
+    coarse_x, coarse_y = faces.shape[1:3]
+    nx, ny = 2 * coarse_x, 2 * coarse_y
+    slabs = coarse_x + 2 * RIM
     half = slabs // 2
-    own = mid[V, RIM : RIM + coarse_x, 2 * RIM : 2 * RIM + coarse_y]
-    values = [
-        wide_slab(
-            slab,
-            lambda layer: rim_slab(x_low, 0, coarse_y, layer),
-            own,
-            lambda layer: rim_slab(x_high, 0, coarse_y, layer),
+    sizes_x, sizes_y = rim_rows_x(nx, ny), rim_rows_y(nx, ny)
+
+    def folded(own, place_x, place_y):
+        values = [
+            wide_slab(
+                slab,
+                lambda layer: rim_slab(x_low, place_x, coarse_y, layer),
+                own,
+                lambda layer: rim_slab(x_high, place_x, coarse_y, layer),
+            )
+            for slab in range(slabs)
+        ]
+        for slab in range(half):
+            both = two_in_one(values[slab], values[slab + half])
+            rows = pl.ds(place_y + slab * RIM, RIM)
+            low[rows] = both[:RIM]
+            high[rows] = both[coarse_y - RIM :]
+
+    folded(kept.at[1], 0, 0)
+    for face in range(3):
+        folded(
+            faces.at[face],
+            sizes_x[0] + sizes_x[1] + face * sizes_x[0],
+            sizes_y[0] + sizes_y[1] + face * sizes_y[0],
         )
-        for slab in range(slabs)
-    ]
-    for slab in range(half):
-        both = two_in_one(values[slab], values[slab + half])
-        low[slab * RIM : (slab + 1) * RIM] = both[:RIM]
-        high[slab * RIM : (slab + 1) * RIM] = both[coarse_y - RIM :]
-    nx, ny = 2 * coarse_x, 2 * coarse_y
-    base_x, base_y = RIM // 2 * coarse_y, half * RIM
+    base_x, base_y = sizes_x[0], sizes_y[0]
     for out, start in ((low, 0), (high, ny - 2)):
         for layer in range(2):
             rows = pl.ds(base_x + layer * ny + start, 2)
@@ -615,10 +619,12 @@
     out[:, PAD + rows :] = jnp.zeros((count + 2 * reach, PAD, LANES), F32)
 
 
-def level_up(axes, grid, coarse, top, mid, x_low, x_high, y_low, y_high, out, one, two, right, post, up):
+def level_up(axes, grid, coarse, top, kept, faces, x_low, x_high, y_low, y_high, *refs):
+    out, mid, one, two, right, post, up = refs
     devices_x, devices_y = grid
     me_x, me_y = lax.axis_index(axes[0]), lax.axis_index(axes[1])
-    coarse_x, coarse_y = mid.shape[1] - 2 * RIM, mid.shape[2] - 4 * RIM
+    coarse_x, coarse_y = faces.shape[1:3]
+    nx, ny = out.shape[:2]
     own_x, own_y = coarse_x // 2, coarse_y // 2
     quarter = LANES // 4
     reach = RIM // 2
@@ -628,8 +634,30 @@
     half = slabs // 2
     inner = pl.ds(2 * RIM, coarse_y)
     body = pl.ds(RIM, high)
-    one[...] = mid[V]
+    sizes_x, sizes_y = rim_rows_x(nx, ny), rim_rows_y(nx, ny)
+    for face, slot in enumerate((FX, FY, ZL)):
+        clear_pads(mid.at[slot], high)
+        mid[slot, RIM : RIM + coarse_x, inner] = faces[face]
+        place_x = sizes_x[0] + sizes_x[1] + face * sizes_x[0]
+        place_y = sizes_y[0] + sizes_y[1] + face * sizes_y[0]
+        for layer in range(RIM):
+            mid[slot, layer, inner] = rim_slab(x_low, place_x, coarse_y, layer)
+            mid[slot, RIM + coarse_x + layer, inner] = rim_slab(x_high, place_x, coarse_y, layer)
+        for slab in range(half):
+            place = pl.ds(place_y + slab * RIM, RIM)
+            for message, row in ((y_low, RIM), (y_high, 2 * RIM + coarse_y)):
+                pair = one_of_two(message[place])
+                mid[slot, slab, row : row + RIM] = pair[0]
+                mid[slot, slab + half, row : row + RIM] = pair[1]
+    row_inside = (rows_of((high, LANES)) >= RIM) | (me_y > 0)
+    for slab in range(slabs - 1):
+        inside = row_inside & (me_x > 0) if slab < RIM else row_inside
+        set_weights(mid, slab, RIM, high, HALF, inside)
+    clear_pads(one, high)
+    clear_pads(right, high)
     clear_pads(two, high)
+    one[RIM : RIM + coarse_x, inner] = kept[1]
+    right[RIM : RIM + coarse_x, inner] = kept[0]
     for layer in range(RIM):
         one[layer, inner] = rim_slab(x_low, 0, coarse_y, layer)
         one[RIM + coarse_x + layer, inner] = rim_slab(x_high, 0, coarse_y, layer)
@@ -644,7 +672,7 @@
     for slab in range(1, slabs - 1):
         f_rim = one[slab, body] * mid[D, slab, body] * (1.0 / OMEGA)
         if RIM <= slab < RIM + coarse_x:
-            f_rim = jnp.where(own_row, mid[F, slab, body], f_rim)
+            f_rim = jnp.where(own_row, right[slab, body], f_rim)
         right[slab, body] = f_rim
         two[slab, body] = swept(mid, one, slab, RIM, high, right)
 
@@ -671,7 +699,6 @@
     for slab in range(3, slabs - 3):
         two[slab, body] = swept(mid, one, slab, RIM, high, right)
 
-    nx, ny = out.shape[:2]
     steps = coarse_x + 2
     fine_rows = ny + 2 * RIM
     e = two[RIM - 1 : RIM - 1 + steps, body]
@@ -782,27 +809,34 @@
     devices_x, devices_y = lax.axis_size("gx"), lax.axis_size("gy")
     nx, ny, nz = fields[0].shape
     coarse_x, coarse_y = nx // 2, ny // 2
-    x_shape = (sum(x_rows(nx, ny)), LANES)
-    y_shape = (sum(y_rows(nx, ny)), LANES)
-    own, x_low, x_high, faces = call(
-        start_pack,
-        [(5, nx, ny, nz), x_shape, x_shape, (3, coarse_x, coarse_y, LANES)],
-        [(coarse_x, ny, LANES), pltpu.SemaphoreType.DMA((5,))],
-        True,
+    x_shape, y_shape = (x_rows(nx, ny), LANES), (y_rows(nx, ny), LANES)
+    own, x_low, x_high = call(
+        start_pack, [(5, nx, ny, nz), x_shape, x_shape], [pltpu.SemaphoreType.DMA((5,))], True
     )(*fields)
     x_low, x_high = from_sides(x_low, x_high, "gx")
-    (coefficients,) = call(coarse_faces, [(16, LANES)], [(coarse_x // 2, coarse_y, LANES)])(faces)
-    y_low, y_high = call(pack_y, [y_shape] * 2)(own, faces, x_low, x_high)
+    faces, coefficients = call(
+        coarse_faces,
+        [(3, coarse_x, coarse_y, LANES), (16, LANES)],
+        [(coarse_x, ny, LANES), (coarse_x // 2, coarse_y, LANES)],
+    )(own)
+    y_low, y_high = call(pack_y, [y_shape] * 2)(own, x_low, x_high)
     y_low, y_high = from_sides(y_low, y_high, "gy")
     stack = (nx + 2 * EDGE, ny + 4 * RIM, LANES)
     stack_1 = (coarse_x + 2 * RIM, coarse_y + 4 * RIM, LANES)
     half = stack_1[0] // 2
-    v_shape = (RIM // 2 * coarse_y + 2 * ny, LANES)
-    w_shape = (half * RIM + 2 * (nx + 4), LANES)
-    top, mid, chunk, v_low, v_high = call(
+    v_shape = (sum(rim_rows_x(nx, ny)), LANES)
+    w_shape = (sum(rim_rows_y(nx, ny)), LANES)
+    top, kept, chunk, v_low, v_high = call(
         functools.partial(level_down, axes),
-        [(D + 1,) + stack, (D + 1,) + stack_1, (BLOCK_ROWS, LANES), v_shape, v_shape],
-        [stack, (nx // 2, ny, LANES), stack_1, (half, coarse_y + 2 * RIM, LANES)],
+        [(D + 1,) + stack, (2, coarse_x, coarse_y, LANES), (BLOCK_ROWS, LANES), v_shape, v_shape],
+        [
+            stack,
+            (nx // 2, ny, LANES),
+            stack_1,
+            (half, coarse_y + 2 * RIM, LANES),
+            (D + 1,) + stack_1,
+            (coarse_x + 3,) + stack[1:],
+        ],
     )(own, faces, coefficients, x_low, x_high, y_low, y_high)
 
     blocks = passed_round(chunk, "gx", 2)
@@ -810,7 +844,7 @@
     slow = (len(blocks),) + chunk.shape
     (pieces,) = call(stack_blocks, [slow])(*blocks, v_low, v_high)
     blocks = passed_across(pieces.reshape(-1, LANES))
-    w_low, w_high = call(pack_v, [w_shape] * 2)(top, mid, v_low, v_high)
+    w_low, w_high = call(pack_v, [w_shape] * 2)(top, kept, faces, v_low, v_high)
     pair, swap = by_partner(w_low, w_high, "gy")
     message = jnp.concatenate(blocks + [pair])
     swap = lax.ppermute(swap, "gy", swap_route("gy"))
@@ -831,14 +865,14 @@
     return pl.pallas_call(
         functools.partial(level_up, axes, grid),
         out_shape=jax.ShapeDtypeStruct((nx, ny, nz), F32),
-        in_specs=[IN_VMEM] * 7,
+        in_specs=[IN_VMEM] * 8,
         out_specs=IN_VMEM,
         scratch_shapes=[
             pltpu.VMEM(shape, F32)
-            for shape in (stack_1, stack_1, stack_1, (2,) + stack, (coarse_x + 2, ny + 2 * RIM, LANES))
+            for shape in ((D + 1,) + stack_1, stack_1, stack_1, stack_1, (2,) + stack, (coarse_x + 2, ny + 2 * RIM, LANES))
         ],
         compiler_params=pltpu.CompilerParams(vmem_limit_bytes=24 * 2**20),
-    )(coarse, top, mid, v_low, v_high, w_low, w_high)
+    )(coarse, top, kept, faces, v_low, v_high, w_low, w_high)
 
 
 def with_halo(block, sides, width):

time: 48.6 us -> 47.2 us (0.971)
  waiting for transfers between devices: 11.4 us -> 10.1 us
    ppermute x3, waiting for transfers between devices: 5.22 us -> 4.13 us  [from_sides(): pair = lax.ppermute(pair, axis, pair_route(axis))]
    ppermute x3, waiting for transfers between devices: 2.6 us -> 1.7 us  [from_sides(): swap = lax.ppermute(swap, axis, swap_route(axis))]
  transfers between devices with their start and end apart: 14 -> 14, of which waited for: 5 -> 6; matrix products, arithmetic and copies ran while one was open for 0% -> 0% of each run, Pallas kernels for 8% -> 9%
where the time goes in v11:
time: 47.2 us; the launch traced here: 47 us
  starting transfers between devices  27.3 us (58%)
  waiting for transfers between devices  10.1 us (21%)
  Pallas kernels  9.25 us (20%)
    ppermute x3, starting transfers between devices, from_sides(): pair = lax.ppermute(pair, axis, pair_route(axis))  9.47 us
    pallas_call x7, Pallas kernels, launch(): pl.pallas_call(kernel, out_shape=[pltpu.VMEM(shape, F32) for shape in out...  7.51 us
    ppermute x3, starting transfers between devices, from_sides(): swap = lax.ppermute(swap, axis, swap_route(axis))  4.89 us
    ppermute x1, starting transfers between devices, fused_cycle(): other = lax.ppermute(message, 'gy', pair_route('gy'))  4.7 us
    ppermute x3, waiting for transfers between devices, from_sides(): pair = lax.ppermute(pair, axis, pair_route(axis))  4.13 us
    ppermute x3, starting transfers between devices, passed_round(): lax.ppermute(block, axis, [(i, i ^ distance) for i in range(count)])  3.55 us
    ppermute x3, starting transfers between devices, passed_across(): blocks.append(lax.ppermute(block, ('gx', 'gy'), route) if moved else block)  2.71 us
    ppermute x3, waiting for transfers between devices, passed_round(): lax.ppermute(block, axis, [(i, i ^ distance) for i in range(count)])  2.27 us
  transfers between devices with their start and end apart: 14, of which 6 were waited for; matrix products, arithmetic and copies ran while one was open for 0% of the time, Pallas kernels for 9%

profile of v11, /device:TPU:1, one launch (start us, length us, event | category | flops | bytes accessed | tf_op | source)
XLA Modules:
  0.0 47.0 jit_solution(15684631068191751945)
XLA Ops:
  0.0 1.2 %shard_map.55 = (f32[5,16,16,128]{3,2,1,0:T(8,128)S(1)}, f32[192,128]{1,0:T(8,128)S(1)}, f32[192,128]{1,0:T(8,128)S(1)}) custom-call(f32[16,16,128]{2,1,0:T(8,128)} %refs_0_.1, f32[16,16,128]{2,1,0:T(8,128)} %refs_1_.1, f32[16,16,128]{2,1,0:T(8,128)} %refs_2_.1, f32[16,16,128]{2,1,0:T(8,128)} %refs_3_.1, f32[16,16,128]{2,1,0:T(8,128)} %refs_4_.1), custom_call_target="tpu_custom_call" | custom-call | tf_op jit(solution)/shard_map/pallas_call | solution.py:753
  1.2 0.7 %collective-permute-start.1 = (f32[192,128]{1,0:T(8,128)S(1)}, f32[192,128]{1,0:T(8,128)S(1)}, u32[]{:S(2)}, u32[]{:S(2)}) collective-permute-start(f32[192,128]{1,0:T(8,128)S(1)} %get-tuple-element.41), channel_id=1, source_target_pairs={{4,8},{8,4},{12,16},{16,12},{20,24},{24,20},{5,9},{9,5},{13,17},{1... | collective-permute-start | bytes 294920 | tf_op jit(solution)/shard_map/ppermute | solution.py:782
  1.9 4.6 %collective-permute-start = (f32[192,128]{1,0:T(8,128)S(1)}, f32[192,128]{1,0:T(8,128)S(1)}, u32[]{:S(2)}, u32[]{:S(2)}) collective-permute-start(f32[192,128]{1,0:T(8,128)S(1)} %get-tuple-element.42), channel_id=1, source_target_pairs={{0,4},{4,0},{8,12},{12,8},{16,20},{20,16},{24,28},{28,24},{1,5},{5... | collective-permute-start | bytes 294920 | tf_op jit(solution)/shard_map/ppermute | solution.py:781
  6.5 0.0 collective-permute-done.1
  6.5 4.1 %collective-permute-done = f32[192,128]{1,0:T(8,128)S(1)} collective-permute-done((f32[192,128]{1,0:T(8,128)S(1)}, f32[192,128]{1,0:T(8,128)S(1)}, u32[]{:S(2)}, u32[]{:S(2)}) %collective-permute-start) | collective-permute-done | bytes 98336 | tf_op jit(solution)/shard_map/ppermute | solution.py:781
  10.7 0.1 shard_map.57
  10.8 3.6 %collective-permute-start.3 = (f32[232,128]{1,0:T(8,128)S(1)}, f32[232,128]{1,0:T(8,128)S(1)}, u32[]{:S(2)}, u32[]{:S(2)}) collective-permute-start(f32[232,128]{1,0:T(8,128)S(1)} %get-tuple-element.37), channel_id=1, source_target_pairs={{1,2},{2,1},{5,6},{6,5},{9,10},{10,9},{13,14},{14,13},{17,18},{18,... | collective-permute-start | bytes 356360 | tf_op jit(solution)/shard_map/ppermute | solution.py:782
  14.4 0.1 collective-permute-start.2
  14.4 0.8 %shard_map.56 = (f32[3,8,8,128]{3,2,1,0:T(8,128)S(1)}, f32[16,128]{1,0:T(8,128)S(1)}) custom-call(f32[5,16,16,128]{3,2,1,0:T(8,128)S(1)} %get-tuple-element.19.own), custom_call_target="tpu_custom_call" | custom-call | tf_op jit(solution)/shard_map/pallas_call | solution.py:753
  15.3 1.7 %collective-permute-done.3 = f32[232,128]{1,0:T(8,128)S(1)} collective-permute-done((f32[232,128]{1,0:T(8,128)S(1)}, f32[232,128]{1,0:T(8,128)S(1)}, u32[]{:S(2)}, u32[]{:S(2)}) %collective-permute-start.3) | collective-permute-done | bytes 118816 | tf_op jit(solution)/shard_map/ppermute | solution.py:782
  16.9 0.0 collective-permute-done.2
  17.0 2.0 %shard_map.58 = (f32[8,22,32,128]{3,2,1,0:T(8,128)S(1)}, f32[2,8,8,128]{3,2,1,0:T(8,128)S(1)}, f32[24,128]{1,0:T(8,128)S(1)}, f32[96,128]{1,0:T(8,128)S(1)}, f32[96,128]{1,0:T(8,128)S(1)}) custom-call(f32[5,16,16,128]{3,2,1,0:T(8,128)S(1)} %get-tuple-element.19.own, f32[3,8,8,128]{3,2,1,0:T(8,128)S(1)} %get-tuple-element.20.faces, ...), custom_call_target="tpu_custom_call" | custom-call | tf_op jit(solution)/shard_map/pallas_call | solution.py:753
  19.0 0.7 %collective-permute-start.8 = (f32[96,128]{1,0:T(8,128)S(1)}, f32[96,128]{1,0:T(8,128)S(1)}, u32[]{:S(2)}, u32[]{:S(2)}) collective-permute-start(f32[96,128]{1,0:T(8,128)S(1)} %get-tuple-element.47), channel_id=1, source_target_pairs={{4,8},{8,4},{12,16},{16,12},{20,24},{24,20},{5,9},{9,5},{13,17},{1... | collective-permute-start | bytes 147464 | tf_op jit(solution)/shard_map/ppermute | solution.py:782
  19.7 4.8 %collective-permute-start.7 = (f32[96,128]{1,0:T(8,128)S(1)}, f32[96,128]{1,0:T(8,128)S(1)}, u32[]{:S(2)}, u32[]{:S(2)}) collective-permute-start(f32[96,128]{1,0:T(8,128)S(1)} %get-tuple-element.48), channel_id=1, source_target_pairs={{0,4},{4,0},{8,12},{12,8},{16,20},{20,16},{24,28},{28,24},{1,5},{5... | collective-permute-start | bytes 147464 | tf_op jit(solution)/shard_map/ppermute | solution.py:781
  24.5 2.0 %collective-permute-start.6 = (f32[24,128]{1,0:T(8,128)S(1)}, f32[24,128]{1,0:T(8,128)S(1)}, u32[]{:S(2)}, u32[]{:S(2)}) collective-permute-start(f32[24,128]{1,0:T(8,128)S(1)} %get-tuple-element.26.refs_0_), channel_id=1, source_target_pairs={{0,24},{4,28},{8,16},{12,20},{16,8},{20,12},{24,0},{28,4},{1,25},{... | collective-permute-start | bytes 36872 | tf_op jit(solution)/shard_map/ppermute | solution.py:789
  26.5 0.5 collective-permute-start.5
  26.9 1.1 %collective-permute-start.4 = (f32[24,128]{1,0:T(8,128)S(1)}, f32[24,128]{1,0:T(8,128)S(1)}, u32[]{:S(2)}, u32[]{:S(2)}) collective-permute-start(f32[24,128]{1,0:T(8,128)S(1)} %get-tuple-element.26.refs_0_), channel_id=1, source_target_pairs={{0,8},{4,12},{8,0},{12,4},{16,24},{20,28},{24,16},{28,20},{1,9},{5... | collective-permute-start | bytes 36872 | tf_op jit(solution)/shard_map/ppermute | solution.py:789
  28.0 0.0 collective-permute-done.8
  28.0 0.0 collective-permute-done.7
  28.0 1.1 %collective-permute-done.6.refs_3_ = f32[24,128]{1,0:T(8,128)S(1)} collective-permute-done((f32[24,128]{1,0:T(8,128)S(1)}, f32[24,128]{1,0:T(8,128)S(1)}, u32[]{:S(2)}, u32[]{:S(2)}) %collective-permute-start.6) | collective-permute-done | bytes 12320 | tf_op jit(solution)/shard_map/ppermute | solution.py:789
  29.2 1.1 %collective-permute-done.5.refs_2_ = f32[24,128]{1,0:T(8,128)S(1)} collective-permute-done((f32[24,128]{1,0:T(8,128)S(1)}, f32[24,128]{1,0:T(8,128)S(1)}, u32[]{:S(2)}, u32[]{:S(2)}) %collective-permute-start.5) | collective-permute-done | bytes 12320 | tf_op jit(solution)/shard_map/ppermute | solution.py:789
  30.3 0.0 collective-permute-done.4.refs_1_
  30.3 0.1 collective-permute-start.11
  30.4 1.1 %collective-permute-start.10 = (f32[96,128]{1,0:T(8,128)S(1)}, f32[96,128]{1,0:T(8,128)S(1)}, u32[]{:S(2)}, u32[]{:S(2)}) collective-permute-start(f32[96,128]{1,0:T(8,128)S(1)} %bitcast.4), channel_id=1, source_target_pairs={{0,4},{1,5},{2,6},{3,7},{4,0},{5,1},{6,2},{7,3},{8,12},{9,13},{10,... | collective-permute-start | bytes 147464 | tf_op jit(solution)/shard_map/ppermute | solution.py:803
  31.5 1.6 %collective-permute-start.9 = (f32[96,128]{1,0:T(8,128)S(1)}, f32[96,128]{1,0:T(8,128)S(1)}, u32[]{:S(2)}, u32[]{:S(2)}) collective-permute-start(f32[96,128]{1,0:T(8,128)S(1)} %bitcast.5), channel_id=1, source_target_pairs={{0,2},{1,3},{2,0},{3,1},{4,6},{5,7},{6,4},{7,5},{8,10},{9,11},{10,... | collective-permute-start | bytes 147464 | tf_op jit(solution)/shard_map/ppermute | solution.py:803
  33.0 0.1 shard_map.60
  33.2 1.6 %collective-permute-done.9 = f32[96,128]{1,0:T(8,128)S(1)} collective-permute-done((f32[96,128]{1,0:T(8,128)S(1)}, f32[96,128]{1,0:T(8,128)S(1)}, u32[]{:S(2)}, u32[]{:S(2)}) %collective-permute-start.9) | collective-permute-done | bytes 49184 | tf_op jit(solution)/shard_map/ppermute | solution.py:803
  34.7 0.0 collective-permute-done.10
  34.8 0.0 collective-permute-done.11
  34.8 4.7 %collective-permute-start.12 = (f32[552,128]{1,0:T(8,128)S(1)}, f32[552,128]{1,0:T(8,128)S(1)}, u32[]{:S(2)}, u32[]{:S(2)}) collective-permute-start(f32[552,128]{1,0:T(8,128)S(1)} %get-tuple-element.44), channel_id=1, source_target_pairs={{0,1},{1,0},{2,3},{3,2},{4,5},{5,4},{6,7},{7,6},{8,9},{9,8},{10,11... | collective-permute-start | bytes 847880 | tf_op jit(solution)/shard_map/ppermute | solution.py:851
  39.5 2.0 %collective-permute-start.13 = (f32[168,128]{1,0:T(8,128)S(1)}, f32[168,128]{1,0:T(8,128)S(1)}, u32[]{:S(2)}, u32[]{:S(2)}) collective-permute-start(f32[168,128]{1,0:T(8,128)S(1)} %get-tuple-element.43), channel_id=1, source_target_pairs={{1,2},{2,1},{5,6},{6,5},{9,10},{10,9},{13,14},{14,13},{17,18},{18,... | collective-permute-start | bytes 258056 | tf_op jit(solution)/shard_map/ppermute | solution.py:850
  41.6 0.0 collective-permute-done.12
  41.6 3.3 %shard_map.61.coarse = f32[12,32,128]{2,1,0:T(8,128)S(1)} custom-call(f32[2,4,4,24,128]{4,3,2,1,0:T(8,128)S(1)} %pad_maximum_fusion.pieces), custom_call_target="tpu_custom_call" | custom-call | tf_op jit(solution)/shard_map/pallas_call | solution.py:753
  44.9 0.4 collective-permute-done.13
  45.3 1.7 %shard_map.62 = f32[16,16,128]{2,1,0:T(8,128)} custom-call(f32[12,32,128]{2,1,0:T(8,128)S(1)} %shard_map.61.coarse, f32[8,22,32,128]{3,2,1,0:T(8,128)S(1)} %get-tuple-element.29.top, f32[2,8,8,128]{3,2,1,0:T(8,128)S(1)} %get-tuple-element.30.kept, f32[3,8,8,128]{3,2,1,0:T(8,128)S(1)} %get-tuple-element.20.faces, ...), custom_call_target="tpu_custom_call" | custom-call | tf_op jit(solution)/shard_map/pallas_call | solution.py:865
  (16 shorter events, 0.2 us)
Async XLA Ops:
  1.2 5.3 %collective-permute-start.1 = (f32[192,128]{1,0:T(8,128)S(1)}, f32[192,128]{1,0:T(8,128)S(1)}, u32[]{:S(2)}, u32[]{:S(2)}) collective-permute-start(f32[192,128]{1,0:T(8,128)S(1)} %get-tuple-element.41), channel_id=1, source_target_pairs={{4,8},{8,4},{12,16},{16,12},{20,24},{24,20},{5,9},{9,5},{13,17},{1... | collective-permute-start | bytes 294920 | tf_op jit(solution)/shard_map/ppermute | solution.py:782
  1.9 8.7 %collective-permute-start = (f32[192,128]{1,0:T(8,128)S(1)}, f32[192,128]{1,0:T(8,128)S(1)}, u32[]{:S(2)}, u32[]{:S(2)}) collective-permute-start(f32[192,128]{1,0:T(8,128)S(1)} %get-tuple-element.42), channel_id=1, source_target_pairs={{0,4},{4,0},{8,12},{12,8},{16,20},{20,16},{24,28},{28,24},{1,5},{5... | collective-permute-start | bytes 294920 | tf_op jit(solution)/shard_map/ppermute | solution.py:781
  10.8 6.2 %collective-permute-start.3 = (f32[232,128]{1,0:T(8,128)S(1)}, f32[232,128]{1,0:T(8,128)S(1)}, u32[]{:S(2)}, u32[]{:S(2)}) collective-permute-start(f32[232,128]{1,0:T(8,128)S(1)} %get-tuple-element.37), channel_id=1, source_target_pairs={{1,2},{2,1},{5,6},{6,5},{9,10},{10,9},{13,14},{14,13},{17,18},{18,... | collective-permute-start | bytes 356360 | tf_op jit(solution)/shard_map/ppermute | solution.py:782
  14.4 2.6 %collective-permute-start.2 = (f32[232,128]{1,0:T(8,128)S(1)}, f32[232,128]{1,0:T(8,128)S(1)}, u32[]{:S(2)}, u32[]{:S(2)}) collective-permute-start(f32[232,128]{1,0:T(8,128)S(1)} %get-tuple-element.38), channel_id=1, source_target_pairs={{0,1},{1,0},{2,3},{3,2},{4,5},{5,4},{6,7},{7,6},{8,9},{9,8},{10,11... | collective-permute-start | bytes 356360 | tf_op jit(solution)/shard_map/ppermute | solution.py:781
  19.0 9.0 %collective-permute-start.8 = (f32[96,128]{1,0:T(8,128)S(1)}, f32[96,128]{1,0:T(8,128)S(1)}, u32[]{:S(2)}, u32[]{:S(2)}) collective-permute-start(f32[96,128]{1,0:T(8,128)S(1)} %get-tuple-element.47), channel_id=1, source_target_pairs={{4,8},{8,4},{12,16},{16,12},{20,24},{24,20},{5,9},{9,5},{13,17},{1... | collective-permute-start | bytes 147464 | tf_op jit(solution)/shard_map/ppermute | solution.py:782
  19.7 8.3 %collective-permute-start.7 = (f32[96,128]{1,0:T(8,128)S(1)}, f32[96,128]{1,0:T(8,128)S(1)}, u32[]{:S(2)}, u32[]{:S(2)}) collective-permute-start(f32[96,128]{1,0:T(8,128)S(1)} %get-tuple-element.48), channel_id=1, source_target_pairs={{0,4},{4,0},{8,12},{12,8},{16,20},{20,16},{24,28},{28,24},{1,5},{5... | collective-permute-start | bytes 147464 | tf_op jit(solution)/shard_map/ppermute | solution.py:781
  24.5 4.7 %collective-permute-start.6 = (f32[24,128]{1,0:T(8,128)S(1)}, f32[24,128]{1,0:T(8,128)S(1)}, u32[]{:S(2)}, u32[]{:S(2)}) collective-permute-start(f32[24,128]{1,0:T(8,128)S(1)} %get-tuple-element.26.refs_0_), channel_id=1, source_target_pairs={{0,24},{4,28},{8,16},{12,20},{16,8},{20,12},{24,0},{28,4},{1,25},{... | collective-permute-start | bytes 36872 | tf_op jit(solution)/shard_map/ppermute | solution.py:789
  26.5 3.8 %collective-permute-start.5 = (f32[24,128]{1,0:T(8,128)S(1)}, f32[24,128]{1,0:T(8,128)S(1)}, u32[]{:S(2)}, u32[]{:S(2)}) collective-permute-start(f32[24,128]{1,0:T(8,128)S(1)} %get-tuple-element.26.refs_0_), channel_id=1, source_target_pairs={{0,16},{4,20},{8,24},{12,28},{16,0},{20,4},{24,8},{28,12},{1,17},{... | collective-permute-start | bytes 36872 | tf_op jit(solution)/shard_map/ppermute | solution.py:789
  26.9 3.4 %collective-permute-start.4 = (f32[24,128]{1,0:T(8,128)S(1)}, f32[24,128]{1,0:T(8,128)S(1)}, u32[]{:S(2)}, u32[]{:S(2)}) collective-permute-start(f32[24,128]{1,0:T(8,128)S(1)} %get-tuple-element.26.refs_0_), channel_id=1, source_target_pairs={{0,8},{4,12},{8,0},{12,4},{16,24},{20,28},{24,16},{28,20},{1,9},{5... | collective-permute-start | bytes 36872 | tf_op jit(solution)/shard_map/ppermute | solution.py:789
  30.3 4.5 %collective-permute-start.11 = (f32[96,128]{1,0:T(8,128)S(1)}, f32[96,128]{1,0:T(8,128)S(1)}, u32[]{:S(2)}, u32[]{:S(2)}) collective-permute-start(f32[96,128]{1,0:T(8,128)S(1)} %bitcast.3), channel_id=1, source_target_pairs={{0,6},{1,7},{2,4},{3,5},{4,2},{5,3},{6,0},{7,1},{8,14},{9,15},{10,... | collective-permute-start | bytes 147464 | tf_op jit(solution)/shard_map/ppermute | solution.py:803
  30.4 4.4 %collective-permute-start.10 = (f32[96,128]{1,0:T(8,128)S(1)}, f32[96,128]{1,0:T(8,128)S(1)}, u32[]{:S(2)}, u32[]{:S(2)}) collective-permute-start(f32[96,128]{1,0:T(8,128)S(1)} %bitcast.4), channel_id=1, source_target_pairs={{0,4},{1,5},{2,6},{3,7},{4,0},{5,1},{6,2},{7,3},{8,12},{9,13},{10,... | collective-permute-start | bytes 147464 | tf_op jit(solution)/shard_map/ppermute | solution.py:803
  31.5 3.3 %collective-permute-start.9 = (f32[96,128]{1,0:T(8,128)S(1)}, f32[96,128]{1,0:T(8,128)S(1)}, u32[]{:S(2)}, u32[]{:S(2)}) collective-permute-start(f32[96,128]{1,0:T(8,128)S(1)} %bitcast.5), channel_id=1, source_target_pairs={{0,2},{1,3},{2,0},{3,1},{4,6},{5,7},{6,4},{7,5},{8,10},{9,11},{10,... | collective-permute-start | bytes 147464 | tf_op jit(solution)/shard_map/ppermute | solution.py:803
  34.8 6.8 %collective-permute-start.12 = (f32[552,128]{1,0:T(8,128)S(1)}, f32[552,128]{1,0:T(8,128)S(1)}, u32[]{:S(2)}, u32[]{:S(2)}) collective-permute-start(f32[552,128]{1,0:T(8,128)S(1)} %get-tuple-element.44), channel_id=1, source_target_pairs={{0,1},{1,0},{2,3},{3,2},{4,5},{5,4},{6,7},{7,6},{8,9},{9,8},{10,11... | collective-permute-start | bytes 847880 | tf_op jit(solution)/shard_map/ppermute | solution.py:851
  39.5 5.8 %collective-permute-start.13 = (f32[168,128]{1,0:T(8,128)S(1)}, f32[168,128]{1,0:T(8,128)S(1)}, u32[]{:S(2)}, u32[]{:S(2)}) collective-permute-start(f32[168,128]{1,0:T(8,128)S(1)} %get-tuple-element.43), channel_id=1, source_target_pairs={{1,2},{2,1},{5,6},{6,5},{9,10},{10,9},{13,14},{14,13},{17,18},{18,... | collective-permute-start | bytes 258056 | tf_op jit(solution)/shard_map/ppermute | solution.py:850

commit v12 on v11

--- a/solution.py
+++ b/solution.py
@@ -423,6 +423,13 @@
         refs[-1][index] = ref[...]
 
 
+def join_blocks(*refs):
+    start = 0
+    for ref in refs[:-2]:
+        refs[-1][start : start + ref.shape[0]] = ref[...]
+        start += ref.shape[0]
+
+
 def pair_rows(values, stride):
     return values + roll_rows(values, -stride)
 
@@ -478,7 +485,7 @@
         scaled = self.start(f)
         slabs = self.count
 
-        def step(index, v):
+        def step(v):
             out = []
             for s in range(slabs):
                 low = v[s - 1] if s > 0 else roll_lanes(v[slabs - 1], self.depth)
@@ -489,7 +496,10 @@
                 out.append((((1.0 - OMEGA) * v[s] + scaled[s]) + y) + (x + z))
             return out
 
-        return lax.fori_loop(1, count, step, scaled)
+        v = scaled
+        for _ in range(count - 1):
+            v = step(v)
+        return v
 
     def start(self, f):
         return [self.w[s] * f[s] for s in range(self.count)]
@@ -846,8 +856,9 @@
     blocks = passed_across(pieces.reshape(-1, LANES))
     w_low, w_high = call(pack_v, [w_shape] * 2)(top, kept, faces, v_low, v_high)
     pair, swap = by_partner(w_low, w_high, "gy")
-    message = jnp.concatenate(blocks + [pair])
     swap = lax.ppermute(swap, "gy", swap_route("gy"))
+    rows = sum(block.shape[0] for block in blocks) + w_shape[0]
+    (message,) = call(join_blocks, [(rows, LANES)])(*blocks, pair, swap)
     other = lax.ppermute(message, "gy", pair_route("gy"))
     rows = message.shape[0] - w_shape[0]
     pieces = jnp.stack((message[:rows], other[:rows])).reshape((2, len(blocks)) + slow)

time: 47.2 us -> 52.4 us (1.11)
  waiting for transfers between devices: 10.1 us -> 13.5 us
  starting transfers between devices: 27.3 us -> 28.8 us
    ppermute x1, starting transfers between devices: 2.03 us -> 4.54 us  [fused_cycle(): swap = lax.ppermute(swap, 'gy', swap_route('gy'))]
    ppermute x3, waiting for transfers between devices: 4.13 us -> 5.78 us  [from_sides(): pair = lax.ppermute(pair, axis, pair_route(axis))]
    ppermute x1, starting transfers between devices: 4.7 us -> 3.09 us  [fused_cycle(): other = lax.ppermute(message, 'gy', pair_route('gy'))]
    ppermute x1, waiting for transfers between devices: 0.01 us -> 1.17 us  [fused_cycle(): other = lax.ppermute(message, 'gy', pair_route('gy'))]
    ppermute x3, waiting for transfers between devices: 2.27 us -> 3.08 us  [passed_round(): lax.ppermute(block, axis, [(i, i ^ distance) for i in range(count)])]
    ppermute x3, starting transfers between devices: 3.55 us -> 4.11 us  [passed_round(): lax.ppermute(block, axis, [(i, i ^ distance) for i in range(count)])]
    pallas_call x7 -> x8, Pallas kernels: 7.51 us -> 7.54 us  [launch(): pl.pallas_call(kernel, out_shape=[pltpu.VMEM(shape, F32) for shape in out...]
  transfers between devices with their start and end apart: 14 -> 14, of which waited for: 6 -> 8; matrix products, arithmetic and copies ran while one was open for 0% -> 0% of each run, Pallas kernels for 9% -> 2%
where the time goes in v12:
time: 52.4 us; the launch traced here: 51.9 us
  starting transfers between devices  28.8 us (55%)
  waiting for transfers between devices  13.5 us (26%)
  Pallas kernels  9.28 us (18%)
    ppermute x3, starting transfers between devices, from_sides(): pair = lax.ppermute(pair, axis, pair_route(axis))  9.47 us
    pallas_call x8, Pallas kernels, launch(): pl.pallas_call(kernel, out_shape=[pltpu.VMEM(shape, F32) for shape in out...  7.54 us
    ppermute x3, waiting for transfers between devices, from_sides(): pair = lax.ppermute(pair, axis, pair_route(axis))  5.78 us
    ppermute x3, starting transfers between devices, from_sides(): swap = lax.ppermute(swap, axis, swap_route(axis))  4.89 us
    ppermute x1, starting transfers between devices, fused_cycle(): swap = lax.ppermute(swap, 'gy', swap_route('gy'))  4.54 us
    ppermute x3, starting transfers between devices, passed_round(): lax.ppermute(block, axis, [(i, i ^ distance) for i in range(count)])  4.11 us
    ppermute x1, starting transfers between devices, fused_cycle(): other = lax.ppermute(message, 'gy', pair_route('gy'))  3.09 us
    ppermute x3, waiting for transfers between devices, passed_round(): lax.ppermute(block, axis, [(i, i ^ distance) for i in range(count)])  3.08 us
  transfers between devices with their start and end apart: 14, of which 8 were waited for; matrix products, arithmetic and copies ran while one was open for 0% of the time, Pallas kernels for 2%

profile of v12, /device:TPU:1, one launch (start us, length us, event | category | flops | bytes accessed | tf_op | source)
XLA Modules:
  0.0 51.9 jit_solution(11204906502872172208)
XLA Ops:
  0.0 1.2 %shard_map.55 = (f32[5,16,16,128]{3,2,1,0:T(8,128)S(1)}, f32[192,128]{1,0:T(8,128)S(1)}, f32[192,128]{1,0:T(8,128)S(1)}) custom-call(f32[16,16,128]{2,1,0:T(8,128)} %refs_0_.1, f32[16,16,128]{2,1,0:T(8,128)} %refs_1_.1, f32[16,16,128]{2,1,0:T(8,128)} %refs_2_.1, f32[16,16,128]{2,1,0:T(8,128)} %refs_3_.1, f32[16,16,128]{2,1,0:T(8,128)} %refs_4_.1), custom_call_target="tpu_custom_call" | custom-call | tf_op jit(solution)/shard_map/pallas_call | solution.py:763
  1.2 0.7 %collective-permute-start.1 = (f32[192,128]{1,0:T(8,128)S(1)}, f32[192,128]{1,0:T(8,128)S(1)}, u32[]{:S(2)}, u32[]{:S(2)}) collective-permute-start(f32[192,128]{1,0:T(8,128)S(1)} %get-tuple-element.41), channel_id=1, source_target_pairs={{4,8},{8,4},{12,16},{16,12},{20,24},{24,20},{5,9},{9,5},{13,17},{1... | collective-permute-start | bytes 294920 | tf_op jit(solution)/shard_map/ppermute | solution.py:792
  1.9 4.6 %collective-permute-start = (f32[192,128]{1,0:T(8,128)S(1)}, f32[192,128]{1,0:T(8,128)S(1)}, u32[]{:S(2)}, u32[]{:S(2)}) collective-permute-start(f32[192,128]{1,0:T(8,128)S(1)} %get-tuple-element.42), channel_id=1, source_target_pairs={{0,4},{4,0},{8,12},{12,8},{16,20},{20,16},{24,28},{28,24},{1,5},{5... | collective-permute-start | bytes 294920 | tf_op jit(solution)/shard_map/ppermute | solution.py:791
  6.5 0.0 collective-permute-done.1
  6.5 4.1 %collective-permute-done = f32[192,128]{1,0:T(8,128)S(1)} collective-permute-done((f32[192,128]{1,0:T(8,128)S(1)}, f32[192,128]{1,0:T(8,128)S(1)}, u32[]{:S(2)}, u32[]{:S(2)}) %collective-permute-start) | collective-permute-done | bytes 98336 | tf_op jit(solution)/shard_map/ppermute | solution.py:791
  10.7 0.1 shard_map.57
  10.8 3.6 %collective-permute-start.3 = (f32[232,128]{1,0:T(8,128)S(1)}, f32[232,128]{1,0:T(8,128)S(1)}, u32[]{:S(2)}, u32[]{:S(2)}) collective-permute-start(f32[232,128]{1,0:T(8,128)S(1)} %get-tuple-element.37), channel_id=1, source_target_pairs={{1,2},{2,1},{5,6},{6,5},{9,10},{10,9},{13,14},{14,13},{17,18},{18,... | collective-permute-start | bytes 356360 | tf_op jit(solution)/shard_map/ppermute | solution.py:792
  14.4 0.1 collective-permute-start.2
  14.4 0.8 %shard_map.56 = (f32[3,8,8,128]{3,2,1,0:T(8,128)S(1)}, f32[16,128]{1,0:T(8,128)S(1)}) custom-call(f32[5,16,16,128]{3,2,1,0:T(8,128)S(1)} %get-tuple-element.19.own), custom_call_target="tpu_custom_call" | custom-call | tf_op jit(solution)/shard_map/pallas_call | solution.py:763
  15.3 1.7 %collective-permute-done.3 = f32[232,128]{1,0:T(8,128)S(1)} collective-permute-done((f32[232,128]{1,0:T(8,128)S(1)}, f32[232,128]{1,0:T(8,128)S(1)}, u32[]{:S(2)}, u32[]{:S(2)}) %collective-permute-start.3) | collective-permute-done | bytes 118816 | tf_op jit(solution)/shard_map/ppermute | solution.py:792
  16.9 0.0 collective-permute-done.2
  17.0 2.0 %shard_map.58 = (f32[8,22,32,128]{3,2,1,0:T(8,128)S(1)}, f32[2,8,8,128]{3,2,1,0:T(8,128)S(1)}, f32[24,128]{1,0:T(8,128)S(1)}, f32[96,128]{1,0:T(8,128)S(1)}, f32[96,128]{1,0:T(8,128)S(1)}) custom-call(f32[5,16,16,128]{3,2,1,0:T(8,128)S(1)} %get-tuple-element.19.own, f32[3,8,8,128]{3,2,1,0:T(8,128)S(1)} %get-tuple-element.20.faces, ...), custom_call_target="tpu_custom_call" | custom-call | tf_op jit(solution)/shard_map/pallas_call | solution.py:763
  19.0 0.7 %collective-permute-start.8 = (f32[96,128]{1,0:T(8,128)S(1)}, f32[96,128]{1,0:T(8,128)S(1)}, u32[]{:S(2)}, u32[]{:S(2)}) collective-permute-start(f32[96,128]{1,0:T(8,128)S(1)} %get-tuple-element.47), channel_id=1, source_target_pairs={{4,8},{8,4},{12,16},{16,12},{20,24},{24,20},{5,9},{9,5},{13,17},{1... | collective-permute-start | bytes 147464 | tf_op jit(solution)/shard_map/ppermute | solution.py:792
  19.7 4.8 %collective-permute-start.7 = (f32[96,128]{1,0:T(8,128)S(1)}, f32[96,128]{1,0:T(8,128)S(1)}, u32[]{:S(2)}, u32[]{:S(2)}) collective-permute-start(f32[96,128]{1,0:T(8,128)S(1)} %get-tuple-element.48), channel_id=1, source_target_pairs={{0,4},{4,0},{8,12},{12,8},{16,20},{20,16},{24,28},{28,24},{1,5},{5... | collective-permute-start | bytes 147464 | tf_op jit(solution)/shard_map/ppermute | solution.py:791
  24.5 0.0 collective-permute-done.8
  24.5 1.6 %collective-permute-done.7 = f32[96,128]{1,0:T(8,128)S(1)} collective-permute-done((f32[96,128]{1,0:T(8,128)S(1)}, f32[96,128]{1,0:T(8,128)S(1)}, u32[]{:S(2)}, u32[]{:S(2)}) %collective-permute-start.7) | collective-permute-done | bytes 49184 | tf_op jit(solution)/shard_map/ppermute | solution.py:791
  26.1 0.1 shard_map.60
  26.3 4.5 %collective-permute-start.12 = (f32[168,128]{1,0:T(8,128)S(1)}, f32[168,128]{1,0:T(8,128)S(1)}, u32[]{:S(2)}, u32[]{:S(2)}) collective-permute-start(f32[168,128]{1,0:T(8,128)S(1)} %get-tuple-element.43), channel_id=1, source_target_pairs={{1,2},{2,1},{5,6},{6,5},{9,10},{10,9},{13,14},{14,13},{17,18},{18,... | collective-permute-start | bytes 258056 | tf_op jit(solution)/shard_map/ppermute | solution.py:859
  30.8 3.7 %collective-permute-start.6 = (f32[24,128]{1,0:T(8,128)S(1)}, f32[24,128]{1,0:T(8,128)S(1)}, u32[]{:S(2)}, u32[]{:S(2)}) collective-permute-start(f32[24,128]{1,0:T(8,128)S(1)} %get-tuple-element.26.refs_0_), channel_id=1, source_target_pairs={{0,24},{4,28},{8,16},{12,20},{16,8},{20,12},{24,0},{28,4},{1,25},{... | collective-permute-start | bytes 36872 | tf_op jit(solution)/shard_map/ppermute | solution.py:799
  34.6 0.0 collective-permute-start.5
  34.6 0.4 collective-permute-start.4
  34.9 0.7 %collective-permute-done.6.refs_3_ = f32[24,128]{1,0:T(8,128)S(1)} collective-permute-done((f32[24,128]{1,0:T(8,128)S(1)}, f32[24,128]{1,0:T(8,128)S(1)}, u32[]{:S(2)}, u32[]{:S(2)}) %collective-permute-start.6) | collective-permute-done | bytes 12320 | tf_op jit(solution)/shard_map/ppermute | solution.py:799
  35.7 2.4 %collective-permute-done.5.refs_2_ = f32[24,128]{1,0:T(8,128)S(1)} collective-permute-done((f32[24,128]{1,0:T(8,128)S(1)}, f32[24,128]{1,0:T(8,128)S(1)}, u32[]{:S(2)}, u32[]{:S(2)}) %collective-permute-start.5) | collective-permute-done | bytes 12320 | tf_op jit(solution)/shard_map/ppermute | solution.py:799
  38.0 0.0 collective-permute-done.4.refs_1_
  38.0 0.1 collective-permute-start.11
  38.1 0.1 collective-permute-start.10
  38.2 2.6 %collective-permute-start.9 = (f32[96,128]{1,0:T(8,128)S(1)}, f32[96,128]{1,0:T(8,128)S(1)}, u32[]{:S(2)}, u32[]{:S(2)}) collective-permute-start(f32[96,128]{1,0:T(8,128)S(1)} %bitcast.5), channel_id=1, source_target_pairs={{0,2},{1,3},{2,0},{3,1},{4,6},{5,7},{6,4},{7,5},{8,10},{9,11},{10,... | collective-permute-start | bytes 147464 | tf_op jit(solution)/shard_map/ppermute | solution.py:813
  40.7 1.2 %collective-permute-done.11.refs_3_ = f32[96,128]{1,0:T(8,128)S(1)} collective-permute-done((f32[96,128]{1,0:T(8,128)S(1)}, f32[96,128]{1,0:T(8,128)S(1)}, u32[]{:S(2)}, u32[]{:S(2)}) %collective-permute-start.11) | collective-permute-done | bytes 49184 | tf_op jit(solution)/shard_map/ppermute | solution.py:813
  42.0 0.0 collective-permute-done.10.refs_2_
  42.0 0.5 collective-permute-done.9.refs_1_
  42.5 0.0 collective-permute-done.12.refs_5_
  42.5 3.1 %collective-permute-start.13 = (f32[552,128]{1,0:T(8,128)S(1)}, f32[552,128]{1,0:T(8,128)S(1)}, u32[]{:S(2)}, u32[]{:S(2)}) collective-permute-start(f32[552,128]{1,0:T(8,128)S(1)} %shard_map.61), channel_id=1, source_target_pairs={{0,1},{1,0},{2,3},{3,2},{4,5},{5,4},{6,7},{7,6},{8,9},{9,8},{10,11... | collective-permute-start | bytes 847880 | tf_op jit(solution)/shard_map/ppermute | solution.py:862
  45.6 1.2 %collective-permute-done.13 = f32[552,128]{1,0:T(8,128)S(1)} collective-permute-done((f32[552,128]{1,0:T(8,128)S(1)}, f32[552,128]{1,0:T(8,128)S(1)}, u32[]{:S(2)}, u32[]{:S(2)}) %collective-permute-start.13) | collective-permute-done | bytes 282656 | tf_op jit(solution)/shard_map/ppermute | solution.py:862
  46.8 3.3 %shard_map.62.coarse = f32[12,32,128]{2,1,0:T(8,128)S(1)} custom-call(f32[2,4,4,24,128]{4,3,2,1,0:T(8,128)S(1)} %pad_maximum_fusion.pieces), custom_call_target="tpu_custom_call" | custom-call | tf_op jit(solution)/shard_map/pallas_call | solution.py:763
  50.1 1.7 %shard_map.63 = f32[16,16,128]{2,1,0:T(8,128)} custom-call(f32[12,32,128]{2,1,0:T(8,128)S(1)} %shard_map.62.coarse, f32[8,22,32,128]{3,2,1,0:T(8,128)S(1)} %get-tuple-element.29.top, f32[2,8,8,128]{3,2,1,0:T(8,128)S(1)} %get-tuple-element.30.kept, f32[3,8,8,128]{3,2,1,0:T(8,128)S(1)} %get-tuple-element.20.faces, ...), custom_call_target="tpu_custom_call" | custom-call | tf_op jit(solution)/shard_map/pallas_call | solution.py:876
  (13 shorter events, 0.2 us)
Async XLA Ops:
  1.2 5.3 %collective-permute-start.1 = (f32[192,128]{1,0:T(8,128)S(1)}, f32[192,128]{1,0:T(8,128)S(1)}, u32[]{:S(2)}, u32[]{:S(2)}) collective-permute-start(f32[192,128]{1,0:T(8,128)S(1)} %get-tuple-element.41), channel_id=1, source_target_pairs={{4,8},{8,4},{12,16},{16,12},{20,24},{24,20},{5,9},{9,5},{13,17},{1... | collective-permute-start | bytes 294920 | tf_op jit(solution)/shard_map/ppermute | solution.py:792
  1.9 8.7 %collective-permute-start = (f32[192,128]{1,0:T(8,128)S(1)}, f32[192,128]{1,0:T(8,128)S(1)}, u32[]{:S(2)}, u32[]{:S(2)}) collective-permute-start(f32[192,128]{1,0:T(8,128)S(1)} %get-tuple-element.42), channel_id=1, source_target_pairs={{0,4},{4,0},{8,12},{12,8},{16,20},{20,16},{24,28},{28,24},{1,5},{5... | collective-permute-start | bytes 294920 | tf_op jit(solution)/shard_map/ppermute | solution.py:791
  10.8 6.2 %collective-permute-start.3 = (f32[232,128]{1,0:T(8,128)S(1)}, f32[232,128]{1,0:T(8,128)S(1)}, u32[]{:S(2)}, u32[]{:S(2)}) collective-permute-start(f32[232,128]{1,0:T(8,128)S(1)} %get-tuple-element.37), channel_id=1, source_target_pairs={{1,2},{2,1},{5,6},{6,5},{9,10},{10,9},{13,14},{14,13},{17,18},{18,... | collective-permute-start | bytes 356360 | tf_op jit(solution)/shard_map/ppermute | solution.py:792
  14.4 2.6 %collective-permute-start.2 = (f32[232,128]{1,0:T(8,128)S(1)}, f32[232,128]{1,0:T(8,128)S(1)}, u32[]{:S(2)}, u32[]{:S(2)}) collective-permute-start(f32[232,128]{1,0:T(8,128)S(1)} %get-tuple-element.38), channel_id=1, source_target_pairs={{0,1},{1,0},{2,3},{3,2},{4,5},{5,4},{6,7},{7,6},{8,9},{9,8},{10,11... | collective-permute-start | bytes 356360 | tf_op jit(solution)/shard_map/ppermute | solution.py:791
  19.0 5.5 %collective-permute-start.8 = (f32[96,128]{1,0:T(8,128)S(1)}, f32[96,128]{1,0:T(8,128)S(1)}, u32[]{:S(2)}, u32[]{:S(2)}) collective-permute-start(f32[96,128]{1,0:T(8,128)S(1)} %get-tuple-element.47), channel_id=1, source_target_pairs={{4,8},{8,4},{12,16},{16,12},{20,24},{24,20},{5,9},{9,5},{13,17},{1... | collective-permute-start | bytes 147464 | tf_op jit(solution)/shard_map/ppermute | solution.py:792
  19.7 6.4 %collective-permute-start.7 = (f32[96,128]{1,0:T(8,128)S(1)}, f32[96,128]{1,0:T(8,128)S(1)}, u32[]{:S(2)}, u32[]{:S(2)}) collective-permute-start(f32[96,128]{1,0:T(8,128)S(1)} %get-tuple-element.48), channel_id=1, source_target_pairs={{0,4},{4,0},{8,12},{12,8},{16,20},{20,16},{24,28},{28,24},{1,5},{5... | collective-permute-start | bytes 147464 | tf_op jit(solution)/shard_map/ppermute | solution.py:791
  26.3 16.2 %collective-permute-start.12 = (f32[168,128]{1,0:T(8,128)S(1)}, f32[168,128]{1,0:T(8,128)S(1)}, u32[]{:S(2)}, u32[]{:S(2)}) collective-permute-start(f32[168,128]{1,0:T(8,128)S(1)} %get-tuple-element.43), channel_id=1, source_target_pairs={{1,2},{2,1},{5,6},{6,5},{9,10},{10,9},{13,14},{14,13},{17,18},{18,... | collective-permute-start | bytes 258056 | tf_op jit(solution)/shard_map/ppermute | solution.py:859
  30.8 4.8 %collective-permute-start.6 = (f32[24,128]{1,0:T(8,128)S(1)}, f32[24,128]{1,0:T(8,128)S(1)}, u32[]{:S(2)}, u32[]{:S(2)}) collective-permute-start(f32[24,128]{1,0:T(8,128)S(1)} %get-tuple-element.26.refs_0_), channel_id=1, source_target_pairs={{0,24},{4,28},{8,16},{12,20},{16,8},{20,12},{24,0},{28,4},{1,25},{... | collective-permute-start | bytes 36872 | tf_op jit(solution)/shard_map/ppermute | solution.py:799
  34.6 3.4 %collective-permute-start.5 = (f32[24,128]{1,0:T(8,128)S(1)}, f32[24,128]{1,0:T(8,128)S(1)}, u32[]{:S(2)}, u32[]{:S(2)}) collective-permute-start(f32[24,128]{1,0:T(8,128)S(1)} %get-tuple-element.26.refs_0_), channel_id=1, source_target_pairs={{0,16},{4,20},{8,24},{12,28},{16,0},{20,4},{24,8},{28,12},{1,17},{... | collective-permute-start | bytes 36872 | tf_op jit(solution)/shard_map/ppermute | solution.py:799
  34.6 3.4 %collective-permute-start.4 = (f32[24,128]{1,0:T(8,128)S(1)}, f32[24,128]{1,0:T(8,128)S(1)}, u32[]{:S(2)}, u32[]{:S(2)}) collective-permute-start(f32[24,128]{1,0:T(8,128)S(1)} %get-tuple-element.26.refs_0_), channel_id=1, source_target_pairs={{0,8},{4,12},{8,0},{12,4},{16,24},{20,28},{24,16},{28,20},{1,9},{5... | collective-permute-start | bytes 36872 | tf_op jit(solution)/shard_map/ppermute | solution.py:799
  38.0 3.9 %collective-permute-start.11 = (f32[96,128]{1,0:T(8,128)S(1)}, f32[96,128]{1,0:T(8,128)S(1)}, u32[]{:S(2)}, u32[]{:S(2)}) collective-permute-start(f32[96,128]{1,0:T(8,128)S(1)} %bitcast.3), channel_id=1, source_target_pairs={{0,6},{1,7},{2,4},{3,5},{4,2},{5,3},{6,0},{7,1},{8,14},{9,15},{10,... | collective-permute-start | bytes 147464 | tf_op jit(solution)/shard_map/ppermute | solution.py:813
  38.1 3.9 %collective-permute-start.10 = (f32[96,128]{1,0:T(8,128)S(1)}, f32[96,128]{1,0:T(8,128)S(1)}, u32[]{:S(2)}, u32[]{:S(2)}) collective-permute-start(f32[96,128]{1,0:T(8,128)S(1)} %bitcast.4), channel_id=1, source_target_pairs={{0,4},{1,5},{2,6},{3,7},{4,0},{5,1},{6,2},{7,3},{8,12},{9,13},{10,... | collective-permute-start | bytes 147464 | tf_op jit(solution)/shard_map/ppermute | solution.py:813
  38.2 4.3 %collective-permute-start.9 = (f32[96,128]{1,0:T(8,128)S(1)}, f32[96,128]{1,0:T(8,128)S(1)}, u32[]{:S(2)}, u32[]{:S(2)}) collective-permute-start(f32[96,128]{1,0:T(8,128)S(1)} %bitcast.5), channel_id=1, source_target_pairs={{0,2},{1,3},{2,0},{3,1},{4,6},{5,7},{6,4},{7,5},{8,10},{9,11},{10,... | collective-permute-start | bytes 147464 | tf_op jit(solution)/shard_map/ppermute | solution.py:813
  42.5 4.3 %collective-permute-start.13 = (f32[552,128]{1,0:T(8,128)S(1)}, f32[552,128]{1,0:T(8,128)S(1)}, u32[]{:S(2)}, u32[]{:S(2)}) collective-permute-start(f32[552,128]{1,0:T(8,128)S(1)} %shard_map.61), channel_id=1, source_target_pairs={{0,1},{1,0},{2,3},{3,2},{4,5},{5,4},{6,7},{7,6},{8,9},{9,8},{10,11... | collective-permute-start | bytes 847880 | tf_op jit(solution)/shard_map/ppermute | solution.py:862

commit v13 on v12

--- a/solution.py
+++ b/solution.py
@@ -378,7 +378,7 @@
     chunk[coarse_rows + quarter_rows :] = coefficients[:BLOCK_ROWS - coarse_rows - quarter_rows]
 
 
-def pack_v(top, kept, faces, x_low, x_high, low, high):
+def pack_v(top, kept, faces, x_low, x_high, _, low, high):
     coarse_x, coarse_y = faces.shape[1:3]
     nx, ny = 2 * coarse_x, 2 * coarse_y
     slabs = coarse_x + 2 * RIM
@@ -854,7 +854,7 @@
     slow = (len(blocks),) + chunk.shape
     (pieces,) = call(stack_blocks, [slow])(*blocks, v_low, v_high)
     blocks = passed_across(pieces.reshape(-1, LANES))
-    w_low, w_high = call(pack_v, [w_shape] * 2)(top, kept, faces, v_low, v_high)
+    w_low, w_high = call(pack_v, [w_shape] * 2)(top, kept, faces, v_low, v_high, pieces)
     pair, swap = by_partner(w_low, w_high, "gy")
     swap = lax.ppermute(swap, "gy", swap_route("gy"))
     rows = sum(block.shape[0] for block in blocks) + w_shape[0]

time: 52.4 us -> 48.4 us (0.924)
  starting transfers between devices: 28.8 us -> 26.8 us
  waiting for transfers between devices: 13.5 us -> 11.5 us
    ppermute x1, starting transfers between devices: 3.09 us -> 1.1 us  [fused_cycle(): other = lax.ppermute(message, 'gy', pair_route('gy'))]
    ppermute x3, waiting for transfers between devices: 5.78 us -> 4.13 us  [from_sides(): pair = lax.ppermute(pair, axis, pair_route(axis))]
    ppermute x3, waiting for transfers between devices: 3.08 us -> 2.27 us  [passed_round(): lax.ppermute(block, axis, [(i, i ^ distance) for i in range(count)])]
    ppermute x3, starting transfers between devices: 4.11 us -> 3.55 us  [passed_round(): lax.ppermute(block, axis, [(i, i ^ distance) for i in range(count)])]
  transfers between devices with their start and end apart: 14 -> 14, of which waited for: 8 -> 7; matrix products, arithmetic and copies ran while one was open for 0% -> 0% of each run, Pallas kernels for 2% -> 2%
where the time goes in v13:
time: 48.4 us; the launch traced here: 47.9 us
  starting transfers between devices  26.8 us (55%)
  waiting for transfers between devices  11.5 us (24%)
  Pallas kernels  9.28 us (19%)
    ppermute x3, starting transfers between devices, from_sides(): pair = lax.ppermute(pair, axis, pair_route(axis))  9.47 us
    pallas_call x8, Pallas kernels, launch(): pl.pallas_call(kernel, out_shape=[pltpu.VMEM(shape, F32) for shape in out...  7.54 us
    ppermute x1, starting transfers between devices, fused_cycle(): swap = lax.ppermute(swap, 'gy', swap_route('gy'))  5.02 us
    ppermute x3, starting transfers between devices, from_sides(): swap = lax.ppermute(swap, axis, swap_route(axis))  4.89 us
    ppermute x3, waiting for transfers between devices, from_sides(): pair = lax.ppermute(pair, axis, pair_route(axis))  4.13 us
    ppermute x3, starting transfers between devices, passed_round(): lax.ppermute(block, axis, [(i, i ^ distance) for i in range(count)])  3.55 us
    ppermute x3, starting transfers between devices, passed_across(): blocks.append(lax.ppermute(block, ('gx', 'gy'), route) if moved else block)  2.79 us
    ppermute x3, waiting for transfers between devices, passed_round(): lax.ppermute(block, axis, [(i, i ^ distance) for i in range(count)])  2.27 us
  transfers between devices with their start and end apart: 14, of which 7 were waited for; matrix products, arithmetic and copies ran while one was open for 0% of the time, Pallas kernels for 2%

profile of v13, /device:TPU:1, one launch (start us, length us, event | category | flops | bytes accessed | tf_op | source)
XLA Modules:
  0.0 47.9 jit_solution(4423417244353806537)
XLA Ops:
  0.0 1.2 %shard_map.55 = (f32[5,16,16,128]{3,2,1,0:T(8,128)S(1)}, f32[192,128]{1,0:T(8,128)S(1)}, f32[192,128]{1,0:T(8,128)S(1)}) custom-call(f32[16,16,128]{2,1,0:T(8,128)} %refs_0_.1, f32[16,16,128]{2,1,0:T(8,128)} %refs_1_.1, f32[16,16,128]{2,1,0:T(8,128)} %refs_2_.1, f32[16,16,128]{2,1,0:T(8,128)} %refs_3_.1, f32[16,16,128]{2,1,0:T(8,128)} %refs_4_.1), custom_call_target="tpu_custom_call" | custom-call | tf_op jit(solution)/shard_map/pallas_call | solution.py:763
  1.2 0.7 %collective-permute-start.1 = (f32[192,128]{1,0:T(8,128)S(1)}, f32[192,128]{1,0:T(8,128)S(1)}, u32[]{:S(2)}, u32[]{:S(2)}) collective-permute-start(f32[192,128]{1,0:T(8,128)S(1)} %get-tuple-element.41), channel_id=1, source_target_pairs={{4,8},{8,4},{12,16},{16,12},{20,24},{24,20},{5,9},{9,5},{13,17},{1... | collective-permute-start | bytes 294920 | tf_op jit(solution)/shard_map/ppermute | solution.py:792
  1.9 4.6 %collective-permute-start = (f32[192,128]{1,0:T(8,128)S(1)}, f32[192,128]{1,0:T(8,128)S(1)}, u32[]{:S(2)}, u32[]{:S(2)}) collective-permute-start(f32[192,128]{1,0:T(8,128)S(1)} %get-tuple-element.42), channel_id=1, source_target_pairs={{0,4},{4,0},{8,12},{12,8},{16,20},{20,16},{24,28},{28,24},{1,5},{5... | collective-permute-start | bytes 294920 | tf_op jit(solution)/shard_map/ppermute | solution.py:791
  6.5 0.0 collective-permute-done.1
  6.5 4.1 %collective-permute-done = f32[192,128]{1,0:T(8,128)S(1)} collective-permute-done((f32[192,128]{1,0:T(8,128)S(1)}, f32[192,128]{1,0:T(8,128)S(1)}, u32[]{:S(2)}, u32[]{:S(2)}) %collective-permute-start) | collective-permute-done | bytes 98336 | tf_op jit(solution)/shard_map/ppermute | solution.py:791
  10.7 0.1 shard_map.57
  10.8 3.6 %collective-permute-start.3 = (f32[232,128]{1,0:T(8,128)S(1)}, f32[232,128]{1,0:T(8,128)S(1)}, u32[]{:S(2)}, u32[]{:S(2)}) collective-permute-start(f32[232,128]{1,0:T(8,128)S(1)} %get-tuple-element.37), channel_id=1, source_target_pairs={{1,2},{2,1},{5,6},{6,5},{9,10},{10,9},{13,14},{14,13},{17,18},{18,... | collective-permute-start | bytes 356360 | tf_op jit(solution)/shard_map/ppermute | solution.py:792
  14.4 0.1 collective-permute-start.2
  14.4 0.8 %shard_map.56 = (f32[3,8,8,128]{3,2,1,0:T(8,128)S(1)}, f32[16,128]{1,0:T(8,128)S(1)}) custom-call(f32[5,16,16,128]{3,2,1,0:T(8,128)S(1)} %get-tuple-element.19.own), custom_call_target="tpu_custom_call" | custom-call | tf_op jit(solution)/shard_map/pallas_call | solution.py:763
  15.3 1.7 %collective-permute-done.3 = f32[232,128]{1,0:T(8,128)S(1)} collective-permute-done((f32[232,128]{1,0:T(8,128)S(1)}, f32[232,128]{1,0:T(8,128)S(1)}, u32[]{:S(2)}, u32[]{:S(2)}) %collective-permute-start.3) | collective-permute-done | bytes 118816 | tf_op jit(solution)/shard_map/ppermute | solution.py:792
  16.9 0.0 collective-permute-done.2
  17.0 2.0 %shard_map.58 = (f32[8,22,32,128]{3,2,1,0:T(8,128)S(1)}, f32[2,8,8,128]{3,2,1,0:T(8,128)S(1)}, f32[24,128]{1,0:T(8,128)S(1)}, f32[96,128]{1,0:T(8,128)S(1)}, f32[96,128]{1,0:T(8,128)S(1)}) custom-call(f32[5,16,16,128]{3,2,1,0:T(8,128)S(1)} %get-tuple-element.19.own, f32[3,8,8,128]{3,2,1,0:T(8,128)S(1)} %get-tuple-element.20.faces, ...), custom_call_target="tpu_custom_call" | custom-call | tf_op jit(solution)/shard_map/pallas_call | solution.py:763
  19.0 0.7 %collective-permute-start.8 = (f32[96,128]{1,0:T(8,128)S(1)}, f32[96,128]{1,0:T(8,128)S(1)}, u32[]{:S(2)}, u32[]{:S(2)}) collective-permute-start(f32[96,128]{1,0:T(8,128)S(1)} %get-tuple-element.47), channel_id=1, source_target_pairs={{4,8},{8,4},{12,16},{16,12},{20,24},{24,20},{5,9},{9,5},{13,17},{1... | collective-permute-start | bytes 147464 | tf_op jit(solution)/shard_map/ppermute | solution.py:792
  19.7 4.8 %collective-permute-start.7 = (f32[96,128]{1,0:T(8,128)S(1)}, f32[96,128]{1,0:T(8,128)S(1)}, u32[]{:S(2)}, u32[]{:S(2)}) collective-permute-start(f32[96,128]{1,0:T(8,128)S(1)} %get-tuple-element.48), channel_id=1, source_target_pairs={{0,4},{4,0},{8,12},{12,8},{16,20},{20,16},{24,28},{28,24},{1,5},{5... | collective-permute-start | bytes 147464 | tf_op jit(solution)/shard_map/ppermute | solution.py:791
  24.5 2.0 %collective-permute-start.6 = (f32[24,128]{1,0:T(8,128)S(1)}, f32[24,128]{1,0:T(8,128)S(1)}, u32[]{:S(2)}, u32[]{:S(2)}) collective-permute-start(f32[24,128]{1,0:T(8,128)S(1)} %get-tuple-element.26.refs_0_), channel_id=1, source_target_pairs={{0,24},{4,28},{8,16},{12,20},{16,8},{20,12},{24,0},{28,4},{1,25},{... | collective-permute-start | bytes 36872 | tf_op jit(solution)/shard_map/ppermute | solution.py:799
  26.5 0.5 collective-permute-start.5
  26.9 1.1 %collective-permute-start.4 = (f32[24,128]{1,0:T(8,128)S(1)}, f32[24,128]{1,0:T(8,128)S(1)}, u32[]{:S(2)}, u32[]{:S(2)}) collective-permute-start(f32[24,128]{1,0:T(8,128)S(1)} %get-tuple-element.26.refs_0_), channel_id=1, source_target_pairs={{0,8},{4,12},{8,0},{12,4},{16,24},{20,28},{24,16},{28,20},{1,9},{5... | collective-permute-start | bytes 36872 | tf_op jit(solution)/shard_map/ppermute | solution.py:799
  28.0 0.0 collective-permute-done.8
  28.0 0.0 collective-permute-done.7
  28.0 1.1 %collective-permute-done.6.refs_3_ = f32[24,128]{1,0:T(8,128)S(1)} collective-permute-done((f32[24,128]{1,0:T(8,128)S(1)}, f32[24,128]{1,0:T(8,128)S(1)}, u32[]{:S(2)}, u32[]{:S(2)}) %collective-permute-start.6) | collective-permute-done | bytes 12320 | tf_op jit(solution)/shard_map/ppermute | solution.py:799
  29.2 1.1 %collective-permute-done.5.refs_2_ = f32[24,128]{1,0:T(8,128)S(1)} collective-permute-done((f32[24,128]{1,0:T(8,128)S(1)}, f32[24,128]{1,0:T(8,128)S(1)}, u32[]{:S(2)}, u32[]{:S(2)}) %collective-permute-start.5) | collective-permute-done | bytes 12320 | tf_op jit(solution)/shard_map/ppermute | solution.py:799
  30.3 0.0 collective-permute-done.4.refs_1_
  30.3 0.1 shard_map.60
  30.5 5.0 %collective-permute-start.12 = (f32[168,128]{1,0:T(8,128)S(1)}, f32[168,128]{1,0:T(8,128)S(1)}, u32[]{:S(2)}, u32[]{:S(2)}) collective-permute-start(f32[168,128]{1,0:T(8,128)S(1)} %get-tuple-element.43), channel_id=1, source_target_pairs={{1,2},{2,1},{5,6},{6,5},{9,10},{10,9},{13,14},{14,13},{17,18},{18,... | collective-permute-start | bytes 258056 | tf_op jit(solution)/shard_map/ppermute | solution.py:859
  35.5 0.1 collective-permute-start.11
  35.6 1.6 %collective-permute-start.10 = (f32[96,128]{1,0:T(8,128)S(1)}, f32[96,128]{1,0:T(8,128)S(1)}, u32[]{:S(2)}, u32[]{:S(2)}) collective-permute-start(f32[96,128]{1,0:T(8,128)S(1)} %bitcast.4), channel_id=1, source_target_pairs={{0,4},{1,5},{2,6},{3,7},{4,0},{5,1},{6,2},{7,3},{8,12},{9,13},{10,... | collective-permute-start | bytes 147464 | tf_op jit(solution)/shard_map/ppermute | solution.py:813
  37.2 1.1 %collective-permute-start.9 = (f32[96,128]{1,0:T(8,128)S(1)}, f32[96,128]{1,0:T(8,128)S(1)}, u32[]{:S(2)}, u32[]{:S(2)}) collective-permute-start(f32[96,128]{1,0:T(8,128)S(1)} %bitcast.5), channel_id=1, source_target_pairs={{0,2},{1,3},{2,0},{3,1},{4,6},{5,7},{6,4},{7,5},{8,10},{9,11},{10,... | collective-permute-start | bytes 147464 | tf_op jit(solution)/shard_map/ppermute | solution.py:813
  38.3 1.4 %collective-permute-done.11.refs_3_ = f32[96,128]{1,0:T(8,128)S(1)} collective-permute-done((f32[96,128]{1,0:T(8,128)S(1)}, f32[96,128]{1,0:T(8,128)S(1)}, u32[]{:S(2)}, u32[]{:S(2)}) %collective-permute-start.11) | collective-permute-done | bytes 49184 | tf_op jit(solution)/shard_map/ppermute | solution.py:813
  39.7 0.0 collective-permute-done.10.refs_2_
  39.7 0.8 %collective-permute-done.9.refs_1_ = f32[96,128]{1,0:T(8,128)S(1)} collective-permute-done((f32[96,128]{1,0:T(8,128)S(1)}, f32[96,128]{1,0:T(8,128)S(1)}, u32[]{:S(2)}, u32[]{:S(2)}) %collective-permute-start.9) | collective-permute-done | bytes 49184 | tf_op jit(solution)/shard_map/ppermute | solution.py:813
  40.5 0.0 collective-permute-done.12.refs_5_
  40.5 1.1 %collective-permute-start.13 = (f32[552,128]{1,0:T(8,128)S(1)}, f32[552,128]{1,0:T(8,128)S(1)}, u32[]{:S(2)}, u32[]{:S(2)}) collective-permute-start(f32[552,128]{1,0:T(8,128)S(1)} %shard_map.61), channel_id=1, source_target_pairs={{0,1},{1,0},{2,3},{3,2},{4,5},{5,4},{6,7},{7,6},{8,9},{9,8},{10,11... | collective-permute-start | bytes 847880 | tf_op jit(solution)/shard_map/ppermute | solution.py:862
  41.6 1.2 %collective-permute-done.13 = f32[552,128]{1,0:T(8,128)S(1)} collective-permute-done((f32[552,128]{1,0:T(8,128)S(1)}, f32[552,128]{1,0:T(8,128)S(1)}, u32[]{:S(2)}, u32[]{:S(2)}) %collective-permute-start.13) | collective-permute-done | bytes 282656 | tf_op jit(solution)/shard_map/ppermute | solution.py:862
  42.9 3.3 %shard_map.62.coarse = f32[12,32,128]{2,1,0:T(8,128)S(1)} custom-call(f32[2,4,4,24,128]{4,3,2,1,0:T(8,128)S(1)} %pad_maximum_fusion.pieces), custom_call_target="tpu_custom_call" | custom-call | tf_op jit(solution)/shard_map/pallas_call | solution.py:763
  46.1 1.7 %shard_map.63 = f32[16,16,128]{2,1,0:T(8,128)} custom-call(f32[12,32,128]{2,1,0:T(8,128)S(1)} %shard_map.62.coarse, f32[8,22,32,128]{3,2,1,0:T(8,128)S(1)} %get-tuple-element.29.top, f32[2,8,8,128]{3,2,1,0:T(8,128)S(1)} %get-tuple-element.30.kept, f32[3,8,8,128]{3,2,1,0:T(8,128)S(1)} %get-tuple-element.20.faces, ...), custom_call_target="tpu_custom_call" | custom-call | tf_op jit(solution)/shard_map/pallas_call | solution.py:876
  (13 shorter events, 0.2 us)
Async XLA Ops:
  1.2 5.3 %collective-permute-start.1 = (f32[192,128]{1,0:T(8,128)S(1)}, f32[192,128]{1,0:T(8,128)S(1)}, u32[]{:S(2)}, u32[]{:S(2)}) collective-permute-start(f32[192,128]{1,0:T(8,128)S(1)} %get-tuple-element.41), channel_id=1, source_target_pairs={{4,8},{8,4},{12,16},{16,12},{20,24},{24,20},{5,9},{9,5},{13,17},{1... | collective-permute-start | bytes 294920 | tf_op jit(solution)/shard_map/ppermute | solution.py:792
  1.9 8.7 %collective-permute-start = (f32[192,128]{1,0:T(8,128)S(1)}, f32[192,128]{1,0:T(8,128)S(1)}, u32[]{:S(2)}, u32[]{:S(2)}) collective-permute-start(f32[192,128]{1,0:T(8,128)S(1)} %get-tuple-element.42), channel_id=1, source_target_pairs={{0,4},{4,0},{8,12},{12,8},{16,20},{20,16},{24,28},{28,24},{1,5},{5... | collective-permute-start | bytes 294920 | tf_op jit(solution)/shard_map/ppermute | solution.py:791
  10.8 6.2 %collective-permute-start.3 = (f32[232,128]{1,0:T(8,128)S(1)}, f32[232,128]{1,0:T(8,128)S(1)}, u32[]{:S(2)}, u32[]{:S(2)}) collective-permute-start(f32[232,128]{1,0:T(8,128)S(1)} %get-tuple-element.37), channel_id=1, source_target_pairs={{1,2},{2,1},{5,6},{6,5},{9,10},{10,9},{13,14},{14,13},{17,18},{18,... | collective-permute-start | bytes 356360 | tf_op jit(solution)/shard_map/ppermute | solution.py:792
  14.4 2.6 %collective-permute-start.2 = (f32[232,128]{1,0:T(8,128)S(1)}, f32[232,128]{1,0:T(8,128)S(1)}, u32[]{:S(2)}, u32[]{:S(2)}) collective-permute-start(f32[232,128]{1,0:T(8,128)S(1)} %get-tuple-element.38), channel_id=1, source_target_pairs={{0,1},{1,0},{2,3},{3,2},{4,5},{5,4},{6,7},{7,6},{8,9},{9,8},{10,11... | collective-permute-start | bytes 356360 | tf_op jit(solution)/shard_map/ppermute | solution.py:791
  19.0 9.0 %collective-permute-start.8 = (f32[96,128]{1,0:T(8,128)S(1)}, f32[96,128]{1,0:T(8,128)S(1)}, u32[]{:S(2)}, u32[]{:S(2)}) collective-permute-start(f32[96,128]{1,0:T(8,128)S(1)} %get-tuple-element.47), channel_id=1, source_target_pairs={{4,8},{8,4},{12,16},{16,12},{20,24},{24,20},{5,9},{9,5},{13,17},{1... | collective-permute-start | bytes 147464 | tf_op jit(solution)/shard_map/ppermute | solution.py:792
  19.7 8.3 %collective-permute-start.7 = (f32[96,128]{1,0:T(8,128)S(1)}, f32[96,128]{1,0:T(8,128)S(1)}, u32[]{:S(2)}, u32[]{:S(2)}) collective-permute-start(f32[96,128]{1,0:T(8,128)S(1)} %get-tuple-element.48), channel_id=1, source_target_pairs={{0,4},{4,0},{8,12},{12,8},{16,20},{20,16},{24,28},{28,24},{1,5},{5... | collective-permute-start | bytes 147464 | tf_op jit(solution)/shard_map/ppermute | solution.py:791
  24.5 4.7 %collective-permute-start.6 = (f32[24,128]{1,0:T(8,128)S(1)}, f32[24,128]{1,0:T(8,128)S(1)}, u32[]{:S(2)}, u32[]{:S(2)}) collective-permute-start(f32[24,128]{1,0:T(8,128)S(1)} %get-tuple-element.26.refs_0_), channel_id=1, source_target_pairs={{0,24},{4,28},{8,16},{12,20},{16,8},{20,12},{24,0},{28,4},{1,25},{... | collective-permute-start | bytes 36872 | tf_op jit(solution)/shard_map/ppermute | solution.py:799
  26.5 3.8 %collective-permute-start.5 = (f32[24,128]{1,0:T(8,128)S(1)}, f32[24,128]{1,0:T(8,128)S(1)}, u32[]{:S(2)}, u32[]{:S(2)}) collective-permute-start(f32[24,128]{1,0:T(8,128)S(1)} %get-tuple-element.26.refs_0_), channel_id=1, source_target_pairs={{0,16},{4,20},{8,24},{12,28},{16,0},{20,4},{24,8},{28,12},{1,17},{... | collective-permute-start | bytes 36872 | tf_op jit(solution)/shard_map/ppermute | solution.py:799
  26.9 3.4 %collective-permute-start.4 = (f32[24,128]{1,0:T(8,128)S(1)}, f32[24,128]{1,0:T(8,128)S(1)}, u32[]{:S(2)}, u32[]{:S(2)}) collective-permute-start(f32[24,128]{1,0:T(8,128)S(1)} %get-tuple-element.26.refs_0_), channel_id=1, source_target_pairs={{0,8},{4,12},{8,0},{12,4},{16,24},{20,28},{24,16},{28,20},{1,9},{5... | collective-permute-start | bytes 36872 | tf_op jit(solution)/shard_map/ppermute | solution.py:799
  30.5 10.0 %collective-permute-start.12 = (f32[168,128]{1,0:T(8,128)S(1)}, f32[168,128]{1,0:T(8,128)S(1)}, u32[]{:S(2)}, u32[]{:S(2)}) collective-permute-start(f32[168,128]{1,0:T(8,128)S(1)} %get-tuple-element.43), channel_id=1, source_target_pairs={{1,2},{2,1},{5,6},{6,5},{9,10},{10,9},{13,14},{14,13},{17,18},{18,... | collective-permute-start | bytes 258056 | tf_op jit(solution)/shard_map/ppermute | solution.py:859
  35.5 4.2 %collective-permute-start.11 = (f32[96,128]{1,0:T(8,128)S(1)}, f32[96,128]{1,0:T(8,128)S(1)}, u32[]{:S(2)}, u32[]{:S(2)}) collective-permute-start(f32[96,128]{1,0:T(8,128)S(1)} %bitcast.3), channel_id=1, source_target_pairs={{0,6},{1,7},{2,4},{3,5},{4,2},{5,3},{6,0},{7,1},{8,14},{9,15},{10,... | collective-permute-start | bytes 147464 | tf_op jit(solution)/shard_map/ppermute | solution.py:813
  35.6 4.1 %collective-permute-start.10 = (f32[96,128]{1,0:T(8,128)S(1)}, f32[96,128]{1,0:T(8,128)S(1)}, u32[]{:S(2)}, u32[]{:S(2)}) collective-permute-start(f32[96,128]{1,0:T(8,128)S(1)} %bitcast.4), channel_id=1, source_target_pairs={{0,4},{1,5},{2,6},{3,7},{4,0},{5,1},{6,2},{7,3},{8,12},{9,13},{10,... | collective-permute-start | bytes 147464 | tf_op jit(solution)/shard_map/ppermute | solution.py:813
  37.2 3.3 %collective-permute-start.9 = (f32[96,128]{1,0:T(8,128)S(1)}, f32[96,128]{1,0:T(8,128)S(1)}, u32[]{:S(2)}, u32[]{:S(2)}) collective-permute-start(f32[96,128]{1,0:T(8,128)S(1)} %bitcast.5), channel_id=1, source_target_pairs={{0,2},{1,3},{2,0},{3,1},{4,6},{5,7},{6,4},{7,5},{8,10},{9,11},{10,... | collective-permute-start | bytes 147464 | tf_op jit(solution)/shard_map/ppermute | solution.py:813
  40.5 2.3 %collective-permute-start.13 = (f32[552,128]{1,0:T(8,128)S(1)}, f32[552,128]{1,0:T(8,128)S(1)}, u32[]{:S(2)}, u32[]{:S(2)}) collective-permute-start(f32[552,128]{1,0:T(8,128)S(1)} %shard_map.61), channel_id=1, source_target_pairs={{0,1},{1,0},{2,3},{3,2},{4,5},{5,4},{6,7},{7,6},{8,9},{9,8},{10,11... | collective-permute-start | bytes 847880 | tf_op jit(solution)/shard_map/ppermute | solution.py:862

commit v14 on v11

--- a/solution.py
+++ b/solution.py
@@ -416,6 +416,11 @@
             out[pl.ds(base_y + 2 * (2 + nx + layer), 2)] = x_high[rows]
         for slab in range(nx):
             out[pl.ds(base_y + 2 * (2 + slab), 2)] = top[V, EDGE + slab, pl.ds(PAD + start, 2)]
+
+
+def hand_on(first, second, _, first_out, second_out):
+    first_out[...] = first[...]
+    second_out[...] = second[...]
 
 
 def stack_blocks(*refs):
@@ -840,6 +845,7 @@
     )(own, faces, coefficients, x_low, x_high, y_low, y_high)
 
     blocks = passed_round(chunk, "gx", 2)
+    v_low, v_high = call(hand_on, [v_shape, v_shape])(v_low, v_high, blocks[1])
     v_low, v_high = from_sides(v_low, v_high, "gx")
     slow = (len(blocks),) + chunk.shape
     (pieces,) = call(stack_blocks, [slow])(*blocks, v_low, v_high)

time: 47.2 us -> 50.8 us (1.076)
  waiting for transfers between devices: 10.1 us -> 12.1 us
  starting transfers between devices: 27.3 us -> 28.9 us
    ppermute x3, waiting for transfers between devices: 2.27 us -> 4.32 us  [passed_round(): lax.ppermute(block, axis, [(i, i ^ distance) for i in range(count)])]
    ppermute x3, starting transfers between devices: 3.55 us -> 4.77 us  [passed_round(): lax.ppermute(block, axis, [(i, i ^ distance) for i in range(count)])]
    ppermute x1, starting transfers between devices: 4.7 us -> 5.86 us  [fused_cycle(): other = lax.ppermute(message, 'gy', pair_route('gy'))]
    ppermute x3, starting transfers between devices: 9.47 us -> 8.66 us  [from_sides(): pair = lax.ppermute(pair, axis, pair_route(axis))]
    pallas_call x7 -> x8, Pallas kernels: 7.51 us -> 7.52 us  [launch(): pl.pallas_call(kernel, out_shape=[pltpu.VMEM(shape, F32) for shape in out...]
  transfers between devices with their start and end apart: 14 -> 14, of which waited for: 6 -> 7; matrix products, arithmetic and copies ran while one was open for 0% -> 0% of each run, Pallas kernels for 9% -> 8%
where the time goes in v14:
time: 50.8 us; the launch traced here: 50.6 us
  starting transfers between devices  28.9 us (57%)
  waiting for transfers between devices  12.1 us (24%)
  Pallas kernels  9.25 us (18%)
    ppermute x3, starting transfers between devices, from_sides(): pair = lax.ppermute(pair, axis, pair_route(axis))  8.66 us
    pallas_call x8, Pallas kernels, launch(): pl.pallas_call(kernel, out_shape=[pltpu.VMEM(shape, F32) for shape in out...  7.52 us
    ppermute x1, starting transfers between devices, fused_cycle(): other = lax.ppermute(message, 'gy', pair_route('gy'))  5.86 us
    ppermute x3, starting transfers between devices, from_sides(): swap = lax.ppermute(swap, axis, swap_route(axis))  4.89 us
    ppermute x3, starting transfers between devices, passed_round(): lax.ppermute(block, axis, [(i, i ^ distance) for i in range(count)])  4.77 us
    ppermute x3, waiting for transfers between devices, passed_round(): lax.ppermute(block, axis, [(i, i ^ distance) for i in range(count)])  4.32 us
    ppermute x3, waiting for transfers between devices, from_sides(): pair = lax.ppermute(pair, axis, pair_route(axis))  4.13 us
    ppermute x3, starting transfers between devices, passed_across(): blocks.append(lax.ppermute(block, ('gx', 'gy'), route) if moved else block)  2.65 us
  transfers between devices with their start and end apart: 14, of which 7 were waited for; matrix products, arithmetic and copies ran while one was open for 0% of the time, Pallas kernels for 8%

profile of v14, /device:TPU:1, one launch (start us, length us, event | category | flops | bytes accessed | tf_op | source)
XLA Modules:
  0.0 50.6 jit_solution(11741691892705623469)
XLA Ops:
  0.0 1.2 %shard_map.55 = (f32[5,16,16,128]{3,2,1,0:T(8,128)S(1)}, f32[192,128]{1,0:T(8,128)S(1)}, f32[192,128]{1,0:T(8,128)S(1)}) custom-call(f32[16,16,128]{2,1,0:T(8,128)} %refs_0_.1, f32[16,16,128]{2,1,0:T(8,128)} %refs_1_.1, f32[16,16,128]{2,1,0:T(8,128)} %refs_2_.1, f32[16,16,128]{2,1,0:T(8,128)} %refs_3_.1, f32[16,16,128]{2,1,0:T(8,128)} %refs_4_.1), custom_call_target="tpu_custom_call" | custom-call | tf_op jit(solution)/shard_map/pallas_call | solution.py:758
  1.2 0.7 %collective-permute-start.1 = (f32[192,128]{1,0:T(8,128)S(1)}, f32[192,128]{1,0:T(8,128)S(1)}, u32[]{:S(2)}, u32[]{:S(2)}) collective-permute-start(f32[192,128]{1,0:T(8,128)S(1)} %get-tuple-element.45), channel_id=1, source_target_pairs={{4,8},{8,4},{12,16},{16,12},{20,24},{24,20},{5,9},{9,5},{13,17},{1... | collective-permute-start | bytes 294920 | tf_op jit(solution)/shard_map/ppermute | solution.py:787
  1.9 4.6 %collective-permute-start = (f32[192,128]{1,0:T(8,128)S(1)}, f32[192,128]{1,0:T(8,128)S(1)}, u32[]{:S(2)}, u32[]{:S(2)}) collective-permute-start(f32[192,128]{1,0:T(8,128)S(1)} %get-tuple-element.46), channel_id=1, source_target_pairs={{0,4},{4,0},{8,12},{12,8},{16,20},{20,16},{24,28},{28,24},{1,5},{5... | collective-permute-start | bytes 294920 | tf_op jit(solution)/shard_map/ppermute | solution.py:786
  6.5 0.0 collective-permute-done.1
  6.5 4.1 %collective-permute-done = f32[192,128]{1,0:T(8,128)S(1)} collective-permute-done((f32[192,128]{1,0:T(8,128)S(1)}, f32[192,128]{1,0:T(8,128)S(1)}, u32[]{:S(2)}, u32[]{:S(2)}) %collective-permute-start) | collective-permute-done | bytes 98336 | tf_op jit(solution)/shard_map/ppermute | solution.py:786
  10.7 0.1 shard_map.57
  10.8 3.6 %collective-permute-start.3 = (f32[232,128]{1,0:T(8,128)S(1)}, f32[232,128]{1,0:T(8,128)S(1)}, u32[]{:S(2)}, u32[]{:S(2)}) collective-permute-start(f32[232,128]{1,0:T(8,128)S(1)} %get-tuple-element.41), channel_id=1, source_target_pairs={{1,2},{2,1},{5,6},{6,5},{9,10},{10,9},{13,14},{14,13},{17,18},{18,... | collective-permute-start | bytes 356360 | tf_op jit(solution)/shard_map/ppermute | solution.py:787
  14.4 0.1 collective-permute-start.2
  14.4 0.8 %shard_map.56 = (f32[3,8,8,128]{3,2,1,0:T(8,128)S(1)}, f32[16,128]{1,0:T(8,128)S(1)}) custom-call(f32[5,16,16,128]{3,2,1,0:T(8,128)S(1)} %get-tuple-element.21.own), custom_call_target="tpu_custom_call" | custom-call | tf_op jit(solution)/shard_map/pallas_call | solution.py:758
  15.3 1.7 %collective-permute-done.3 = f32[232,128]{1,0:T(8,128)S(1)} collective-permute-done((f32[232,128]{1,0:T(8,128)S(1)}, f32[232,128]{1,0:T(8,128)S(1)}, u32[]{:S(2)}, u32[]{:S(2)}) %collective-permute-start.3) | collective-permute-done | bytes 118816 | tf_op jit(solution)/shard_map/ppermute | solution.py:787
  16.9 0.0 collective-permute-done.2
  17.0 2.0 %shard_map.58 = (f32[8,22,32,128]{3,2,1,0:T(8,128)S(1)}, f32[2,8,8,128]{3,2,1,0:T(8,128)S(1)}, f32[24,128]{1,0:T(8,128)S(1)}, f32[96,128]{1,0:T(8,128)S(1)}, f32[96,128]{1,0:T(8,128)S(1)}) custom-call(f32[5,16,16,128]{3,2,1,0:T(8,128)S(1)} %get-tuple-element.21.own, f32[3,8,8,128]{3,2,1,0:T(8,128)S(1)} %get-tuple-element.22.faces, ...), custom_call_target="tpu_custom_call" | custom-call | tf_op jit(solution)/shard_map/pallas_call | solution.py:758
  19.0 2.3 %collective-permute-start.4 = (f32[24,128]{1,0:T(8,128)S(1)}, f32[24,128]{1,0:T(8,128)S(1)}, u32[]{:S(2)}, u32[]{:S(2)}) collective-permute-start(f32[24,128]{1,0:T(8,128)S(1)} %get-tuple-element.28.refs_0_), channel_id=1, source_target_pairs={{0,8},{4,12},{8,0},{12,4},{16,24},{20,28},{24,16},{28,20},{1,9},{5... | collective-permute-start | bytes 36872 | tf_op jit(solution)/shard_map/ppermute | solution.py:794
  21.3 1.1 %collective-permute-done.4._.refs_1_ = f32[24,128]{1,0:T(8,128)S(1)} collective-permute-done((f32[24,128]{1,0:T(8,128)S(1)}, f32[24,128]{1,0:T(8,128)S(1)}, u32[]{:S(2)}, u32[]{:S(2)}) %collective-permute-start.4) | collective-permute-done | bytes 12320 | tf_op jit(solution)/shard_map/ppermute | solution.py:794
  22.4 0.7 %collective-permute-start.8 = (f32[96,128]{1,0:T(8,128)S(1)}, f32[96,128]{1,0:T(8,128)S(1)}, u32[]{:S(2)}, u32[]{:S(2)}) collective-permute-start(f32[96,128]{1,0:T(8,128)S(1)} %get-tuple-element.51), channel_id=1, source_target_pairs={{4,8},{8,4},{12,16},{16,12},{20,24},{24,20},{5,9},{9,5},{13,17},{1... | collective-permute-start | bytes 147464 | tf_op jit(solution)/shard_map/ppermute | solution.py:787
  23.1 4.0 %collective-permute-start.7 = (f32[96,128]{1,0:T(8,128)S(1)}, f32[96,128]{1,0:T(8,128)S(1)}, u32[]{:S(2)}, u32[]{:S(2)}) collective-permute-start(f32[96,128]{1,0:T(8,128)S(1)} %get-tuple-element.52), channel_id=1, source_target_pairs={{0,4},{4,0},{8,12},{12,8},{16,20},{20,16},{24,28},{28,24},{1,5},{5... | collective-permute-start | bytes 147464 | tf_op jit(solution)/shard_map/ppermute | solution.py:786
  27.0 2.0 %collective-permute-start.6 = (f32[24,128]{1,0:T(8,128)S(1)}, f32[24,128]{1,0:T(8,128)S(1)}, u32[]{:S(2)}, u32[]{:S(2)}) collective-permute-start(f32[24,128]{1,0:T(8,128)S(1)} %get-tuple-element.28.refs_0_), channel_id=1, source_target_pairs={{0,24},{4,28},{8,16},{12,20},{16,8},{20,12},{24,0},{28,4},{1,25},{... | collective-permute-start | bytes 36872 | tf_op jit(solution)/shard_map/ppermute | solution.py:794
  29.1 0.5 collective-permute-start.5
  29.5 0.0 collective-permute-done.8
  29.5 0.0 collective-permute-done.7
  29.5 1.8 %collective-permute-done.6.refs_3_ = f32[24,128]{1,0:T(8,128)S(1)} collective-permute-done((f32[24,128]{1,0:T(8,128)S(1)}, f32[24,128]{1,0:T(8,128)S(1)}, u32[]{:S(2)}, u32[]{:S(2)}) %collective-permute-start.6) | collective-permute-done | bytes 12320 | tf_op jit(solution)/shard_map/ppermute | solution.py:794
  31.4 1.4 %collective-permute-done.5.refs_2_ = f32[24,128]{1,0:T(8,128)S(1)} collective-permute-done((f32[24,128]{1,0:T(8,128)S(1)}, f32[24,128]{1,0:T(8,128)S(1)}, u32[]{:S(2)}, u32[]{:S(2)}) %collective-permute-start.5) | collective-permute-done | bytes 12320 | tf_op jit(solution)/shard_map/ppermute | solution.py:794
  32.8 0.0 collective-permute-start.11
  32.8 1.2 %collective-permute-start.10 = (f32[96,128]{1,0:T(8,128)S(1)}, f32[96,128]{1,0:T(8,128)S(1)}, u32[]{:S(2)}, u32[]{:S(2)}) collective-permute-start(f32[96,128]{1,0:T(8,128)S(1)} %bitcast.4), channel_id=1, source_target_pairs={{0,4},{1,5},{2,6},{3,7},{4,0},{5,1},{6,2},{7,3},{8,12},{9,13},{10,... | collective-permute-start | bytes 147464 | tf_op jit(solution)/shard_map/ppermute | solution.py:808
  34.0 1.5 %collective-permute-start.9 = (f32[96,128]{1,0:T(8,128)S(1)}, f32[96,128]{1,0:T(8,128)S(1)}, u32[]{:S(2)}, u32[]{:S(2)}) collective-permute-start(f32[96,128]{1,0:T(8,128)S(1)} %bitcast.5), channel_id=1, source_target_pairs={{0,2},{1,3},{2,0},{3,1},{4,6},{5,7},{6,4},{7,5},{8,10},{9,11},{10,... | collective-permute-start | bytes 147464 | tf_op jit(solution)/shard_map/ppermute | solution.py:808
  35.4 0.1 shard_map.61
  35.6 1.6 %collective-permute-done.9 = f32[96,128]{1,0:T(8,128)S(1)} collective-permute-done((f32[96,128]{1,0:T(8,128)S(1)}, f32[96,128]{1,0:T(8,128)S(1)}, u32[]{:S(2)}, u32[]{:S(2)}) %collective-permute-start.9) | collective-permute-done | bytes 49184 | tf_op jit(solution)/shard_map/ppermute | solution.py:808
  37.2 0.0 collective-permute-done.10
  37.2 0.0 collective-permute-done.11
  37.2 5.9 %collective-permute-start.12 = (f32[552,128]{1,0:T(8,128)S(1)}, f32[552,128]{1,0:T(8,128)S(1)}, u32[]{:S(2)}, u32[]{:S(2)}) collective-permute-start(f32[552,128]{1,0:T(8,128)S(1)} %get-tuple-element.48), channel_id=1, source_target_pairs={{0,1},{1,0},{2,3},{3,2},{4,5},{5,4},{6,7},{7,6},{8,9},{9,8},{10,11... | collective-permute-start | bytes 847880 | tf_op jit(solution)/shard_map/ppermute | solution.py:857
  43.1 2.1 %collective-permute-start.13 = (f32[168,128]{1,0:T(8,128)S(1)}, f32[168,128]{1,0:T(8,128)S(1)}, u32[]{:S(2)}, u32[]{:S(2)}) collective-permute-start(f32[168,128]{1,0:T(8,128)S(1)} %get-tuple-element.47), channel_id=1, source_target_pairs={{1,2},{2,1},{5,6},{6,5},{9,10},{10,9},{13,14},{14,13},{17,18},{18,... | collective-permute-start | bytes 258056 | tf_op jit(solution)/shard_map/ppermute | solution.py:856
  45.2 0.0 collective-permute-done.12
  45.3 3.3 %shard_map.62.coarse = f32[12,32,128]{2,1,0:T(8,128)S(1)} custom-call(f32[2,4,4,24,128]{4,3,2,1,0:T(8,128)S(1)} %pad_maximum_fusion.pieces), custom_call_target="tpu_custom_call" | custom-call | tf_op jit(solution)/shard_map/pallas_call | solution.py:758
  48.5 0.3 collective-permute-done.13
  48.9 1.7 %shard_map.63 = f32[16,16,128]{2,1,0:T(8,128)} custom-call(f32[12,32,128]{2,1,0:T(8,128)S(1)} %shard_map.62.coarse, f32[8,22,32,128]{3,2,1,0:T(8,128)S(1)} %get-tuple-element.33.top, f32[2,8,8,128]{3,2,1,0:T(8,128)S(1)} %get-tuple-element.34.kept, f32[3,8,8,128]{3,2,1,0:T(8,128)S(1)} %get-tuple-element.22.faces, ...), custom_call_target="tpu_custom_call" | custom-call | tf_op jit(solution)/shard_map/pallas_call | solution.py:871
  (17 shorter events, 0.2 us)
Async XLA Ops:
  1.2 5.3 %collective-permute-start.1 = (f32[192,128]{1,0:T(8,128)S(1)}, f32[192,128]{1,0:T(8,128)S(1)}, u32[]{:S(2)}, u32[]{:S(2)}) collective-permute-start(f32[192,128]{1,0:T(8,128)S(1)} %get-tuple-element.45), channel_id=1, source_target_pairs={{4,8},{8,4},{12,16},{16,12},{20,24},{24,20},{5,9},{9,5},{13,17},{1... | collective-permute-start | bytes 294920 | tf_op jit(solution)/shard_map/ppermute | solution.py:787
  1.9 8.7 %collective-permute-start = (f32[192,128]{1,0:T(8,128)S(1)}, f32[192,128]{1,0:T(8,128)S(1)}, u32[]{:S(2)}, u32[]{:S(2)}) collective-permute-start(f32[192,128]{1,0:T(8,128)S(1)} %get-tuple-element.46), channel_id=1, source_target_pairs={{0,4},{4,0},{8,12},{12,8},{16,20},{20,16},{24,28},{28,24},{1,5},{5... | collective-permute-start | bytes 294920 | tf_op jit(solution)/shard_map/ppermute | solution.py:786
  10.8 6.2 %collective-permute-start.3 = (f32[232,128]{1,0:T(8,128)S(1)}, f32[232,128]{1,0:T(8,128)S(1)}, u32[]{:S(2)}, u32[]{:S(2)}) collective-permute-start(f32[232,128]{1,0:T(8,128)S(1)} %get-tuple-element.41), channel_id=1, source_target_pairs={{1,2},{2,1},{5,6},{6,5},{9,10},{10,9},{13,14},{14,13},{17,18},{18,... | collective-permute-start | bytes 356360 | tf_op jit(solution)/shard_map/ppermute | solution.py:787
  14.4 2.6 %collective-permute-start.2 = (f32[232,128]{1,0:T(8,128)S(1)}, f32[232,128]{1,0:T(8,128)S(1)}, u32[]{:S(2)}, u32[]{:S(2)}) collective-permute-start(f32[232,128]{1,0:T(8,128)S(1)} %get-tuple-element.42), channel_id=1, source_target_pairs={{0,1},{1,0},{2,3},{3,2},{4,5},{5,4},{6,7},{7,6},{8,9},{9,8},{10,11... | collective-permute-start | bytes 356360 | tf_op jit(solution)/shard_map/ppermute | solution.py:786
  19.0 3.4 %collective-permute-start.4 = (f32[24,128]{1,0:T(8,128)S(1)}, f32[24,128]{1,0:T(8,128)S(1)}, u32[]{:S(2)}, u32[]{:S(2)}) collective-permute-start(f32[24,128]{1,0:T(8,128)S(1)} %get-tuple-element.28.refs_0_), channel_id=1, source_target_pairs={{0,8},{4,12},{8,0},{12,4},{16,24},{20,28},{24,16},{28,20},{1,9},{5... | collective-permute-start | bytes 36872 | tf_op jit(solution)/shard_map/ppermute | solution.py:794
  22.4 7.1 %collective-permute-start.8 = (f32[96,128]{1,0:T(8,128)S(1)}, f32[96,128]{1,0:T(8,128)S(1)}, u32[]{:S(2)}, u32[]{:S(2)}) collective-permute-start(f32[96,128]{1,0:T(8,128)S(1)} %get-tuple-element.51), channel_id=1, source_target_pairs={{4,8},{8,4},{12,16},{16,12},{20,24},{24,20},{5,9},{9,5},{13,17},{1... | collective-permute-start | bytes 147464 | tf_op jit(solution)/shard_map/ppermute | solution.py:787
  23.1 6.5 %collective-permute-start.7 = (f32[96,128]{1,0:T(8,128)S(1)}, f32[96,128]{1,0:T(8,128)S(1)}, u32[]{:S(2)}, u32[]{:S(2)}) collective-permute-start(f32[96,128]{1,0:T(8,128)S(1)} %get-tuple-element.52), channel_id=1, source_target_pairs={{0,4},{4,0},{8,12},{12,8},{16,20},{20,16},{24,28},{28,24},{1,5},{5... | collective-permute-start | bytes 147464 | tf_op jit(solution)/shard_map/ppermute | solution.py:786
  27.0 4.3 %collective-permute-start.6 = (f32[24,128]{1,0:T(8,128)S(1)}, f32[24,128]{1,0:T(8,128)S(1)}, u32[]{:S(2)}, u32[]{:S(2)}) collective-permute-start(f32[24,128]{1,0:T(8,128)S(1)} %get-tuple-element.28.refs_0_), channel_id=1, source_target_pairs={{0,24},{4,28},{8,16},{12,20},{16,8},{20,12},{24,0},{28,4},{1,25},{... | collective-permute-start | bytes 36872 | tf_op jit(solution)/shard_map/ppermute | solution.py:794
  29.1 3.7 %collective-permute-start.5 = (f32[24,128]{1,0:T(8,128)S(1)}, f32[24,128]{1,0:T(8,128)S(1)}, u32[]{:S(2)}, u32[]{:S(2)}) collective-permute-start(f32[24,128]{1,0:T(8,128)S(1)} %get-tuple-element.28.refs_0_), channel_id=1, source_target_pairs={{0,16},{4,20},{8,24},{12,28},{16,0},{20,4},{24,8},{28,12},{1,17},{... | collective-permute-start | bytes 36872 | tf_op jit(solution)/shard_map/ppermute | solution.py:794
  32.8 4.4 %collective-permute-start.11 = (f32[96,128]{1,0:T(8,128)S(1)}, f32[96,128]{1,0:T(8,128)S(1)}, u32[]{:S(2)}, u32[]{:S(2)}) collective-permute-start(f32[96,128]{1,0:T(8,128)S(1)} %bitcast.3), channel_id=1, source_target_pairs={{0,6},{1,7},{2,4},{3,5},{4,2},{5,3},{6,0},{7,1},{8,14},{9,15},{10,... | collective-permute-start | bytes 147464 | tf_op jit(solution)/shard_map/ppermute | solution.py:808
  32.8 4.4 %collective-permute-start.10 = (f32[96,128]{1,0:T(8,128)S(1)}, f32[96,128]{1,0:T(8,128)S(1)}, u32[]{:S(2)}, u32[]{:S(2)}) collective-permute-start(f32[96,128]{1,0:T(8,128)S(1)} %bitcast.4), channel_id=1, source_target_pairs={{0,4},{1,5},{2,6},{3,7},{4,0},{5,1},{6,2},{7,3},{8,12},{9,13},{10,... | collective-permute-start | bytes 147464 | tf_op jit(solution)/shard_map/ppermute | solution.py:808
  34.0 3.2 %collective-permute-start.9 = (f32[96,128]{1,0:T(8,128)S(1)}, f32[96,128]{1,0:T(8,128)S(1)}, u32[]{:S(2)}, u32[]{:S(2)}) collective-permute-start(f32[96,128]{1,0:T(8,128)S(1)} %bitcast.5), channel_id=1, source_target_pairs={{0,2},{1,3},{2,0},{3,1},{4,6},{5,7},{6,4},{7,5},{8,10},{9,11},{10,... | collective-permute-start | bytes 147464 | tf_op jit(solution)/shard_map/ppermute | solution.py:808
  37.2 8.0 %collective-permute-start.12 = (f32[552,128]{1,0:T(8,128)S(1)}, f32[552,128]{1,0:T(8,128)S(1)}, u32[]{:S(2)}, u32[]{:S(2)}) collective-permute-start(f32[552,128]{1,0:T(8,128)S(1)} %get-tuple-element.48), channel_id=1, source_target_pairs={{0,1},{1,0},{2,3},{3,2},{4,5},{5,4},{6,7},{7,6},{8,9},{9,8},{10,11... | collective-permute-start | bytes 847880 | tf_op jit(solution)/shard_map/ppermute | solution.py:857
  43.1 5.8 %collective-permute-start.13 = (f32[168,128]{1,0:T(8,128)S(1)}, f32[168,128]{1,0:T(8,128)S(1)}, u32[]{:S(2)}, u32[]{:S(2)}) collective-permute-start(f32[168,128]{1,0:T(8,128)S(1)} %get-tuple-element.47), channel_id=1, source_target_pairs={{1,2},{2,1},{5,6},{6,5},{9,10},{10,9},{13,14},{14,13},{17,18},{18,... | collective-permute-start | bytes 258056 | tf_op jit(solution)/shard_map/ppermute | solution.py:856

commit v15 on v11

--- a/solution.py
+++ b/solution.py
@@ -376,6 +376,10 @@
     rest_of = [pieces[5 + i // 2][i % 2 * quarter_rows :][:quarter_rows] for i in range(4)]
     chunk[coarse_rows : coarse_rows + quarter_rows] = 0.5 * fold_four(rest_of)
     chunk[coarse_rows + quarter_rows :] = coefficients[:BLOCK_ROWS - coarse_rows - quarter_rows]
+    block = me_x // (lax.axis_size(axes[0]) // 4)
+    values = chunk[...]
+    for turn in range(1, 4):
+        chunk[...] = jnp.where(block == turn, roll_lanes(values, turn * (LANES // 4)), chunk[...])
 
 
 def pack_v(top, kept, faces, x_low, x_high, low, high):
@@ -559,25 +563,34 @@
 
     for ref in (wide, tall):
         ref[...] = jnp.zeros(ref.shape, F32)
+    per_block = count // own_x
+
+    def merged(values, shift, turn):
+        at = lanes_of(values[0].shape) // quarter
+        out = values[0]
+        for block in range(1, blocks):
+            out = jnp.where(at == (shift + block) % blocks, values[block], out)
+        return roll_lanes(out, (turn - shift) * quarter)
+
     lane = lanes_of((window, LANES))
     for gy in range(devices_y):
         sums = [None] * count
-        for gx in range(devices_x):
-            where = piece(gx, gy)
-            first = pieces[where + (pl.ds(0, window),)]
-            second = pieces[where + (pl.ds(window, window // 2),)]
+        for turn in range(per_block):
+            where = [piece(block * per_block + turn, gy) for block in range(blocks)]
+            first = [pieces[at + (pl.ds(0, window),)] for at in where]
+            second = [pieces[at + (pl.ds(window, window // 2),)] for at in where]
             for local in range(1, 2 * blocks - 1):
-                x = own_x * gx - reach + local
-                if not 0 <= x < devices_x * own_x:
-                    continue
-                block, slab = x // count, x % count
+                offset = own_x * turn - reach + local
+                over, slab = offset // count, offset % count
                 if local <= blocks:
-                    moved = roll_lanes(first, (block - local + 1) * quarter)
+                    moved = merged(first, local - 1, over)
                 else:
                     at = 2 * (local - blocks - 1)
-                    halves = [roll_lanes(second, (block - at - odd) * quarter) for odd in range(2)]
-                    moved = jnp.concatenate(halves)
-                moved = jnp.where(lane // quarter == block, moved, 0.0)
+                    moved = jnp.concatenate([merged(second, at + odd, over) for odd in range(2)])
+                if over < 0:
+                    moved = jnp.where(lane // quarter == blocks - 1, 0.0, moved)
+                elif over > 0:
+                    moved = jnp.where(lane // quarter == 0, 0.0, moved)
                 sums[slab] = moved if sums[slab] is None else sums[slab] + moved
         place = pl.ds(PAD + own_y * gy - reach, window)
         for slab in range(count):
@@ -593,15 +606,10 @@
                 wide[face, gx, gy * own_y : (gy + 1) * own_y] = values
     faces = []
     for face in range(3):
-        slabs = [None] * count
-        for gx in range(devices_x):
-            values = wide[face, gx]
-            for local in range(own_x):
-                x = own_x * gx + local
-                block, slab = x // count, x % count
-                moved = roll_lanes(values, (block - local) * quarter)
-                moved = jnp.where(lane // quarter == block, moved, 0.0)
-                slabs[slab] = moved if slabs[slab] is None else slabs[slab] + moved
+        slabs = []
+        for turn in range(per_block):
+            values = [wide[face, block * per_block + turn] for block in range(blocks)]
+            slabs += [merged(values, local, 0) for local in range(own_x)]
         faces.append(slabs)
     levels = [Listed(*faces, 1, quarter)]
     while len(levels) < LEVELS - 2:

time: 47.2 us -> 47.3 us (level)
  no operation moved by 1% of the time
where the time goes in v15:
time: 47.3 us; the launch traced here: 47.1 us
  starting transfers between devices  27.3 us (58%)
  waiting for transfers between devices  10.3 us (22%)
  Pallas kernels  9.14 us (19%)
    ppermute x3, starting transfers between devices, from_sides(): pair = lax.ppermute(pair, axis, pair_route(axis))  9.47 us
    pallas_call x7, Pallas kernels, launch(): pl.pallas_call(kernel, out_shape=[pltpu.VMEM(shape, F32) for shape in out...  7.4 us
    ppermute x3, starting transfers between devices, from_sides(): swap = lax.ppermute(swap, axis, swap_route(axis))  4.89 us
    ppermute x1, starting transfers between devices, fused_cycle(): other = lax.ppermute(message, 'gy', pair_route('gy'))  4.7 us
    ppermute x3, waiting for transfers between devices, from_sides(): pair = lax.ppermute(pair, axis, pair_route(axis))  4.13 us
    ppermute x3, starting transfers between devices, passed_round(): lax.ppermute(block, axis, [(i, i ^ distance) for i in range(count)])  3.55 us
    ppermute x3, starting transfers between devices, passed_across(): blocks.append(lax.ppermute(block, ('gx', 'gy'), route) if moved else block)  2.71 us
    ppermute x3, waiting for transfers between devices, passed_round(): lax.ppermute(block, axis, [(i, i ^ distance) for i in range(count)])  2.27 us
  transfers between devices with their start and end apart: 14, of which 6 were waited for; matrix products, arithmetic and copies ran while one was open for 0% of the time, Pallas kernels for 9%

profile of v15, /device:TPU:1, one launch (start us, length us, event | category | flops | bytes accessed | tf_op | source)
XLA Modules:
  0.0 47.1 jit_solution(17321228220308168536)
XLA Ops:
  0.0 1.2 %shard_map.55 = (f32[5,16,16,128]{3,2,1,0:T(8,128)S(1)}, f32[192,128]{1,0:T(8,128)S(1)}, f32[192,128]{1,0:T(8,128)S(1)}) custom-call(f32[16,16,128]{2,1,0:T(8,128)} %refs_0_.1, f32[16,16,128]{2,1,0:T(8,128)} %refs_1_.1, f32[16,16,128]{2,1,0:T(8,128)} %refs_2_.1, f32[16,16,128]{2,1,0:T(8,128)} %refs_3_.1, f32[16,16,128]{2,1,0:T(8,128)} %refs_4_.1), custom_call_target="tpu_custom_call" | custom-call | tf_op jit(solution)/shard_map/pallas_call | solution.py:761
  1.2 0.7 %collective-permute-start.1 = (f32[192,128]{1,0:T(8,128)S(1)}, f32[192,128]{1,0:T(8,128)S(1)}, u32[]{:S(2)}, u32[]{:S(2)}) collective-permute-start(f32[192,128]{1,0:T(8,128)S(1)} %get-tuple-element.41), channel_id=1, source_target_pairs={{4,8},{8,4},{12,16},{16,12},{20,24},{24,20},{5,9},{9,5},{13,17},{1... | collective-permute-start | bytes 294920 | tf_op jit(solution)/shard_map/ppermute | solution.py:790
  1.9 4.6 %collective-permute-start = (f32[192,128]{1,0:T(8,128)S(1)}, f32[192,128]{1,0:T(8,128)S(1)}, u32[]{:S(2)}, u32[]{:S(2)}) collective-permute-start(f32[192,128]{1,0:T(8,128)S(1)} %get-tuple-element.42), channel_id=1, source_target_pairs={{0,4},{4,0},{8,12},{12,8},{16,20},{20,16},{24,28},{28,24},{1,5},{5... | collective-permute-start | bytes 294920 | tf_op jit(solution)/shard_map/ppermute | solution.py:789
  6.5 0.0 collective-permute-done.1
  6.5 4.1 %collective-permute-done = f32[192,128]{1,0:T(8,128)S(1)} collective-permute-done((f32[192,128]{1,0:T(8,128)S(1)}, f32[192,128]{1,0:T(8,128)S(1)}, u32[]{:S(2)}, u32[]{:S(2)}) %collective-permute-start) | collective-permute-done | bytes 98336 | tf_op jit(solution)/shard_map/ppermute | solution.py:789
  10.7 0.1 shard_map.57
  10.8 3.6 %collective-permute-start.3 = (f32[232,128]{1,0:T(8,128)S(1)}, f32[232,128]{1,0:T(8,128)S(1)}, u32[]{:S(2)}, u32[]{:S(2)}) collective-permute-start(f32[232,128]{1,0:T(8,128)S(1)} %get-tuple-element.37), channel_id=1, source_target_pairs={{1,2},{2,1},{5,6},{6,5},{9,10},{10,9},{13,14},{14,13},{17,18},{18,... | collective-permute-start | bytes 356360 | tf_op jit(solution)/shard_map/ppermute | solution.py:790
  14.4 0.1 collective-permute-start.2
  14.4 0.8 %shard_map.56 = (f32[3,8,8,128]{3,2,1,0:T(8,128)S(1)}, f32[16,128]{1,0:T(8,128)S(1)}) custom-call(f32[5,16,16,128]{3,2,1,0:T(8,128)S(1)} %get-tuple-element.19.own), custom_call_target="tpu_custom_call" | custom-call | tf_op jit(solution)/shard_map/pallas_call | solution.py:761
  15.3 1.7 %collective-permute-done.3 = f32[232,128]{1,0:T(8,128)S(1)} collective-permute-done((f32[232,128]{1,0:T(8,128)S(1)}, f32[232,128]{1,0:T(8,128)S(1)}, u32[]{:S(2)}, u32[]{:S(2)}) %collective-permute-start.3) | collective-permute-done | bytes 118816 | tf_op jit(solution)/shard_map/ppermute | solution.py:790
  16.9 0.0 collective-permute-done.2
  17.0 2.1 %shard_map.58 = (f32[8,22,32,128]{3,2,1,0:T(8,128)S(1)}, f32[2,8,8,128]{3,2,1,0:T(8,128)S(1)}, f32[24,128]{1,0:T(8,128)S(1)}, f32[96,128]{1,0:T(8,128)S(1)}, f32[96,128]{1,0:T(8,128)S(1)}) custom-call(f32[5,16,16,128]{3,2,1,0:T(8,128)S(1)} %get-tuple-element.19.own, f32[3,8,8,128]{3,2,1,0:T(8,128)S(1)} %get-tuple-element.20.faces, ...), custom_call_target="tpu_custom_call" | custom-call | tf_op jit(solution)/shard_map/pallas_call | solution.py:761
  19.1 0.7 %collective-permute-start.8 = (f32[96,128]{1,0:T(8,128)S(1)}, f32[96,128]{1,0:T(8,128)S(1)}, u32[]{:S(2)}, u32[]{:S(2)}) collective-permute-start(f32[96,128]{1,0:T(8,128)S(1)} %get-tuple-element.47), channel_id=1, source_target_pairs={{4,8},{8,4},{12,16},{16,12},{20,24},{24,20},{5,9},{9,5},{13,17},{1... | collective-permute-start | bytes 147464 | tf_op jit(solution)/shard_map/ppermute | solution.py:790
  19.8 4.8 %collective-permute-start.7 = (f32[96,128]{1,0:T(8,128)S(1)}, f32[96,128]{1,0:T(8,128)S(1)}, u32[]{:S(2)}, u32[]{:S(2)}) collective-permute-start(f32[96,128]{1,0:T(8,128)S(1)} %get-tuple-element.48), channel_id=1, source_target_pairs={{0,4},{4,0},{8,12},{12,8},{16,20},{20,16},{24,28},{28,24},{1,5},{5... | collective-permute-start | bytes 147464 | tf_op jit(solution)/shard_map/ppermute | solution.py:789
  24.5 2.0 %collective-permute-start.6 = (f32[24,128]{1,0:T(8,128)S(1)}, f32[24,128]{1,0:T(8,128)S(1)}, u32[]{:S(2)}, u32[]{:S(2)}) collective-permute-start(f32[24,128]{1,0:T(8,128)S(1)} %get-tuple-element.26.refs_0_), channel_id=1, source_target_pairs={{0,24},{4,28},{8,16},{12,20},{16,8},{20,12},{24,0},{28,4},{1,25},{... | collective-permute-start | bytes 36872 | tf_op jit(solution)/shard_map/ppermute | solution.py:797
  26.6 0.5 collective-permute-start.5
  27.0 1.1 %collective-permute-start.4 = (f32[24,128]{1,0:T(8,128)S(1)}, f32[24,128]{1,0:T(8,128)S(1)}, u32[]{:S(2)}, u32[]{:S(2)}) collective-permute-start(f32[24,128]{1,0:T(8,128)S(1)} %get-tuple-element.26.refs_0_), channel_id=1, source_target_pairs={{0,8},{4,12},{8,0},{12,4},{16,24},{20,28},{24,16},{28,20},{1,9},{5... | collective-permute-start | bytes 36872 | tf_op jit(solution)/shard_map/ppermute | solution.py:797
  28.1 0.0 collective-permute-done.8
  28.1 0.0 collective-permute-done.7
  28.1 1.1 %collective-permute-done.6.refs_3_ = f32[24,128]{1,0:T(8,128)S(1)} collective-permute-done((f32[24,128]{1,0:T(8,128)S(1)}, f32[24,128]{1,0:T(8,128)S(1)}, u32[]{:S(2)}, u32[]{:S(2)}) %collective-permute-start.6) | collective-permute-done | bytes 12320 | tf_op jit(solution)/shard_map/ppermute | solution.py:797
  29.3 1.1 %collective-permute-done.5.refs_2_ = f32[24,128]{1,0:T(8,128)S(1)} collective-permute-done((f32[24,128]{1,0:T(8,128)S(1)}, f32[24,128]{1,0:T(8,128)S(1)}, u32[]{:S(2)}, u32[]{:S(2)}) %collective-permute-start.5) | collective-permute-done | bytes 12320 | tf_op jit(solution)/shard_map/ppermute | solution.py:797
  30.4 0.0 collective-permute-done.4.refs_1_
  30.4 0.1 collective-permute-start.11
  30.5 1.1 %collective-permute-start.10 = (f32[96,128]{1,0:T(8,128)S(1)}, f32[96,128]{1,0:T(8,128)S(1)}, u32[]{:S(2)}, u32[]{:S(2)}) collective-permute-start(f32[96,128]{1,0:T(8,128)S(1)} %bitcast.4), channel_id=1, source_target_pairs={{0,4},{1,5},{2,6},{3,7},{4,0},{5,1},{6,2},{7,3},{8,12},{9,13},{10,... | collective-permute-start | bytes 147464 | tf_op jit(solution)/shard_map/ppermute | solution.py:811
  31.5 1.6 %collective-permute-start.9 = (f32[96,128]{1,0:T(8,128)S(1)}, f32[96,128]{1,0:T(8,128)S(1)}, u32[]{:S(2)}, u32[]{:S(2)}) collective-permute-start(f32[96,128]{1,0:T(8,128)S(1)} %bitcast.5), channel_id=1, source_target_pairs={{0,2},{1,3},{2,0},{3,1},{4,6},{5,7},{6,4},{7,5},{8,10},{9,11},{10,... | collective-permute-start | bytes 147464 | tf_op jit(solution)/shard_map/ppermute | solution.py:811
  33.1 0.1 shard_map.60
  33.2 1.6 %collective-permute-done.9 = f32[96,128]{1,0:T(8,128)S(1)} collective-permute-done((f32[96,128]{1,0:T(8,128)S(1)}, f32[96,128]{1,0:T(8,128)S(1)}, u32[]{:S(2)}, u32[]{:S(2)}) %collective-permute-start.9) | collective-permute-done | bytes 49184 | tf_op jit(solution)/shard_map/ppermute | solution.py:811
  34.8 0.0 collective-permute-done.10
  34.8 0.0 collective-permute-done.11
  34.9 4.7 %collective-permute-start.12 = (f32[552,128]{1,0:T(8,128)S(1)}, f32[552,128]{1,0:T(8,128)S(1)}, u32[]{:S(2)}, u32[]{:S(2)}) collective-permute-start(f32[552,128]{1,0:T(8,128)S(1)} %get-tuple-element.44), channel_id=1, source_target_pairs={{0,1},{1,0},{2,3},{3,2},{4,5},{5,4},{6,7},{7,6},{8,9},{9,8},{10,11... | collective-permute-start | bytes 847880 | tf_op jit(solution)/shard_map/ppermute | solution.py:859
  39.6 2.0 %collective-permute-start.13 = (f32[168,128]{1,0:T(8,128)S(1)}, f32[168,128]{1,0:T(8,128)S(1)}, u32[]{:S(2)}, u32[]{:S(2)}) collective-permute-start(f32[168,128]{1,0:T(8,128)S(1)} %get-tuple-element.43), channel_id=1, source_target_pairs={{1,2},{2,1},{5,6},{6,5},{9,10},{10,9},{13,14},{14,13},{17,18},{18,... | collective-permute-start | bytes 258056 | tf_op jit(solution)/shard_map/ppermute | solution.py:858
  41.6 0.0 collective-permute-done.12
  41.7 3.1 %shard_map.61.coarse = f32[12,32,128]{2,1,0:T(8,128)S(1)} custom-call(f32[2,4,4,24,128]{4,3,2,1,0:T(8,128)S(1)} %pad_maximum_fusion.pieces), custom_call_target="tpu_custom_call" | custom-call | tf_op jit(solution)/shard_map/pallas_call | solution.py:761
  44.8 0.6 %collective-permute-done.13 = f32[168,128]{1,0:T(8,128)S(1)} collective-permute-done((f32[168,128]{1,0:T(8,128)S(1)}, f32[168,128]{1,0:T(8,128)S(1)}, u32[]{:S(2)}, u32[]{:S(2)}) %collective-permute-start.13) | collective-permute-done | bytes 86048 | tf_op jit(solution)/shard_map/ppermute | solution.py:858
  45.4 1.7 %shard_map.62 = f32[16,16,128]{2,1,0:T(8,128)} custom-call(f32[12,32,128]{2,1,0:T(8,128)S(1)} %shard_map.61.coarse, f32[8,22,32,128]{3,2,1,0:T(8,128)S(1)} %get-tuple-element.29.top, f32[2,8,8,128]{3,2,1,0:T(8,128)S(1)} %get-tuple-element.30.kept, f32[3,8,8,128]{3,2,1,0:T(8,128)S(1)} %get-tuple-element.20.faces, ...), custom_call_target="tpu_custom_call" | custom-call | tf_op jit(solution)/shard_map/pallas_call | solution.py:873
  (16 shorter events, 0.2 us)
Async XLA Ops:
  1.2 5.3 %collective-permute-start.1 = (f32[192,128]{1,0:T(8,128)S(1)}, f32[192,128]{1,0:T(8,128)S(1)}, u32[]{:S(2)}, u32[]{:S(2)}) collective-permute-start(f32[192,128]{1,0:T(8,128)S(1)} %get-tuple-element.41), channel_id=1, source_target_pairs={{4,8},{8,4},{12,16},{16,12},{20,24},{24,20},{5,9},{9,5},{13,17},{1... | collective-permute-start | bytes 294920 | tf_op jit(solution)/shard_map/ppermute | solution.py:790
  1.9 8.7 %collective-permute-start = (f32[192,128]{1,0:T(8,128)S(1)}, f32[192,128]{1,0:T(8,128)S(1)}, u32[]{:S(2)}, u32[]{:S(2)}) collective-permute-start(f32[192,128]{1,0:T(8,128)S(1)} %get-tuple-element.42), channel_id=1, source_target_pairs={{0,4},{4,0},{8,12},{12,8},{16,20},{20,16},{24,28},{28,24},{1,5},{5... | collective-permute-start | bytes 294920 | tf_op jit(solution)/shard_map/ppermute | solution.py:789
  10.8 6.2 %collective-permute-start.3 = (f32[232,128]{1,0:T(8,128)S(1)}, f32[232,128]{1,0:T(8,128)S(1)}, u32[]{:S(2)}, u32[]{:S(2)}) collective-permute-start(f32[232,128]{1,0:T(8,128)S(1)} %get-tuple-element.37), channel_id=1, source_target_pairs={{1,2},{2,1},{5,6},{6,5},{9,10},{10,9},{13,14},{14,13},{17,18},{18,... | collective-permute-start | bytes 356360 | tf_op jit(solution)/shard_map/ppermute | solution.py:790
  14.4 2.6 %collective-permute-start.2 = (f32[232,128]{1,0:T(8,128)S(1)}, f32[232,128]{1,0:T(8,128)S(1)}, u32[]{:S(2)}, u32[]{:S(2)}) collective-permute-start(f32[232,128]{1,0:T(8,128)S(1)} %get-tuple-element.38), channel_id=1, source_target_pairs={{0,1},{1,0},{2,3},{3,2},{4,5},{5,4},{6,7},{7,6},{8,9},{9,8},{10,11... | collective-permute-start | bytes 356360 | tf_op jit(solution)/shard_map/ppermute | solution.py:789
  19.1 9.0 %collective-permute-start.8 = (f32[96,128]{1,0:T(8,128)S(1)}, f32[96,128]{1,0:T(8,128)S(1)}, u32[]{:S(2)}, u32[]{:S(2)}) collective-permute-start(f32[96,128]{1,0:T(8,128)S(1)} %get-tuple-element.47), channel_id=1, source_target_pairs={{4,8},{8,4},{12,16},{16,12},{20,24},{24,20},{5,9},{9,5},{13,17},{1... | collective-permute-start | bytes 147464 | tf_op jit(solution)/shard_map/ppermute | solution.py:790
  19.8 8.3 %collective-permute-start.7 = (f32[96,128]{1,0:T(8,128)S(1)}, f32[96,128]{1,0:T(8,128)S(1)}, u32[]{:S(2)}, u32[]{:S(2)}) collective-permute-start(f32[96,128]{1,0:T(8,128)S(1)} %get-tuple-element.48), channel_id=1, source_target_pairs={{0,4},{4,0},{8,12},{12,8},{16,20},{20,16},{24,28},{28,24},{1,5},{5... | collective-permute-start | bytes 147464 | tf_op jit(solution)/shard_map/ppermute | solution.py:789
  24.5 4.7 %collective-permute-start.6 = (f32[24,128]{1,0:T(8,128)S(1)}, f32[24,128]{1,0:T(8,128)S(1)}, u32[]{:S(2)}, u32[]{:S(2)}) collective-permute-start(f32[24,128]{1,0:T(8,128)S(1)} %get-tuple-element.26.refs_0_), channel_id=1, source_target_pairs={{0,24},{4,28},{8,16},{12,20},{16,8},{20,12},{24,0},{28,4},{1,25},{... | collective-permute-start | bytes 36872 | tf_op jit(solution)/shard_map/ppermute | solution.py:797
  26.6 3.8 %collective-permute-start.5 = (f32[24,128]{1,0:T(8,128)S(1)}, f32[24,128]{1,0:T(8,128)S(1)}, u32[]{:S(2)}, u32[]{:S(2)}) collective-permute-start(f32[24,128]{1,0:T(8,128)S(1)} %get-tuple-element.26.refs_0_), channel_id=1, source_target_pairs={{0,16},{4,20},{8,24},{12,28},{16,0},{20,4},{24,8},{28,12},{1,17},{... | collective-permute-start | bytes 36872 | tf_op jit(solution)/shard_map/ppermute | solution.py:797
  27.0 3.4 %collective-permute-start.4 = (f32[24,128]{1,0:T(8,128)S(1)}, f32[24,128]{1,0:T(8,128)S(1)}, u32[]{:S(2)}, u32[]{:S(2)}) collective-permute-start(f32[24,128]{1,0:T(8,128)S(1)} %get-tuple-element.26.refs_0_), channel_id=1, source_target_pairs={{0,8},{4,12},{8,0},{12,4},{16,24},{20,28},{24,16},{28,20},{1,9},{5... | collective-permute-start | bytes 36872 | tf_op jit(solution)/shard_map/ppermute | solution.py:797
  30.4 4.5 %collective-permute-start.11 = (f32[96,128]{1,0:T(8,128)S(1)}, f32[96,128]{1,0:T(8,128)S(1)}, u32[]{:S(2)}, u32[]{:S(2)}) collective-permute-start(f32[96,128]{1,0:T(8,128)S(1)} %bitcast.3), channel_id=1, source_target_pairs={{0,6},{1,7},{2,4},{3,5},{4,2},{5,3},{6,0},{7,1},{8,14},{9,15},{10,... | collective-permute-start | bytes 147464 | tf_op jit(solution)/shard_map/ppermute | solution.py:811
  30.5 4.4 %collective-permute-start.10 = (f32[96,128]{1,0:T(8,128)S(1)}, f32[96,128]{1,0:T(8,128)S(1)}, u32[]{:S(2)}, u32[]{:S(2)}) collective-permute-start(f32[96,128]{1,0:T(8,128)S(1)} %bitcast.4), channel_id=1, source_target_pairs={{0,4},{1,5},{2,6},{3,7},{4,0},{5,1},{6,2},{7,3},{8,12},{9,13},{10,... | collective-permute-start | bytes 147464 | tf_op jit(solution)/shard_map/ppermute | solution.py:811
  31.5 3.3 %collective-permute-start.9 = (f32[96,128]{1,0:T(8,128)S(1)}, f32[96,128]{1,0:T(8,128)S(1)}, u32[]{:S(2)}, u32[]{:S(2)}) collective-permute-start(f32[96,128]{1,0:T(8,128)S(1)} %bitcast.5), channel_id=1, source_target_pairs={{0,2},{1,3},{2,0},{3,1},{4,6},{5,7},{6,4},{7,5},{8,10},{9,11},{10,... | collective-permute-start | bytes 147464 | tf_op jit(solution)/shard_map/ppermute | solution.py:811
  34.9 6.8 %collective-permute-start.12 = (f32[552,128]{1,0:T(8,128)S(1)}, f32[552,128]{1,0:T(8,128)S(1)}, u32[]{:S(2)}, u32[]{:S(2)}) collective-permute-start(f32[552,128]{1,0:T(8,128)S(1)} %get-tuple-element.44), channel_id=1, source_target_pairs={{0,1},{1,0},{2,3},{3,2},{4,5},{5,4},{6,7},{7,6},{8,9},{9,8},{10,11... | collective-permute-start | bytes 847880 | tf_op jit(solution)/shard_map/ppermute | solution.py:859
  39.6 5.8 %collective-permute-start.13 = (f32[168,128]{1,0:T(8,128)S(1)}, f32[168,128]{1,0:T(8,128)S(1)}, u32[]{:S(2)}, u32[]{:S(2)}) collective-permute-start(f32[168,128]{1,0:T(8,128)S(1)} %get-tuple-element.43), channel_id=1, source_target_pairs={{1,2},{2,1},{5,6},{6,5},{9,10},{10,9},{13,14},{14,13},{17,18},{18,... | collective-permute-start | bytes 258056 | tf_op jit(solution)/shard_map/ppermute | solution.py:858

commit v16 on v15

--- a/solution.py
+++ b/solution.py
@@ -423,8 +423,13 @@
 
 
 def stack_blocks(*refs):
-    for index, ref in enumerate(refs[:-3]):
+    for index, ref in enumerate(refs[:-1]):
         refs[-1][index] = ref[...]
+
+
+def hand_on(first, second, _, first_out, second_out):
+    first_out[...] = first[...]
+    second_out[...] = second[...]
 
 
 def pair_rows(values, stride):
@@ -799,17 +804,22 @@
     ]
 
 
-def passed_across(block):
+def passed_across(block, rider):
     count, size = lax.axis_size("gx"), lax.axis_size("gy")
-    blocks = []
+    rows = block.shape[0]
+    blocks = [block]
     for side in range(2):
         for distance in range(0, size, 2):
             route = [
                 (x * size + y, (x ^ side) * size + (y ^ distance)) for x in range(count) for y in range(size)
             ]
-            moved = side + distance > 0
-            blocks.append(lax.ppermute(block, ("gx", "gy"), route) if moved else block)
-    return blocks
+            if side == 1 and distance == 0:
+                both = lax.ppermute(jnp.concatenate((block, rider)), ("gx", "gy"), route)
+                blocks.append(both[:rows])
+                rider = both[rows:]
+            elif distance > 0:
+                blocks.append(lax.ppermute(block, ("gx", "gy"), route))
+    return blocks, rider
 
 
 def fused_cycle(*fields):
@@ -848,10 +858,13 @@
     )(own, faces, coefficients, x_low, x_high, y_low, y_high)
 
     blocks = passed_round(chunk, "gx", 2)
-    v_low, v_high = from_sides(v_low, v_high, "gx")
     slow = (len(blocks),) + chunk.shape
-    (pieces,) = call(stack_blocks, [slow])(*blocks, v_low, v_high)
-    blocks = passed_across(pieces.reshape(-1, LANES))
+    (pieces,) = call(stack_blocks, [slow])(*blocks)
+    v_low, v_high = call(hand_on, [v_shape, v_shape])(v_low, v_high, pieces)
+    pair, swap = by_partner(v_low, v_high, "gx")
+    swap = lax.ppermute(swap, "gx", swap_route("gx"))
+    blocks, pair = passed_across(pieces.reshape(-1, LANES), pair)
+    v_low, v_high = by_partner(pair, swap, "gx")
     w_low, w_high = call(pack_v, [w_shape] * 2)(top, kept, faces, v_low, v_high)
     pair, swap = by_partner(w_low, w_high, "gy")
     message = jnp.concatenate(blocks + [pair])

time: 47.3 us -> 46.6 us (0.985)
  starting transfers between devices: 27.3 us -> 25.5 us
  waiting for transfers between devices: 10.3 us -> 11 us
    ppermute x3 -> x2, starting transfers between devices: 9.47 us -> 4.69 us  [from_sides(): pair = lax.ppermute(pair, axis, pair_route(axis))]
    ppermute x3 -> x4, starting transfers between devices: 2.71 us -> 5.24 us  [the longest x1 3.56 us: passed_across(): both = lax.ppermute(jnp.concatenate((block, rider)), ('gx', 'gy'), route)]
    ppermute x1, starting transfers between devices: 4.7 us -> 3.08 us  [fused_cycle(): other = lax.ppermute(message, 'gy', pair_route('gy'))]
    ppermute x1, starting transfers between devices: 2.03 us -> 3.55 us  [fused_cycle(): swap = lax.ppermute(swap, 'gy', swap_route('gy'))]
    ppermute x3, starting transfers between devices: 3.55 us -> 4.74 us  [passed_round(): lax.ppermute(block, axis, [(i, i ^ distance) for i in range(count)])]
    ppermute x3, waiting for transfers between devices: 2.27 us -> 3.08 us  [passed_round(): lax.ppermute(block, axis, [(i, i ^ distance) for i in range(count)])]
    ppermute x3 -> x2, starting transfers between devices: 4.89 us -> 4.23 us  [from_sides(): swap = lax.ppermute(swap, axis, swap_route(axis))]
    ppermute x1, waiting for transfers between devices: 0.59 us -> 0.01 us  [fused_cycle(): swap = lax.ppermute(swap, 'gy', swap_route('gy'))]
  transfers between devices with their start and end apart: 14 -> 13, of which waited for: 6 -> 5; matrix products, arithmetic and copies ran while one was open for 0% -> 0% of each run, Pallas kernels for 9% -> 9%
where the time goes in v16:
time: 46.6 us; the launch traced here: 46.1 us
  starting transfers between devices  25.5 us (55%)
  waiting for transfers between devices  11 us (24%)
  Pallas kernels  9.15 us (20%)
    pallas_call x8, Pallas kernels, launch(): pl.pallas_call(kernel, out_shape=[pltpu.VMEM(shape, F32) for shape in out...  7.41 us
    ppermute x3, starting transfers between devices, passed_round(): lax.ppermute(block, axis, [(i, i ^ distance) for i in range(count)])  4.74 us
    ppermute x2, starting transfers between devices, from_sides(): pair = lax.ppermute(pair, axis, pair_route(axis))  4.69 us
    ppermute x2, starting transfers between devices, from_sides(): swap = lax.ppermute(swap, axis, swap_route(axis))  4.23 us
    ppermute x2, waiting for transfers between devices, from_sides(): pair = lax.ppermute(pair, axis, pair_route(axis))  4.13 us
    ppermute x1, starting transfers between devices, passed_across(): both = lax.ppermute(jnp.concatenate((block, rider)), ('gx', 'gy'), route)  3.56 us
    ppermute x1, starting transfers between devices, fused_cycle(): swap = lax.ppermute(swap, 'gy', swap_route('gy'))  3.55 us
    ppermute x3, waiting for transfers between devices, passed_round(): lax.ppermute(block, axis, [(i, i ^ distance) for i in range(count)])  3.08 us
  transfers between devices with their start and end apart: 13, of which 5 were waited for; matrix products, arithmetic and copies ran while one was open for 0% of the time, Pallas kernels for 9%

profile of v16, /device:TPU:1, one launch (start us, length us, event | category | flops | bytes accessed | tf_op | source)
XLA Modules:
  0.0 46.1 jit_solution(4301523434435002402)
XLA Ops:
  0.0 1.2 %shard_map.55 = (f32[5,16,16,128]{3,2,1,0:T(8,128)S(1)}, f32[192,128]{1,0:T(8,128)S(1)}, f32[192,128]{1,0:T(8,128)S(1)}) custom-call(f32[16,16,128]{2,1,0:T(8,128)} %refs_0_.1, f32[16,16,128]{2,1,0:T(8,128)} %refs_1_.1, f32[16,16,128]{2,1,0:T(8,128)} %refs_2_.1, f32[16,16,128]{2,1,0:T(8,128)} %refs_3_.1, f32[16,16,128]{2,1,0:T(8,128)} %refs_4_.1), custom_call_target="tpu_custom_call" | custom-call | tf_op jit(solution)/shard_map/pallas_call | solution.py:766
  1.2 0.7 %collective-permute-start.1 = (f32[192,128]{1,0:T(8,128)S(1)}, f32[192,128]{1,0:T(8,128)S(1)}, u32[]{:S(2)}, u32[]{:S(2)}) collective-permute-start(f32[192,128]{1,0:T(8,128)S(1)} %get-tuple-element.45), channel_id=1, source_target_pairs={{4,8},{8,4},{12,16},{16,12},{20,24},{24,20},{5,9},{9,5},{13,17},{1... | collective-permute-start | bytes 294920 | tf_op jit(solution)/shard_map/ppermute | solution.py:795
  1.9 4.6 %collective-permute-start = (f32[192,128]{1,0:T(8,128)S(1)}, f32[192,128]{1,0:T(8,128)S(1)}, u32[]{:S(2)}, u32[]{:S(2)}) collective-permute-start(f32[192,128]{1,0:T(8,128)S(1)} %get-tuple-element.46), channel_id=1, source_target_pairs={{0,4},{4,0},{8,12},{12,8},{16,20},{20,16},{24,28},{28,24},{1,5},{5... | collective-permute-start | bytes 294920 | tf_op jit(solution)/shard_map/ppermute | solution.py:794
  6.5 0.0 collective-permute-done.1
  6.5 4.1 %collective-permute-done = f32[192,128]{1,0:T(8,128)S(1)} collective-permute-done((f32[192,128]{1,0:T(8,128)S(1)}, f32[192,128]{1,0:T(8,128)S(1)}, u32[]{:S(2)}, u32[]{:S(2)}) %collective-permute-start) | collective-permute-done | bytes 98336 | tf_op jit(solution)/shard_map/ppermute | solution.py:794
  10.7 0.1 shard_map.57
  10.8 3.6 %collective-permute-start.3 = (f32[232,128]{1,0:T(8,128)S(1)}, f32[232,128]{1,0:T(8,128)S(1)}, u32[]{:S(2)}, u32[]{:S(2)}) collective-permute-start(f32[232,128]{1,0:T(8,128)S(1)} %get-tuple-element.41), channel_id=1, source_target_pairs={{1,2},{2,1},{5,6},{6,5},{9,10},{10,9},{13,14},{14,13},{17,18},{18,... | collective-permute-start | bytes 356360 | tf_op jit(solution)/shard_map/ppermute | solution.py:795
  14.4 0.1 collective-permute-start.2
  14.4 0.8 %shard_map.56 = (f32[3,8,8,128]{3,2,1,0:T(8,128)S(1)}, f32[16,128]{1,0:T(8,128)S(1)}) custom-call(f32[5,16,16,128]{3,2,1,0:T(8,128)S(1)} %get-tuple-element.21.own), custom_call_target="tpu_custom_call" | custom-call | tf_op jit(solution)/shard_map/pallas_call | solution.py:766
  15.3 1.7 %collective-permute-done.3 = f32[232,128]{1,0:T(8,128)S(1)} collective-permute-done((f32[232,128]{1,0:T(8,128)S(1)}, f32[232,128]{1,0:T(8,128)S(1)}, u32[]{:S(2)}, u32[]{:S(2)}) %collective-permute-start.3) | collective-permute-done | bytes 118816 | tf_op jit(solution)/shard_map/ppermute | solution.py:795
  16.9 0.0 collective-permute-done.2
  17.0 2.1 %shard_map.58 = (f32[8,22,32,128]{3,2,1,0:T(8,128)S(1)}, f32[2,8,8,128]{3,2,1,0:T(8,128)S(1)}, f32[24,128]{1,0:T(8,128)S(1)}, f32[96,128]{1,0:T(8,128)S(1)}, f32[96,128]{1,0:T(8,128)S(1)}) custom-call(f32[5,16,16,128]{3,2,1,0:T(8,128)S(1)} %get-tuple-element.21.own, f32[3,8,8,128]{3,2,1,0:T(8,128)S(1)} %get-tuple-element.22.faces, ...), custom_call_target="tpu_custom_call" | custom-call | tf_op jit(solution)/shard_map/pallas_call | solution.py:766
  19.1 4.4 %collective-permute-start.6 = (f32[24,128]{1,0:T(8,128)S(1)}, f32[24,128]{1,0:T(8,128)S(1)}, u32[]{:S(2)}, u32[]{:S(2)}) collective-permute-start(f32[24,128]{1,0:T(8,128)S(1)} %get-tuple-element.28.refs_0_), channel_id=1, source_target_pairs={{0,24},{4,28},{8,16},{12,20},{16,8},{20,12},{24,0},{28,4},{1,25},{... | collective-permute-start | bytes 36872 | tf_op jit(solution)/shard_map/ppermute | solution.py:802
  23.4 0.0 collective-permute-start.5
  23.4 0.4 collective-permute-start.4
  23.8 0.7 %collective-permute-done.6.refs_3_ = f32[24,128]{1,0:T(8,128)S(1)} collective-permute-done((f32[24,128]{1,0:T(8,128)S(1)}, f32[24,128]{1,0:T(8,128)S(1)}, u32[]{:S(2)}, u32[]{:S(2)}) %collective-permute-start.6) | collective-permute-done | bytes 12320 | tf_op jit(solution)/shard_map/ppermute | solution.py:802
  24.5 2.4 %collective-permute-done.5.refs_2_ = f32[24,128]{1,0:T(8,128)S(1)} collective-permute-done((f32[24,128]{1,0:T(8,128)S(1)}, f32[24,128]{1,0:T(8,128)S(1)}, u32[]{:S(2)}, u32[]{:S(2)}) %collective-permute-start.5) | collective-permute-done | bytes 12320 | tf_op jit(solution)/shard_map/ppermute | solution.py:802
  26.9 0.0 collective-permute-done.4.refs_1_
  26.9 0.1 collective-permute-start.9
  27.0 0.9 %collective-permute-start.7 = (f32[96,128]{1,0:T(8,128)S(1)}, f32[96,128]{1,0:T(8,128)S(1)}, u32[]{:S(2)}, u32[]{:S(2)}) collective-permute-start(f32[96,128]{1,0:T(8,128)S(1)} %bitcast.4), channel_id=1, source_target_pairs={{0,2},{1,3},{2,0},{3,1},{4,6},{5,7},{6,4},{7,5},{8,10},{9,11},{10,... | collective-permute-start | bytes 147464 | tf_op jit(solution)/shard_map/ppermute | solution.py:821
  28.0 0.7 %collective-permute-start.10 = (f32[96,128]{1,0:T(8,128)S(1)}, f32[96,128]{1,0:T(8,128)S(1)}, u32[]{:S(2)}, u32[]{:S(2)}) collective-permute-start(f32[96,128]{1,0:T(8,128)S(1)} %get-tuple-element.55), channel_id=1, source_target_pairs={{4,8},{8,4},{12,16},{16,12},{20,24},{24,20},{5,9},{9,5},{13,17},{1... | collective-permute-start | bytes 147464 | tf_op jit(solution)/shard_map/ppermute | solution.py:865
  28.6 3.6 %collective-permute-start.8 = (f32[192,128]{1,0:T(8,128)S(1)}, f32[192,128]{1,0:T(8,128)S(1)}, u32[]{:S(2)}, u32[]{:S(2)}) collective-permute-start(f32[192,128]{1,0:T(8,128)S(1)} %pad_maximum_fusion.2), channel_id=1, source_target_pairs={{0,4},{1,5},{2,6},{3,7},{4,0},{5,1},{6,2},{7,3},{8,12},{9,13},{10,... | collective-permute-start | bytes 294920 | tf_op jit(solution)/shard_map/ppermute | solution.py:817
  32.2 0.0 collective-permute-done.7
  32.2 0.0 collective-permute-done.10
  32.2 2.1 %collective-permute-done.8 = f32[192,128]{1,0:T(8,128)S(1)} collective-permute-done((f32[192,128]{1,0:T(8,128)S(1)}, f32[192,128]{1,0:T(8,128)S(1)}, u32[]{:S(2)}, u32[]{:S(2)}) %collective-permute-start.8) | collective-permute-done | bytes 98336 | tf_op jit(solution)/shard_map/ppermute | solution.py:817
  34.4 0.1 shard_map.61
  34.5 0.0 collective-permute-done.9
  34.5 3.1 %collective-permute-start.11 = (f32[552,128]{1,0:T(8,128)S(1)}, f32[552,128]{1,0:T(8,128)S(1)}, u32[]{:S(2)}, u32[]{:S(2)}) collective-permute-start(f32[552,128]{1,0:T(8,128)S(1)} %get-tuple-element.48), channel_id=1, source_target_pairs={{0,1},{1,0},{2,3},{3,2},{4,5},{5,4},{6,7},{7,6},{8,9},{9,8},{10,11... | collective-permute-start | bytes 847880 | tf_op jit(solution)/shard_map/ppermute | solution.py:872
  37.6 3.5 %collective-permute-start.12 = (f32[168,128]{1,0:T(8,128)S(1)}, f32[168,128]{1,0:T(8,128)S(1)}, u32[]{:S(2)}, u32[]{:S(2)}) collective-permute-start(f32[168,128]{1,0:T(8,128)S(1)} %get-tuple-element.47), channel_id=1, source_target_pairs={{1,2},{2,1},{5,6},{6,5},{9,10},{10,9},{13,14},{14,13},{17,18},{18,... | collective-permute-start | bytes 258056 | tf_op jit(solution)/shard_map/ppermute | solution.py:871
  41.2 0.0 collective-permute-done.11
  41.3 3.1 %shard_map.62.coarse = f32[12,32,128]{2,1,0:T(8,128)S(1)} custom-call(f32[2,4,4,24,128]{4,3,2,1,0:T(8,128)S(1)} %pad_maximum_fusion.pieces), custom_call_target="tpu_custom_call" | custom-call | tf_op jit(solution)/shard_map/pallas_call | solution.py:766
  44.3 0.0 collective-permute-done.12
  44.4 1.7 %shard_map.63 = f32[16,16,128]{2,1,0:T(8,128)} custom-call(f32[12,32,128]{2,1,0:T(8,128)S(1)} %shard_map.62.coarse, f32[8,22,32,128]{3,2,1,0:T(8,128)S(1)} %get-tuple-element.33.top, f32[2,8,8,128]{3,2,1,0:T(8,128)S(1)} %get-tuple-element.34.kept, f32[3,8,8,128]{3,2,1,0:T(8,128)S(1)} %get-tuple-element.22.faces, f32[96,128]{1,0:T(8,128)S(1)} %get-tuple-element.53.x_low, ...), custom_call_target="tpu_custom_call" | custom-call | tf_op jit(solution)/shard_map/pallas_call | solution.py:886
  (17 shorter events, 0.2 us)
Async XLA Ops:
  1.2 5.3 %collective-permute-start.1 = (f32[192,128]{1,0:T(8,128)S(1)}, f32[192,128]{1,0:T(8,128)S(1)}, u32[]{:S(2)}, u32[]{:S(2)}) collective-permute-start(f32[192,128]{1,0:T(8,128)S(1)} %get-tuple-element.45), channel_id=1, source_target_pairs={{4,8},{8,4},{12,16},{16,12},{20,24},{24,20},{5,9},{9,5},{13,17},{1... | collective-permute-start | bytes 294920 | tf_op jit(solution)/shard_map/ppermute | solution.py:795
  1.9 8.7 %collective-permute-start = (f32[192,128]{1,0:T(8,128)S(1)}, f32[192,128]{1,0:T(8,128)S(1)}, u32[]{:S(2)}, u32[]{:S(2)}) collective-permute-start(f32[192,128]{1,0:T(8,128)S(1)} %get-tuple-element.46), channel_id=1, source_target_pairs={{0,4},{4,0},{8,12},{12,8},{16,20},{20,16},{24,28},{28,24},{1,5},{5... | collective-permute-start | bytes 294920 | tf_op jit(solution)/shard_map/ppermute | solution.py:794
  10.8 6.2 %collective-permute-start.3 = (f32[232,128]{1,0:T(8,128)S(1)}, f32[232,128]{1,0:T(8,128)S(1)}, u32[]{:S(2)}, u32[]{:S(2)}) collective-permute-start(f32[232,128]{1,0:T(8,128)S(1)} %get-tuple-element.41), channel_id=1, source_target_pairs={{1,2},{2,1},{5,6},{6,5},{9,10},{10,9},{13,14},{14,13},{17,18},{18,... | collective-permute-start | bytes 356360 | tf_op jit(solution)/shard_map/ppermute | solution.py:795
  14.4 2.6 %collective-permute-start.2 = (f32[232,128]{1,0:T(8,128)S(1)}, f32[232,128]{1,0:T(8,128)S(1)}, u32[]{:S(2)}, u32[]{:S(2)}) collective-permute-start(f32[232,128]{1,0:T(8,128)S(1)} %get-tuple-element.42), channel_id=1, source_target_pairs={{0,1},{1,0},{2,3},{3,2},{4,5},{5,4},{6,7},{7,6},{8,9},{9,8},{10,11... | collective-permute-start | bytes 356360 | tf_op jit(solution)/shard_map/ppermute | solution.py:794
  19.1 5.5 %collective-permute-start.6 = (f32[24,128]{1,0:T(8,128)S(1)}, f32[24,128]{1,0:T(8,128)S(1)}, u32[]{:S(2)}, u32[]{:S(2)}) collective-permute-start(f32[24,128]{1,0:T(8,128)S(1)} %get-tuple-element.28.refs_0_), channel_id=1, source_target_pairs={{0,24},{4,28},{8,16},{12,20},{16,8},{20,12},{24,0},{28,4},{1,25},{... | collective-permute-start | bytes 36872 | tf_op jit(solution)/shard_map/ppermute | solution.py:802
  23.4 3.4 %collective-permute-start.5 = (f32[24,128]{1,0:T(8,128)S(1)}, f32[24,128]{1,0:T(8,128)S(1)}, u32[]{:S(2)}, u32[]{:S(2)}) collective-permute-start(f32[24,128]{1,0:T(8,128)S(1)} %get-tuple-element.28.refs_0_), channel_id=1, source_target_pairs={{0,16},{4,20},{8,24},{12,28},{16,0},{20,4},{24,8},{28,12},{1,17},{... | collective-permute-start | bytes 36872 | tf_op jit(solution)/shard_map/ppermute | solution.py:802
  23.4 3.4 %collective-permute-start.4 = (f32[24,128]{1,0:T(8,128)S(1)}, f32[24,128]{1,0:T(8,128)S(1)}, u32[]{:S(2)}, u32[]{:S(2)}) collective-permute-start(f32[24,128]{1,0:T(8,128)S(1)} %get-tuple-element.28.refs_0_), channel_id=1, source_target_pairs={{0,8},{4,12},{8,0},{12,4},{16,24},{20,28},{24,16},{28,20},{1,9},{5... | collective-permute-start | bytes 36872 | tf_op jit(solution)/shard_map/ppermute | solution.py:802
  26.9 7.6 %collective-permute-start.9 = (f32[96,128]{1,0:T(8,128)S(1)}, f32[96,128]{1,0:T(8,128)S(1)}, u32[]{:S(2)}, u32[]{:S(2)}) collective-permute-start(f32[96,128]{1,0:T(8,128)S(1)} %bitcast.3), channel_id=1, source_target_pairs={{0,6},{1,7},{2,4},{3,5},{4,2},{5,3},{6,0},{7,1},{8,14},{9,15},{10,... | collective-permute-start | bytes 147464 | tf_op jit(solution)/shard_map/ppermute | solution.py:821
  27.0 5.2 %collective-permute-start.7 = (f32[96,128]{1,0:T(8,128)S(1)}, f32[96,128]{1,0:T(8,128)S(1)}, u32[]{:S(2)}, u32[]{:S(2)}) collective-permute-start(f32[96,128]{1,0:T(8,128)S(1)} %bitcast.4), channel_id=1, source_target_pairs={{0,2},{1,3},{2,0},{3,1},{4,6},{5,7},{6,4},{7,5},{8,10},{9,11},{10,... | collective-permute-start | bytes 147464 | tf_op jit(solution)/shard_map/ppermute | solution.py:821
  28.0 4.3 %collective-permute-start.10 = (f32[96,128]{1,0:T(8,128)S(1)}, f32[96,128]{1,0:T(8,128)S(1)}, u32[]{:S(2)}, u32[]{:S(2)}) collective-permute-start(f32[96,128]{1,0:T(8,128)S(1)} %get-tuple-element.55), channel_id=1, source_target_pairs={{4,8},{8,4},{12,16},{16,12},{20,24},{24,20},{5,9},{9,5},{13,17},{1... | collective-permute-start | bytes 147464 | tf_op jit(solution)/shard_map/ppermute | solution.py:865
  28.6 5.7 %collective-permute-start.8 = (f32[192,128]{1,0:T(8,128)S(1)}, f32[192,128]{1,0:T(8,128)S(1)}, u32[]{:S(2)}, u32[]{:S(2)}) collective-permute-start(f32[192,128]{1,0:T(8,128)S(1)} %pad_maximum_fusion.2), channel_id=1, source_target_pairs={{0,4},{1,5},{2,6},{3,7},{4,0},{5,1},{6,2},{7,3},{8,12},{9,13},{10,... | collective-permute-start | bytes 294920 | tf_op jit(solution)/shard_map/ppermute | solution.py:817
  34.5 6.7 %collective-permute-start.11 = (f32[552,128]{1,0:T(8,128)S(1)}, f32[552,128]{1,0:T(8,128)S(1)}, u32[]{:S(2)}, u32[]{:S(2)}) collective-permute-start(f32[552,128]{1,0:T(8,128)S(1)} %get-tuple-element.48), channel_id=1, source_target_pairs={{0,1},{1,0},{2,3},{3,2},{4,5},{5,4},{6,7},{7,6},{8,9},{9,8},{10,11... | collective-permute-start | bytes 847880 | tf_op jit(solution)/shard_map/ppermute | solution.py:872
  37.6 6.7 %collective-permute-start.12 = (f32[168,128]{1,0:T(8,128)S(1)}, f32[168,128]{1,0:T(8,128)S(1)}, u32[]{:S(2)}, u32[]{:S(2)}) collective-permute-start(f32[168,128]{1,0:T(8,128)S(1)} %get-tuple-element.47), channel_id=1, source_target_pairs={{1,2},{2,1},{5,6},{6,5},{9,10},{10,9},{13,14},{14,13},{17,18},{18,... | collective-permute-start | bytes 258056 | tf_op jit(solution)/shard_map/ppermute | solution.py:871

commit v17 on v16

--- a/solution.py
+++ b/solution.py
@@ -290,8 +290,9 @@
     for slot in (FX, FY, ZL, ZH, W, D):
         mid[slot] = jnp.zeros(mid.shape[1:], F32)
     x, y, z = coarse_slab_sums(top.at[FX], top.at[FY], top.at[ZL], coarse_x + 2, EDGE - 2, wide)
-    mid[FX, near : near + coarse_x + 3, RIM : 3 * RIM + coarse_y] = halved(x)
-    mid[FY, near : near + coarse_x + 2, RIM : 3 * RIM + coarse_y] = halved(y)
+    both = halved(jnp.concatenate((x, y)))
+    mid[FX, near : near + coarse_x + 3, RIM : 3 * RIM + coarse_y] = both[: coarse_x + 3]
+    mid[FY, near : near + coarse_x + 2, RIM : 3 * RIM + coarse_y] = both[coarse_x + 3 :]
     mid[ZL, near : near + coarse_x + 2, RIM : 3 * RIM + coarse_y] = halved(z, True)
 
     row_inside = (rows_of((rows, LANES)) >= RIM) | (me_y > 0)
@@ -377,9 +378,10 @@
     chunk[coarse_rows : coarse_rows + quarter_rows] = 0.5 * fold_four(rest_of)
     chunk[coarse_rows + quarter_rows :] = coefficients[:BLOCK_ROWS - coarse_rows - quarter_rows]
     block = me_x // (lax.axis_size(axes[0]) // 4)
-    values = chunk[...]
+    values = turned = chunk[...]
     for turn in range(1, 4):
-        chunk[...] = jnp.where(block == turn, roll_lanes(values, turn * (LANES // 4)), chunk[...])
+        turned = jnp.where(block == turn, roll_lanes(values, turn * (LANES // 4)), turned)
+    chunk[...] = turned
 
 
 def pack_v(top, kept, faces, x_low, x_high, low, high):

time: 46.6 us -> 46.5 us (level)
  no operation moved by 1% of the time
where the time goes in v17:
time: 46.5 us; the launch traced here: 46.1 us
  starting transfers between devices  25.5 us (55%)
  waiting for transfers between devices  11 us (24%)
  Pallas kernels  9.17 us (20%)
    pallas_call x8, Pallas kernels, launch(): pl.pallas_call(kernel, out_shape=[pltpu.VMEM(shape, F32) for shape in out...  7.44 us
    ppermute x3, starting transfers between devices, passed_round(): lax.ppermute(block, axis, [(i, i ^ distance) for i in range(count)])  4.69 us
    ppermute x2, starting transfers between devices, from_sides(): pair = lax.ppermute(pair, axis, pair_route(axis))  4.69 us
    ppermute x2, starting transfers between devices, from_sides(): swap = lax.ppermute(swap, axis, swap_route(axis))  4.23 us
    ppermute x2, waiting for transfers between devices, from_sides(): pair = lax.ppermute(pair, axis, pair_route(axis))  4.13 us
    ppermute x1, starting transfers between devices, passed_across(): both = lax.ppermute(jnp.concatenate((block, rider)), ('gx', 'gy'), route)  3.56 us
    ppermute x1, starting transfers between devices, fused_cycle(): swap = lax.ppermute(swap, 'gy', swap_route('gy'))  3.55 us
    ppermute x3, waiting for transfers between devices, passed_round(): lax.ppermute(block, axis, [(i, i ^ distance) for i in range(count)])  3.08 us
  transfers between devices with their start and end apart: 13, of which 5 were waited for; matrix products, arithmetic and copies ran while one was open for 0% of the time, Pallas kernels for 9%

profile of v17, /device:TPU:1, one launch (start us, length us, event | category | flops | bytes accessed | tf_op | source)
XLA Modules:
  0.0 46.1 jit_solution(13332849737560693714)
XLA Ops:
  0.0 1.2 %shard_map.55 = (f32[5,16,16,128]{3,2,1,0:T(8,128)S(1)}, f32[192,128]{1,0:T(8,128)S(1)}, f32[192,128]{1,0:T(8,128)S(1)}) custom-call(f32[16,16,128]{2,1,0:T(8,128)} %refs_0_.1, f32[16,16,128]{2,1,0:T(8,128)} %refs_1_.1, f32[16,16,128]{2,1,0:T(8,128)} %refs_2_.1, f32[16,16,128]{2,1,0:T(8,128)} %refs_3_.1, f32[16,16,128]{2,1,0:T(8,128)} %refs_4_.1), custom_call_target="tpu_custom_call" | custom-call | tf_op jit(solution)/shard_map/pallas_call | solution.py:768
  1.2 0.7 %collective-permute-start.1 = (f32[192,128]{1,0:T(8,128)S(1)}, f32[192,128]{1,0:T(8,128)S(1)}, u32[]{:S(2)}, u32[]{:S(2)}) collective-permute-start(f32[192,128]{1,0:T(8,128)S(1)} %get-tuple-element.45), channel_id=1, source_target_pairs={{4,8},{8,4},{12,16},{16,12},{20,24},{24,20},{5,9},{9,5},{13,17},{1... | collective-permute-start | bytes 294920 | tf_op jit(solution)/shard_map/ppermute | solution.py:797
  1.9 4.6 %collective-permute-start = (f32[192,128]{1,0:T(8,128)S(1)}, f32[192,128]{1,0:T(8,128)S(1)}, u32[]{:S(2)}, u32[]{:S(2)}) collective-permute-start(f32[192,128]{1,0:T(8,128)S(1)} %get-tuple-element.46), channel_id=1, source_target_pairs={{0,4},{4,0},{8,12},{12,8},{16,20},{20,16},{24,28},{28,24},{1,5},{5... | collective-permute-start | bytes 294920 | tf_op jit(solution)/shard_map/ppermute | solution.py:796
  6.5 0.0 collective-permute-done.1
  6.5 4.1 %collective-permute-done = f32[192,128]{1,0:T(8,128)S(1)} collective-permute-done((f32[192,128]{1,0:T(8,128)S(1)}, f32[192,128]{1,0:T(8,128)S(1)}, u32[]{:S(2)}, u32[]{:S(2)}) %collective-permute-start) | collective-permute-done | bytes 98336 | tf_op jit(solution)/shard_map/ppermute | solution.py:796
  10.7 0.1 shard_map.57
  10.8 3.6 %collective-permute-start.3 = (f32[232,128]{1,0:T(8,128)S(1)}, f32[232,128]{1,0:T(8,128)S(1)}, u32[]{:S(2)}, u32[]{:S(2)}) collective-permute-start(f32[232,128]{1,0:T(8,128)S(1)} %get-tuple-element.41), channel_id=1, source_target_pairs={{1,2},{2,1},{5,6},{6,5},{9,10},{10,9},{13,14},{14,13},{17,18},{18,... | collective-permute-start | bytes 356360 | tf_op jit(solution)/shard_map/ppermute | solution.py:797
  14.4 0.1 collective-permute-start.2
  14.4 0.8 %shard_map.56 = (f32[3,8,8,128]{3,2,1,0:T(8,128)S(1)}, f32[16,128]{1,0:T(8,128)S(1)}) custom-call(f32[5,16,16,128]{3,2,1,0:T(8,128)S(1)} %get-tuple-element.21.own), custom_call_target="tpu_custom_call" | custom-call | tf_op jit(solution)/shard_map/pallas_call | solution.py:768
  15.3 1.7 %collective-permute-done.3 = f32[232,128]{1,0:T(8,128)S(1)} collective-permute-done((f32[232,128]{1,0:T(8,128)S(1)}, f32[232,128]{1,0:T(8,128)S(1)}, u32[]{:S(2)}, u32[]{:S(2)}) %collective-permute-start.3) | collective-permute-done | bytes 118816 | tf_op jit(solution)/shard_map/ppermute | solution.py:797
  16.9 0.0 collective-permute-done.2
  17.0 2.1 %shard_map.58 = (f32[8,22,32,128]{3,2,1,0:T(8,128)S(1)}, f32[2,8,8,128]{3,2,1,0:T(8,128)S(1)}, f32[24,128]{1,0:T(8,128)S(1)}, f32[96,128]{1,0:T(8,128)S(1)}, f32[96,128]{1,0:T(8,128)S(1)}) custom-call(f32[5,16,16,128]{3,2,1,0:T(8,128)S(1)} %get-tuple-element.21.own, f32[3,8,8,128]{3,2,1,0:T(8,128)S(1)} %get-tuple-element.22.faces, ...), custom_call_target="tpu_custom_call" | custom-call | tf_op jit(solution)/shard_map/pallas_call | solution.py:768
  19.1 4.3 %collective-permute-start.6 = (f32[24,128]{1,0:T(8,128)S(1)}, f32[24,128]{1,0:T(8,128)S(1)}, u32[]{:S(2)}, u32[]{:S(2)}) collective-permute-start(f32[24,128]{1,0:T(8,128)S(1)} %get-tuple-element.28.refs_0_), channel_id=1, source_target_pairs={{0,24},{4,28},{8,16},{12,20},{16,8},{20,12},{24,0},{28,4},{1,25},{... | collective-permute-start | bytes 36872 | tf_op jit(solution)/shard_map/ppermute | solution.py:804
  23.4 0.0 collective-permute-start.5
  23.4 0.4 collective-permute-start.4
  23.8 0.7 %collective-permute-done.6.refs_3_ = f32[24,128]{1,0:T(8,128)S(1)} collective-permute-done((f32[24,128]{1,0:T(8,128)S(1)}, f32[24,128]{1,0:T(8,128)S(1)}, u32[]{:S(2)}, u32[]{:S(2)}) %collective-permute-start.6) | collective-permute-done | bytes 12320 | tf_op jit(solution)/shard_map/ppermute | solution.py:804
  24.5 2.4 %collective-permute-done.5.refs_2_ = f32[24,128]{1,0:T(8,128)S(1)} collective-permute-done((f32[24,128]{1,0:T(8,128)S(1)}, f32[24,128]{1,0:T(8,128)S(1)}, u32[]{:S(2)}, u32[]{:S(2)}) %collective-permute-start.5) | collective-permute-done | bytes 12320 | tf_op jit(solution)/shard_map/ppermute | solution.py:804
  26.9 0.0 collective-permute-done.4.refs_1_
  26.9 0.1 collective-permute-start.9
  26.9 0.9 %collective-permute-start.7 = (f32[96,128]{1,0:T(8,128)S(1)}, f32[96,128]{1,0:T(8,128)S(1)}, u32[]{:S(2)}, u32[]{:S(2)}) collective-permute-start(f32[96,128]{1,0:T(8,128)S(1)} %bitcast.4), channel_id=1, source_target_pairs={{0,2},{1,3},{2,0},{3,1},{4,6},{5,7},{6,4},{7,5},{8,10},{9,11},{10,... | collective-permute-start | bytes 147464 | tf_op jit(solution)/shard_map/ppermute | solution.py:823
  27.9 0.7 %collective-permute-start.10 = (f32[96,128]{1,0:T(8,128)S(1)}, f32[96,128]{1,0:T(8,128)S(1)}, u32[]{:S(2)}, u32[]{:S(2)}) collective-permute-start(f32[96,128]{1,0:T(8,128)S(1)} %get-tuple-element.55), channel_id=1, source_target_pairs={{4,8},{8,4},{12,16},{16,12},{20,24},{24,20},{5,9},{9,5},{13,17},{1... | collective-permute-start | bytes 147464 | tf_op jit(solution)/shard_map/ppermute | solution.py:867
  28.6 3.6 %collective-permute-start.8 = (f32[192,128]{1,0:T(8,128)S(1)}, f32[192,128]{1,0:T(8,128)S(1)}, u32[]{:S(2)}, u32[]{:S(2)}) collective-permute-start(f32[192,128]{1,0:T(8,128)S(1)} %pad_maximum_fusion.2), channel_id=1, source_target_pairs={{0,4},{1,5},{2,6},{3,7},{4,0},{5,1},{6,2},{7,3},{8,12},{9,13},{10,... | collective-permute-start | bytes 294920 | tf_op jit(solution)/shard_map/ppermute | solution.py:819
  32.2 0.0 collective-permute-done.7
  32.2 0.0 collective-permute-done.10
  32.2 2.1 %collective-permute-done.8 = f32[192,128]{1,0:T(8,128)S(1)} collective-permute-done((f32[192,128]{1,0:T(8,128)S(1)}, f32[192,128]{1,0:T(8,128)S(1)}, u32[]{:S(2)}, u32[]{:S(2)}) %collective-permute-start.8) | collective-permute-done | bytes 98336 | tf_op jit(solution)/shard_map/ppermute | solution.py:819
  34.3 0.1 shard_map.61
  34.5 0.0 collective-permute-done.9
  34.5 3.1 %collective-permute-start.11 = (f32[552,128]{1,0:T(8,128)S(1)}, f32[552,128]{1,0:T(8,128)S(1)}, u32[]{:S(2)}, u32[]{:S(2)}) collective-permute-start(f32[552,128]{1,0:T(8,128)S(1)} %get-tuple-element.48), channel_id=1, source_target_pairs={{0,1},{1,0},{2,3},{3,2},{4,5},{5,4},{6,7},{7,6},{8,9},{9,8},{10,11... | collective-permute-start | bytes 847880 | tf_op jit(solution)/shard_map/ppermute | solution.py:874
  37.6 3.5 %collective-permute-start.12 = (f32[168,128]{1,0:T(8,128)S(1)}, f32[168,128]{1,0:T(8,128)S(1)}, u32[]{:S(2)}, u32[]{:S(2)}) collective-permute-start(f32[168,128]{1,0:T(8,128)S(1)} %get-tuple-element.47), channel_id=1, source_target_pairs={{1,2},{2,1},{5,6},{6,5},{9,10},{10,9},{13,14},{14,13},{17,18},{18,... | collective-permute-start | bytes 258056 | tf_op jit(solution)/shard_map/ppermute | solution.py:873
  41.2 0.0 collective-permute-done.11
  41.2 3.1 %shard_map.62.coarse = f32[12,32,128]{2,1,0:T(8,128)S(1)} custom-call(f32[2,4,4,24,128]{4,3,2,1,0:T(8,128)S(1)} %pad_maximum_fusion.pieces), custom_call_target="tpu_custom_call" | custom-call | tf_op jit(solution)/shard_map/pallas_call | solution.py:768
  44.3 0.0 collective-permute-done.12
  44.3 1.7 %shard_map.63 = f32[16,16,128]{2,1,0:T(8,128)} custom-call(f32[12,32,128]{2,1,0:T(8,128)S(1)} %shard_map.62.coarse, f32[8,22,32,128]{3,2,1,0:T(8,128)S(1)} %get-tuple-element.33.top, f32[2,8,8,128]{3,2,1,0:T(8,128)S(1)} %get-tuple-element.34.kept, f32[3,8,8,128]{3,2,1,0:T(8,128)S(1)} %get-tuple-element.22.faces, f32[96,128]{1,0:T(8,128)S(1)} %get-tuple-element.53.x_low, ...), custom_call_target="tpu_custom_call" | custom-call | tf_op jit(solution)/shard_map/pallas_call | solution.py:888
  (17 shorter events, 0.2 us)
Async XLA Ops:
  1.2 5.3 %collective-permute-start.1 = (f32[192,128]{1,0:T(8,128)S(1)}, f32[192,128]{1,0:T(8,128)S(1)}, u32[]{:S(2)}, u32[]{:S(2)}) collective-permute-start(f32[192,128]{1,0:T(8,128)S(1)} %get-tuple-element.45), channel_id=1, source_target_pairs={{4,8},{8,4},{12,16},{16,12},{20,24},{24,20},{5,9},{9,5},{13,17},{1... | collective-permute-start | bytes 294920 | tf_op jit(solution)/shard_map/ppermute | solution.py:797
  1.9 8.7 %collective-permute-start = (f32[192,128]{1,0:T(8,128)S(1)}, f32[192,128]{1,0:T(8,128)S(1)}, u32[]{:S(2)}, u32[]{:S(2)}) collective-permute-start(f32[192,128]{1,0:T(8,128)S(1)} %get-tuple-element.46), channel_id=1, source_target_pairs={{0,4},{4,0},{8,12},{12,8},{16,20},{20,16},{24,28},{28,24},{1,5},{5... | collective-permute-start | bytes 294920 | tf_op jit(solution)/shard_map/ppermute | solution.py:796
  10.8 6.2 %collective-permute-start.3 = (f32[232,128]{1,0:T(8,128)S(1)}, f32[232,128]{1,0:T(8,128)S(1)}, u32[]{:S(2)}, u32[]{:S(2)}) collective-permute-start(f32[232,128]{1,0:T(8,128)S(1)} %get-tuple-element.41), channel_id=1, source_target_pairs={{1,2},{2,1},{5,6},{6,5},{9,10},{10,9},{13,14},{14,13},{17,18},{18,... | collective-permute-start | bytes 356360 | tf_op jit(solution)/shard_map/ppermute | solution.py:797
  14.4 2.6 %collective-permute-start.2 = (f32[232,128]{1,0:T(8,128)S(1)}, f32[232,128]{1,0:T(8,128)S(1)}, u32[]{:S(2)}, u32[]{:S(2)}) collective-permute-start(f32[232,128]{1,0:T(8,128)S(1)} %get-tuple-element.42), channel_id=1, source_target_pairs={{0,1},{1,0},{2,3},{3,2},{4,5},{5,4},{6,7},{7,6},{8,9},{9,8},{10,11... | collective-permute-start | bytes 356360 | tf_op jit(solution)/shard_map/ppermute | solution.py:796
  19.1 5.4 %collective-permute-start.6 = (f32[24,128]{1,0:T(8,128)S(1)}, f32[24,128]{1,0:T(8,128)S(1)}, u32[]{:S(2)}, u32[]{:S(2)}) collective-permute-start(f32[24,128]{1,0:T(8,128)S(1)} %get-tuple-element.28.refs_0_), channel_id=1, source_target_pairs={{0,24},{4,28},{8,16},{12,20},{16,8},{20,12},{24,0},{28,4},{1,25},{... | collective-permute-start | bytes 36872 | tf_op jit(solution)/shard_map/ppermute | solution.py:804
  23.4 3.4 %collective-permute-start.5 = (f32[24,128]{1,0:T(8,128)S(1)}, f32[24,128]{1,0:T(8,128)S(1)}, u32[]{:S(2)}, u32[]{:S(2)}) collective-permute-start(f32[24,128]{1,0:T(8,128)S(1)} %get-tuple-element.28.refs_0_), channel_id=1, source_target_pairs={{0,16},{4,20},{8,24},{12,28},{16,0},{20,4},{24,8},{28,12},{1,17},{... | collective-permute-start | bytes 36872 | tf_op jit(solution)/shard_map/ppermute | solution.py:804
  23.4 3.4 %collective-permute-start.4 = (f32[24,128]{1,0:T(8,128)S(1)}, f32[24,128]{1,0:T(8,128)S(1)}, u32[]{:S(2)}, u32[]{:S(2)}) collective-permute-start(f32[24,128]{1,0:T(8,128)S(1)} %get-tuple-element.28.refs_0_), channel_id=1, source_target_pairs={{0,8},{4,12},{8,0},{12,4},{16,24},{20,28},{24,16},{28,20},{1,9},{5... | collective-permute-start | bytes 36872 | tf_op jit(solution)/shard_map/ppermute | solution.py:804
  26.9 7.6 %collective-permute-start.9 = (f32[96,128]{1,0:T(8,128)S(1)}, f32[96,128]{1,0:T(8,128)S(1)}, u32[]{:S(2)}, u32[]{:S(2)}) collective-permute-start(f32[96,128]{1,0:T(8,128)S(1)} %bitcast.3), channel_id=1, source_target_pairs={{0,6},{1,7},{2,4},{3,5},{4,2},{5,3},{6,0},{7,1},{8,14},{9,15},{10,... | collective-permute-start | bytes 147464 | tf_op jit(solution)/shard_map/ppermute | solution.py:823
  26.9 5.2 %collective-permute-start.7 = (f32[96,128]{1,0:T(8,128)S(1)}, f32[96,128]{1,0:T(8,128)S(1)}, u32[]{:S(2)}, u32[]{:S(2)}) collective-permute-start(f32[96,128]{1,0:T(8,128)S(1)} %bitcast.4), channel_id=1, source_target_pairs={{0,2},{1,3},{2,0},{3,1},{4,6},{5,7},{6,4},{7,5},{8,10},{9,11},{10,... | collective-permute-start | bytes 147464 | tf_op jit(solution)/shard_map/ppermute | solution.py:823
  27.9 4.3 %collective-permute-start.10 = (f32[96,128]{1,0:T(8,128)S(1)}, f32[96,128]{1,0:T(8,128)S(1)}, u32[]{:S(2)}, u32[]{:S(2)}) collective-permute-start(f32[96,128]{1,0:T(8,128)S(1)} %get-tuple-element.55), channel_id=1, source_target_pairs={{4,8},{8,4},{12,16},{16,12},{20,24},{24,20},{5,9},{9,5},{13,17},{1... | collective-permute-start | bytes 147464 | tf_op jit(solution)/shard_map/ppermute | solution.py:867
  28.6 5.7 %collective-permute-start.8 = (f32[192,128]{1,0:T(8,128)S(1)}, f32[192,128]{1,0:T(8,128)S(1)}, u32[]{:S(2)}, u32[]{:S(2)}) collective-permute-start(f32[192,128]{1,0:T(8,128)S(1)} %pad_maximum_fusion.2), channel_id=1, source_target_pairs={{0,4},{1,5},{2,6},{3,7},{4,0},{5,1},{6,2},{7,3},{8,12},{9,13},{10,... | collective-permute-start | bytes 294920 | tf_op jit(solution)/shard_map/ppermute | solution.py:819
  34.5 6.7 %collective-permute-start.11 = (f32[552,128]{1,0:T(8,128)S(1)}, f32[552,128]{1,0:T(8,128)S(1)}, u32[]{:S(2)}, u32[]{:S(2)}) collective-permute-start(f32[552,128]{1,0:T(8,128)S(1)} %get-tuple-element.48), channel_id=1, source_target_pairs={{0,1},{1,0},{2,3},{3,2},{4,5},{5,4},{6,7},{7,6},{8,9},{9,8},{10,11... | collective-permute-start | bytes 847880 | tf_op jit(solution)/shard_map/ppermute | solution.py:874
  37.6 6.7 %collective-permute-start.12 = (f32[168,128]{1,0:T(8,128)S(1)}, f32[168,128]{1,0:T(8,128)S(1)}, u32[]{:S(2)}, u32[]{:S(2)}) collective-permute-start(f32[168,128]{1,0:T(8,128)S(1)} %get-tuple-element.47), channel_id=1, source_target_pairs={{1,2},{2,1},{5,6},{6,5},{9,10},{10,9},{13,14},{14,13},{17,18},{18,... | collective-permute-start | bytes 258056 | tf_op jit(solution)/shard_map/ppermute | solution.py:873

commit v18 on v16

--- a/solution.py
+++ b/solution.py
@@ -566,8 +566,7 @@
         slow, far = (me_x // 2) ^ (gx // 2), (me_y // 2) ^ (gy // 2)
         return ((me_y + gy) % 2, (me_x + gx) % 2 * (devices_y // 2) + far, slow)
 
-    for ref in (wide, tall):
-        ref[...] = jnp.zeros(ref.shape, F32)
+    tall[...] = jnp.zeros(tall.shape, F32)
     per_block = count // own_x
 
     def merged(values, shift, turn):

time: 46.6 us -> 46.6 us (level)
  no operation moved by 1% of the time
where the time goes in v18:
time: 46.6 us; the launch traced here: 46.1 us
  starting transfers between devices  25.5 us (55%)
  waiting for transfers between devices  11 us (24%)
  Pallas kernels  9.14 us (20%)
    pallas_call x8, Pallas kernels, launch(): pl.pallas_call(kernel, out_shape=[pltpu.VMEM(shape, F32) for shape in out...  7.41 us
    ppermute x3, starting transfers between devices, passed_round(): lax.ppermute(block, axis, [(i, i ^ distance) for i in range(count)])  4.74 us
    ppermute x2, starting transfers between devices, from_sides(): pair = lax.ppermute(pair, axis, pair_route(axis))  4.69 us
    ppermute x2, starting transfers between devices, from_sides(): swap = lax.ppermute(swap, axis, swap_route(axis))  4.23 us
    ppermute x2, waiting for transfers between devices, from_sides(): pair = lax.ppermute(pair, axis, pair_route(axis))  4.13 us
    ppermute x1, starting transfers between devices, passed_across(): both = lax.ppermute(jnp.concatenate((block, rider)), ('gx', 'gy'), route)  3.56 us
    ppermute x1, starting transfers between devices, fused_cycle(): swap = lax.ppermute(swap, 'gy', swap_route('gy'))  3.55 us
    ppermute x3, waiting for transfers between devices, passed_round(): lax.ppermute(block, axis, [(i, i ^ distance) for i in range(count)])  3.08 us
  transfers between devices with their start and end apart: 13, of which 5 were waited for; matrix products, arithmetic and copies ran while one was open for 0% of the time, Pallas kernels for 9%

profile of v18, /device:TPU:1, one launch (start us, length us, event | category | flops | bytes accessed | tf_op | source)
XLA Modules:
  0.0 46.1 jit_solution(7005974696363527727)
XLA Ops:
  0.0 1.2 %shard_map.55 = (f32[5,16,16,128]{3,2,1,0:T(8,128)S(1)}, f32[192,128]{1,0:T(8,128)S(1)}, f32[192,128]{1,0:T(8,128)S(1)}) custom-call(f32[16,16,128]{2,1,0:T(8,128)} %refs_0_.1, f32[16,16,128]{2,1,0:T(8,128)} %refs_1_.1, f32[16,16,128]{2,1,0:T(8,128)} %refs_2_.1, f32[16,16,128]{2,1,0:T(8,128)} %refs_3_.1, f32[16,16,128]{2,1,0:T(8,128)} %refs_4_.1), custom_call_target="tpu_custom_call" | custom-call | tf_op jit(solution)/shard_map/pallas_call | solution.py:765
  1.2 0.7 %collective-permute-start.1 = (f32[192,128]{1,0:T(8,128)S(1)}, f32[192,128]{1,0:T(8,128)S(1)}, u32[]{:S(2)}, u32[]{:S(2)}) collective-permute-start(f32[192,128]{1,0:T(8,128)S(1)} %get-tuple-element.45), channel_id=1, source_target_pairs={{4,8},{8,4},{12,16},{16,12},{20,24},{24,20},{5,9},{9,5},{13,17},{1... | collective-permute-start | bytes 294920 | tf_op jit(solution)/shard_map/ppermute | solution.py:794
  1.9 4.6 %collective-permute-start = (f32[192,128]{1,0:T(8,128)S(1)}, f32[192,128]{1,0:T(8,128)S(1)}, u32[]{:S(2)}, u32[]{:S(2)}) collective-permute-start(f32[192,128]{1,0:T(8,128)S(1)} %get-tuple-element.46), channel_id=1, source_target_pairs={{0,4},{4,0},{8,12},{12,8},{16,20},{20,16},{24,28},{28,24},{1,5},{5... | collective-permute-start | bytes 294920 | tf_op jit(solution)/shard_map/ppermute | solution.py:793
  6.5 0.0 collective-permute-done.1
  6.5 4.1 %collective-permute-done = f32[192,128]{1,0:T(8,128)S(1)} collective-permute-done((f32[192,128]{1,0:T(8,128)S(1)}, f32[192,128]{1,0:T(8,128)S(1)}, u32[]{:S(2)}, u32[]{:S(2)}) %collective-permute-start) | collective-permute-done | bytes 98336 | tf_op jit(solution)/shard_map/ppermute | solution.py:793
  10.7 0.1 shard_map.57
  10.8 3.6 %collective-permute-start.3 = (f32[232,128]{1,0:T(8,128)S(1)}, f32[232,128]{1,0:T(8,128)S(1)}, u32[]{:S(2)}, u32[]{:S(2)}) collective-permute-start(f32[232,128]{1,0:T(8,128)S(1)} %get-tuple-element.41), channel_id=1, source_target_pairs={{1,2},{2,1},{5,6},{6,5},{9,10},{10,9},{13,14},{14,13},{17,18},{18,... | collective-permute-start | bytes 356360 | tf_op jit(solution)/shard_map/ppermute | solution.py:794
  14.4 0.1 collective-permute-start.2
  14.4 0.8 %shard_map.56 = (f32[3,8,8,128]{3,2,1,0:T(8,128)S(1)}, f32[16,128]{1,0:T(8,128)S(1)}) custom-call(f32[5,16,16,128]{3,2,1,0:T(8,128)S(1)} %get-tuple-element.21.own), custom_call_target="tpu_custom_call" | custom-call | tf_op jit(solution)/shard_map/pallas_call | solution.py:765
  15.3 1.7 %collective-permute-done.3 = f32[232,128]{1,0:T(8,128)S(1)} collective-permute-done((f32[232,128]{1,0:T(8,128)S(1)}, f32[232,128]{1,0:T(8,128)S(1)}, u32[]{:S(2)}, u32[]{:S(2)}) %collective-permute-start.3) | collective-permute-done | bytes 118816 | tf_op jit(solution)/shard_map/ppermute | solution.py:794
  16.9 0.0 collective-permute-done.2
  17.0 2.1 %shard_map.58 = (f32[8,22,32,128]{3,2,1,0:T(8,128)S(1)}, f32[2,8,8,128]{3,2,1,0:T(8,128)S(1)}, f32[24,128]{1,0:T(8,128)S(1)}, f32[96,128]{1,0:T(8,128)S(1)}, f32[96,128]{1,0:T(8,128)S(1)}) custom-call(f32[5,16,16,128]{3,2,1,0:T(8,128)S(1)} %get-tuple-element.21.own, f32[3,8,8,128]{3,2,1,0:T(8,128)S(1)} %get-tuple-element.22.faces, ...), custom_call_target="tpu_custom_call" | custom-call | tf_op jit(solution)/shard_map/pallas_call | solution.py:765
  19.1 4.4 %collective-permute-start.6 = (f32[24,128]{1,0:T(8,128)S(1)}, f32[24,128]{1,0:T(8,128)S(1)}, u32[]{:S(2)}, u32[]{:S(2)}) collective-permute-start(f32[24,128]{1,0:T(8,128)S(1)} %get-tuple-element.28.refs_0_), channel_id=1, source_target_pairs={{0,24},{4,28},{8,16},{12,20},{16,8},{20,12},{24,0},{28,4},{1,25},{... | collective-permute-start | bytes 36872 | tf_op jit(solution)/shard_map/ppermute | solution.py:801
  23.4 0.0 collective-permute-start.5
  23.4 0.4 collective-permute-start.4
  23.8 0.7 %collective-permute-done.6.refs_3_ = f32[24,128]{1,0:T(8,128)S(1)} collective-permute-done((f32[24,128]{1,0:T(8,128)S(1)}, f32[24,128]{1,0:T(8,128)S(1)}, u32[]{:S(2)}, u32[]{:S(2)}) %collective-permute-start.6) | collective-permute-done | bytes 12320 | tf_op jit(solution)/shard_map/ppermute | solution.py:801
  24.5 2.4 %collective-permute-done.5.refs_2_ = f32[24,128]{1,0:T(8,128)S(1)} collective-permute-done((f32[24,128]{1,0:T(8,128)S(1)}, f32[24,128]{1,0:T(8,128)S(1)}, u32[]{:S(2)}, u32[]{:S(2)}) %collective-permute-start.5) | collective-permute-done | bytes 12320 | tf_op jit(solution)/shard_map/ppermute | solution.py:801
  26.9 0.0 collective-permute-done.4.refs_1_
  26.9 0.1 collective-permute-start.9
  27.0 0.9 %collective-permute-start.7 = (f32[96,128]{1,0:T(8,128)S(1)}, f32[96,128]{1,0:T(8,128)S(1)}, u32[]{:S(2)}, u32[]{:S(2)}) collective-permute-start(f32[96,128]{1,0:T(8,128)S(1)} %bitcast.4), channel_id=1, source_target_pairs={{0,2},{1,3},{2,0},{3,1},{4,6},{5,7},{6,4},{7,5},{8,10},{9,11},{10,... | collective-permute-start | bytes 147464 | tf_op jit(solution)/shard_map/ppermute | solution.py:820
  28.0 0.7 %collective-permute-start.10 = (f32[96,128]{1,0:T(8,128)S(1)}, f32[96,128]{1,0:T(8,128)S(1)}, u32[]{:S(2)}, u32[]{:S(2)}) collective-permute-start(f32[96,128]{1,0:T(8,128)S(1)} %get-tuple-element.55), channel_id=1, source_target_pairs={{4,8},{8,4},{12,16},{16,12},{20,24},{24,20},{5,9},{9,5},{13,17},{1... | collective-permute-start | bytes 147464 | tf_op jit(solution)/shard_map/ppermute | solution.py:864
  28.6 3.6 %collective-permute-start.8 = (f32[192,128]{1,0:T(8,128)S(1)}, f32[192,128]{1,0:T(8,128)S(1)}, u32[]{:S(2)}, u32[]{:S(2)}) collective-permute-start(f32[192,128]{1,0:T(8,128)S(1)} %pad_maximum_fusion.2), channel_id=1, source_target_pairs={{0,4},{1,5},{2,6},{3,7},{4,0},{5,1},{6,2},{7,3},{8,12},{9,13},{10,... | collective-permute-start | bytes 294920 | tf_op jit(solution)/shard_map/ppermute | solution.py:816
  32.2 0.0 collective-permute-done.7
  32.2 0.0 collective-permute-done.10
  32.2 2.1 %collective-permute-done.8 = f32[192,128]{1,0:T(8,128)S(1)} collective-permute-done((f32[192,128]{1,0:T(8,128)S(1)}, f32[192,128]{1,0:T(8,128)S(1)}, u32[]{:S(2)}, u32[]{:S(2)}) %collective-permute-start.8) | collective-permute-done | bytes 98336 | tf_op jit(solution)/shard_map/ppermute | solution.py:816
  34.4 0.1 shard_map.61
  34.5 0.0 collective-permute-done.9
  34.5 3.1 %collective-permute-start.11 = (f32[552,128]{1,0:T(8,128)S(1)}, f32[552,128]{1,0:T(8,128)S(1)}, u32[]{:S(2)}, u32[]{:S(2)}) collective-permute-start(f32[552,128]{1,0:T(8,128)S(1)} %get-tuple-element.48), channel_id=1, source_target_pairs={{0,1},{1,0},{2,3},{3,2},{4,5},{5,4},{6,7},{7,6},{8,9},{9,8},{10,11... | collective-permute-start | bytes 847880 | tf_op jit(solution)/shard_map/ppermute | solution.py:871
  37.6 3.5 %collective-permute-start.12 = (f32[168,128]{1,0:T(8,128)S(1)}, f32[168,128]{1,0:T(8,128)S(1)}, u32[]{:S(2)}, u32[]{:S(2)}) collective-permute-start(f32[168,128]{1,0:T(8,128)S(1)} %get-tuple-element.47), channel_id=1, source_target_pairs={{1,2},{2,1},{5,6},{6,5},{9,10},{10,9},{13,14},{14,13},{17,18},{18,... | collective-permute-start | bytes 258056 | tf_op jit(solution)/shard_map/ppermute | solution.py:870
  41.2 0.0 collective-permute-done.11
  41.3 3.1 %shard_map.62.coarse = f32[12,32,128]{2,1,0:T(8,128)S(1)} custom-call(f32[2,4,4,24,128]{4,3,2,1,0:T(8,128)S(1)} %pad_maximum_fusion.pieces), custom_call_target="tpu_custom_call" | custom-call | tf_op jit(solution)/shard_map/pallas_call | solution.py:765
  44.3 0.0 collective-permute-done.12
  44.4 1.7 %shard_map.63 = f32[16,16,128]{2,1,0:T(8,128)} custom-call(f32[12,32,128]{2,1,0:T(8,128)S(1)} %shard_map.62.coarse, f32[8,22,32,128]{3,2,1,0:T(8,128)S(1)} %get-tuple-element.33.top, f32[2,8,8,128]{3,2,1,0:T(8,128)S(1)} %get-tuple-element.34.kept, f32[3,8,8,128]{3,2,1,0:T(8,128)S(1)} %get-tuple-element.22.faces, f32[96,128]{1,0:T(8,128)S(1)} %get-tuple-element.53.x_low, ...), custom_call_target="tpu_custom_call" | custom-call | tf_op jit(solution)/shard_map/pallas_call | solution.py:885
  (17 shorter events, 0.2 us)
Async XLA Ops:
  1.2 5.3 %collective-permute-start.1 = (f32[192,128]{1,0:T(8,128)S(1)}, f32[192,128]{1,0:T(8,128)S(1)}, u32[]{:S(2)}, u32[]{:S(2)}) collective-permute-start(f32[192,128]{1,0:T(8,128)S(1)} %get-tuple-element.45), channel_id=1, source_target_pairs={{4,8},{8,4},{12,16},{16,12},{20,24},{24,20},{5,9},{9,5},{13,17},{1... | collective-permute-start | bytes 294920 | tf_op jit(solution)/shard_map/ppermute | solution.py:794
  1.9 8.7 %collective-permute-start = (f32[192,128]{1,0:T(8,128)S(1)}, f32[192,128]{1,0:T(8,128)S(1)}, u32[]{:S(2)}, u32[]{:S(2)}) collective-permute-start(f32[192,128]{1,0:T(8,128)S(1)} %get-tuple-element.46), channel_id=1, source_target_pairs={{0,4},{4,0},{8,12},{12,8},{16,20},{20,16},{24,28},{28,24},{1,5},{5... | collective-permute-start | bytes 294920 | tf_op jit(solution)/shard_map/ppermute | solution.py:793
  10.8 6.2 %collective-permute-start.3 = (f32[232,128]{1,0:T(8,128)S(1)}, f32[232,128]{1,0:T(8,128)S(1)}, u32[]{:S(2)}, u32[]{:S(2)}) collective-permute-start(f32[232,128]{1,0:T(8,128)S(1)} %get-tuple-element.41), channel_id=1, source_target_pairs={{1,2},{2,1},{5,6},{6,5},{9,10},{10,9},{13,14},{14,13},{17,18},{18,... | collective-permute-start | bytes 356360 | tf_op jit(solution)/shard_map/ppermute | solution.py:794
  14.4 2.6 %collective-permute-start.2 = (f32[232,128]{1,0:T(8,128)S(1)}, f32[232,128]{1,0:T(8,128)S(1)}, u32[]{:S(2)}, u32[]{:S(2)}) collective-permute-start(f32[232,128]{1,0:T(8,128)S(1)} %get-tuple-element.42), channel_id=1, source_target_pairs={{0,1},{1,0},{2,3},{3,2},{4,5},{5,4},{6,7},{7,6},{8,9},{9,8},{10,11... | collective-permute-start | bytes 356360 | tf_op jit(solution)/shard_map/ppermute | solution.py:793
  19.1 5.5 %collective-permute-start.6 = (f32[24,128]{1,0:T(8,128)S(1)}, f32[24,128]{1,0:T(8,128)S(1)}, u32[]{:S(2)}, u32[]{:S(2)}) collective-permute-start(f32[24,128]{1,0:T(8,128)S(1)} %get-tuple-element.28.refs_0_), channel_id=1, source_target_pairs={{0,24},{4,28},{8,16},{12,20},{16,8},{20,12},{24,0},{28,4},{1,25},{... | collective-permute-start | bytes 36872 | tf_op jit(solution)/shard_map/ppermute | solution.py:801
  23.4 3.4 %collective-permute-start.5 = (f32[24,128]{1,0:T(8,128)S(1)}, f32[24,128]{1,0:T(8,128)S(1)}, u32[]{:S(2)}, u32[]{:S(2)}) collective-permute-start(f32[24,128]{1,0:T(8,128)S(1)} %get-tuple-element.28.refs_0_), channel_id=1, source_target_pairs={{0,16},{4,20},{8,24},{12,28},{16,0},{20,4},{24,8},{28,12},{1,17},{... | collective-permute-start | bytes 36872 | tf_op jit(solution)/shard_map/ppermute | solution.py:801
  23.4 3.4 %collective-permute-start.4 = (f32[24,128]{1,0:T(8,128)S(1)}, f32[24,128]{1,0:T(8,128)S(1)}, u32[]{:S(2)}, u32[]{:S(2)}) collective-permute-start(f32[24,128]{1,0:T(8,128)S(1)} %get-tuple-element.28.refs_0_), channel_id=1, source_target_pairs={{0,8},{4,12},{8,0},{12,4},{16,24},{20,28},{24,16},{28,20},{1,9},{5... | collective-permute-start | bytes 36872 | tf_op jit(solution)/shard_map/ppermute | solution.py:801
  26.9 7.6 %collective-permute-start.9 = (f32[96,128]{1,0:T(8,128)S(1)}, f32[96,128]{1,0:T(8,128)S(1)}, u32[]{:S(2)}, u32[]{:S(2)}) collective-permute-start(f32[96,128]{1,0:T(8,128)S(1)} %bitcast.3), channel_id=1, source_target_pairs={{0,6},{1,7},{2,4},{3,5},{4,2},{5,3},{6,0},{7,1},{8,14},{9,15},{10,... | collective-permute-start | bytes 147464 | tf_op jit(solution)/shard_map/ppermute | solution.py:820
  27.0 5.2 %collective-permute-start.7 = (f32[96,128]{1,0:T(8,128)S(1)}, f32[96,128]{1,0:T(8,128)S(1)}, u32[]{:S(2)}, u32[]{:S(2)}) collective-permute-start(f32[96,128]{1,0:T(8,128)S(1)} %bitcast.4), channel_id=1, source_target_pairs={{0,2},{1,3},{2,0},{3,1},{4,6},{5,7},{6,4},{7,5},{8,10},{9,11},{10,... | collective-permute-start | bytes 147464 | tf_op jit(solution)/shard_map/ppermute | solution.py:820
  28.0 4.3 %collective-permute-start.10 = (f32[96,128]{1,0:T(8,128)S(1)}, f32[96,128]{1,0:T(8,128)S(1)}, u32[]{:S(2)}, u32[]{:S(2)}) collective-permute-start(f32[96,128]{1,0:T(8,128)S(1)} %get-tuple-element.55), channel_id=1, source_target_pairs={{4,8},{8,4},{12,16},{16,12},{20,24},{24,20},{5,9},{9,5},{13,17},{1... | collective-permute-start | bytes 147464 | tf_op jit(solution)/shard_map/ppermute | solution.py:864
  28.6 5.7 %collective-permute-start.8 = (f32[192,128]{1,0:T(8,128)S(1)}, f32[192,128]{1,0:T(8,128)S(1)}, u32[]{:S(2)}, u32[]{:S(2)}) collective-permute-start(f32[192,128]{1,0:T(8,128)S(1)} %pad_maximum_fusion.2), channel_id=1, source_target_pairs={{0,4},{1,5},{2,6},{3,7},{4,0},{5,1},{6,2},{7,3},{8,12},{9,13},{10,... | collective-permute-start | bytes 294920 | tf_op jit(solution)/shard_map/ppermute | solution.py:816
  34.5 6.7 %collective-permute-start.11 = (f32[552,128]{1,0:T(8,128)S(1)}, f32[552,128]{1,0:T(8,128)S(1)}, u32[]{:S(2)}, u32[]{:S(2)}) collective-permute-start(f32[552,128]{1,0:T(8,128)S(1)} %get-tuple-element.48), channel_id=1, source_target_pairs={{0,1},{1,0},{2,3},{3,2},{4,5},{5,4},{6,7},{7,6},{8,9},{9,8},{10,11... | collective-permute-start | bytes 847880 | tf_op jit(solution)/shard_map/ppermute | solution.py:871
  37.6 6.7 %collective-permute-start.12 = (f32[168,128]{1,0:T(8,128)S(1)}, f32[168,128]{1,0:T(8,128)S(1)}, u32[]{:S(2)}, u32[]{:S(2)}) collective-permute-start(f32[168,128]{1,0:T(8,128)S(1)} %get-tuple-element.47), channel_id=1, source_target_pairs={{1,2},{2,1},{5,6},{6,5},{9,10},{10,9},{13,14},{14,13},{17,18},{18,... | collective-permute-start | bytes 258056 | tf_op jit(solution)/shard_map/ppermute | solution.py:870
